TPU v7x, 256 devices: a whole 4x4x8 slice. The times are simulated.
256 devices in a mesh: expert: 32 (over x, z), tensor: 4 (over y), dp: 2 (over core).
Axes of the slice: x: 4, y: 4, z: 8, core: 2. Of those that a mesh axis runs over, the one named last changes fastest.
Arguments:
- tokens: bfloat16 [32768, 5120], P(('dp', 'expert', 'tensor')), parts along dimension 0, may hold values from -6 to 6
- out_grad: bfloat16 [32768, 5120], P(('dp', 'expert', 'tensor')), parts along dimension 0, may hold values from -1.5 to 1.5
- gate: float32 [32768], P(('dp', 'expert', 'tensor')), parts along dimension 0, may hold values from 0.25 to 2
- route: int32 [32768, 1], P(('dp', 'expert', 'tensor')), parts along dimension 0, may hold values from 0 to 32; in each aligned block of 128 rows (0 to 127, 128 to 255, ...) at most 6 rows name the same one
- gate_weight: bfloat16 [32, 5120, 1024], P('expert', None, 'tensor'), may hold values from -0.078125 to 0.078125
- up_weight: bfloat16 [32, 5120, 1024], P('expert', None, 'tensor'), may hold values from -0.078125 to 0.078125
- down_weight: bfloat16 [32, 1024, 5120], P('expert', 'tensor'), may hold values from -0.1875 to 0.1875
Outputs:
- token_grad: bfloat16 [32768, 5120], P(('dp', 'expert', 'tensor')), parts along dimension 0
- gate_grad: bfloat16 [32768], P(('dp', 'expert', 'tensor')), parts along dimension 0
There are 2 independent parts, one for each index of `dp`. A program takes and returns all parts, laid end to end along the dimension named above; an argument that names none is the same for every part. Nothing has to cross between parts.
Inputs may be any that keep to these rules, and one draw needn't show every extreme that they name: `route`: id 32 is the no-op expert. Among the 128 rows of one device (aligned blocks), no id is named by more than 6 rows, a bound that some block reaches.
All inputs are finite; a program needn't handle non-finite values.
Results may differ from a plain program's by a relative error of at most 0.019.
Values may be sent and summed in bfloat16 or wider, within the bound.
No kernel may reach another device: no remote copies, remote signals or barrier semaphores. Data moves between devices by JAX's collectives and lax.ppermute only.
A program may use at most 128 MiB of HBM per device.

v0:
```python
import jax
import jax.numpy as jnp
from jax import lax
from jax.sharding import PartitionSpec as P


def silu_parts(value):
    sigmoid_value = jax.nn.sigmoid(value)
    return (value * sigmoid_value, sigmoid_value * (1.0 + value * (1.0 - sigmoid_value)))


def expert_grads(rows_x, rows_dy, w_gate, w_up, w_down):
    pre_gate = jnp.dot(rows_x, w_gate, preferred_element_type=jnp.float32)
    pre_up = jnp.dot(rows_x, w_up, preferred_element_type=jnp.float32)
    back_hidden = lax.dot_general(
        rows_dy, w_down, (((1,), (1,)), ((), ())), preferred_element_type=jnp.float32
    )
    activated, slope = silu_parts(pre_gate)
    gate_term = jnp.sum(activated * pre_up * back_hidden, axis=-1)
    grad_gate = (back_hidden * pre_up * slope).astype(jnp.bfloat16)
    grad_up = (back_hidden * activated).astype(jnp.bfloat16)
    grad_rows = lax.dot_general(
        grad_gate, w_gate, (((1,), (1,)), ((), ())), preferred_element_type=jnp.float32
    )
    grad_rows = grad_rows + lax.dot_general(
        grad_up, w_up, (((1,), (1,)), ((), ())), preferred_element_type=jnp.float32
    )
    return (grad_rows, gate_term)


def per_device(tokens, out_grad, gate, route, gate_weight, up_weight, down_weight):
    experts = lax.axis_size("expert")
    groups = lax.axis_size("tensor")
    tok_rows, width = tokens.shape
    capacity = max(2, 3 * tok_rows // (2 * (experts + 1)) + 1)
    expert_id = route[:, 0]
    routed = expert_id < experts
    onehot = (expert_id[:, None] == jnp.arange(experts + 1, dtype=jnp.int32)[None, :]).astype(
        jnp.int32
    )
    before = jnp.cumsum(onehot, axis=0) - onehot
    slot_index = jnp.sum(before * onehot, axis=1)
    target = jnp.where(routed, expert_id * capacity + slot_index, experts * capacity)
    places = jnp.arange(experts * capacity, dtype=jnp.int32)
    select = (places[:, None] == target[None, :]).astype(jnp.bfloat16)
    send_x = (
        jnp.dot(select, tokens, preferred_element_type=jnp.float32)
        .astype(jnp.bfloat16)
        .reshape(experts, capacity, width)
    )
    send_dy = (
        jnp.dot(select, out_grad, preferred_element_type=jnp.float32)
        .astype(jnp.bfloat16)
        .reshape(experts, capacity, width)
    )
    got_x, got_dy = (
        lax.all_to_all(send_x, "expert", split_axis=0, concat_axis=0, tiled=True),
        lax.all_to_all(send_dy, "expert", split_axis=0, concat_axis=0, tiled=True),
    )
    got_x, got_dy = (
        lax.all_gather(got_x[:, None], "tensor", axis=1, tiled=True),
        lax.all_gather(got_dy[:, None], "tensor", axis=1, tiled=True),
    )
    rows, terms = expert_grads(
        got_x.reshape(-1, width),
        got_dy.reshape(-1, width),
        gate_weight[0],
        up_weight[0],
        down_weight[0],
    )
    summed, term_sum = (
        lax.psum_scatter(
            rows.reshape(experts, groups, capacity, width).astype(jnp.bfloat16),
            "tensor",
            scatter_dimension=1,
            tiled=True,
        ).astype(jnp.float32),
        lax.psum_scatter(
            terms.reshape(experts, groups, capacity).astype(jnp.bfloat16),
            "tensor",
            scatter_dimension=1,
            tiled=True,
        ).astype(jnp.float32),
    )
    back_rows = summed.reshape(experts, capacity, width).astype(jnp.bfloat16)
    back_terms = term_sum.reshape(experts, capacity).astype(jnp.bfloat16)
    ret_rows, ret_terms = (
        lax.all_to_all(back_rows, "expert", split_axis=0, concat_axis=0, tiled=True),
        lax.all_to_all(back_terms, "expert", split_axis=0, concat_axis=0, tiled=True),
    )
    token_rows = lax.dot_general(
        select,
        ret_rows.reshape(experts * capacity, width),
        (((0,), (0,)), ((), ())),
        preferred_element_type=jnp.float32,
    )
    token_terms = lax.dot_general(
        select,
        ret_terms.reshape(experts * capacity),
        (((0,), (0,)), ((), ())),
        preferred_element_type=jnp.float32,
    )
    own_term = jnp.sum(out_grad.astype(jnp.float32) * tokens.astype(jnp.float32), axis=1)
    token_grad = jnp.where(
        routed[:, None], gate[:, None] * token_rows, gate[:, None] * out_grad.astype(jnp.float32)
    ).astype(jnp.bfloat16)
    gate_grad = jnp.where(routed, token_terms, own_term).astype(jnp.bfloat16)
    return (token_grad, gate_grad)


def solution(mesh):
    return jax.shard_map(
        per_device,
        mesh=mesh,
        in_specs=(
            P(("dp", "expert", "tensor"), None),
            P(("dp", "expert", "tensor"), None),
            P(("dp", "expert", "tensor")),
            P(("dp", "expert", "tensor"), None),
            P("expert", None, "tensor"),
            P("expert", None, "tensor"),
            P("expert", "tensor", None),
        ),
        out_specs=(P(("dp", "expert", "tensor"), None), P(("dp", "expert", "tensor"))),
        check_vma=False,
    )
```

profile of v0, /device:TPU:24, one launch (start us, length us, event | category | flops | bytes accessed | tf_op | source)
XLA Modules:
  0.0 484.0 jit_solution(17854989846845248969)
XLA Ops:
  7.2 0.0 copy-start
  7.2 0.0 all-gather.7.cloned.1.call-start
  7.2 0.9 fusion.17
  8.1 0.2 reduce_window_sum.11
  8.3 0.8 select_reduce_fusion
  9.1 0.7 compare_select_fusion
  9.8 3.2 convolution_convert_fusion
  13.0 4.1 reshape.48
  17.1 73.1 %all_to_all.21 = bf16[32,6,5120]{2,1,0:T(8,128)(2,1)S(1)} all-to-all(bf16[32,6,5120]{2,1,0:T(8,128)(2,1)} %reshape.48), channel_id=1, replica_groups=mesh['expert'=32,'tensor'=4,'dp'=2] {'expert'}, dimensions={0} | all-to-all | bytes 3932160 | tf_op jit(solution)/shard_map/all_to_all | solution.py:57
  90.3 2.3 copy.25
  92.6 0.0 all-gather.7.cloned.1.call-update
  92.6 0.0 all-gather.5.cloned.1.call-start
  92.7 3.2 convolution_convert_fusion.1
  95.9 4.1 reshape.46
  100.1 67.5 %all_to_all.22 = bf16[32,6,5120]{2,1,0:T(8,128)(2,1)S(1)} all-to-all(bf16[32,6,5120]{2,1,0:T(8,128)(2,1)} %reshape.46), channel_id=1, replica_groups=mesh['expert'=32,'tensor'=4,'dp'=2] {'expert'}, dimensions={0} | all-to-all | bytes 3932160 | tf_op jit(solution)/shard_map/all_to_all | solution.py:58
  167.5 2.4 copy.23
  170.0 0.0 all-gather.5.cloned.1.call-update
  170.0 0.2 reduce-scatter.2.cloned.1.call-start
  170.2 0.0 all-gather.7.cloned.1.call-done
  170.3 10.6 %copy.26 = bf16[32,24,5120]{2,1,0:T(8,128)(2,1)} copy(bf16[32,24,5120]{2,0,1:T(8,128)(2,1)} %all-gather.7.cloned.1.call-done) | data formatting | bytes 15728640 | tf_op jit(solution)/shard_map/all_gather | solution.py:61
  180.9 0.0 copy-done
  180.9 0.0 copy-start.2
  180.9 0.0 copy-start.5
  180.9 5.6 %fusion.5 = f32[768,256]{0,1:T(8,128)S(1)} fusion(bf16[768,5120]{1,0:T(8,128)(2,1)} %bitcast.38, bf16[1,5120,256]{2,1,0:T(8,128)(2,1)S(1)} %copy-done), kind=kOutput, calls=%fused_computation.11 | convolution fusion | flops 2013265920 | bytes 11272192 | tf_op jit(solution)/shard_map/dot_general | solution.py:13
  186.5 0.4 copy-done.2
  186.9 1.1 copy-done.5
  188.0 3.3 fusion.8
  191.3 62.6 %all-gather.5.cloned.1.call-done = bf16[32,24,5120]{2,0,1:T(8,128)(2,1)} async-done(((bf16[32,6,5120]{2,0,1:T(8,128)(2,1)}), bf16[32,24,5120]{2,0,1:T(8,128)(2,1)}) %all-gather.5.cloned.1.call-update) | async-done | bytes 7864336 | tf_op jit(solution)/shard_map/all_gather | solution.py:62
  253.9 11.0 %copy.24 = bf16[32,24,5120]{2,1,0:T(8,128)(2,1)} copy(bf16[32,24,5120]{2,0,1:T(8,128)(2,1)} %all-gather.5.cloned.1.call-done) | data formatting | bytes 15728640 | tf_op jit(solution)/shard_map/all_gather | solution.py:62
  264.9 0.0 copy-done.7
  264.9 0.0 copy-done.9
  264.9 5.6 %multiply_reduce_fusion = (bf16[768]{0:T(1024)(128)(2,1)S(1)}, f32[768,256]{0,1:T(8,128)S(1)}) fusion(f32[768,256]{0,1:T(8,128)S(1)} %copy-done.7, f32[768,256]{0,1:T(8,128)S(1)} %fusion.5, bf16[768,5120]{1,0:T(8,128)(2,1)} %bitcast.37, bf16[1,256,5120]{2,1,0:T(8,128)(2,1)S(1)} %copy-done.9), kind=kOutput, calls=%fused_computation.21 | convolution fusion | flops 2014641408 | bytes 12846592 | tf_op jit(solution)/shard_map/dot_general | solution.py:15
  270.5 0.0 copy-start.6
  270.5 8.0 %fusion.3 = f32[768,5120]{1,0:T(8,128)} fusion(bf16[1,5120,256]{2,1,0:T(8,128)(2,1)S(1)} %copy-done, f32[768,256]{0,1:T(8,128)S(1)} %fusion.5, f32[768,256]{0,1:T(8,128)S(1)} %get-tuple-element.3, f32[768,256]{0,1:T(8,128)S(1)} %copy-done.7), kind=kOutput, calls=%fused_computation.9 | convolution fusion | flops 2015232000 | bytes 20709376 | tf_op jit(solution)/shard_map/dot_general | solution.py:22
  278.5 0.0 copy-done.6
  278.5 11.0 %add_convert_fusion = bf16[768,5120]{1,0:T(8,128)(2,1)} fusion(f32[768,5120]{1,0:T(8,128)} %fusion.3, bf16[1,5120,256]{2,1,0:T(8,128)(2,1)S(1)} %copy-done.6, f32[768,256]{0,1:T(8,128)S(1)} %get-tuple-element.3, f32[768,256]{0,1:T(8,128)S(1)} %fusion.5), kind=kOutput, calls=%fused_computation | convolution fusion | flops 2022309888 | bytes 27787264 | tf_op jit(solution)/shard_map/dot_general | solution.py:25
  289.5 13.1 %convert_element_type.55 = bf16[32,4,6,5120]{3,2,1,0:T(8,128)(2,1)} reshape(bf16[768,5120]{1,0:T(8,128)(2,1)} %add_convert_fusion) | data formatting | bytes 15728640 | tf_op jit(solution)/shard_map/convert_element_type | solution.py:73
  302.6 11.4 %copy.27 = bf16[32,4,6,5120]{3,0,2,1:T(8,128)(2,1)} copy(bf16[32,4,6,5120]{3,2,1,0:T(8,128)(2,1)} %convert_element_type.55) | data formatting | bytes 15728640 | tf_op jit(solution)/shard_map/convert_element_type | solution.py:73
  314.0 0.0 reduce-scatter.2.cloned.1.call-update
  314.0 0.6 copy-done.11
  314.7 0.6 dynamic-slice
  315.3 0.1 convert_element_type.60
  315.4 0.1 copy.29
  315.5 8.5 %all-reduce = bf16[32,4,6]{0,2,1:T(8,128)(2,1)S(1)} all-reduce(bf16[32,4,6]{0,2,1:T(8,128)(2,1)S(1)} %copy.29), channel_id=5, replica_groups=mesh['expert'=32,'tensor'=4,'dp'=2] {'tensor'}, use_global_device_ids=true, to_apply=%region_4.5.clone | all-reduce | flops 768 | bytes 3072
  324.0 0.7 constant_dynamic-slice_fusion
  324.6 0.7 copy.30
  325.4 9.8 %all-to-all-start.3 = ((bf16[32,1,6]{2,1,0:T(2,128)(2,1)}), bf16[32,1,6]{2,1,0:T(2,128)(2,1)S(1)}, u32[]{:S(2)}, u32[]{:S(2)}) async-start(bf16[32,1,6]{2,1,0:T(2,128)(2,1)} %copy.30), calls=%async_computation.4 | async-start | bytes 32768 | tf_op jit(solution)/shard_map/all_to_all | solution.py:89
  335.2 58.7 %reduce-scatter.2.cloned.1.call-done = bf16[32,1,6,5120]{3,0,2,1:T(8,128)(2,1)} async-done(((bf16[32,4,6,5120]{3,0,2,1:T(8,128)(2,1)}), bf16[32,1,6,5120]{3,0,2,1:T(8,128)(2,1)}) %reduce-scatter.2.cloned.1.call-update) | async-done | bytes 1966096 | tf_op jit(solution)/shard_map/reduce_scatter | solution.py:72
  393.9 4.1 copy.28
  398.0 0.0 all-to-all-done.3
  398.0 10.3 %all-to-all-start.2 = ((bf16[32,6,5120]{2,1,0:T(8,128)(2,1)}), bf16[32,6,5120]{2,1,0:T(8,128)(2,1)}, u32[]{:S(2)}, u32[]{:S(2)}) async-start(bf16[32,6,5120]{2,1,0:T(8,128)(2,1)} %copy.28), calls=%async_computation.3 | async-start | bytes 5242880 | tf_op jit(solution)/shard_map/all_to_all | solution.py:88
  408.3 0.0 copy-done.8
  408.4 0.0 copy-done.3
  408.4 0.0 copy-done.4
  408.4 0.4 fusion.2
  408.8 0.0 copy-start.10
  408.8 0.1 reduce
  408.9 0.1 reshape.56
  409.0 0.7 fusion.13
  409.7 59.8 %all-to-all-done.2 = bf16[32,6,5120]{2,1,0:T(8,128)(2,1)} async-done(((bf16[32,6,5120]{2,1,0:T(8,128)(2,1)}), bf16[32,6,5120]{2,1,0:T(8,128)(2,1)}, u32[]{:S(2)}, u32[]{:S(2)}) %all-to-all-start.2) | async-done | bytes 1966112 | tf_op jit(solution)/shard_map/all_to_all | solution.py:88
  469.4 4.3 reshape.50
  473.7 0.0 copy-done.10
  473.7 3.7 fusion.1
  477.4 0.0 copy-done.1
  (8 shorter events, 0.0 us)
Async XLA Ops:
  7.2 173.7 %copy-start = (bf16[1,5120,256]{2,1,0:T(8,128)(2,1)S(1)}, bf16[1,5120,256]{2,1,0:T(8,128)(2,1)}, u32[]{:S(2)}) copy-start(bf16[1,5120,256]{2,1,0:T(8,128)(2,1)} %param.11) | copy-start | bytes 7864324
  7.2 163.1 %all-gather.7.cloned.1.call-start = ((), (), s32[]{:S(2)}) async-start(), calls=%async_computation.7 | async-start | bytes 9830400 | tf_op jit(solution)/shard_map/all_gather | solution.py:61
  92.6 161.3 %all-gather.5.cloned.1.call-start = ((), (), s32[]{:S(2)}) async-start(), calls=%async_computation.6 | async-start | bytes 9830400 | tf_op jit(solution)/shard_map/all_gather | solution.py:62
  170.0 223.9 %reduce-scatter.2.cloned.1.call-start = ((), (), s32[]{:S(2)}) async-start(), calls=%async_computation.5 | async-start | bytes 9830400 | tf_op jit(solution)/shard_map/reduce_scatter | solution.py:72
  180.9 6.0 %copy-start.2 = (bf16[32,24,5120]{2,1,0:T(8,128)(2,1)S(1)}, bf16[32,24,5120]{2,1,0:T(8,128)(2,1)}, u32[]{:S(2)}) copy-start(bf16[32,24,5120]{2,1,0:T(8,128)(2,1)} %copy.26) | copy-start | bytes 23592964
  180.9 7.1 %copy-start.5 = (bf16[1,5120,256]{2,1,0:T(8,128)(2,1)S(1)}, bf16[1,5120,256]{2,1,0:T(8,128)(2,1)}, u32[]{:S(2)}) copy-start(bf16[1,5120,256]{2,1,0:T(8,128)(2,1)} %param.12) | copy-start | bytes 7864324
  253.9 11.0 %copy-start.7 = (f32[768,256]{0,1:T(8,128)S(1)}, f32[768,256]{0,1:T(8,128)}, u32[]{:S(2)}) copy-start(f32[768,256]{0,1:T(8,128)} %fusion.8) | copy-start | bytes 2359300
  253.9 11.0 %copy-start.9 = (bf16[1,256,5120]{2,1,0:T(8,128)(2,1)S(1)}, bf16[1,256,5120]{2,1,0:T(8,128)(2,1)}, u32[]{:S(2)}) copy-start(bf16[1,256,5120]{2,1,0:T(8,128)(2,1)} %param.13) | copy-start | bytes 7864324
  270.5 8.0 %copy-start.6 = (bf16[1,5120,256]{2,1,0:T(8,128)(2,1)S(1)}, bf16[1,5120,256]{2,1,0:T(8,128)(2,1)}, u32[]{:S(2)}) copy-start(bf16[1,5120,256]{2,1,0:T(8,128)(2,1)} %param.12) | copy-start | bytes 7864324
  314.0 0.7 copy-start.11
  325.4 72.7 %all-to-all-start.3 = ((bf16[32,1,6]{2,1,0:T(2,128)(2,1)}), bf16[32,1,6]{2,1,0:T(2,128)(2,1)S(1)}, u32[]{:S(2)}, u32[]{:S(2)}) async-start(bf16[32,1,6]{2,1,0:T(2,128)(2,1)} %copy.30), calls=%async_computation.4 | async-start | bytes 32768 | tf_op jit(solution)/shard_map/all_to_all | solution.py:89
  398.0 10.3 %copy-start.8 = (s32[128,1]{0,1:T(1,128)S(1)}, s32[128,1]{0,1:T(1,128)}, u32[]{:S(2)}) copy-start(s32[128,1]{0,1:T(1,128)} %param.10) | copy-start | bytes 1540
  398.0 10.3 %copy-start.3 = (bf16[128,5120]{1,0:T(8,128)(2,1)S(1)}, bf16[128,5120]{1,0:T(8,128)(2,1)}, u32[]{:S(2)}) copy-start(bf16[128,5120]{1,0:T(8,128)(2,1)} %param.7) | copy-start | bytes 3932164
  398.0 10.3 %copy-start.4 = (bf16[128,5120]{1,0:T(8,128)(2,1)S(1)}, bf16[128,5120]{1,0:T(8,128)(2,1)}, u32[]{:S(2)}) copy-start(bf16[128,5120]{1,0:T(8,128)(2,1)} %param.8) | copy-start | bytes 3932164
  398.0 71.4 %all-to-all-start.2 = ((bf16[32,6,5120]{2,1,0:T(8,128)(2,1)}), bf16[32,6,5120]{2,1,0:T(8,128)(2,1)}, u32[]{:S(2)}, u32[]{:S(2)}) async-start(bf16[32,6,5120]{2,1,0:T(8,128)(2,1)} %copy.28), calls=%async_computation.3 | async-start | bytes 5242880 | tf_op jit(solution)/shard_map/all_to_all | solution.py:88
  408.8 64.9 %copy-start.10 = (f32[128]{0:T(128)S(1)}, f32[128]{0:T(128)}, u32[]{:S(2)}) copy-start(f32[128]{0:T(128)} %param.9) | copy-start | bytes 1540
  469.4 8.0 %copy-start.1 = (bf16[1,5120,256]{2,1,0:T(8,128)(2,1)S(1)}, bf16[1,5120,256]{2,1,0:T(8,128)(2,1)}, u32[]{:S(2)}) copy-start(bf16[1,5120,256]{2,1,0:T(8,128)(2,1)} %param.11) | copy-start | bytes 7864324
Sparse Core Ops, SparseCore 0:
  92.8 77.0 all-gather.6
  171.6 82.2 all-gather.4
  314.1 79.6 reduce-scatter.1
where the time goes:
time: 488 us; the launch traced here: 484 us
  waiting for transfers between devices  181 us (37%)
  blocking collectives  149 us (31%)
  local copies, waits for them, and re-layouts  72.1 us (15%)
  matrix products  44.4 us (9%)
  starting transfers between devices  20.4 us (4%)
  between operations  13.9 us (3%)
    all_to_all x1, blocking collectives, per_device(): lax.all_to_all(send_x, 'expert', split_axis=0, concat_axis=0, tiled=True)  73.1 us
    all_to_all x1, blocking collectives, per_device(): lax.all_to_all(send_dy, 'expert', split_axis=0, concat_axis=0, tiled=True)  67.5 us
    all_gather x1, waiting for transfers between devices, per_device(): lax.all_gather(got_dy[:, None], 'tensor', axis=1, tiled=True)  62.6 us
    all_to_all x1, waiting for transfers between devices, per_device(): lax.all_to_all(back_rows, 'expert', split_axis=0, concat_axis=0, tiled=True)  59.8 us
    reduce_scatter x1, waiting for transfers between devices, per_device(): lax.psum_scatter(rows.reshape(experts, groups, capacity, width).astype(jn...  58.7 us
    convert_element_type x2, local copies, waits for them, and re-layouts, per_device(): rows.reshape(experts, groups, capacity, width).astype(jnp.bfloat16)  24.5 us
    dot_general x1, matrix products, expert_grads(): lax.dot_general(grad_up, w_up, (((1,), (1,)), ((), ())), preferred_elemen...  11 us
    all_gather x1, local copies, waits for them, and re-layouts, per_device(): lax.all_gather(got_dy[:, None], 'tensor', axis=1, tiled=True)  11 us
  transfers between devices with their start and end apart: 5, of which 3 were waited for; matrix products, arithmetic and copies ran while one was open for 8% of the time, Pallas kernels for 0%

commit v1 on v0

v1 whole, which is shorter than its diff:
```python
import jax
import jax.numpy as jnp
from jax import lax
from jax.experimental import pallas as pl
from jax.experimental.pallas import tpu as pltpu
from jax.sharding import PartitionSpec as P

BF = jnp.bfloat16
F32 = jnp.float32
CAP = 6
ROWS = 8
TERM_LANES = 128
VMEM_LIMIT = 56 * 1024 * 1024


def dot(a, b):
    return jnp.dot(a, b, preferred_element_type=F32)


def dot_t(a, b):
    return lax.dot_general(a, b, (((1,), (1,)), ((), ())), preferred_element_type=F32)


def eye(n):
    return lax.broadcasted_iota(jnp.int32, (n, n), 0) == lax.broadcasted_iota(jnp.int32, (n, n), 1)


def to_column(row):
    n = row.shape[1]
    return jnp.sum(jnp.where(eye(n), jnp.broadcast_to(row, (n, n)), 0), axis=1, keepdims=True)


def to_row(column):
    n = column.shape[0]
    return jnp.sum(jnp.where(eye(n), jnp.broadcast_to(column, (n, n)), 0), axis=0, keepdims=True)


def places(route_row):
    n = route_row.shape[1]
    across = jnp.broadcast_to(route_row, (n, n))
    down = jnp.broadcast_to(to_column(route_row), (n, n))
    earlier = lax.broadcasted_iota(jnp.int32, (n, n), 0) < lax.broadcasted_iota(jnp.int32, (n, n), 1)
    slot = jnp.sum(jnp.where((across == down) & earlier, 1, 0), axis=0, keepdims=True)
    second = jnp.where(slot >= 3, 1, 0)
    base = route_row * ROWS
    return base + slot, base + CAP + second, slot - 3 * second


def pack_kernel(route_ref, rows_ref, out_ref):
    n, width = rows_ref.shape
    total = out_ref.shape[0]
    part = width // 4
    main, tail, block = places(route_ref[...])
    row = lax.broadcasted_iota(jnp.int32, (total, n), 0)
    select = jnp.where(row == main, 1.0, 0.0).astype(BF)
    last = rows_ref[:, 3 * part :]
    for j in range(3):
        tail_select = jnp.where((row == tail) & (block == j), 1.0, 0.0).astype(BF)
        cols = pl.ds(j * part, part)
        out_ref[:, cols] = (dot(select, rows_ref[:, cols]) + dot(tail_select, last)).astype(BF)


def pack(route_row, rows, experts):
    n, width = rows.shape
    return pl.pallas_call(
        pack_kernel,
        out_shape=jax.ShapeDtypeStruct((experts * ROWS, width // 4 * 3), BF),
        compiler_params=pltpu.CompilerParams(vmem_limit_bytes=VMEM_LIMIT),
        cost_estimate=pl.CostEstimate(
            flops=2 * experts * ROWS * n * width * 3 // 2,
            bytes_accessed=2 * width * (n + experts * CAP),
            transcendentals=0,
        ),
        name="pack",
    )(route_row, rows)


def slot_matrix(slots, packed, slot_dim, tail):
    shape = (slots, packed) if slot_dim == 0 else (packed, slots)
    slot = lax.broadcasted_iota(jnp.int32, shape, slot_dim)
    row = lax.broadcasted_iota(jnp.int32, shape, 1 - slot_dim)
    group, place = row >> 3, row & 7
    if tail is None:
        hit = (slot == group * CAP + place) & (place < CAP)
    else:
        hit = (slot == group * CAP + (place - CAP) * 3 + tail) & (place >= CAP)
    return jnp.where(hit, 1.0, 0.0).astype(BF)


def expert_kernel(
    xo_hbm, xt_hbm, dyo_hbm, dyt_hbm, wgu_hbm, wdn_hbm,
    own_ref, other_ref,
    x_raw, dy_raw, x, dy, wgu, wdn, grads, term, sems,
):
    packed, main_width = x_raw.shape[1:]
    blocks, width, both = wgu.shape
    hidden = both // 2
    slots = x.shape[0] // 2
    part = width // 4
    x_copies = [
        pltpu.make_async_copy(src, x_raw.at[i], sems.at[i]) for i, src in enumerate((xo_hbm, xt_hbm))
    ]
    dy_copies = [
        pltpu.make_async_copy(src, dy_raw.at[i], sems.at[2 + i]) for i, src in enumerate((dyo_hbm, dyt_hbm))
    ]
    wgu_copies = [
        pltpu.make_async_copy(wgu_hbm.at[i], wgu.at[i], sems.at[4 + i]) for i in range(blocks)
    ]
    wdn_copy = pltpu.make_async_copy(wdn_hbm, wdn, sems.at[4 + blocks])
    for copy in x_copies + dy_copies + [wdn_copy] + wgu_copies:
        copy.start()
    spread = slot_matrix(slots, packed, 0, None)
    spread_tail = [slot_matrix(slots, packed, 0, j) for j in range(3)]

    def unpack(raw, copies, full):
        for i in range(2):
            copies[i].wait()
            low = i * slots
            for j in range(3):
                full[low : low + slots, j * part : (j + 1) * part] = dot(
                    spread, raw[i, :, j * part : (j + 1) * part]
                ).astype(BF)
            last = dot(spread_tail[0], raw[i, :, :part])
            last += dot(spread_tail[1], raw[i, :, part : 2 * part])
            last += dot(spread_tail[2], raw[i, :, 2 * part :])
            full[low : low + slots, 3 * part :] = last.astype(BF)

    unpack(x_raw, x_copies, x)
    unpack(dy_raw, dy_copies, dy)
    wdn_copy.wait()
    for copy in wgu_copies:
        copy.wait()
    term[...] = jnp.zeros_like(term)

    def forward(b, _):
        pre = dot(x[...], wgu[b])
        back = dot_t(dy[...], wdn[pl.ds(pl.multiple_of(b * hidden, hidden), hidden), :])
        pre_gate, pre_up = pre[:, :hidden], pre[:, hidden:]
        s = jax.nn.sigmoid(pre_gate)
        activated = pre_gate * s
        slope = s * (1.0 + pre_gate * (1.0 - s))
        term[...] += activated * pre_up * back
        grads[b, :, :hidden] = (back * pre_up * slope).astype(BF)
        grads[b, :, hidden:] = (back * activated).astype(BF)
        return 0

    lax.fori_loop(0, blocks, forward, 0)
    terms = jnp.broadcast_to(jnp.sum(term[...], axis=1, keepdims=True), (2 * slots, TERM_LANES)).astype(BF)

    gather = slot_matrix(slots, packed, 1, None)
    gather_tail = [slot_matrix(slots, packed, 1, j) for j in range(3)]
    outs = (own_ref, other_ref)
    for i in range(2):
        outs[i][:, main_width:] = dot(gather, terms[i * slots : (i + 1) * slots]).astype(BF)

    def backward(low):
        total = dot_t(grads[0], wgu[0, low : low + part, :])
        for b in range(1, blocks):
            total += dot_t(grads[b], wgu[b, low : low + part, :])
        return total.astype(BF)

    last = backward(3 * part)
    for j in range(3):
        rows = backward(j * part)
        for i in range(2):
            span = slice(i * slots, (i + 1) * slots)
            outs[i][:, j * part : (j + 1) * part] = (
                dot(gather, rows[span]) + dot(gather_tail[j], last[span])
            ).astype(BF)


def expert_part(xo, xt, dyo, dyt, wgu, wdn):
    packed, main_width = xo.shape
    blocks, width, both = wgu.shape
    slots = packed // ROWS * CAP
    out = jax.ShapeDtypeStruct((packed, main_width + TERM_LANES), BF)
    return pl.pallas_call(
        expert_kernel,
        out_shape=(out, out),
        in_specs=[pl.BlockSpec(memory_space=pl.ANY)] * 6,
        scratch_shapes=[
            pltpu.VMEM((2, packed, main_width), BF),
            pltpu.VMEM((2, packed, main_width), BF),
            pltpu.VMEM((2 * slots, width), BF),
            pltpu.VMEM((2 * slots, width), BF),
            pltpu.VMEM(wgu.shape, BF),
            pltpu.VMEM(wdn.shape, BF),
            pltpu.VMEM((blocks, 2 * slots, both), BF),
            pltpu.VMEM((2 * slots, both // 2), F32),
            pltpu.SemaphoreType.DMA((5 + blocks,)),
        ],
        compiler_params=pltpu.CompilerParams(vmem_limit_bytes=VMEM_LIMIT),
        cost_estimate=pl.CostEstimate(
            flops=2 * 2 * slots * width * both // 2 * blocks * 5,
            bytes_accessed=2 * (wgu.size + wdn.size + 6 * xo.size),
            transcendentals=2 * slots * both // 2 * blocks,
        ),
        name="expert",
    )(xo, xt, dyo, dyt, wgu, wdn)


def combine_kernel(route_ref, gate_ref, own_term_ref, out_grad_ref, ret_ref, token_grad_ref, gate_grad_ref):
    n, width = out_grad_ref.shape
    packed = ret_ref.shape[0]
    part = width // 4
    experts = packed // ROWS
    route_row = route_ref[...]
    main, tail, block = (to_column(v) for v in places(route_row))
    routed = to_column(route_row) < experts
    gate = to_column(gate_ref[...])
    row = lax.broadcasted_iota(jnp.int32, (n, packed), 1)
    select = jnp.where(row == main, 1.0, 0.0).astype(BF)
    last = jnp.zeros((n, part), F32)
    for j in range(4):
        cols = pl.ds(j * part, part)
        if j < 3:
            tail_select = jnp.where((row == tail) & (block == j), 1.0, 0.0).astype(BF)
            piece = ret_ref[:, cols]
            rows = dot(select, piece)
            last += dot(tail_select, piece)
        else:
            rows = last
        rows = jnp.where(routed, rows, out_grad_ref[:, cols].astype(F32))
        token_grad_ref[:, cols] = (gate * rows).astype(BF)
    terms = dot(select, ret_ref[:, 3 * part :])[:, :1]
    gate_grad_ref[...] = jnp.where(route_row < experts, to_row(terms), own_term_ref[...]).astype(BF)


def combine(route_row, gate_row, own_term, out_grad, ret):
    n, width = out_grad.shape
    return pl.pallas_call(
        combine_kernel,
        out_shape=(jax.ShapeDtypeStruct((n, width), BF), jax.ShapeDtypeStruct((1, n), BF)),
        compiler_params=pltpu.CompilerParams(vmem_limit_bytes=VMEM_LIMIT),
        cost_estimate=pl.CostEstimate(
            flops=2 * ret.shape[0] * n * width * 3 // 2,
            bytes_accessed=2 * (2 * out_grad.size + ret.size),
            transcendentals=0,
        ),
        name="combine",
    )(route_row, gate_row, own_term, out_grad, ret)


def per_device(tokens, out_grad, gate, route, gate_weight, up_weight, down_weight):
    experts = lax.axis_size("expert")
    n, width = tokens.shape
    hidden = gate_weight.shape[2] // 2
    core = lax.axis_index("dp")
    swap = [(0, 1), (1, 0)]
    route_row = route.reshape(1, n)

    halves = [lax.dynamic_slice(w[0], (0, core * hidden), (width, hidden)) for w in (gate_weight, up_weight)]
    wgu = lax.all_gather(jnp.concatenate(halves, axis=1), "tensor", axis=0, tiled=False)
    wdn = lax.all_gather(
        lax.dynamic_slice(down_weight[0], (core * hidden, 0), (hidden, width)), "tensor", axis=0, tiled=True
    )

    def send(rows):
        packed = pack(route_row, rows, experts).reshape(experts, ROWS, -1)
        got = lax.all_to_all(packed, "expert", split_axis=0, concat_axis=0, tiled=True)
        got = got.reshape(experts * ROWS, -1)
        return got, lax.ppermute(got, "dp", swap)

    xo, xt = send(tokens)
    dyo, dyt = send(out_grad)
    own, other = expert_part(xo, xt, dyo, dyt, wgu, wdn)
    from_other = lax.ppermute(other, "dp", swap)
    total = (own.astype(F32) + from_other.astype(F32)).astype(BF).reshape(experts, ROWS, -1)
    ret = lax.all_to_all(total, "expert", split_axis=0, concat_axis=0, tiled=True)
    own_term = jnp.sum(out_grad.astype(F32) * tokens.astype(F32), axis=1)
    token_grad, gate_grad = combine(
        route_row, gate.reshape(1, n), own_term.reshape(1, n), out_grad, ret.reshape(experts * ROWS, -1)
    )
    return token_grad, gate_grad.reshape(n)


def solution(mesh):
    rows = P(("dp", "expert", "tensor"), None)
    return jax.shard_map(
        per_device,
        mesh=mesh,
        in_specs=(
            rows,
            rows,
            P(("dp", "expert", "tensor")),
            rows,
            P("expert", None, "tensor"),
            P("expert", None, "tensor"),
            P("expert", "tensor", None),
        ),
        out_specs=(rows, P(("dp", "expert", "tensor"))),
        check_vma=False,
    )
```

time: 488 us -> 282 us (0.58)
  blocking collectives: 149 us -> 0 us
  local copies, waits for them, and re-layouts: 72.1 us -> 4.72 us
  matrix products: 44.4 us -> 0 us
  Pallas kernels: 0 us -> 37.3 us
  starting transfers between devices: 20.4 us -> 28 us
  waiting for transfers between devices: 181 us -> 188 us
    all_to_all x2 -> x0, blocking collectives: 141 us -> none  [the longest x1 73.1 us: per_device(): lax.all_to_all(send_x, 'expert', split_axis=0, concat_axis=0, tiled=True)]
    all_to_all x2 -> x3, waiting for transfers between devices: 59.8 us -> 137 us  [the longest x2 90.3 us: send(): lax.all_to_all(packed, 'expert', split_axis=0, concat_axis=0, tiled=True)]
    reduce_scatter x1 -> x0, waiting for transfers between devices: 58.7 us -> none  [per_device(): lax.psum_scatter(rows.reshape(experts, groups, capacity, width).astype(jn...]
    dot_general x9 -> x0, matrix products: 44.4 us -> none  [the longest x1 11 us: expert_grads(): lax.dot_general(grad_up, w_up, (((1,), (1,)), ((), ())), preferred_elemen...]
    pallas_call x0 -> x4, Pallas kernels: none -> 37.3 us  [the longest x1 25.3 us: expert_part(): pl.pallas_call(expert_kernel, out_shape=(out, out), in_specs=[pl.BlockSpe...]
    convert_element_type x5 -> x0, local copies, waits for them, and re-layouts: 28.9 us -> none  [the longest x2 24.5 us: per_device(): rows.reshape(experts, groups, capacity, width).astype(jnp.bfloat16)]
    all_gather x2 -> x0, local copies, waits for them, and re-layouts: 21.6 us -> none  [the longest x1 11 us: per_device(): lax.all_gather(got_dy[:, None], 'tensor', axis=1, tiled=True)]
    all_gather x2, waiting for transfers between devices: 62.6 us -> 43.2 us  [the longest x1 43.2 us: per_device(): lax.all_gather(jnp.concatenate(halves, axis=1), 'tensor', axis=0, tiled=F...]
  transfers between devices with their start and end apart: 5 -> 8, of which waited for: 3 -> 6; matrix products, arithmetic and copies ran while one was open for 8% -> 2% of each run, Pallas kernels for 0% -> 3%
where the time goes in v1:
time: 282 us; the launch traced here: 280 us
  waiting for transfers between devices  188 us (67%)
  Pallas kernels  37.3 us (13%)
  starting transfers between devices  28 us (10%)
  between operations  14.1 us (5%)
  other arithmetic  7.82 us (3%)
  local copies, waits for them, and re-layouts  4.72 us (2%)
    all_to_all x2, waiting for transfers between devices, send(): lax.all_to_all(packed, 'expert', split_axis=0, concat_axis=0, tiled=True)  90.3 us
    all_to_all x1, waiting for transfers between devices, per_device(): lax.all_to_all(total, 'expert', split_axis=0, concat_axis=0, tiled=True)  46.3 us
    all_gather x1, waiting for transfers between devices, per_device(): lax.all_gather(jnp.concatenate(halves, axis=1), 'tensor', axis=0, tiled=F...  43.2 us
    pallas_call x1, Pallas kernels, expert_part(): pl.pallas_call(expert_kernel, out_shape=(out, out), in_specs=[pl.BlockSpe...  25.3 us
    all_to_all x2, starting transfers between devices, send(): lax.all_to_all(packed, 'expert', split_axis=0, concat_axis=0, tiled=True)  17.5 us
    all_to_all x1, starting transfers between devices, per_device(): lax.all_to_all(total, 'expert', split_axis=0, concat_axis=0, tiled=True)  10.2 us
    pallas_call x2, Pallas kernels, pack(): pl.pallas_call(pack_kernel, out_shape=jax.ShapeDtypeStruct((experts * ROW...  7.84 us
  transfers between devices with their start and end apart: 8, of which 6 were waited for; matrix products, arithmetic and copies ran while one was open for 2% of the time, Pallas kernels for 3%

profile of v1, /device:TPU:24, one launch (start us, length us, event | category | flops | bytes accessed | tf_op | source)
XLA Modules:
  0.0 280.4 jit_solution(14208262465706257353)
XLA Ops:
  7.2 0.0 copy-start
  7.2 0.0 all-gather.7.cloned.1.call-start
  7.2 1.7 copy-done
  8.9 1.1 constant_dynamic-slice_fusion
  10.1 0.0 all-gather.7.cloned.1.call-update
  10.1 0.0 all-gather.5.cloned.1.call-start
  10.1 1.9 dynamic-slice_bitcast_fusion
  12.0 1.8 pad_maximum_fusion
  13.8 0.0 all-gather.5.cloned.1.call-update
  13.8 3.9 %pack.2 = bf16[256,3840]{1,0:T(8,128)(2,1)} custom-call(s32[1,128]{1,0:T(1,128)} %bitcast.19, bf16[128,5120]{1,0:T(8,128)(2,1)} %rows_ref.2), custom_call_target="tpu_custom_call" | custom-call | flops 503316480 | bytes 3276800 | tf_op jit(solution)/shard_map/pack/pallas_call | solution.py:65
  17.8 11.4 %all-to-all-start = ((bf16[32,8,3840]{2,1,0:T(8,128)(2,1)}), bf16[32,8,3840]{2,1,0:T(8,128)(2,1)}, u32[]{:S(2)}, u32[]{:S(2)}) async-start(bf16[32,8,3840]{2,1,0:T(8,128)(2,1)} %bitcast.18), calls=%async_computation | async-start | bytes 3932160 | tf_op jit(solution)/shard_map/all_to_all | solution.py:260
  29.2 3.9 %pack.3 = bf16[256,3840]{1,0:T(8,128)(2,1)} custom-call(s32[1,128]{1,0:T(1,128)} %bitcast.20, bf16[128,5120]{1,0:T(8,128)(2,1)} %out_grad_ref.1), custom_call_target="tpu_custom_call" | custom-call | flops 503316480 | bytes 3276800 | tf_op jit(solution)/shard_map/pack/pallas_call | solution.py:65
  33.1 43.4 %all-to-all-done = bf16[32,8,3840]{2,1,0:T(8,128)(2,1)} async-done(((bf16[32,8,3840]{2,1,0:T(8,128)(2,1)}), bf16[32,8,3840]{2,1,0:T(8,128)(2,1)}, u32[]{:S(2)}, u32[]{:S(2)}) %all-to-all-start) | async-done | bytes 1966112 | tf_op jit(solution)/shard_map/all_to_all | solution.py:260
  76.6 6.1 %all-to-all-start.1 = ((bf16[32,8,3840]{2,1,0:T(8,128)(2,1)}), bf16[32,8,3840]{2,1,0:T(8,128)(2,1)}, u32[]{:S(2)}, u32[]{:S(2)}) async-start(bf16[32,8,3840]{2,1,0:T(8,128)(2,1)} %bitcast.17), calls=%async_computation.1 | async-start | bytes 3932160 | tf_op jit(solution)/shard_map/all_to_all | solution.py:260
  82.7 0.1 collective-permute-start
  82.8 46.9 %all-to-all-done.1 = bf16[32,8,3840]{2,1,0:T(8,128)(2,1)} async-done(((bf16[32,8,3840]{2,1,0:T(8,128)(2,1)}), bf16[32,8,3840]{2,1,0:T(8,128)(2,1)}, u32[]{:S(2)}, u32[]{:S(2)}) %all-to-all-start.1) | async-done | bytes 1966112 | tf_op jit(solution)/shard_map/all_to_all | solution.py:260
  129.7 0.0 collective-permute-start.1
  129.7 0.0 collective-permute-done.xt_hbm
  129.7 4.3 %collective-permute-done.1.dyt_hbm = bf16[256,3840]{1,0:T(8,128)(2,1)} collective-permute-done((bf16[256,3840]{1,0:T(8,128)(2,1)}, bf16[256,3840]{1,0:T(8,128)(2,1)}, u32[]{:S(2)}, u32[]{:S(2)}) %collective-permute-start.1) | collective-permute-done | bytes 1966112 | tf_op jit(solution)/shard_map/ppermute | solution.py:262
  134.0 0.0 all-gather.7.cloned.1.call-done
  134.0 43.2 %all-gather.5.cloned.1.call-done = bf16[20480,256]{1,0:T(8,128)(2,1)} async-done(((bf16[5120,256]{1,0:T(8,128)(2,1)}), bf16[20480,256]{1,0:T(8,128)(2,1)}) %all-gather.5.cloned.1.call-update) | async-done | bytes 10485776 | tf_op jit(solution)/shard_map/all_gather | solution.py:253
  177.2 25.3 %expert.1 = (bf16[256,3968]{1,0:T(8,128)(2,1)}, bf16[256,3968]{1,0:T(8,128)(2,1)}) custom-call(bf16[256,3840]{1,0:T(8,128)(2,1)} %bitcast.4.xo_hbm, bf16[256,3840]{1,0:T(8,128)(2,1)} %collective-permute-done.xt_hbm, bf16[256,3840]{1,0:T(8,128)(2,1)} %bitcast.6.dyo_hbm, bf16[256,3840]{1,0:T(8,128)(2,1)} %collective-permute-done.1.dyt_hbm, ...), custom_call_target="tpu_custom_call" | custom-call | flops 10066329600 | bytes 27525120 | tf_op jit(solution)/shard_map/expert/pallas_call | solution.py:177
  202.5 0.1 collective-permute-start.2
  202.6 4.3 %collective-permute-done.2 = bf16[256,3968]{1,0:T(8,128)(2,1)S(1)} collective-permute-done((bf16[256,3968]{1,0:T(8,128)(2,1)}, bf16[256,3968]{1,0:T(8,128)(2,1)S(1)}, u32[]{:S(2)}, u32[]{:S(2)}) %collective-permute-start.2) | collective-permute-done | bytes 2031648 | tf_op jit(solution)/shard_map/ppermute | solution.py:267
  206.9 3.3 %fusion = bf16[32,8,3968]{2,1,0:T(8,128)(2,1)} fusion(bf16[256,3968]{1,0:T(8,128)(2,1)S(1)} %collective-permute-done.2, bf16[256,3968]{1,0:T(8,128)(2,1)} %get-tuple-element.6), kind=kLoop, calls=%fused_computation.3 | loop fusion | flops 4063232 | bytes 6094848 | tf_op jit(solution)/shard_map/reshape | solution.py:268
  210.2 10.2 %all-to-all-start.2 = ((bf16[32,8,3968]{2,1,0:T(8,128)(2,1)}), bf16[32,8,3968]{2,1,0:T(8,128)(2,1)}, u32[]{:S(2)}, u32[]{:S(2)}) async-start(bf16[32,8,3968]{2,1,0:T(8,128)(2,1)} %fusion), calls=%async_computation.2 | async-start | bytes 4063232 | tf_op jit(solution)/shard_map/all_to_all | solution.py:269
  220.4 2.7 multiply_reduce_fusion
  223.1 46.3 %all-to-all-done.2 = bf16[32,8,3968]{2,1,0:T(8,128)(2,1)} async-done(((bf16[32,8,3968]{2,1,0:T(8,128)(2,1)}), bf16[32,8,3968]{2,1,0:T(8,128)(2,1)}, u32[]{:S(2)}, u32[]{:S(2)}) %all-to-all-start.2) | async-done | bytes 2031648 | tf_op jit(solution)/shard_map/all_to_all | solution.py:269
  269.4 4.1 %combine.1 = (bf16[128,5120]{1,0:T(8,128)(2,1)}, bf16[1,128]{1,0:T(2,128)(2,1)}) custom-call(s32[1,128]{1,0:T(1,128)} %bitcast.21, f32[1,128]{1,0:T(1,128)} %bitcast.23, f32[1,128]{1,0:T(1,128)} %bitcast.22, bf16[128,5120]{1,0:T(8,128)(2,1)} %out_grad_ref.1, bf16[256,3968]{1,0:T(8,128)(2,1)} %bitcast.12.ret_ref), custom_call_target="tpu_custom_call" | custom-call | flops 503316480 | bytes 4653056 | tf_op jit(solution)/shard_map/combine/pallas_call | solution.py:231
Async XLA Ops:
  7.2 1.7 copy-start
  7.2 126.8 %all-gather.7.cloned.1.call-start = ((), (), s32[]{:S(2)}) async-start(), calls=%async_computation.4 | async-start | bytes 6553600 | tf_op jit(solution)/shard_map/all_gather | solution.py:254
  10.1 167.1 %all-gather.5.cloned.1.call-start = ((), (), s32[]{:S(2)}) async-start(), calls=%async_computation.3 | async-start | bytes 13107200 | tf_op jit(solution)/shard_map/all_gather | solution.py:253
  17.8 58.8 %all-to-all-start = ((bf16[32,8,3840]{2,1,0:T(8,128)(2,1)}), bf16[32,8,3840]{2,1,0:T(8,128)(2,1)}, u32[]{:S(2)}, u32[]{:S(2)}) async-start(bf16[32,8,3840]{2,1,0:T(8,128)(2,1)} %bitcast.18), calls=%async_computation | async-start | bytes 3932160 | tf_op jit(solution)/shard_map/all_to_all | solution.py:260
  76.6 53.1 %all-to-all-start.1 = ((bf16[32,8,3840]{2,1,0:T(8,128)(2,1)}), bf16[32,8,3840]{2,1,0:T(8,128)(2,1)}, u32[]{:S(2)}, u32[]{:S(2)}) async-start(bf16[32,8,3840]{2,1,0:T(8,128)(2,1)} %bitcast.17), calls=%async_computation.1 | async-start | bytes 3932160 | tf_op jit(solution)/shard_map/all_to_all | solution.py:260
  82.7 47.0 %collective-permute-start = (bf16[256,3840]{1,0:T(8,128)(2,1)}, bf16[256,3840]{1,0:T(8,128)(2,1)}, u32[]{:S(2)}, u32[]{:S(2)}) collective-permute-start(bf16[256,3840]{1,0:T(8,128)(2,1)} %bitcast.4.xo_hbm), channel_id=1, source_target_pairs={{0,1},{1,0},{2,3},{3,2},{4,5},{5,4},{6,7},{7,6},{8,9},{9,8},{10,11... | collective-permute-start | bytes 5898248 | tf_op jit(solution)/shard_map/ppermute | solution.py:262
  129.7 4.3 %collective-permute-start.1 = (bf16[256,3840]{1,0:T(8,128)(2,1)}, bf16[256,3840]{1,0:T(8,128)(2,1)}, u32[]{:S(2)}, u32[]{:S(2)}) collective-permute-start(bf16[256,3840]{1,0:T(8,128)(2,1)} %bitcast.6.dyo_hbm), channel_id=1, source_target_pairs={{0,1},{1,0},{2,3},{3,2},{4,5},{5,4},{6,7},{7,6},{8,9},{9,8},{10,11... | collective-permute-start | bytes 5898248 | tf_op jit(solution)/shard_map/ppermute | solution.py:262
  202.5 4.4 %collective-permute-start.2 = (bf16[256,3968]{1,0:T(8,128)(2,1)}, bf16[256,3968]{1,0:T(8,128)(2,1)S(1)}, u32[]{:S(2)}, u32[]{:S(2)}) collective-permute-start(bf16[256,3968]{1,0:T(8,128)(2,1)} %get-tuple-element.7), channel_id=1, source_target_pairs={{0,1},{1,0},{2,3},{3,2},{4,5},{5,4},{6,7},{7,6},{8,9},{9,8},{10,11... | collective-permute-start | bytes 6094856 | tf_op jit(solution)/shard_map/ppermute | solution.py:267
  210.2 59.2 %all-to-all-start.2 = ((bf16[32,8,3968]{2,1,0:T(8,128)(2,1)}), bf16[32,8,3968]{2,1,0:T(8,128)(2,1)}, u32[]{:S(2)}, u32[]{:S(2)}) async-start(bf16[32,8,3968]{2,1,0:T(8,128)(2,1)} %fusion), calls=%async_computation.2 | async-start | bytes 4063232 | tf_op jit(solution)/shard_map/all_to_all | solution.py:269
Sparse Core Ops, SparseCore 0:
  10.4 60.5 all-gather.6
  72.8 104.4 all-gather.4

commit v2 on v1

v2 whole, which is shorter than its diff:
```python
import jax
import jax.numpy as jnp
from jax import lax
from jax.experimental import pallas as pl
from jax.experimental.pallas import tpu as pltpu
from jax.sharding import PartitionSpec as P

BF = jnp.bfloat16
F32 = jnp.float32
CAP = 6
ROWS = 8
TERM_LANES = 128
FIRST_COST = 1000
UNITS = 10
VMEM_LIMIT = 56 * 1024 * 1024


def dot(a, b):
    return jnp.dot(a, b, preferred_element_type=F32)


def dot_t(a, b):
    return lax.dot_general(a, b, (((1,), (1,)), ((), ())), preferred_element_type=F32)


def eye(n):
    return lax.broadcasted_iota(jnp.int32, (n, n), 0) == lax.broadcasted_iota(jnp.int32, (n, n), 1)


def to_column(row):
    n = row.shape[1]
    return jnp.sum(jnp.where(eye(n), jnp.broadcast_to(row, (n, n)), 0), axis=1, keepdims=True)


def to_row(column):
    n = column.shape[0]
    return jnp.sum(jnp.where(eye(n), jnp.broadcast_to(column, (n, n)), 0), axis=0, keepdims=True)


def places(route_row):
    n = route_row.shape[1]
    across = jnp.broadcast_to(route_row, (n, n))
    down = jnp.broadcast_to(to_column(route_row), (n, n))
    earlier = lax.broadcasted_iota(jnp.int32, (n, n), 0) < lax.broadcasted_iota(jnp.int32, (n, n), 1)
    slot = jnp.sum(jnp.where((across == down) & earlier, 1, 0), axis=0, keepdims=True)
    second = jnp.where(slot >= 3, 1, 0)
    base = route_row * ROWS
    return base + slot, base + CAP + second, slot - 3 * second


def pack_kernel(route_ref, rows_ref, out_ref):
    n, width = rows_ref.shape
    total = out_ref.shape[0]
    part = width // 4
    main, tail, block = places(route_ref[...])
    row = lax.broadcasted_iota(jnp.int32, (total, n), 0)
    select = jnp.where(row == main, 1.0, 0.0).astype(BF)
    last = rows_ref[:, 3 * part :]
    for j in range(3):
        tail_select = jnp.where((row == tail) & (block == j), 1.0, 0.0).astype(BF)
        cols = pl.ds(j * part, part)
        out_ref[:, cols] = (dot(select, rows_ref[:, cols]) + dot(tail_select, last)).astype(BF)


def pack(route_row, rows, experts):
    n, width = rows.shape
    return pl.pallas_call(
        pack_kernel,
        out_shape=jax.ShapeDtypeStruct((experts * ROWS, width // 4 * 3), BF),
        compiler_params=pltpu.CompilerParams(vmem_limit_bytes=VMEM_LIMIT),
        cost_estimate=pl.CostEstimate(
            flops=2 * experts * ROWS * n * width * 3 // 2,
            bytes_accessed=2 * width * (n + experts * CAP),
            transcendentals=0,
        ),
        name="pack",
    )(route_row, rows)


def weight_pieces(core, gate_weight, up_weight, down_weight, units, pieces):
    width, hidden = gate_weight.shape[0], gate_weight.shape[1] // 2
    rows = width // UNITS
    first, stride, steps = units

    def unit(i):
        return first + stride * i

    def kernel(core_ref, gate_ref, up_ref, down_ref, *outs):
        here = unit(pl.program_id(0))
        block = jnp.concatenate([gate_ref[...], up_ref[...], down_ref[...].T], axis=1)
        for (low, high), out in zip(pieces, outs):

            @pl.when((here >= low) & (here < high))
            def _(out=out):
                out[...] = block

    def place(low, high):
        return pl.BlockSpec((rows, 3 * hidden), lambda i, c: (jnp.clip(unit(i), low, high - 1) - low, 0))

    return pl.pallas_call(
        kernel,
        grid_spec=pltpu.PrefetchScalarGridSpec(
            num_scalar_prefetch=1,
            grid=(steps,),
            in_specs=[pl.BlockSpec((rows, hidden), lambda i, c: (unit(i), c[0]))] * 2
            + [pl.BlockSpec((hidden, rows), lambda i, c: (c[0], unit(i)))],
            out_specs=[place(*piece) for piece in pieces],
        ),
        out_shape=[jax.ShapeDtypeStruct(((high - low) * rows, 3 * hidden), BF) for low, high in pieces],
        compiler_params=pltpu.CompilerParams(vmem_limit_bytes=VMEM_LIMIT),
        cost_estimate=pl.CostEstimate(
            flops=0, bytes_accessed=2 * 3 * 3 * steps * rows * hidden, transcendentals=0
        ),
        name="weights",
    )(core, gate_weight, up_weight, down_weight)


def copy_pieces(pieces, full, sems):
    copies, low = [], 0
    for piece in pieces:
        rows = piece.shape[0]
        copies.append(pltpu.make_async_copy(piece, full.at[pl.ds(low, rows)], sems.at[len(copies)]))
        low += rows
    return copies


def slot_matrix(slots, packed, slot_dim, tail):
    shape = (slots, packed) if slot_dim == 0 else (packed, slots)
    slot = lax.broadcasted_iota(jnp.int32, shape, slot_dim)
    row = lax.broadcasted_iota(jnp.int32, shape, 1 - slot_dim)
    group, place = row >> 3, row & 7
    if tail is None:
        hit = (slot == group * CAP + place) & (place < CAP)
    else:
        hit = (slot == group * CAP + (place - CAP) * 3 + tail) & (place >= CAP)
    return jnp.where(hit, 1.0, 0.0).astype(BF)


def block_forward(x, dy, w, grads):
    both = grads.shape[1]
    hidden = both // 2
    pre = dot(x[...], w[:, :both])
    back = dot(dy[...], w[:, both:])
    pre_gate, pre_up = pre[:, :hidden], pre[:, hidden:]
    s = jax.nn.sigmoid(pre_gate)
    activated = pre_gate * s
    slope = s * (1.0 + pre_gate * (1.0 - s))
    grads[:, :hidden] = (back * pre_up * slope).astype(BF)
    grads[:, hidden:] = (back * activated).astype(BF)
    return activated * pre_up * back


def first_kernel(
    x_own, x_other, dy_own, dy_other, o0, o1, o2, u0, u1, u2, d0, d1, d2,
    x_hbm, dy_hbm, sum_hbm, term_ref,
    raw, x, dy, w, grads, total, sems,
):
    packed = raw.shape[1]
    blocks, width, triple = w.shape
    both = triple // 3 * 2
    slots = x.shape[0] // 2
    part = width // 4
    raw_copies = [
        pltpu.make_async_copy(src, raw.at[i], sems.at[i])
        for i, src in enumerate((x_own, x_other, dy_own, dy_other))
    ]
    w_copies = []
    for i, pieces in enumerate(((o0, o1, o2), (u0, u1, u2), (d0, d1, d2))):
        w_copies += copy_pieces(pieces, w.at[i], sems.at[pl.ds(7 + 3 * i, 3)])
    for copy in raw_copies + w_copies:
        copy.start()
    spread = slot_matrix(slots, packed, 0, None)
    spread_tail = [slot_matrix(slots, packed, 0, j) for j in range(3)]
    for i, copy in enumerate(raw_copies):
        copy.wait()
        full = (x, dy)[i // 2]
        rows = slice(i % 2 * slots, (i % 2 + 1) * slots)
        pieces = [slice(j * part, (j + 1) * part) for j in range(3)]
        for j in range(3):
            full[rows, pieces[j]] = dot(spread, raw[i, :, pieces[j]]).astype(BF)
        last = dot(spread_tail[0], raw[i, :, pieces[0]])
        last += dot(spread_tail[1], raw[i, :, pieces[1]])
        last += dot(spread_tail[2], raw[i, :, pieces[2]])
        full[rows, 3 * part :] = last.astype(BF)
    x_out = pltpu.make_async_copy(x, x_hbm, sems.at[4])
    dy_out = pltpu.make_async_copy(dy, dy_hbm, sems.at[5])
    x_out.start()
    dy_out.start()
    for copy in w_copies:
        copy.wait()
    term_ref[...] = jnp.zeros_like(term_ref)

    def forward(b, _):
        term_ref[...] += block_forward(x, dy, w.at[b], grads.at[b])
        return 0

    lax.fori_loop(0, blocks, forward, 0)
    for j in range(4):
        cols = slice(j * part, (j + 1) * part)
        piece = dot_t(grads[0], w[0, cols, :both])
        for b in range(1, blocks):
            piece += dot_t(grads[b], w[b, cols, :both])
        total[:, cols] = piece.astype(BF)
    out = pltpu.make_async_copy(total, sum_hbm, sems.at[6])
    out.start()
    x_out.wait()
    dy_out.wait()
    out.wait()


def first_blocks(rows, weights):
    packed = rows[0].shape[0]
    slots = packed // ROWS * CAP
    triple = weights[0].shape[1]
    width = sum(w.shape[0] for w in weights[:3])
    hidden = triple // 3
    full = jax.ShapeDtypeStruct((2 * slots, width), BF)
    return pl.pallas_call(
        first_kernel,
        out_shape=(full, full, full, jax.ShapeDtypeStruct((2 * slots, hidden), F32)),
        in_specs=[pl.BlockSpec(memory_space=pl.ANY)] * 13,
        out_specs=(pl.BlockSpec(memory_space=pl.ANY),) * 3 + (pl.BlockSpec(memory_space=pltpu.VMEM),),
        scratch_shapes=[
            pltpu.VMEM((4,) + rows[0].shape, BF),
            pltpu.VMEM((2 * slots, width), BF),
            pltpu.VMEM((2 * slots, width), BF),
            pltpu.VMEM((3, width, triple), BF),
            pltpu.VMEM((3, 2 * slots, 2 * hidden), BF),
            pltpu.VMEM((2 * slots, width), BF),
            pltpu.SemaphoreType.DMA((16,)),
        ],
        compiler_params=pltpu.CompilerParams(vmem_limit_bytes=VMEM_LIMIT),
        cost_estimate=pl.CostEstimate(flops=FIRST_COST, bytes_accessed=FIRST_COST, transcendentals=0),
        name="first",
    )(*rows, *weights)


def last_kernel(
    x_hbm, dy_hbm, w0, w1, w2, w3, w4, w5, sum_hbm, term_ref,
    own_ref, other_ref,
    x, dy, w, total, grads, sems,
):
    packed = own_ref.shape[0]
    slots = x.shape[0] // 2
    part = x.shape[1] // 4
    both = grads.shape[1]
    copies = [
        pltpu.make_async_copy(src, dst, sems.at[i])
        for i, (src, dst) in enumerate(((x_hbm, x), (dy_hbm, dy), (sum_hbm, total)))
    ]
    copies = copies[:2] + copy_pieces((w0, w1, w2, w3, w4, w5), w, sems.at[pl.ds(3, 6)]) + copies[2:]
    for copy in copies:
        copy.start()
    gather = slot_matrix(slots, packed, 1, None)
    gather_tail = [slot_matrix(slots, packed, 1, j) for j in range(3)]
    for copy in copies[:-1]:
        copy.wait()
    term = term_ref[...] + block_forward(x, dy, w, grads)
    terms = jnp.broadcast_to(jnp.sum(term, axis=1, keepdims=True), (2 * slots, TERM_LANES)).astype(BF)
    copies[-1].wait()

    def backward(j):
        cols = slice(j * part, (j + 1) * part)
        piece = dot_t(grads[...], w[cols, :both])
        return (total[:, cols].astype(F32) + piece).astype(BF)

    outs = (own_ref, other_ref)
    spans = [slice(i * slots, (i + 1) * slots) for i in range(2)]
    for i in range(2):
        outs[i][:, 3 * part :] = dot(gather, terms[spans[i]]).astype(BF)
    last = backward(3)
    for j in range(3):
        rows = backward(j)
        for i in range(2):
            outs[i][:, j * part : (j + 1) * part] = (
                dot(gather, rows[spans[i]]) + dot(gather_tail[j], last[spans[i]])
            ).astype(BF)


def last_block(x, dy, weights, total, term, packed):
    rows, width = x.shape
    triple = weights[0].shape[1]
    hidden = triple // 3
    out = jax.ShapeDtypeStruct((packed, width // 4 * 3 + TERM_LANES), BF)
    return pl.pallas_call(
        last_kernel,
        out_shape=(out, out),
        in_specs=[pl.BlockSpec(memory_space=pl.ANY)] * 9 + [pl.BlockSpec(memory_space=pltpu.VMEM)],
        scratch_shapes=[
            pltpu.VMEM((rows, width), BF),
            pltpu.VMEM((rows, width), BF),
            pltpu.VMEM((width, triple), BF),
            pltpu.VMEM((rows, width), BF),
            pltpu.VMEM((rows, 2 * hidden), BF),
            pltpu.SemaphoreType.DMA((9,)),
        ],
        compiler_params=pltpu.CompilerParams(vmem_limit_bytes=VMEM_LIMIT),
        cost_estimate=pl.CostEstimate(
            flops=2 * rows * width * hidden * 5,
            bytes_accessed=2 * (width * triple + 5 * rows * width),
            transcendentals=rows * hidden,
        ),
        name="last",
    )(x, dy, *weights, total, term)


def add_kernel(a_ref, b_ref, out_ref):
    out_ref[...] = (a_ref[...].astype(F32) + b_ref[...].astype(F32)).astype(BF)


def add(a, b):
    rows, cols = a.shape
    spec = pl.BlockSpec((rows // 4, cols), lambda i: (i, 0))
    return pl.pallas_call(
        add_kernel,
        grid=(4,),
        out_shape=jax.ShapeDtypeStruct((rows, cols), BF),
        in_specs=[spec, spec],
        out_specs=spec,
        compiler_params=pltpu.CompilerParams(vmem_limit_bytes=VMEM_LIMIT),
        cost_estimate=pl.CostEstimate(flops=rows * cols, bytes_accessed=6 * rows * cols, transcendentals=0),
        name="add",
    )(a, b)


def combine_kernel(route_ref, gate_ref, own_term_ref, out_grad_ref, ret_ref, token_grad_ref, gate_grad_ref):
    n, width = out_grad_ref.shape
    packed = ret_ref.shape[0]
    part = width // 4
    experts = packed // ROWS
    route_row = route_ref[...]
    main, tail, block = (to_column(v) for v in places(route_row))
    routed = to_column(route_row) < experts
    gate = to_column(gate_ref[...])
    row = lax.broadcasted_iota(jnp.int32, (n, packed), 1)
    select = jnp.where(row == main, 1.0, 0.0).astype(BF)
    last = jnp.zeros((n, part), F32)
    for j in range(4):
        cols = pl.ds(j * part, part)
        if j < 3:
            tail_select = jnp.where((row == tail) & (block == j), 1.0, 0.0).astype(BF)
            piece = ret_ref[:, cols]
            rows = dot(select, piece)
            last += dot(tail_select, piece)
        else:
            rows = last
        rows = jnp.where(routed, rows, out_grad_ref[:, cols].astype(F32))
        token_grad_ref[:, cols] = (gate * rows).astype(BF)
    terms = dot(select, ret_ref[:, 3 * part :])[:, :1]
    gate_grad_ref[...] = jnp.where(route_row < experts, to_row(terms), own_term_ref[...]).astype(BF)


def combine(route_row, gate_row, own_term, out_grad, ret):
    n, width = out_grad.shape
    return pl.pallas_call(
        combine_kernel,
        out_shape=(jax.ShapeDtypeStruct((n, width), BF), jax.ShapeDtypeStruct((1, n), BF)),
        compiler_params=pltpu.CompilerParams(vmem_limit_bytes=VMEM_LIMIT),
        cost_estimate=pl.CostEstimate(
            flops=2 * ret.shape[0] * n * width * 3 // 2,
            bytes_accessed=2 * (2 * out_grad.size + ret.size),
            transcendentals=0,
        ),
        name="combine",
    )(route_row, gate_row, own_term, out_grad, ret)


def per_device(tokens, out_grad, gate, route, gate_weight, up_weight, down_weight):
    experts = lax.axis_size("expert")
    groups = lax.axis_size("tensor")
    n, width = tokens.shape
    core = lax.axis_index("dp")
    swap = [(0, 1), (1, 0)]
    up = [(i, (i + 1) % groups) for i in range(groups)]
    down = [(i, (i - 1) % groups) for i in range(groups)]
    route_row = route.reshape(1, n)

    weights = (gate_weight[0], up_weight[0], down_weight[0])
    core_id = core.reshape(1)
    first_part, last_part = weight_pieces(core_id, *weights, (0, UNITS - 1, 2), ((0, 1), (9, 10)))
    up_0 = lax.ppermute(first_part, "tensor", up)
    down_0 = lax.ppermute(last_part, "tensor", down)
    core_id, first_part, last_part = lax.optimization_barrier((core_id, first_part, last_part))
    pieces = weight_pieces(core_id, *weights, (0, 1, UNITS), ((1, 6), (6, 10), (4, 9), (0, 4)))
    route_row, up_next, up_rest, down_next, down_rest = lax.optimization_barrier((route_row, *pieces))
    unit = width // UNITS

    def exchange(rows):
        got = lax.all_to_all(
            rows.reshape(experts, ROWS, -1), "expert", split_axis=0, concat_axis=0, tiled=True
        )
        return got.reshape(experts * ROWS, -1)

    x_packed = pack(route_row, tokens, experts)
    x_packed, up_0, down_0 = lax.optimization_barrier((x_packed, up_0, down_0))
    x_own = exchange(x_packed)
    up_1 = lax.ppermute(up_next, "tensor", up)
    down_1 = lax.ppermute(down_next, "tensor", down)
    x_other = lax.ppermute(x_own, "dp", swap)

    dy_packed = pack(route_row, out_grad, experts)
    dy_packed, up_1, down_1 = lax.optimization_barrier((dy_packed, up_1, down_1))
    dy_own = exchange(dy_packed)
    up_2 = lax.ppermute(up_rest, "tensor", up)
    down_2 = lax.ppermute(down_rest, "tensor", down)
    far = {
        0: lax.ppermute(up_0, "tensor", up),
        9: lax.ppermute(down_0, "tensor", down),
        1: lax.ppermute(up_1[:unit], "tensor", up),
        8: lax.ppermute(down_1[4 * unit :], "tensor", down),
    }
    dy_own, up_2, down_2, far[0], far[1], far[8], far[9] = lax.optimization_barrier(
        (dy_own, up_2, down_2, far[0], far[1], far[8], far[9])
    )
    far[2] = lax.ppermute(up_1[unit : 4 * unit], "tensor", up)
    far[5] = lax.ppermute(down_1[unit : 4 * unit], "tensor", down)
    dy_other = lax.ppermute(dy_own, "dp", swap)

    x, dy, total, term = first_blocks(
        (x_own, x_other, dy_own, dy_other),
        (down_rest, down_next, last_part, up_0, up_1, up_2, down_2, down_1, down_0),
    )
    own, other = last_block(x, dy, [far[i] for i in (0, 1, 2, 5, 8, 9)], total, term, experts * ROWS)
    back = add(own, lax.ppermute(other, "dp", swap)).reshape(experts, ROWS, -1)
    ret = lax.all_to_all(back, "expert", split_axis=0, concat_axis=0, tiled=True)
    own_term = jnp.sum(out_grad.astype(F32) * tokens.astype(F32), axis=1)
    token_grad, gate_grad = combine(
        route_row, gate.reshape(1, n), own_term.reshape(1, n), out_grad, ret.reshape(experts * ROWS, -1)
    )
    return token_grad, gate_grad.reshape(n)


def solution(mesh):
    rows = P(("dp", "expert", "tensor"), None)
    return jax.shard_map(
        per_device,
        mesh=mesh,
        in_specs=(
            rows,
            rows,
            P(("dp", "expert", "tensor")),
            rows,
            P("expert", None, "tensor"),
            P("expert", None, "tensor"),
            P("expert", "tensor", None),
        ),
        out_specs=(rows, P(("dp", "expert", "tensor"))),
        check_vma=False,
    )
```

time: 282 us -> 262 us (0.929)
  waiting for transfers between devices: 188 us -> 136 us
  Pallas kernels: 37.3 us -> 62.1 us
  starting transfers between devices: 28 us -> 46.1 us
  between operations: 14.1 us -> 0.78 us
  local copies, waits for them, and re-layouts: 4.72 us -> 13.1 us
  other arithmetic: 7.82 us -> 2.26 us
    all_to_all x3, waiting for transfers between devices: 137 us -> 47.2 us  [the longest x1 46.7 us: per_device(): lax.all_to_all(back, 'expert', split_axis=0, concat_axis=0, tiled=True)]
    ppermute x3 -> x15, waiting for transfers between devices: 8.57 us -> 88.9 us  [the longest x1 38 us: per_device(): down_1 = lax.ppermute(down_next, 'tensor', down)]
    all_gather x2 -> x0, waiting for transfers between devices: 43.2 us -> none  [the longest x1 43.2 us: per_device(): lax.all_gather(jnp.concatenate(halves, axis=1), 'tensor', axis=0, tiled=F...]
    pallas_call x1 -> x5, Pallas kernels: 25.3 us -> 50.2 us  [the longest x1 22 us: first_blocks(): pl.pallas_call(first_kernel, out_shape=(full, full, full, jax.ShapeDtypeS...]
    ppermute x3 -> x15, starting transfers between devices: 0.19 us -> 15.7 us  [the longest x1 3.63 us: per_device(): far[2] = lax.ppermute(up_1[unit:4 * unit], 'tensor', up)]
    unnamed x2 -> x28, local copies, waits for them, and re-layouts: 1.69 us -> 8.4 us
    slice x0 -> x4, local copies, waits for them, and re-layouts: none -> 4.73 us  [the longest x1 2.54 us: per_device(): far[2] = lax.ppermute(up_1[unit:4 * unit], 'tensor', up)]
    reshape x1 -> x0, other arithmetic: 3.34 us -> none  [per_device(): (own.astype(F32) + from_other.astype(F32)).astype(BF)]
  transfers between devices with their start and end apart: 8 -> 18, of which waited for: 6 -> 10; matrix products, arithmetic and copies ran while one was open for 2% -> 3% of each run, Pallas kernels for 3% -> 15%
where the time goes in v2:
time: 262 us; the launch traced here: 260 us
  waiting for transfers between devices  136 us (52%)
  Pallas kernels  62.1 us (24%)
  starting transfers between devices  46.1 us (18%)
  local copies, waits for them, and re-layouts  13.1 us (5%)
    all_to_all x1, waiting for transfers between devices, per_device(): lax.all_to_all(back, 'expert', split_axis=0, concat_axis=0, tiled=True)  46.7 us
    ppermute x1, waiting for transfers between devices, per_device(): down_1 = lax.ppermute(down_next, 'tensor', down)  38 us
    ppermute x1, waiting for transfers between devices, per_device(): lax.ppermute(down_0, 'tensor', down)  34.8 us
    pallas_call x1, Pallas kernels, first_blocks(): pl.pallas_call(first_kernel, out_shape=(full, full, full, jax.ShapeDtypeS...  22 us
    all_to_all x2, starting transfers between devices, exchange(): lax.all_to_all(rows.reshape(experts, ROWS, -1), 'expert', split_axis=0, c...  20.8 us
    pallas_call x1, Pallas kernels, last_block(): pl.pallas_call(last_kernel, out_shape=(out, out), in_specs=[pl.BlockSpec(...  12.5 us
    pallas_call x2, Pallas kernels, weight_pieces(): pl.pallas_call(kernel, grid_spec=pltpu.PrefetchScalarGridSpec(num_scalar_...  11.4 us
    all_to_all x1, starting transfers between devices, per_device(): lax.all_to_all(back, 'expert', split_axis=0, concat_axis=0, tiled=True)  9.57 us
  transfers between devices with their start and end apart: 18, of which 10 were waited for; matrix products, arithmetic and copies ran while one was open for 3% of the time, Pallas kernels for 15%

profile of v2, /device:TPU:24, one launch (start us, length us, event | category | flops | bytes accessed | tf_op | source)
XLA Modules:
  0.0 260.4 jit_solution(16777162665536593560)
XLA Ops:
  0.6 2.3 weights.2
  2.9 2.0 collective-permute-start
  4.9 0.1 collective-permute-start.1
  5.0 9.1 %weights.3 = (bf16[2560,384]{1,0:T(8,128)(2,1)}, bf16[2048,384]{1,0:T(8,128)(2,1)}, bf16[2560,384]{1,0:T(8,128)(2,1)}, bf16[2048,384]{1,0:T(8,128)(2,1)}) custom-call(s32[1]{0:T(128)} %bitcast.1.core_ref, bf16[5120,256]{1,0:T(8,128)(2,1)} %bitcast.15, bf16[5120,256]{1,0:T(8,128)(2,1)} %bitcast.17, bf16[256,5120]{1,0:T(8,128)(2,1)} %bitcast.19), custom_call_target="tpu_custom_call" | custom-call | bytes 11796480 | tf_op jit(solution)/shard_map/weights/pallas_call | solution.py:100
  14.0 3.9 %pack.2 = bf16[256,3840]{1,0:T(8,128)(2,1)} custom-call(s32[1,128]{1,0:T(1,128)} %bitcast.26, bf16[128,5120]{1,0:T(8,128)(2,1)} %rows_ref.2), custom_call_target="tpu_custom_call" | custom-call | flops 503316480 | bytes 3276800 | tf_op jit(solution)/shard_map/pack/pallas_call | solution.py:67
  17.9 0.0 collective-permute-done.u0
  17.9 0.0 collective-permute-done.1.d2
  17.9 11.3 %all-to-all-start = ((bf16[32,8,3840]{2,1,0:T(8,128)(2,1)}), bf16[32,8,3840]{2,1,0:T(8,128)(2,1)S(1)}, u32[]{:S(2)}, u32[]{:S(2)}) async-start(bf16[32,8,3840]{2,1,0:T(8,128)(2,1)} %bitcast.25), calls=%async_computation | async-start | bytes 3932160 | tf_op jit(solution)/shard_map/all_to_all | solution.py:389
  29.3 0.8 collective-permute-start.4
  30.1 2.5 collective-permute-start.3
  32.6 3.9 %pack.3 = bf16[256,3840]{1,0:T(8,128)(2,1)} custom-call(s32[1,128]{1,0:T(1,128)} %bitcast.27, bf16[128,5120]{1,0:T(8,128)(2,1)} %out_grad_ref.1), custom_call_target="tpu_custom_call" | custom-call | flops 503316480 | bytes 3276800 | tf_op jit(solution)/shard_map/pack/pallas_call | solution.py:67
  36.5 38.0 %collective-permute-done.4.d1 = bf16[2560,384]{1,0:T(8,128)(2,1)S(1)} collective-permute-done((bf16[2560,384]{1,0:T(8,128)(2,1)}, bf16[2560,384]{1,0:T(8,128)(2,1)S(1)}, u32[]{:S(2)}, u32[]{:S(2)}) %collective-permute-start.4) | collective-permute-done | bytes 1966112 | tf_op jit(solution)/shard_map/ppermute | solution.py:398
  74.5 1.3 copy-done.3
  75.8 0.0 collective-permute-done.3.u1
  75.8 0.4 all-to-all-done
  76.2 9.5 %all-to-all-start.1 = ((bf16[32,8,3840]{2,1,0:T(8,128)(2,1)}), bf16[32,8,3840]{2,1,0:T(8,128)(2,1)}, u32[]{:S(2)}, u32[]{:S(2)}) async-start(bf16[32,8,3840]{2,1,0:T(8,128)(2,1)} %bitcast.24), calls=%async_computation.1 | async-start | bytes 3932160 | tf_op jit(solution)/shard_map/all_to_all | solution.py:389
  85.7 0.0 copy-done.7
  85.7 0.1 collective-permute-start.6
  85.8 3.2 %collective-permute-start.5 = (bf16[2048,384]{1,0:T(8,128)(2,1)}, bf16[2048,384]{1,0:T(8,128)(2,1)S(1)}, u32[]{:S(2)}, u32[]{:S(2)}) collective-permute-start(bf16[2048,384]{1,0:T(8,128)(2,1)} %get-tuple-element.48), channel_id=1, source_target_pairs={{0,2},{2,4},{4,6},{6,0},{1,3},{3,5},{5,7},{7,1},{8,10},{10,12},{12... | collective-permute-start | bytes 4718600 | tf_op jit(solution)/shard_map/ppermute | solution.py:404
  89.0 0.0 collective-permute-start.10
  89.0 3.2 %collective-permute-start.7 = (bf16[512,384]{1,0:T(8,128)(2,1)}, bf16[512,384]{1,0:T(8,128)(2,1)S(1)}, u32[]{:S(2)}, u32[]{:S(2)}) collective-permute-start(bf16[512,384]{1,0:T(8,128)(2,1)} %collective-permute-done.u0), channel_id=1, source_target_pairs={{0,2},{2,4},{4,6},{6,0},{1,3},{3,5},{5,7},{7,1},{8,10},{10,12},{12... | collective-permute-start | bytes 1179656 | tf_op jit(solution)/shard_map/ppermute | solution.py:407
  92.3 1.0 slice.12
  93.3 0.1 collective-permute-start.8
  93.4 1.0 slice.13
  94.4 34.8 %collective-permute-done.10.w5 = bf16[512,384]{1,0:T(8,128)(2,1)S(1)} collective-permute-done((bf16[512,384]{1,0:T(8,128)(2,1)}, bf16[512,384]{1,0:T(8,128)(2,1)S(1)}, u32[]{:S(2)}, u32[]{:S(2)}) %collective-permute-start.10) | collective-permute-done | bytes 393248 | tf_op jit(solution)/shard_map/ppermute | solution.py:408
  129.2 0.0 collective-permute-start.9
  129.2 3.4 %collective-permute-done.7.w0 = bf16[512,384]{1,0:T(8,128)(2,1)S(1)} collective-permute-done((bf16[512,384]{1,0:T(8,128)(2,1)}, bf16[512,384]{1,0:T(8,128)(2,1)S(1)}, u32[]{:S(2)}, u32[]{:S(2)}) %collective-permute-start.7) | collective-permute-done | bytes 393248 | tf_op jit(solution)/shard_map/ppermute | solution.py:407
  132.6 0.0 copy-done.2
  132.6 0.0 collective-permute-start.2
  132.6 0.0 collective-permute-done.6.d0
  132.6 0.0 copy-start.8
  132.6 1.2 copy-done.8
  133.8 0.0 collective-permute-done.5.u2
  133.8 1.2 copy-done.9
  135.0 2.1 collective-permute-done.8.w1
  137.1 0.0 copy-done.11
  137.1 0.0 copy-done.12
  137.1 0.8 copy-done.13
  137.9 0.4 collective-permute-done.9.w4
  138.3 0.0 all-to-all-done.1
  138.3 0.0 collective-permute-start.11
  138.3 2.5 slice.14
  140.9 0.0 copy-done.4
  140.9 0.1 slice.15
  141.0 3.6 %collective-permute-start.12 = (bf16[1536,384]{1,0:T(8,128)(2,1)}, bf16[1536,384]{1,0:T(8,128)(2,1)S(1)}, u32[]{:S(2)}, u32[]{:S(2)}) collective-permute-start(bf16[1536,384]{1,0:T(8,128)(2,1)} %slice.14), channel_id=1, source_target_pairs={{0,2},{2,4},{4,6},{6,0},{1,3},{3,5},{5,7},{7,1},{8,10},{10,12},{12... | collective-permute-start | bytes 3538952 | tf_op jit(solution)/shard_map/ppermute | solution.py:415
  144.6 0.0 collective-permute-start.13
  144.6 0.0 collective-permute-done.2.x_other
  144.6 0.0 collective-permute-done.11.dy_other
  144.7 0.0 copy-start.6
  144.7 1.3 copy-done.6
  146.0 22.0 %first.1 = (bf16[384,5120]{1,0:T(8,128)(2,1)}, bf16[384,5120]{1,0:T(8,128)(2,1)}, bf16[384,5120]{1,0:T(8,128)(2,1)}, f32[384,128]{1,0:T(8,128)}) custom-call(bf16[256,3840]{1,0:T(8,128)(2,1)} %bitcast.23, bf16[256,3840]{1,0:T(8,128)(2,1)} %collective-permute-done.2.x_other, bf16[256,3840]{1,0:T(8,128)(2,1)} %bitcast.10.dy_own, bf16[256,3840]{1,0:T(8,128)(2,1)} %copy-done.6, ...), custom_call_target="tpu_custom_call" | custom-call | flops 1000 | bytes 1000 | tf_op jit(solution)/shard_map/first/pallas_call | solution.py:218
  168.0 2.7 %collective-permute-done.12.w2 = bf16[1536,384]{1,0:T(8,128)(2,1)S(1)} collective-permute-done((bf16[1536,384]{1,0:T(8,128)(2,1)}, bf16[1536,384]{1,0:T(8,128)(2,1)S(1)}, u32[]{:S(2)}, u32[]{:S(2)}) %collective-permute-start.12) | collective-permute-done | bytes 1179680 | tf_op jit(solution)/shard_map/ppermute | solution.py:415
  170.7 3.2 %collective-permute-done.13.w3 = bf16[1536,384]{1,0:T(8,128)(2,1)} collective-permute-done((bf16[1536,384]{1,0:T(8,128)(2,1)S(1)}, bf16[1536,384]{1,0:T(8,128)(2,1)}, u32[]{:S(2)}, u32[]{:S(2)}) %collective-permute-start.13) | collective-permute-done | bytes 1179680 | tf_op jit(solution)/shard_map/ppermute | solution.py:416
  173.9 0.0 copy-done.10
  173.9 12.5 %last.1 = (bf16[256,3968]{1,0:T(8,128)(2,1)}, bf16[256,3968]{1,0:T(8,128)(2,1)}) custom-call(bf16[384,5120]{1,0:T(8,128)(2,1)} %get-tuple-element.58.x_hbm, bf16[384,5120]{1,0:T(8,128)(2,1)} %get-tuple-element.59.dy_hbm, bf16[512,384]{1,0:T(8,128)(2,1)} %copy-done.12, bf16[512,384]{1,0:T(8,128)(2,1)} %copy-done.13, bf16[1536,384]{1,0:T(8,128)(2,1)} %copy-done.10, ...), custom_call_target="tpu_custom_call" | custom-call | flops 2516582400 | bytes 23592960 | tf_op jit(solution)/shard_map/last/pallas_call | solution.py:285
  186.5 0.1 collective-permute-start.14
  186.6 4.3 %collective-permute-done.14.b_ref = bf16[256,3968]{1,0:T(8,128)(2,1)S(1)} collective-permute-done((bf16[256,3968]{1,0:T(8,128)(2,1)}, bf16[256,3968]{1,0:T(8,128)(2,1)S(1)}, u32[]{:S(2)}, u32[]{:S(2)}) %collective-permute-start.14) | collective-permute-done | bytes 2031648 | tf_op jit(solution)/shard_map/ppermute | solution.py:424
  190.8 1.3 copy-done.5
  192.1 4.3 %add.1 = bf16[256,3968]{1,0:T(8,128)(2,1)} custom-call(bf16[256,3968]{1,0:T(8,128)(2,1)} %get-tuple-element.66.a_ref, bf16[256,3968]{1,0:T(8,128)(2,1)} %copy-done.5), custom_call_target="tpu_custom_call" | custom-call | flops 1015808 | bytes 6094848 | tf_op jit(solution)/shard_map/add/pallas_call | solution.py:314
  196.4 9.6 %all-to-all-start.2 = ((bf16[32,8,3968]{2,1,0:T(8,128)(2,1)}), bf16[32,8,3968]{2,1,0:T(8,128)(2,1)S(1)}, u32[]{:S(2)}, u32[]{:S(2)}) async-start(bf16[32,8,3968]{2,1,0:T(8,128)(2,1)} %bitcast.20), calls=%async_computation.2 | async-start | bytes 4063232 | tf_op jit(solution)/shard_map/all_to_all | solution.py:425
  206.0 2.3 multiply_reduce_fusion
  208.2 46.7 %all-to-all-done.2 = bf16[32,8,3968]{2,1,0:T(8,128)(2,1)S(1)} async-done(((bf16[32,8,3968]{2,1,0:T(8,128)(2,1)}), bf16[32,8,3968]{2,1,0:T(8,128)(2,1)S(1)}, u32[]{:S(2)}, u32[]{:S(2)}) %all-to-all-start.2) | async-done | bytes 2031648 | tf_op jit(solution)/shard_map/all_to_all | solution.py:425
  255.0 1.3 copy-done.1
  256.3 4.1 %combine.1 = (bf16[128,5120]{1,0:T(8,128)(2,1)}, bf16[1,128]{1,0:T(2,128)(2,1)}) custom-call(s32[1,128]{1,0:T(1,128)} %bitcast.28, f32[1,128]{1,0:T(1,128)} %bitcast.30, f32[1,128]{1,0:T(1,128)} %bitcast.29, bf16[128,5120]{1,0:T(8,128)(2,1)} %out_grad_ref.1, bf16[256,3968]{1,0:T(8,128)(2,1)} %bitcast.21), custom_call_target="tpu_custom_call" | custom-call | flops 503316480 | bytes 4653056 | tf_op jit(solution)/shard_map/combine/pallas_call | solution.py:355
  (13 shorter events, 0.0 us)
Async XLA Ops:
  2.9 15.0 %collective-permute-start = (bf16[512,384]{1,0:T(8,128)(2,1)}, bf16[512,384]{1,0:T(8,128)(2,1)}, u32[]{:S(2)}, u32[]{:S(2)}) collective-permute-start(bf16[512,384]{1,0:T(8,128)(2,1)} %get-tuple-element.36), channel_id=1, source_target_pairs={{0,2},{2,4},{4,6},{6,0},{1,3},{3,5},{5,7},{7,1},{8,10},{10,12},{12... | collective-permute-start | bytes 1179656 | tf_op jit(solution)/shard_map/ppermute | solution.py:381
  4.9 13.0 %collective-permute-start.1 = (bf16[512,384]{1,0:T(8,128)(2,1)}, bf16[512,384]{1,0:T(8,128)(2,1)}, u32[]{:S(2)}, u32[]{:S(2)}) collective-permute-start(bf16[512,384]{1,0:T(8,128)(2,1)} %get-tuple-element.55.o2), channel_id=1, source_target_pairs={{0,6},{2,0},{4,2},{6,4},{1,7},{3,1},{5,3},{7,5},{8,14},{10,8},{12,... | collective-permute-start | bytes 1179656 | tf_op jit(solution)/shard_map/ppermute | solution.py:382
  17.9 58.3 %all-to-all-start = ((bf16[32,8,3840]{2,1,0:T(8,128)(2,1)}), bf16[32,8,3840]{2,1,0:T(8,128)(2,1)S(1)}, u32[]{:S(2)}, u32[]{:S(2)}) async-start(bf16[32,8,3840]{2,1,0:T(8,128)(2,1)} %bitcast.25), calls=%async_computation | async-start | bytes 3932160 | tf_op jit(solution)/shard_map/all_to_all | solution.py:389
  29.3 45.2 %collective-permute-start.4 = (bf16[2560,384]{1,0:T(8,128)(2,1)}, bf16[2560,384]{1,0:T(8,128)(2,1)S(1)}, u32[]{:S(2)}, u32[]{:S(2)}) collective-permute-start(bf16[2560,384]{1,0:T(8,128)(2,1)} %get-tuple-element.46.o1), channel_id=1, source_target_pairs={{0,6},{2,0},{4,2},{6,4},{1,7},{3,1},{5,3},{7,5},{8,14},{10,8},{12,... | collective-permute-start | bytes 5898248 | tf_op jit(solution)/shard_map/ppermute | solution.py:398
  30.1 45.7 %collective-permute-start.3 = (bf16[2560,384]{1,0:T(8,128)(2,1)}, bf16[2560,384]{1,0:T(8,128)(2,1)}, u32[]{:S(2)}, u32[]{:S(2)}) collective-permute-start(bf16[2560,384]{1,0:T(8,128)(2,1)} %get-tuple-element.45), channel_id=1, source_target_pairs={{0,2},{2,4},{4,6},{6,0},{1,3},{3,5},{5,7},{7,1},{8,10},{10,12},{12... | collective-permute-start | bytes 5898248 | tf_op jit(solution)/shard_map/ppermute | solution.py:397
  74.5 1.3 copy-start.3
  76.2 56.4 %copy-start.2 = (bf16[32,8,3840]{2,1,0:T(8,128)(2,1)}, bf16[32,8,3840]{2,1,0:T(8,128)(2,1)S(1)}, u32[]{:S(2)}) copy-start(bf16[32,8,3840]{2,1,0:T(8,128)(2,1)S(1)} %all-to-all-done) | copy-start | bytes 5898244
  76.2 9.5 %copy-start.7 = (bf16[2048,384]{1,0:T(8,128)(2,1)S(1)}, bf16[2048,384]{1,0:T(8,128)(2,1)}, u32[]{:S(2)}) copy-start(bf16[2048,384]{1,0:T(8,128)(2,1)} %get-tuple-element.49.o0) | copy-start | bytes 4718596
  76.2 62.1 %all-to-all-start.1 = ((bf16[32,8,3840]{2,1,0:T(8,128)(2,1)}), bf16[32,8,3840]{2,1,0:T(8,128)(2,1)}, u32[]{:S(2)}, u32[]{:S(2)}) async-start(bf16[32,8,3840]{2,1,0:T(8,128)(2,1)} %bitcast.24), calls=%async_computation.1 | async-start | bytes 3932160 | tf_op jit(solution)/shard_map/all_to_all | solution.py:389
  85.7 46.9 %collective-permute-start.6 = (bf16[2048,384]{1,0:T(8,128)(2,1)S(1)}, bf16[2048,384]{1,0:T(8,128)(2,1)S(1)}, u32[]{:S(2)}, u32[]{:S(2)}) collective-permute-start(bf16[2048,384]{1,0:T(8,128)(2,1)S(1)} %copy-done.7), channel_id=1, source_target_pairs={{0,6},{2,0},{4,2},{6,4},{1,7},{3,1},{5,3},{7,5},{8,14},{10,8},{12,... | collective-permute-start | bytes 4718600 | tf_op jit(solution)/shard_map/ppermute | solution.py:405
  85.8 48.0 %collective-permute-start.5 = (bf16[2048,384]{1,0:T(8,128)(2,1)}, bf16[2048,384]{1,0:T(8,128)(2,1)S(1)}, u32[]{:S(2)}, u32[]{:S(2)}) collective-permute-start(bf16[2048,384]{1,0:T(8,128)(2,1)} %get-tuple-element.48), channel_id=1, source_target_pairs={{0,2},{2,4},{4,6},{6,0},{1,3},{3,5},{5,7},{7,1},{8,10},{10,12},{12... | collective-permute-start | bytes 4718600 | tf_op jit(solution)/shard_map/ppermute | solution.py:404
  89.0 40.2 %collective-permute-start.10 = (bf16[512,384]{1,0:T(8,128)(2,1)}, bf16[512,384]{1,0:T(8,128)(2,1)S(1)}, u32[]{:S(2)}, u32[]{:S(2)}) collective-permute-start(bf16[512,384]{1,0:T(8,128)(2,1)} %collective-permute-done.1.d2), channel_id=1, source_target_pairs={{0,6},{2,0},{4,2},{6,4},{1,7},{3,1},{5,3},{7,5},{8,14},{10,8},{12,... | collective-permute-start | bytes 1179656 | tf_op jit(solution)/shard_map/ppermute | solution.py:408
  89.0 43.6 %collective-permute-start.7 = (bf16[512,384]{1,0:T(8,128)(2,1)}, bf16[512,384]{1,0:T(8,128)(2,1)S(1)}, u32[]{:S(2)}, u32[]{:S(2)}) collective-permute-start(bf16[512,384]{1,0:T(8,128)(2,1)} %collective-permute-done.u0), channel_id=1, source_target_pairs={{0,2},{2,4},{4,6},{6,0},{1,3},{3,5},{5,7},{7,1},{8,10},{10,12},{12... | collective-permute-start | bytes 1179656 | tf_op jit(solution)/shard_map/ppermute | solution.py:407
  93.3 43.8 %collective-permute-start.8 = (bf16[512,384]{1,0:T(8,128)(2,1)S(1)}, bf16[512,384]{1,0:T(8,128)(2,1)S(1)}, u32[]{:S(2)}, u32[]{:S(2)}) collective-permute-start(bf16[512,384]{1,0:T(8,128)(2,1)S(1)} %slice.12), channel_id=1, source_target_pairs={{0,2},{2,4},{4,6},{6,0},{1,3},{3,5},{5,7},{7,1},{8,10},{10,12},{12... | collective-permute-start | bytes 1179656 | tf_op jit(solution)/shard_map/ppermute | solution.py:409
  129.2 7.9 %copy-start.11 = (bf16[512,384]{1,0:T(8,128)(2,1)}, bf16[512,384]{1,0:T(8,128)(2,1)S(1)}, u32[]{:S(2)}) copy-start(bf16[512,384]{1,0:T(8,128)(2,1)S(1)} %collective-permute-done.10.w5) | copy-start | bytes 1179652
  129.2 9.1 %collective-permute-start.9 = (bf16[512,384]{1,0:T(8,128)(2,1)S(1)}, bf16[512,384]{1,0:T(8,128)(2,1)}, u32[]{:S(2)}, u32[]{:S(2)}) collective-permute-start(bf16[512,384]{1,0:T(8,128)(2,1)S(1)} %slice.13), channel_id=1, source_target_pairs={{0,6},{2,0},{4,2},{6,4},{1,7},{3,1},{5,3},{7,5},{8,14},{10,8},{12,... | collective-permute-start | bytes 1179656 | tf_op jit(solution)/shard_map/ppermute | solution.py:410
  132.6 4.5 %copy-start.12 = (bf16[512,384]{1,0:T(8,128)(2,1)}, bf16[512,384]{1,0:T(8,128)(2,1)S(1)}, u32[]{:S(2)}) copy-start(bf16[512,384]{1,0:T(8,128)(2,1)S(1)} %collective-permute-done.7.w0) | copy-start | bytes 1179652
  132.6 12.0 %collective-permute-start.2 = (bf16[256,3840]{1,0:T(8,128)(2,1)S(1)}, bf16[256,3840]{1,0:T(8,128)(2,1)}, u32[]{:S(2)}, u32[]{:S(2)}) collective-permute-start(bf16[256,3840]{1,0:T(8,128)(2,1)S(1)} %bitcast.22), channel_id=1, source_target_pairs={{0,1},{1,0},{2,3},{3,2},{4,5},{5,4},{6,7},{7,6},{8,9},{9,8},{10,11... | collective-permute-start | bytes 5898248 | tf_op jit(solution)/shard_map/ppermute | solution.py:399
  132.6 1.2 copy-start.8
  133.8 1.2 copy-start.9
  137.1 0.8 copy-start.13
  138.3 2.6 copy-start.4
  138.3 6.3 %collective-permute-start.11 = (bf16[256,3840]{1,0:T(8,128)(2,1)}, bf16[256,3840]{1,0:T(8,128)(2,1)S(1)}, u32[]{:S(2)}, u32[]{:S(2)}) collective-permute-start(bf16[256,3840]{1,0:T(8,128)(2,1)} %bitcast.10.dy_own), channel_id=1, source_target_pairs={{0,1},{1,0},{2,3},{3,2},{4,5},{5,4},{6,7},{7,6},{8,9},{9,8},{10,11... | collective-permute-start | bytes 5898248 | tf_op jit(solution)/shard_map/ppermute | solution.py:417
  141.0 29.7 %collective-permute-start.12 = (bf16[1536,384]{1,0:T(8,128)(2,1)}, bf16[1536,384]{1,0:T(8,128)(2,1)S(1)}, u32[]{:S(2)}, u32[]{:S(2)}) collective-permute-start(bf16[1536,384]{1,0:T(8,128)(2,1)} %slice.14), channel_id=1, source_target_pairs={{0,2},{2,4},{4,6},{6,0},{1,3},{3,5},{5,7},{7,1},{8,10},{10,12},{12... | collective-permute-start | bytes 3538952 | tf_op jit(solution)/shard_map/ppermute | solution.py:415
  144.6 29.3 %collective-permute-start.13 = (bf16[1536,384]{1,0:T(8,128)(2,1)S(1)}, bf16[1536,384]{1,0:T(8,128)(2,1)}, u32[]{:S(2)}, u32[]{:S(2)}) collective-permute-start(bf16[1536,384]{1,0:T(8,128)(2,1)S(1)} %slice.15), channel_id=1, source_target_pairs={{0,6},{2,0},{4,2},{6,4},{1,7},{3,1},{5,3},{7,5},{8,14},{10,8},{12,... | collective-permute-start | bytes 3538952 | tf_op jit(solution)/shard_map/ppermute | solution.py:416
  144.7 1.3 copy-start.6
  170.7 3.2 %copy-start.10 = (bf16[1536,384]{1,0:T(8,128)(2,1)}, bf16[1536,384]{1,0:T(8,128)(2,1)S(1)}, u32[]{:S(2)}) copy-start(bf16[1536,384]{1,0:T(8,128)(2,1)S(1)} %collective-permute-done.12.w2) | copy-start | bytes 3538948
  186.5 4.4 %collective-permute-start.14 = (bf16[256,3968]{1,0:T(8,128)(2,1)}, bf16[256,3968]{1,0:T(8,128)(2,1)S(1)}, u32[]{:S(2)}, u32[]{:S(2)}) collective-permute-start(bf16[256,3968]{1,0:T(8,128)(2,1)} %get-tuple-element.67), channel_id=1, source_target_pairs={{0,1},{1,0},{2,3},{3,2},{4,5},{5,4},{6,7},{7,6},{8,9},{9,8},{10,11... | collective-permute-start | bytes 6094856 | tf_op jit(solution)/shard_map/ppermute | solution.py:424
  190.8 1.3 copy-start.5
  196.4 9.6 %copy-start = (bf16[128,5120]{1,0:T(8,128)(2,1)S(1)}, bf16[128,5120]{1,0:T(8,128)(2,1)}, u32[]{:S(2)}) copy-start(bf16[128,5120]{1,0:T(8,128)(2,1)} %out_grad_ref.1) | copy-start | bytes 3932164
  196.4 58.6 %all-to-all-start.2 = ((bf16[32,8,3968]{2,1,0:T(8,128)(2,1)}), bf16[32,8,3968]{2,1,0:T(8,128)(2,1)S(1)}, u32[]{:S(2)}, u32[]{:S(2)}) async-start(bf16[32,8,3968]{2,1,0:T(8,128)(2,1)} %bitcast.20), calls=%async_computation.2 | async-start | bytes 4063232 | tf_op jit(solution)/shard_map/all_to_all | solution.py:425
  255.0 1.3 copy-start.1

commit v3 on v1

v3 whole, which is shorter than its diff:
```python
import jax
import jax.numpy as jnp
from jax import lax
from jax.experimental import pallas as pl
from jax.experimental.pallas import tpu as pltpu
from jax.sharding import PartitionSpec as P

BF = jnp.bfloat16
F32 = jnp.float32
CAP = 6
ROWS = 8
TERM_LANES = 128
HALF_STEPS = 2
VMEM_ALL = 56 * 1024 * 1024
SMALL_VMEM = 20 * 1024 * 1024


def dot(a, b):
    return jnp.dot(a, b, preferred_element_type=F32)


def dot_t(a, b):
    return lax.dot_general(a, b, (((1,), (1,)), ((), ())), preferred_element_type=F32)


def eye(n):
    return lax.broadcasted_iota(jnp.int32, (n, n), 0) == lax.broadcasted_iota(jnp.int32, (n, n), 1)


def to_column(row):
    n = row.shape[1]
    return jnp.sum(jnp.where(eye(n), jnp.broadcast_to(row, (n, n)), 0), axis=1, keepdims=True)


def to_row(column):
    n = column.shape[0]
    return jnp.sum(jnp.where(eye(n), jnp.broadcast_to(column, (n, n)), 0), axis=0, keepdims=True)


def places(route_row):
    n = route_row.shape[1]
    across = jnp.broadcast_to(route_row, (n, n))
    down = jnp.broadcast_to(to_column(route_row), (n, n))
    earlier = lax.broadcasted_iota(jnp.int32, (n, n), 0) < lax.broadcasted_iota(jnp.int32, (n, n), 1)
    slot = jnp.sum(jnp.where((across == down) & earlier, 1, 0), axis=0, keepdims=True)
    second = jnp.where(slot >= 3, 1, 0)
    base = route_row * ROWS
    return base + slot, base + CAP + second, slot - 3 * second


def pack_kernel(route_ref, x_ref, dy_ref, out_ref):
    n, width = x_ref.shape
    total = out_ref.shape[0]
    part = width // 4
    main, tail, block = places(route_ref[...])
    row = lax.broadcasted_iota(jnp.int32, (total, n), 0)
    select = jnp.where(row == main, 1.0, 0.0).astype(BF)
    for j in range(3):
        tail_select = jnp.where((row == tail) & (block == j), 1.0, 0.0).astype(BF)
        cols = pl.ds(j * part, part)
        for i, rows_ref in enumerate((x_ref, dy_ref)):
            last = rows_ref[:, 3 * part :]
            out_ref[:, pl.ds((3 * i + j) * part, part)] = (
                dot(select, rows_ref[:, cols]) + dot(tail_select, last)
            ).astype(BF)


def pack(route_row, x, dy, experts):
    n, width = x.shape
    return pl.pallas_call(
        pack_kernel,
        out_shape=jax.ShapeDtypeStruct((experts * ROWS, width // 4 * 6), BF),
        compiler_params=pltpu.CompilerParams(vmem_limit_bytes=VMEM_ALL),
        cost_estimate=pl.CostEstimate(
            flops=2 * experts * ROWS * n * width * 3,
            bytes_accessed=4 * width * (n + experts * CAP),
            transcendentals=0,
        ),
        name="pack",
    )(route_row, x, dy)


def weights_kernel(core_ref, gate_ref, up_ref, down_ref, out_ref):
    rows, span = out_ref.shape
    hidden = down_ref.shape[0]
    i = pl.program_id(0)
    for part, ref in enumerate((gate_ref, up_ref)):

        @pl.when(i // HALF_STEPS == part)
        def _(ref=ref):
            out_ref[...] = ref[...]

    @pl.when(i // HALF_STEPS == 2)
    def _():
        for k in range(rows // hidden):
            out_ref[k * hidden : (k + 1) * hidden, :] = down_ref[:, k * span : (k + 1) * span]


def weight_stack(core, gate_weight, up_weight, down_weight):
    width, span = gate_weight.shape
    rows = width // 2 // HALF_STEPS

    def up_place(part):
        return lambda i, c: (c[0] * HALF_STEPS + jnp.clip(i - part * HALF_STEPS, 0, HALF_STEPS - 1), 0)

    return pl.pallas_call(
        weights_kernel,
        grid_spec=pltpu.PrefetchScalarGridSpec(
            num_scalar_prefetch=1,
            grid=(3 * HALF_STEPS,),
            in_specs=[
                pl.BlockSpec((rows, span), up_place(0)),
                pl.BlockSpec((rows, span), up_place(1)),
                pl.BlockSpec((span // 2, width // HALF_STEPS), lambda i, c: (c[0], jnp.maximum(i - 2 * HALF_STEPS, 0))),
            ],
            out_specs=pl.BlockSpec((rows, span), lambda i, c: (i, 0)),
        ),
        out_shape=jax.ShapeDtypeStruct((width * 3 // 2, span), BF),
        compiler_params=pltpu.CompilerParams(vmem_limit_bytes=VMEM_ALL),
        cost_estimate=pl.CostEstimate(
            flops=0, bytes_accessed=2 * 3 * width * span, transcendentals=0
        ),
        name="weights",
    )(core, gate_weight, up_weight, down_weight)


def slot_matrix(slots, packed, slot_dim, tail):
    shape = (slots, packed) if slot_dim == 0 else (packed, slots)
    slot = lax.broadcasted_iota(jnp.int32, shape, slot_dim)
    row = lax.broadcasted_iota(jnp.int32, shape, 1 - slot_dim)
    group, place = row >> 3, row & 7
    if tail is None:
        hit = (slot == group * CAP + place) & (place < CAP)
    else:
        hit = (slot == group * CAP + (place - CAP) * 3 + tail) & (place >= CAP)
    return jnp.where(hit, 1.0, 0.0).astype(BF)


def hidden_grads(pre_gate, pre_up, back):
    s = jax.nn.sigmoid(pre_gate)
    activated = pre_gate * s
    slope = s * (1.0 + pre_gate * (1.0 - s))
    return (back * pre_up * slope).astype(BF), (back * activated).astype(BF), activated * pre_up * back


def first_kernel(
    rows_hbm, gate_hbm, up_hbm, down_hbm,
    x_hbm, dy_hbm, sum_hbm, term_ref,
    raw, x, dy, gate, up, down, total, sems,
):
    packed = raw.shape[0]
    slots, part = x.shape[0], x.shape[1] // 4
    copies = [
        pltpu.make_async_copy(src, dst, sems.at[i])
        for i, (src, dst) in enumerate(((rows_hbm, raw), (gate_hbm, gate), (up_hbm, up), (down_hbm, down)))
    ]
    for copy in copies:
        copy.start()
    spread = slot_matrix(slots, packed, 0, None)
    spread_tail = [slot_matrix(slots, packed, 0, j) for j in range(3)]
    copies[0].wait()
    for k, full in enumerate((x, dy)):
        pieces = [slice((3 * k + j) * part, (3 * k + j + 1) * part) for j in range(3)]
        for j in range(3):
            full[:, j * part : (j + 1) * part] = dot(spread, raw[:, pieces[j]]).astype(BF)
        last = dot(spread_tail[0], raw[:, pieces[0]])
        last += dot(spread_tail[1], raw[:, pieces[1]])
        last += dot(spread_tail[2], raw[:, pieces[2]])
        full[:, 3 * part :] = last.astype(BF)
    outs = [
        pltpu.make_async_copy(src, dst, sems.at[4 + i])
        for i, (src, dst) in enumerate(((x, x_hbm), (dy, dy_hbm), (total, sum_hbm)))
    ]
    outs[0].start()
    outs[1].start()
    copies[1].wait()
    pre_gate = dot(x[...], gate[...])
    copies[2].wait()
    pre_up = dot(x[...], up[...])
    copies[3].wait()
    grad_gate, grad_up, term_ref[...] = hidden_grads(pre_gate, pre_up, dot_t(dy[...], down[...]))
    for j in range(4):
        cols = slice(j * part, (j + 1) * part)
        total[:, cols] = (dot_t(grad_gate, gate[cols, :]) + dot_t(grad_up, up[cols, :])).astype(BF)
    outs[2].start()
    for copy in outs:
        copy.wait()


def first_block(rows, gate_weight, up_weight, down_weight):
    packed = rows.shape[0]
    slots = packed // ROWS * CAP
    width, span = gate_weight.shape
    full = jax.ShapeDtypeStruct((slots, width), BF)
    any_spec = pl.BlockSpec(memory_space=pl.ANY)
    return pl.pallas_call(
        first_kernel,
        out_shape=(full, full, full, jax.ShapeDtypeStruct((slots, span), F32)),
        in_specs=[any_spec] * 4,
        out_specs=(any_spec,) * 3 + (pl.BlockSpec(memory_space=pltpu.VMEM),),
        scratch_shapes=[
            pltpu.VMEM(rows.shape, BF),
            pltpu.VMEM((slots, width), BF),
            pltpu.VMEM((slots, width), BF),
            pltpu.VMEM((width, span), BF),
            pltpu.VMEM((width, span), BF),
            pltpu.VMEM((span, width), BF),
            pltpu.VMEM((slots, width), BF),
            pltpu.SemaphoreType.DMA((7,)),
        ],
        compiler_params=pltpu.CompilerParams(vmem_limit_bytes=VMEM_ALL),
        cost_estimate=pl.CostEstimate(
            flops=2 * slots * width * span * 5,
            bytes_accessed=2 * (3 * width * span + rows.size + 3 * slots * width),
            transcendentals=slots * span,
        ),
        name="first",
    )(rows, gate_weight, up_weight, down_weight)


def rest_kernel(
    index_ref, x_hbm, dy_hbm, stack, stack_blocks, sum_hbm, term_ref,
    out_ref,
    x, dy, gu, down, total, grads, sems,
):
    packed = out_ref.shape[0]
    slots, width = x.shape
    part = width // 4
    span = stack.shape[3]
    half = width // 2
    hidden = span // 2
    groups = stack.shape[0]
    blocks = groups - 1
    x_copy = pltpu.make_async_copy(x_hbm, x, sems.at[0])
    dy_copy = pltpu.make_async_copy(dy_hbm, dy, sems.at[1])
    sum_copy = pltpu.make_async_copy(sum_hbm, total, sems.at[2])
    gu_copies, down_copies = [], []
    for b in range(blocks):
        index = lax.rem(index_ref[0] + 1 + b, groups)
        low = 3 + 6 * b
        gu_copies.append(
            [
                pltpu.make_async_copy(
                    stack.at[index, c, pl.ds(part_id * half, half)],
                    gu.at[pl.ds(c * half, half), pl.ds((2 * b + part_id) * span, span)],
                    sems.at[low + 2 * c + part_id],
                )
                for c in range(2)
                for part_id in range(2)
            ]
        )
        down_copies.append(
            [
                pltpu.make_async_copy(
                    stack_blocks.at[index, c, pl.ds(width // hidden, width // span)],
                    down.at[:, pl.ds((2 * b + c) * hidden, hidden)],
                    sems.at[low + 4 + c],
                )
                for c in range(2)
            ]
        )
    x_copy.start()
    for copy in gu_copies[0]:
        copy.start()
    dy_copy.start()
    for copies in gu_copies[1:] + down_copies:
        for copy in copies:
            copy.start()
    sum_copy.start()
    gather = slot_matrix(slots, packed, 1, None)
    gather_tail = [slot_matrix(slots, packed, 1, j) for j in range(3)]
    x_copy.wait()
    pres = []
    for b in range(blocks):
        for copy in gu_copies[b]:
            copy.wait()
        pres.append(dot(x[...], gu[:, 2 * b * span : 2 * (b + 1) * span]))
    dy_copy.wait()
    for copies in down_copies:
        for copy in copies:
            copy.wait()
    back = dot_t(dy[:, :span], down[0])
    for k in range(1, width // span):
        back += dot_t(dy[:, k * span : (k + 1) * span], down[k])
    term = term_ref[...]
    for b in range(blocks):
        low = 2 * b * span
        grad_gate, grad_up, more = hidden_grads(
            pres[b][:, :span], pres[b][:, span:], back[:, b * span : (b + 1) * span]
        )
        grads[:, low : low + span] = grad_gate
        grads[:, low + span : low + 2 * span] = grad_up
        term += more
    terms = jnp.broadcast_to(jnp.sum(term, axis=1, keepdims=True), (slots, TERM_LANES)).astype(BF)
    out_ref[:, 3 * part :] = dot(gather, terms).astype(BF)
    sum_copy.wait()

    def backward(j):
        cols = slice(j * part, (j + 1) * part)
        return (total[:, cols].astype(F32) + dot_t(grads[...], gu[cols, :])).astype(BF)

    last = backward(3)
    for j in range(3):
        out_ref[:, j * part : (j + 1) * part] = (dot(gather, backward(j)) + dot(gather_tail[j], last)).astype(BF)


def rest_blocks(index, x, dy, stacks, total, term, packed):
    slots, width = x.shape
    groups, cores, rows, span = stacks.shape
    blocks, hidden = groups - 1, span // 2
    any_spec = pl.BlockSpec(memory_space=pl.ANY)
    vmem_spec = pl.BlockSpec(memory_space=pltpu.VMEM)
    return pl.pallas_call(
        rest_kernel,
        out_shape=jax.ShapeDtypeStruct((packed, width // 4 * 3 + TERM_LANES), BF),
        in_specs=[pl.BlockSpec(memory_space=pltpu.SMEM)] + [any_spec] * 5 + [vmem_spec],
        out_specs=vmem_spec,
        scratch_shapes=[
            pltpu.VMEM((slots, width), BF),
            pltpu.VMEM((slots, width), BF),
            pltpu.VMEM((width, 2 * blocks * span), BF),
            pltpu.VMEM((width // span, blocks * span, span), BF),
            pltpu.VMEM((slots, width), BF),
            pltpu.VMEM((slots, 2 * blocks * span), BF),
            pltpu.SemaphoreType.DMA((3 + 6 * blocks,)),
        ],
        compiler_params=pltpu.CompilerParams(vmem_limit_bytes=VMEM_ALL),
        cost_estimate=pl.CostEstimate(
            flops=2 * slots * width * span * 5 * blocks,
            bytes_accessed=2 * (blocks * width * span * 3 + 4 * slots * width),
            transcendentals=slots * span * blocks,
        ),
        name="rest",
    )(index, x, dy, stacks, stacks.reshape(groups, cores, -1, hidden, span), total, term)


def combine_kernel(route_ref, gate_ref, own_term_ref, out_grad_ref, ret_ref, token_grad_ref, gate_grad_ref):
    n, width = out_grad_ref.shape
    packed = ret_ref.shape[0]
    part = width // 4
    experts = packed // ROWS
    route_row = route_ref[...]
    main, tail, block = (to_column(v) for v in places(route_row))
    routed = to_column(route_row) < experts
    gate = to_column(gate_ref[...])
    row = lax.broadcasted_iota(jnp.int32, (n, packed), 1)
    select = jnp.where(row == main, 1.0, 0.0).astype(BF)
    last = jnp.zeros((n, part), F32)
    for j in range(4):
        cols = pl.ds(j * part, part)
        if j < 3:
            tail_select = jnp.where((row == tail) & (block == j), 1.0, 0.0).astype(BF)
            piece = ret_ref[:, cols]
            rows = dot(select, piece)
            last += dot(tail_select, piece)
        else:
            rows = last
        rows = jnp.where(routed, rows, out_grad_ref[:, cols].astype(F32))
        token_grad_ref[:, cols] = (gate * rows).astype(BF)
    terms = dot(select, ret_ref[:, 3 * part :])[:, :1]
    gate_grad_ref[...] = jnp.where(route_row < experts, to_row(terms), own_term_ref[...]).astype(BF)


def combine(route_row, gate_row, own_term, out_grad, ret):
    n, width = out_grad.shape
    return pl.pallas_call(
        combine_kernel,
        out_shape=(jax.ShapeDtypeStruct((n, width), BF), jax.ShapeDtypeStruct((1, n), BF)),
        compiler_params=pltpu.CompilerParams(vmem_limit_bytes=SMALL_VMEM),
        cost_estimate=pl.CostEstimate(
            flops=2 * ret.shape[0] * n * width * 3 // 2,
            bytes_accessed=2 * (2 * out_grad.size + ret.size),
            transcendentals=0,
        ),
        name="combine",
    )(route_row, gate_row, own_term, out_grad, ret)


def per_device(tokens, out_grad, gate, route, gate_weight, up_weight, down_weight):
    experts = lax.axis_size("expert")
    n, width = tokens.shape
    core = lax.axis_index("dp")
    route_row = route.reshape(1, n)
    weights = (gate_weight[0], up_weight[0], down_weight[0])

    stack = weight_stack(core.reshape(1), *weights)
    stacks = lax.all_gather(stack, ("tensor", "dp"), axis=0, tiled=False)
    stacks = stacks.reshape(-1, 2, *stack.shape)

    pack_route, stack = lax.optimization_barrier((route_row, stack))
    packed = pack(pack_route, tokens, out_grad, experts).reshape(experts, ROWS, -1)
    got = lax.all_to_all(packed, "expert", split_axis=0, concat_axis=0, tiled=True)
    x, dy, total, term = first_block(got.reshape(experts * ROWS, -1), *weights)
    back = rest_blocks(
        lax.axis_index("tensor").reshape(1), x, dy, stacks, total, term, experts * ROWS
    ).reshape(experts, ROWS, -1)
    ret = lax.all_to_all(back, "expert", split_axis=0, concat_axis=0, tiled=True)
    own_term = jnp.sum(out_grad.astype(F32) * tokens.astype(F32), axis=1)
    token_grad, gate_grad = combine(
        route_row, gate.reshape(1, n), own_term.reshape(1, n), out_grad, ret.reshape(experts * ROWS, -1)
    )
    return token_grad, gate_grad.reshape(n)


def solution(mesh):
    rows = P(("dp", "expert", "tensor"), None)
    return jax.shard_map(
        per_device,
        mesh=mesh,
        in_specs=(
            rows,
            rows,
            P(("dp", "expert", "tensor")),
            rows,
            P("expert", None, "tensor"),
            P("expert", None, "tensor"),
            P("expert", "tensor", None),
        ),
        out_specs=(rows, P(("dp", "expert", "tensor"))),
        check_vma=False,
    )
```

time: 282 us -> 256 us (0.908)
  waiting for transfers between devices: 188 us -> 169 us
  Pallas kernels: 37.3 us -> 48 us
  starting transfers between devices: 28 us -> 21.8 us
  other arithmetic: 7.82 us -> 1.75 us
  local copies, waits for them, and re-layouts: 4.72 us -> 0.02 us
    pallas_call x1 -> x3, Pallas kernels: 25.3 us -> 39.9 us  [the longest x1 21.5 us: rest_blocks(): pl.pallas_call(rest_kernel, out_shape=jax.ShapeDtypeStruct((packed, width...]
    all_gather x2 -> x1, waiting for transfers between devices: 43.2 us -> 30.3 us  [per_device(): stacks = lax.all_gather(stack, ('tensor', 'dp'), axis=0, tiled=False)]
    ppermute x3 -> x0, waiting for transfers between devices: 8.57 us -> none  [the longest x2 4.31 us: send(): return (got, lax.ppermute(got, 'dp', swap))]
    all_to_all x3 -> x2, starting transfers between devices: 27.7 us -> 21.8 us  [the longest x1 11.6 us: per_device(): lax.all_to_all(packed, 'expert', split_axis=0, concat_axis=0, tiled=True)]
    reshape x1 -> x0, other arithmetic: 3.34 us -> none  [per_device(): (own.astype(F32) + from_other.astype(F32)).astype(BF)]
    dynamic_slice x2 -> x0, local copies, waits for them, and re-layouts: 3.03 us -> none  [the longest x1 1.89 us: per_device(): lax.dynamic_slice(w[0], (0, core * hidden), (width, hidden))]
    pallas_call x2 -> x1, Pallas kernels: 7.84 us -> 5.92 us  [pack(): pl.pallas_call(pack_kernel, out_shape=jax.ShapeDtypeStruct((experts * ROW...]
    all_to_all x3 -> x2, waiting for transfers between devices: 137 us -> 138 us  [the longest x1 91.2 us: per_device(): lax.all_to_all(packed, 'expert', split_axis=0, concat_axis=0, tiled=True)]
  transfers between devices with their start and end apart: 8 -> 3, of which waited for: 6 -> 3; matrix products, arithmetic and copies ran while one was open for 2% -> 1% of each run, Pallas kernels for 3% -> 7%
where the time goes in v3:
time: 256 us; the launch traced here: 254 us
  waiting for transfers between devices  169 us (66%)
  Pallas kernels  48 us (19%)
  starting transfers between devices  21.8 us (9%)
  between operations  14.1 us (6%)
    all_to_all x1, waiting for transfers between devices, per_device(): lax.all_to_all(packed, 'expert', split_axis=0, concat_axis=0, tiled=True)  91.2 us
    all_to_all x1, waiting for transfers between devices, per_device(): lax.all_to_all(back, 'expert', split_axis=0, concat_axis=0, tiled=True)  47.3 us
    all_gather x1, waiting for transfers between devices, per_device(): stacks = lax.all_gather(stack, ('tensor', 'dp'), axis=0, tiled=False)  30.3 us
    pallas_call x1, Pallas kernels, rest_blocks(): pl.pallas_call(rest_kernel, out_shape=jax.ShapeDtypeStruct((packed, width...  21.5 us
    pallas_call x1, Pallas kernels, first_block(): pl.pallas_call(first_kernel, out_shape=(full, full, full, jax.ShapeDtypeS...  12.1 us
    all_to_all x1, starting transfers between devices, per_device(): lax.all_to_all(packed, 'expert', split_axis=0, concat_axis=0, tiled=True)  11.6 us
    all_to_all x1, starting transfers between devices, per_device(): lax.all_to_all(back, 'expert', split_axis=0, concat_axis=0, tiled=True)  10.2 us
    pallas_call x1, Pallas kernels, weight_stack(): pl.pallas_call(weights_kernel, grid_spec=pltpu.PrefetchScalarGridSpec(num...  6.26 us
  transfers between devices with their start and end apart: 3, of which 3 were waited for; matrix products, arithmetic and copies ran while one was open for 1% of the time, Pallas kernels for 7%

profile of v3, /device:TPU:24, one launch (start us, length us, event | category | flops | bytes accessed | tf_op | source)
XLA Modules:
  0.0 254.5 jit_solution(13899924229517234717)
XLA Ops:
  7.2 0.0 all-gather.3.cloned.1.call-start
  7.2 6.3 %weights.1 = bf16[7680,256]{1,0:T(8,128)(2,1)} custom-call(s32[1]{0:T(128)} %bitcast.4.core_ref, bf16[5120,256]{1,0:T(8,128)(2,1)} %bitcast.23, bf16[5120,256]{1,0:T(8,128)(2,1)} %bitcast.25, bf16[256,5120]{1,0:T(8,128)(2,1)} %bitcast.27), custom_call_target="tpu_custom_call" | custom-call | bytes 7864320 | tf_op jit(solution)/shard_map/weights/pallas_call | solution.py:106
  13.5 0.0 all-gather.3.cloned.1.call-update
  13.5 5.9 %pack.1 = bf16[256,7680]{1,0:T(8,128)(2,1)} custom-call(s32[1,128]{1,0:T(1,128)} %bitcast.17, bf16[128,5120]{1,0:T(8,128)(2,1)} %x_ref.1, bf16[128,5120]{1,0:T(8,128)(2,1)} %out_grad_ref.1), custom_call_target="tpu_custom_call" | custom-call | flops 1006632960 | bytes 6553600 | tf_op jit(solution)/shard_map/pack/pallas_call | solution.py:70
  19.4 11.6 %all-to-all-start = ((bf16[32,8,7680]{2,1,0:T(8,128)(2,1)}), bf16[32,8,7680]{2,1,0:T(8,128)(2,1)}, u32[]{:S(2)}, u32[]{:S(2)}) async-start(bf16[32,8,7680]{2,1,0:T(8,128)(2,1)} %bitcast.22), calls=%async_computation | async-start | bytes 7864320 | tf_op jit(solution)/shard_map/all_to_all | solution.py:392
  31.0 91.2 %all-to-all-done = bf16[32,8,7680]{2,1,0:T(8,128)(2,1)} async-done(((bf16[32,8,7680]{2,1,0:T(8,128)(2,1)}), bf16[32,8,7680]{2,1,0:T(8,128)(2,1)}, u32[]{:S(2)}, u32[]{:S(2)}) %all-to-all-start) | async-done | bytes 3932192 | tf_op jit(solution)/shard_map/all_to_all | solution.py:392
  122.2 12.1 %first.1 = (bf16[192,5120]{1,0:T(8,128)(2,1)}, bf16[192,5120]{1,0:T(8,128)(2,1)}, bf16[192,5120]{1,0:T(8,128)(2,1)}, f32[192,256]{1,0:T(8,128)}) custom-call(bf16[256,7680]{1,0:T(8,128)(2,1)} %bitcast.9.rows_hbm, bf16[5120,256]{1,0:T(8,128)(2,1)} %bitcast.24, bf16[5120,256]{1,0:T(8,128)(2,1)} %bitcast.26, bf16[256,5120]{1,0:T(8,128)(2,1)} %bitcast.28), custom_call_target="tpu_custom_call" | custom-call | flops 2516582400 | bytes 17694720 | tf_op jit(solution)/shard_map/first/pallas_call | solution.py:196
  134.4 30.3 %all-gather.3.cloned.1.call-done = bf16[61440,256]{1,0:T(8,128)(2,1)} async-done(((bf16[7680,256]{1,0:T(8,128)(2,1)}), bf16[61440,256]{1,0:T(8,128)(2,1)}) %all-gather.3.cloned.1.call-update) | async-done | bytes 31457296 | tf_op jit(solution)/shard_map/all_gather | solution.py:387
  164.7 21.5 %rest.1 = bf16[256,3968]{1,0:T(8,128)(2,1)} custom-call(s32[1]{0:T(128)} %bitcast.3.index_ref, bf16[192,5120]{1,0:T(8,128)(2,1)} %get-tuple-element.10.x_hbm, bf16[192,5120]{1,0:T(8,128)(2,1)} %get-tuple-element.11.dy_hbm, bf16[4,2,7680,256]{3,2,1,0:T(8,128)(2,1)} %bitcast.20, bf16[4,2,60,128,256]{4,3,2,1,0:T(8,128)(2,1)} %bitcast.21, ...), custom_call_target="tpu_custom_call" | custom-call | flops 7549747200 | bytes 31457280 | tf_op jit(solution)/shard_map/rest/pallas_call | solution.py:313
  186.2 0.0 copy-start
  186.2 0.0 copy-start.1
  186.2 0.0 copy-start.2
  186.2 10.2 %all-to-all-start.1 = ((bf16[32,8,3968]{2,1,0:T(8,128)(2,1)}), bf16[32,8,3968]{2,1,0:T(8,128)(2,1)S(1)}, u32[]{:S(2)}, u32[]{:S(2)}) async-start(bf16[32,8,3968]{2,1,0:T(8,128)(2,1)} %bitcast.29), calls=%async_computation.1 | async-start | bytes 4063232 | tf_op jit(solution)/shard_map/all_to_all | solution.py:397
  196.4 0.0 copy-done
  196.5 1.7 multiply_reduce_fusion
  198.2 47.3 %all-to-all-done.1 = bf16[32,8,3968]{2,1,0:T(8,128)(2,1)S(1)} async-done(((bf16[32,8,3968]{2,1,0:T(8,128)(2,1)}), bf16[32,8,3968]{2,1,0:T(8,128)(2,1)S(1)}, u32[]{:S(2)}, u32[]{:S(2)}) %all-to-all-start.1) | async-done | bytes 2031648 | tf_op jit(solution)/shard_map/all_to_all | solution.py:397
  245.5 0.0 copy-done.1
  245.5 0.0 copy-done.2
  245.5 2.2 combine.1
Async XLA Ops:
  7.2 157.5 %all-gather.3.cloned.1.call-start = ((), (), s32[]{:S(2)}) async-start(), calls=%async_computation.2 | async-start | bytes 35389440 | tf_op jit(solution)/shard_map/all_gather | solution.py:387
  19.4 102.8 %all-to-all-start = ((bf16[32,8,7680]{2,1,0:T(8,128)(2,1)}), bf16[32,8,7680]{2,1,0:T(8,128)(2,1)}, u32[]{:S(2)}, u32[]{:S(2)}) async-start(bf16[32,8,7680]{2,1,0:T(8,128)(2,1)} %bitcast.22), calls=%async_computation | async-start | bytes 7864320 | tf_op jit(solution)/shard_map/all_to_all | solution.py:392
  186.2 10.2 %copy-start = (bf16[128,5120]{1,0:T(8,128)(2,1)S(1)}, bf16[128,5120]{1,0:T(8,128)(2,1)}, u32[]{:S(2)}) copy-start(bf16[128,5120]{1,0:T(8,128)(2,1)} %out_grad_ref.1) | copy-start | bytes 3932164
  186.2 59.3 %copy-start.1 = (s32[128,1]{0,1:T(1,128)S(1)}, s32[128,1]{0,1:T(1,128)}, u32[]{:S(2)}) copy-start(s32[128,1]{0,1:T(1,128)} %param.10) | copy-start | bytes 1540
  186.2 59.3 %copy-start.2 = (f32[128]{0:T(128)S(1)}, f32[128]{0:T(128)}, u32[]{:S(2)}) copy-start(f32[128]{0:T(128)} %param.9) | copy-start | bytes 1540
  186.2 59.2 %all-to-all-start.1 = ((bf16[32,8,3968]{2,1,0:T(8,128)(2,1)}), bf16[32,8,3968]{2,1,0:T(8,128)(2,1)S(1)}, u32[]{:S(2)}, u32[]{:S(2)}) async-start(bf16[32,8,3968]{2,1,0:T(8,128)(2,1)} %bitcast.29), calls=%async_computation.1 | async-start | bytes 4063232 | tf_op jit(solution)/shard_map/all_to_all | solution.py:397
Sparse Core Ops, SparseCore 0:
  13.6 151.0 all-gather.2

commit v4 on v1

v4 whole, which is shorter than its diff:
```python
import functools

import jax
import jax.numpy as jnp
from jax import lax
from jax.experimental import pallas as pl
from jax.experimental.pallas import tpu as pltpu
from jax.sharding import PartitionSpec as P

BF = jnp.bfloat16
F32 = jnp.float32
CAP = 6
ROWS = 8
TERM_LANES = 128
PARTS = 60
UP_PARTS = 40
HEAD = 6
HALF = 30
VMEM_ALL = 56 * 1024 * 1024
SMALL_VMEM = 20 * 1024 * 1024


def dot(a, b):
    return jnp.dot(a, b, preferred_element_type=F32)


def dot_t(a, b):
    return lax.dot_general(a, b, (((1,), (1,)), ((), ())), preferred_element_type=F32)


def eye(n):
    return lax.broadcasted_iota(jnp.int32, (n, n), 0) == lax.broadcasted_iota(jnp.int32, (n, n), 1)


def to_column(row):
    n = row.shape[1]
    return jnp.sum(jnp.where(eye(n), jnp.broadcast_to(row, (n, n)), 0), axis=1, keepdims=True)


def to_row(column):
    n = column.shape[0]
    return jnp.sum(jnp.where(eye(n), jnp.broadcast_to(column, (n, n)), 0), axis=0, keepdims=True)


def places(route_row):
    n = route_row.shape[1]
    across = jnp.broadcast_to(route_row, (n, n))
    down = jnp.broadcast_to(to_column(route_row), (n, n))
    earlier = lax.broadcasted_iota(jnp.int32, (n, n), 0) < lax.broadcasted_iota(jnp.int32, (n, n), 1)
    slot = jnp.sum(jnp.where((across == down) & earlier, 1, 0), axis=0, keepdims=True)
    second = jnp.where(slot >= 3, 1, 0)
    base = route_row * ROWS
    return base + slot, base + CAP + second, slot - 3 * second


def pack_kernel(route_ref, x_ref, dy_ref, out_ref):
    n, width = x_ref.shape
    total = out_ref.shape[0]
    part = width // 4
    main, tail, block = places(route_ref[...])
    row = lax.broadcasted_iota(jnp.int32, (total, n), 0)
    select = jnp.where(row == main, 1.0, 0.0).astype(BF)
    for j in range(3):
        tail_select = jnp.where((row == tail) & (block == j), 1.0, 0.0).astype(BF)
        cols = pl.ds(j * part, part)
        for i, rows_ref in enumerate((x_ref, dy_ref)):
            last = rows_ref[:, 3 * part :]
            out_ref[:, pl.ds((3 * i + j) * part, part)] = (
                dot(select, rows_ref[:, cols]) + dot(tail_select, last)
            ).astype(BF)


def pack(route_row, x, dy, experts):
    n, width = x.shape
    return pl.pallas_call(
        pack_kernel,
        out_shape=jax.ShapeDtypeStruct((experts * ROWS, width // 4 * 6), BF),
        compiler_params=pltpu.CompilerParams(vmem_limit_bytes=VMEM_ALL),
        cost_estimate=pl.CostEstimate(
            flops=2 * experts * ROWS * n * width * 3,
            bytes_accessed=4 * width * (n + experts * CAP),
            transcendentals=0,
        ),
        name="pack",
    )(route_row, x, dy)


def part_copies(weights, core, low, high, out, sems):
    gate, up, down = weights
    hidden, span = out.shape[0] // (high - low), out.shape[1]
    columns = pl.ds(pl.multiple_of(core * hidden, hidden), hidden)
    last_up = min(high, UP_PARTS)
    copies = []
    if low < last_up:
        rows = slice(low * hidden, last_up * hidden)
        for i, ref in enumerate((gate, up)):
            dst = out.at[0 : (last_up - low) * hidden, i * hidden : (i + 1) * hidden]
            copies.append(pltpu.make_async_copy(ref.at[rows, columns], dst, sems.at[len(copies)]))
    for k in range(max(low, UP_PARTS), high):
        src = down.at[columns, (k - UP_PARTS) * span : (k - UP_PARTS + 1) * span]
        dst = out.at[(k - low) * hidden : (k - low + 1) * hidden, :]
        copies.append(pltpu.make_async_copy(src, dst, sems.at[len(copies)]))
    return copies


def weights_kernel(read, write, core_ref, gate, up, down, *refs):
    outs, held, sems = refs[: len(write)], refs[len(write) : -1], refs[-1]
    hidden = held[0].shape[1] // 2
    copies = []
    for (low, high), buffer in zip(read, held):
        copies += part_copies((gate, up, down), core_ref[0], low, high, buffer, sems.at[pl.ds(len(copies), PARTS)])
    for copy in copies:
        copy.start()
    for copy in copies:
        copy.wait()
    copies = []
    for i, ((low, high), out) in enumerate(zip(write, outs)):
        for (first, last), buffer in zip(read, held):
            if first <= low and high <= last:
                src = buffer.at[(low - first) * hidden : (high - first) * hidden, :]
                copies.append(pltpu.make_async_copy(src, out, sems.at[i]))
    for copy in copies:
        copy.start()
    for copy in copies:
        copy.wait()


def weight_parts(core, weights, read, write):
    width, span = weights[0].shape
    hidden = span // 2
    any_spec = pl.BlockSpec(memory_space=pl.ANY)
    size = lambda parts: ((parts[1] - parts[0]) * hidden, span)
    return pl.pallas_call(
        functools.partial(weights_kernel, read, write),
        out_shape=[jax.ShapeDtypeStruct(size(parts), BF) for parts in write],
        in_specs=[pl.BlockSpec(memory_space=pltpu.SMEM)] + [any_spec] * 3,
        out_specs=[any_spec] * len(write),
        scratch_shapes=[pltpu.VMEM(size(parts), BF) for parts in read]
        + [pltpu.SemaphoreType.DMA((2 * PARTS,))],
        compiler_params=pltpu.CompilerParams(vmem_limit_bytes=VMEM_ALL),
        cost_estimate=pl.CostEstimate(
            flops=0, bytes_accessed=4 * span * hidden * sum(b - a for a, b in read + write), transcendentals=0
        ),
        name="weights",
    )(core, *weights)


def block_copies(pieces, ranges, gu, down, place, sems):
    hidden, span = pieces[0].shape[1:]
    up_copies, down_copies = [], []
    for i, (piece, (low, high)) in enumerate(zip(pieces, ranges)):
        middle = min(max(low, UP_PARTS), high)
        if low < middle:
            up_copies.append(
                pltpu.make_async_copy(
                    piece.at[pl.ds(0, middle - low)],
                    gu.at[pl.ds(low, middle - low), :, pl.ds(place * span, span)],
                    sems.at[2 * i],
                )
            )
        if middle < high:
            down_copies.append(
                pltpu.make_async_copy(
                    piece.at[pl.ds(middle - low, high - middle)],
                    down.at[pl.ds(middle - UP_PARTS, high - middle), pl.ds(place * hidden, hidden)],
                    sems.at[2 * i + 1],
                )
            )
    return up_copies, down_copies


def slot_matrix(slots, packed, slot_dim, tail):
    shape = (slots, packed) if slot_dim == 0 else (packed, slots)
    slot = lax.broadcasted_iota(jnp.int32, shape, slot_dim)
    row = lax.broadcasted_iota(jnp.int32, shape, 1 - slot_dim)
    group, place = row >> 3, row & 7
    if tail is None:
        hit = (slot == group * CAP + place) & (place < CAP)
    else:
        hit = (slot == group * CAP + (place - CAP) * 3 + tail) & (place >= CAP)
    return jnp.where(hit, 1.0, 0.0).astype(BF)


def hidden_grads(x, dy, gu, down, grads, up_copies, down_copies):
    spans, total, span = down.shape
    blocks = len(up_copies)
    hidden = total // blocks
    width = x.shape[1]
    pres = []
    for b in range(blocks):
        for copy in up_copies[b]:
            copy.wait()
        pres.append(dot(x[...], gu[:, :, b * span : (b + 1) * span].reshape(width, span)))
    for copies in down_copies:
        for copy in copies:
            copy.wait()
    back = dot_t(dy[:, :span], down[0])
    for k in range(1, spans):
        back += dot_t(dy[:, k * span : (k + 1) * span], down[k])
    terms = None
    for b in range(blocks):
        pre_gate, pre_up = pres[b][:, :hidden], pres[b][:, hidden:]
        here = back[:, b * hidden : (b + 1) * hidden]
        s = jax.nn.sigmoid(pre_gate)
        activated = pre_gate * s
        slope = s * (1.0 + pre_gate * (1.0 - s))
        low = b * span
        grads[:, low : low + hidden] = (here * pre_up * slope).astype(BF)
        grads[:, low + hidden : low + span] = (here * activated).astype(BF)
        term = activated * pre_up * here
        terms = term if terms is None else terms + term
    return terms


def row_grads(grads, gu, j):
    parts, hidden, columns = gu.shape
    rows = slice(j * parts // 4, (j + 1) * parts // 4)
    return dot_t(grads[...], gu[rows].reshape(parts // 4 * hidden, columns))


def first_kernel(ranges, *refs):
    own_hbm, other_hbm = refs[:2]
    pieces, refs = refs[2 : 2 + sum(map(len, ranges))], refs[2 + sum(map(len, ranges)) :]
    x_hbm, dy_hbm, sum_hbm, term_ref, raw, x, dy, gu, down, grads, total, sems = refs
    packed = raw.shape[1]
    slots, part = x.shape[0] // 2, x.shape[1] // 4
    raw_copies = [pltpu.make_async_copy(src, raw.at[i], sems.at[i]) for i, src in enumerate((own_hbm, other_hbm))]
    up_copies, down_copies, used = [], [], 0
    for b, block in enumerate(ranges):
        here = pieces[used : used + len(block)]
        ups, downs = block_copies(here, block, gu, down, b, sems.at[pl.ds(5 + 2 * used, 2 * len(block))])
        used += len(block)
        up_copies.append(ups)
        down_copies.append(downs)
    for copies in [raw_copies] + up_copies + down_copies:
        for copy in copies:
            copy.start()
    spread = slot_matrix(slots, packed, 0, None)
    spread_tail = [slot_matrix(slots, packed, 0, j) for j in range(3)]
    for i in range(2):
        raw_copies[i].wait()
        rows = slice(i * slots, (i + 1) * slots)
        for k, full in enumerate((x, dy)):
            cols = [slice((3 * k + j) * part, (3 * k + j + 1) * part) for j in range(3)]
            for j in range(3):
                full[rows, j * part : (j + 1) * part] = dot(spread, raw[i, :, cols[j]]).astype(BF)
            last = dot(spread_tail[0], raw[i, :, cols[0]])
            last += dot(spread_tail[1], raw[i, :, cols[1]])
            last += dot(spread_tail[2], raw[i, :, cols[2]])
            full[rows, 3 * part :] = last.astype(BF)
    outs = [
        pltpu.make_async_copy(src, dst, sems.at[2 + i])
        for i, (src, dst) in enumerate(((x, x_hbm), (dy, dy_hbm), (total, sum_hbm)))
    ]
    outs[0].start()
    outs[1].start()
    term_ref[...] = hidden_grads(x, dy, gu, down, grads, up_copies, down_copies)
    for j in range(4):
        total[:, j * part : (j + 1) * part] = row_grads(grads, gu, j).astype(BF)
    outs[2].start()
    for copy in outs:
        copy.wait()


def first_blocks(own, other, blocks, ranges, width):
    packed = own.shape[0]
    slots = packed // ROWS * CAP
    hidden, span = blocks[0][0].shape[1:]
    count = len(blocks)
    pieces = [piece for block in blocks for piece in block]
    full = jax.ShapeDtypeStruct((2 * slots, width), BF)
    any_spec = pl.BlockSpec(memory_space=pl.ANY)
    return pl.pallas_call(
        functools.partial(first_kernel, ranges),
        out_shape=(full, full, full, jax.ShapeDtypeStruct((2 * slots, hidden), F32)),
        in_specs=[any_spec] * (2 + len(pieces)),
        out_specs=(any_spec,) * 3 + (pl.BlockSpec(memory_space=pltpu.VMEM),),
        scratch_shapes=[
            pltpu.VMEM((2,) + own.shape, BF),
            pltpu.VMEM((2 * slots, width), BF),
            pltpu.VMEM((2 * slots, width), BF),
            pltpu.VMEM((UP_PARTS, hidden, count * span), BF),
            pltpu.VMEM((PARTS - UP_PARTS, count * hidden, span), BF),
            pltpu.VMEM((2 * slots, count * span), BF),
            pltpu.VMEM((2 * slots, width), BF),
            pltpu.SemaphoreType.DMA((5 + 2 * len(pieces),)),
        ],
        compiler_params=pltpu.CompilerParams(vmem_limit_bytes=VMEM_ALL),
        cost_estimate=pl.CostEstimate(
            flops=2 * 2 * slots * width * hidden * count * 5,
            bytes_accessed=2 * (count * 3 * width * hidden + 2 * own.size + 6 * slots * width),
            transcendentals=2 * slots * hidden * count,
        ),
        name="first",
    )(own, other, *pieces)


def last_kernel(ranges, *refs):
    pieces, refs = refs[: len(ranges)], refs[len(ranges) :]
    x_hbm, dy_hbm, sum_hbm, term_ref, own_ref, other_ref, x, dy, gu, down, total, grads, sems = refs
    packed = own_ref.shape[0]
    slots, part = x.shape[0] // 2, x.shape[1] // 4
    x_copy = pltpu.make_async_copy(x_hbm, x, sems.at[0])
    dy_copy = pltpu.make_async_copy(dy_hbm, dy, sems.at[1])
    sum_copy = pltpu.make_async_copy(sum_hbm, total, sems.at[2])
    up_copies, down_copies = block_copies(pieces, ranges, gu, down, 0, sems.at[pl.ds(3, 2 * len(ranges))])
    for copy in [x_copy] + up_copies + [dy_copy] + down_copies + [sum_copy]:
        copy.start()
    gather = slot_matrix(slots, packed, 1, None)
    gather_tail = [slot_matrix(slots, packed, 1, j) for j in range(3)]
    x_copy.wait()
    terms = hidden_grads(x, dy, gu, down, grads, [up_copies], [down_copies + [dy_copy]]) + term_ref[...]
    terms = jnp.broadcast_to(jnp.sum(terms, axis=1, keepdims=True), (2 * slots, TERM_LANES)).astype(BF)
    sum_copy.wait()

    def backward(j):
        return (total[:, j * part : (j + 1) * part].astype(F32) + row_grads(grads, gu, j)).astype(BF)

    outs = (own_ref, other_ref)
    spans = [slice(i * slots, (i + 1) * slots) for i in range(2)]
    for i in range(2):
        outs[i][:, 3 * part :] = dot(gather, terms[spans[i]]).astype(BF)
    last = backward(3)
    for j in range(3):
        rows = backward(j)
        for i in range(2):
            outs[i][:, j * part : (j + 1) * part] = (
                dot(gather, rows[spans[i]]) + dot(gather_tail[j], last[spans[i]])
            ).astype(BF)


def last_block(pieces, ranges, x, dy, total, term, packed):
    rows, width = x.shape
    hidden, span = pieces[0].shape[1:]
    out = jax.ShapeDtypeStruct((packed, width // 4 * 3 + TERM_LANES), BF)
    any_spec = pl.BlockSpec(memory_space=pl.ANY)
    vmem_spec = pl.BlockSpec(memory_space=pltpu.VMEM)
    return pl.pallas_call(
        functools.partial(last_kernel, ranges),
        out_shape=(out, out),
        in_specs=[any_spec] * (len(pieces) + 3) + [vmem_spec],
        out_specs=(vmem_spec, vmem_spec),
        scratch_shapes=[
            pltpu.VMEM((rows, width), BF),
            pltpu.VMEM((rows, width), BF),
            pltpu.VMEM((UP_PARTS, hidden, span), BF),
            pltpu.VMEM((PARTS - UP_PARTS, hidden, span), BF),
            pltpu.VMEM((rows, width), BF),
            pltpu.VMEM((rows, span), BF),
            pltpu.SemaphoreType.DMA((3 + 2 * len(pieces),)),
        ],
        compiler_params=pltpu.CompilerParams(vmem_limit_bytes=VMEM_ALL),
        cost_estimate=pl.CostEstimate(
            flops=2 * rows * width * hidden * 5,
            bytes_accessed=2 * (3 * width * hidden + 5 * rows * width),
            transcendentals=rows * hidden,
        ),
        name="last",
    )(*pieces, x, dy, total, term)


def combine_kernel(route_ref, gate_ref, own_term_ref, out_grad_ref, ret_ref, token_grad_ref, gate_grad_ref):
    n, width = out_grad_ref.shape
    packed = ret_ref.shape[0]
    part = width // 4
    experts = packed // ROWS
    route_row = route_ref[...]
    main, tail, block = (to_column(v) for v in places(route_row))
    routed = to_column(route_row) < experts
    gate = to_column(gate_ref[...])
    row = lax.broadcasted_iota(jnp.int32, (n, packed), 1)
    select = jnp.where(row == main, 1.0, 0.0).astype(BF)
    last = jnp.zeros((n, part), F32)
    for j in range(4):
        cols = pl.ds(j * part, part)
        if j < 3:
            tail_select = jnp.where((row == tail) & (block == j), 1.0, 0.0).astype(BF)
            piece = ret_ref[:, cols]
            rows = dot(select, piece)
            last += dot(tail_select, piece)
        else:
            rows = last
        rows = jnp.where(routed, rows, out_grad_ref[:, cols].astype(F32))
        token_grad_ref[:, cols] = (gate * rows).astype(BF)
    terms = dot(select, ret_ref[:, 3 * part :])[:, :1]
    gate_grad_ref[...] = jnp.where(route_row < experts, to_row(terms), own_term_ref[...]).astype(BF)


def combine(route_row, gate_row, own_term, out_grad, ret):
    n, width = out_grad.shape
    return pl.pallas_call(
        combine_kernel,
        out_shape=(jax.ShapeDtypeStruct((n, width), BF), jax.ShapeDtypeStruct((1, n), BF)),
        compiler_params=pltpu.CompilerParams(vmem_limit_bytes=SMALL_VMEM),
        cost_estimate=pl.CostEstimate(
            flops=2 * ret.shape[0] * n * width * 3 // 2,
            bytes_accessed=2 * (2 * out_grad.size + ret.size),
            transcendentals=0,
        ),
        name="combine",
    )(route_row, gate_row, own_term, out_grad, ret)


def per_device(tokens, out_grad, gate, route, gate_weight, up_weight, down_weight):
    experts = lax.axis_size("expert")
    groups = lax.axis_size("tensor")
    n, width = tokens.shape
    swap = [(0, 1), (1, 0)]
    up = [(i, (i + 1) % groups) for i in range(groups)]
    down = [(i, (i - 1) % groups) for i in range(groups)]
    route_row = route.reshape(1, n)

    core = lax.axis_index("dp").reshape(1)
    weights = (gate_weight[0], up_weight[0], down_weight[0])
    ends = ((0, HEAD), (PARTS - HEAD, PARTS))
    rests = ((HEAD, PARTS), (0, PARTS - HEAD))
    head, tail = weight_parts(core, weights, ends, ends)
    up_head = lax.ppermute(head, "tensor", up)
    down_tail = lax.ppermute(tail, "tensor", down)
    core, head, tail = lax.optimization_barrier((core, head, tail))
    up_rest, down_rest = weight_parts(core, weights, ((0, PARTS),), rests)

    route_row, up_rest, down_rest = lax.optimization_barrier((route_row, up_rest, down_rest))
    packed = pack(route_row, tokens, out_grad, experts)
    packed, up_head, down_tail = lax.optimization_barrier((packed, up_head, down_tail))
    got = lax.all_to_all(
        packed.reshape(experts, ROWS, -1), "expert", split_axis=0, concat_axis=0, tiled=True
    ).reshape(experts * ROWS, -1)

    from_up = lax.ppermute(up_rest, "tensor", up)
    from_down = lax.ppermute(down_rest, "tensor", down)
    far_head = lax.ppermute(up_head, "tensor", up)
    far_tail = lax.ppermute(down_tail, "tensor", down)
    got, from_up, from_down, far_head, far_tail = lax.optimization_barrier(
        (got, from_up, from_down, far_head, far_tail)
    )
    part = width // UP_PARTS
    far_up = lax.ppermute(from_up[: (HALF - HEAD) * part], "tensor", up)
    far_down = lax.ppermute(from_down[HALF * part :], "tensor", down)
    got_other = lax.ppermute(got, "dp", swap)

    squares = lambda piece: piece.reshape(-1, part, 2 * part)
    blocks = ((head, up_rest), (up_head, from_up), (from_down, down_tail))
    ranges = ((ends[0], rests[0]),) * 2 + ((rests[1], ends[1]),)
    x, dy, total, term = first_blocks(got, got_other, [list(map(squares, b)) for b in blocks], ranges, width)
    far = (far_head, far_up, far_down, far_tail)
    far_ranges = (ends[0], (HEAD, HALF), (HALF, PARTS - HEAD), ends[1])
    own, other = last_block(list(map(squares, far)), far_ranges, x, dy, total, term, experts * ROWS)
    from_other = lax.ppermute(other, "dp", swap)
    back = (own.astype(F32) + from_other.astype(F32)).astype(BF).reshape(experts, ROWS, -1)
    ret = lax.all_to_all(back, "expert", split_axis=0, concat_axis=0, tiled=True)
    own_term = jnp.sum(out_grad.astype(F32) * tokens.astype(F32), axis=1)
    token_grad, gate_grad = combine(
        route_row, gate.reshape(1, n), own_term.reshape(1, n), out_grad, ret.reshape(experts * ROWS, -1)
    )
    return token_grad, gate_grad.reshape(n)


def solution(mesh):
    rows = P(("dp", "expert", "tensor"), None)
    return jax.shard_map(
        per_device,
        mesh=mesh,
        in_specs=(
            rows,
            rows,
            P(("dp", "expert", "tensor")),
            rows,
            P("expert", None, "tensor"),
            P("expert", None, "tensor"),
            P("expert", "tensor", None),
        ),
        out_specs=(rows, P(("dp", "expert", "tensor"))),
        check_vma=False,
    )
```

time: 282 us -> 242 us (0.86)
  waiting for transfers between devices: 188 us -> 151 us
  Pallas kernels: 37.3 us -> 53.9 us
  between operations: 14.1 us -> 0.73 us
    ppermute x2 -> x9, waiting for transfers between devices: 4.31 us -> 97.8 us  [the longest x1 81.4 us: per_device(): far_head = lax.ppermute(up_head, 'tensor', up)]
    all_to_all x3 -> x2, waiting for transfers between devices: 137 us -> 48.7 us  [the longest x1 47.3 us: per_device(): lax.all_to_all(back, 'expert', split_axis=0, concat_axis=0, tiled=True)]
    all_gather x2 -> x0, waiting for transfers between devices: 43.2 us -> none  [the longest x1 43.2 us: per_device(): lax.all_gather(jnp.concatenate(halves, axis=1), 'tensor', axis=0, tiled=F...]
    pallas_call x1 -> x4, Pallas kernels: 25.3 us -> 45.8 us  [the longest x1 23.3 us: first_blocks(): pl.pallas_call(functools.partial(first_kernel, ranges), out_shape=(full,...]
    all_to_all x3 -> x2, starting transfers between devices: 27.7 us -> 18.5 us  [the longest x1 11.4 us: per_device(): lax.all_to_all(packed.reshape(experts, ROWS, -1), 'expert', split_axis=0,...]
    ppermute x2 -> x9, starting transfers between devices: 0.1 us -> 9.22 us  [the longest x1 2.65 us: per_device(): far_head = lax.ppermute(up_head, 'tensor', up)]
    dynamic_slice x2 -> x0, local copies, waits for them, and re-layouts: 3.03 us -> none  [the longest x1 1.89 us: per_device(): lax.dynamic_slice(w[0], (0, core * hidden), (width, hidden))]
    pallas_call x2 -> x1, Pallas kernels: 7.84 us -> 5.89 us  [pack(): pl.pallas_call(pack_kernel, out_shape=jax.ShapeDtypeStruct((experts * ROW...]
  transfers between devices with their start and end apart: 8 -> 12, of which waited for: 6 -> 8; matrix products, arithmetic and copies ran while one was open for 2% -> 1% of each run, Pallas kernels for 3% -> 15%
where the time goes in v4:
time: 242 us
  waiting for transfers between devices  151 us (62%)
  Pallas kernels  53.9 us (22%)
  starting transfers between devices  27.8 us (11%)
  other arithmetic  5.09 us (2%)
  local copies, waits for them, and re-layouts  3.58 us (1%)
    ppermute x1, waiting for transfers between devices, per_device(): far_head = lax.ppermute(up_head, 'tensor', up)  81.4 us
    all_to_all x1, waiting for transfers between devices, per_device(): lax.all_to_all(back, 'expert', split_axis=0, concat_axis=0, tiled=True)  47.3 us
    pallas_call x1, Pallas kernels, first_blocks(): pl.pallas_call(functools.partial(first_kernel, ranges), out_shape=(full,...  23.3 us
    pallas_call x1, Pallas kernels, last_block(): pl.pallas_call(functools.partial(last_kernel, ranges), out_shape=(out, ou...  13.4 us
    all_to_all x1, starting transfers between devices, per_device(): lax.all_to_all(packed.reshape(experts, ROWS, -1), 'expert', split_axis=0,...  11.4 us
    pallas_call x2, Pallas kernels, weight_parts(): pl.pallas_call(functools.partial(weights_kernel, read, write), out_shape=...  9.02 us
    all_to_all x1, starting transfers between devices, per_device(): lax.all_to_all(back, 'expert', split_axis=0, concat_axis=0, tiled=True)  7.07 us
    ppermute x1, waiting for transfers between devices, per_device(): far_up = lax.ppermute(from_up[:(HALF - HEAD) * part], 'tensor', up)  6.51 us
  transfers between devices with their start and end apart: 12, of which 8 were waited for; matrix products, arithmetic and copies ran while one was open for 1% of the time, Pallas kernels for 15%

profile of v4, /device:TPU:24, one launch (start us, length us, event | category | flops | bytes accessed | tf_op | source)
XLA Modules:
  0.0 241.8 jit_solution(622687477742479755)
XLA Ops:
  0.6 3.1 %weights.2 = (bf16[768,256]{1,0:T(8,128)(2,1)}, bf16[768,256]{1,0:T(8,128)(2,1)}) custom-call(s32[1]{0:T(128)} %bitcast.1.core_ref, bf16[5120,256]{1,0:T(8,128)(2,1)} %bitcast.29, bf16[5120,256]{1,0:T(8,128)(2,1)} %bitcast.31, bf16[256,5120]{1,0:T(8,128)(2,1)} %bitcast.33), custom_call_target="tpu_custom_call" | custom-call | bytes 3145728 | tf_op jit(solution)/shard_map/weights/pallas_call | solution.py:133
  3.7 2.0 collective-permute-start
  5.8 0.1 collective-permute-start.1
  5.9 5.9 %weights.3 = (bf16[6912,256]{1,0:T(8,128)(2,1)}, bf16[6912,256]{1,0:T(8,128)(2,1)}) custom-call(s32[1]{0:T(128)} %bitcast.1.core_ref, bf16[5120,256]{1,0:T(8,128)(2,1)} %bitcast.30, bf16[5120,256]{1,0:T(8,128)(2,1)} %bitcast.32, bf16[256,5120]{1,0:T(8,128)(2,1)} %bitcast.34), custom_call_target="tpu_custom_call" | custom-call | bytes 22020096 | tf_op jit(solution)/shard_map/weights/pallas_call | solution.py:133
  11.8 5.9 %pack.1 = bf16[256,7680]{1,0:T(8,128)(2,1)} custom-call(s32[1,128]{1,0:T(1,128)} %bitcast.25, bf16[128,5120]{1,0:T(8,128)(2,1)} %x_ref.1, bf16[128,5120]{1,0:T(8,128)(2,1)} %out_grad_ref.1), custom_call_target="tpu_custom_call" | custom-call | flops 1006632960 | bytes 6553600 | tf_op jit(solution)/shard_map/pack/pallas_call | solution.py:75
  17.7 0.0 collective-permute-done
  17.7 0.0 collective-permute-done.1
  17.7 11.4 %all-to-all-start = ((bf16[32,8,7680]{2,1,0:T(8,128)(2,1)}), bf16[32,8,7680]{2,1,0:T(8,128)(2,1)}, u32[]{:S(2)}, u32[]{:S(2)}) async-start(bf16[32,8,7680]{2,1,0:T(8,128)(2,1)} %bitcast.28), calls=%async_computation | async-start | bytes 7864320 | tf_op jit(solution)/shard_map/all_to_all | solution.py:426
  29.1 1.5 collective-permute-start.2
  30.6 0.6 collective-permute-start.3
  31.2 2.6 %collective-permute-start.4 = (bf16[768,256]{1,0:T(8,128)(2,1)}, bf16[768,256]{1,0:T(8,128)(2,1)S(1)}, u32[]{:S(2)}, u32[]{:S(2)}) collective-permute-start(bf16[768,256]{1,0:T(8,128)(2,1)} %collective-permute-done), channel_id=1, source_target_pairs={{0,2},{2,4},{4,6},{6,0},{1,3},{3,5},{5,7},{7,1},{8,10},{10,12},{12... | collective-permute-start | bytes 1179656 | tf_op jit(solution)/shard_map/ppermute | solution.py:432
  33.9 0.0 collective-permute-start.5
  33.9 81.4 %collective-permute-done.4 = bf16[768,256]{1,0:T(8,128)(2,1)S(1)} collective-permute-done((bf16[768,256]{1,0:T(8,128)(2,1)}, bf16[768,256]{1,0:T(8,128)(2,1)S(1)}, u32[]{:S(2)}, u32[]{:S(2)}) %collective-permute-start.4) | collective-permute-done | bytes 393248 | tf_op jit(solution)/shard_map/ppermute | solution.py:432
  115.2 0.0 copy-start.6
  115.3 2.5 %collective-permute-done.5 = bf16[768,256]{1,0:T(8,128)(2,1)S(1)} collective-permute-done((bf16[768,256]{1,0:T(8,128)(2,1)}, bf16[768,256]{1,0:T(8,128)(2,1)S(1)}, u32[]{:S(2)}, u32[]{:S(2)}) %collective-permute-start.5) | collective-permute-done | bytes 393248 | tf_op jit(solution)/shard_map/ppermute | solution.py:433
  117.8 0.0 copy-start.7
  117.8 0.0 collective-permute-done.2
  117.8 0.0 copy-done.6
  117.8 0.7 copy-done.7
  118.5 0.0 copy-start.5
  118.5 0.0 collective-permute-done.3
  118.5 1.5 all-to-all-done
  120.0 0.0 collective-permute-start.8
  120.0 0.1 slice.6
  120.1 1.6 collective-permute-start.6
  121.7 0.0 copy-done.5
  121.7 1.5 slice.7
  123.2 0.8 collective-permute-start.7
  124.0 3.1 %collective-permute-done.8.refs_1_ = bf16[256,7680]{1,0:T(8,128)(2,1)} collective-permute-done((bf16[256,7680]{1,0:T(8,128)(2,1)}, bf16[256,7680]{1,0:T(8,128)(2,1)}, u32[]{:S(2)}, u32[]{:S(2)}) %collective-permute-start.8) | collective-permute-done | bytes 3932192 | tf_op jit(solution)/shard_map/ppermute | solution.py:440
  127.2 23.3 %first.1 = (bf16[384,5120]{1,0:T(8,128)(2,1)}, bf16[384,5120]{1,0:T(8,128)(2,1)}, bf16[384,5120]{1,0:T(8,128)(2,1)}, f32[384,128]{1,0:T(8,128)}) custom-call(bf16[256,7680]{1,0:T(8,128)(2,1)} %bitcast.8.refs_0_, bf16[256,7680]{1,0:T(8,128)(2,1)} %collective-permute-done.8.refs_1_, bf16[6,128,256]{2,1,0:T(8,128)(2,1)} %bitcast.41, ...), custom_call_target="tpu_custom_call" | custom-call | flops 7549747200 | bytes 31457280 | tf_op jit(solution)/shard_map/first/pallas_call | solution.py:273
  150.5 6.5 %collective-permute-done.6 = bf16[3072,256]{1,0:T(8,128)(2,1)S(1)} collective-permute-done((bf16[3072,256]{1,0:T(8,128)(2,1)S(1)}, bf16[3072,256]{1,0:T(8,128)(2,1)S(1)}, u32[]{:S(2)}, u32[]{:S(2)}) %collective-permute-start.6) | collective-permute-done | bytes 1572896 | tf_op jit(solution)/shard_map/ppermute | solution.py:438
  157.0 0.0 copy-start.3
  157.0 4.2 %collective-permute-done.7 = bf16[3072,256]{1,0:T(8,128)(2,1)S(1)} collective-permute-done((bf16[3072,256]{1,0:T(8,128)(2,1)S(1)}, bf16[3072,256]{1,0:T(8,128)(2,1)S(1)}, u32[]{:S(2)}, u32[]{:S(2)}) %collective-permute-start.7) | collective-permute-done | bytes 1572896 | tf_op jit(solution)/shard_map/ppermute | solution.py:439
  161.2 0.0 copy-start.4
  161.2 0.0 copy-done.3
  161.2 1.2 copy-done.4
  162.4 13.4 %last.1 = (bf16[256,3968]{1,0:T(8,128)(2,1)}, bf16[256,3968]{1,0:T(8,128)(2,1)}) custom-call(bf16[6,128,256]{2,1,0:T(8,128)(2,1)} %bitcast.38, bf16[24,128,256]{2,1,0:T(8,128)(2,1)} %bitcast.35, bf16[24,128,256]{2,1,0:T(8,128)(2,1)} %bitcast.36, bf16[6,128,256]{2,1,0:T(8,128)(2,1)} %bitcast.39, bf16[384,5120]{1,0:T(8,128)(2,1)} %get-tuple-element.44.refs_4_, ...), custom_call_target="tpu_custom_call" | custom-call | flops 2516582400 | bytes 23592960 | tf_op jit(solution)/shard_map/last/pallas_call | solution.py:338
  175.9 0.1 collective-permute-start.9
  176.0 4.3 %collective-permute-done.9 = bf16[256,3968]{1,0:T(8,128)(2,1)S(1)} collective-permute-done((bf16[256,3968]{1,0:T(8,128)(2,1)}, bf16[256,3968]{1,0:T(8,128)(2,1)S(1)}, u32[]{:S(2)}, u32[]{:S(2)}) %collective-permute-start.9) | collective-permute-done | bytes 2031648 | tf_op jit(solution)/shard_map/ppermute | solution.py:449
  180.2 3.3 %fusion = bf16[32,8,3968]{2,1,0:T(8,128)(2,1)} fusion(bf16[256,3968]{1,0:T(8,128)(2,1)S(1)} %collective-permute-done.9, bf16[256,3968]{1,0:T(8,128)(2,1)} %get-tuple-element.48), kind=kLoop, calls=%fused_computation.2 | loop fusion | flops 4063232 | bytes 6094848 | tf_op jit(solution)/shard_map/reshape | solution.py:450
  183.6 0.0 copy-start
  183.6 0.0 copy-start.1
  183.6 0.0 copy-start.2
  183.6 7.1 %all-to-all-start.1 = ((bf16[32,8,3968]{2,1,0:T(8,128)(2,1)}), bf16[32,8,3968]{2,1,0:T(8,128)(2,1)S(1)}, u32[]{:S(2)}, u32[]{:S(2)}) async-start(bf16[32,8,3968]{2,1,0:T(8,128)(2,1)} %fusion), calls=%async_computation.1 | async-start | bytes 4063232 | tf_op jit(solution)/shard_map/all_to_all | solution.py:451
  190.7 0.0 copy-done
  190.7 1.7 multiply_reduce_fusion
  192.4 47.3 %all-to-all-done.1 = bf16[32,8,3968]{2,1,0:T(8,128)(2,1)S(1)} async-done(((bf16[32,8,3968]{2,1,0:T(8,128)(2,1)}), bf16[32,8,3968]{2,1,0:T(8,128)(2,1)S(1)}, u32[]{:S(2)}, u32[]{:S(2)}) %all-to-all-start.1) | async-done | bytes 2031648 | tf_op jit(solution)/shard_map/all_to_all | solution.py:451
  239.7 0.0 copy-done.1
  239.7 0.0 copy-done.2
  239.7 2.2 combine.1
Async XLA Ops:
  3.7 13.9 %collective-permute-start = (bf16[768,256]{1,0:T(8,128)(2,1)}, bf16[768,256]{1,0:T(8,128)(2,1)}, u32[]{:S(2)}, u32[]{:S(2)}) collective-permute-start(bf16[768,256]{1,0:T(8,128)(2,1)} %get-tuple-element.43), channel_id=1, source_target_pairs={{0,2},{2,4},{4,6},{6,0},{1,3},{3,5},{5,7},{7,1},{8,10},{10,12},{12... | collective-permute-start | bytes 1179656 | tf_op jit(solution)/shard_map/ppermute | solution.py:418
  5.8 11.9 %collective-permute-start.1 = (bf16[768,256]{1,0:T(8,128)(2,1)}, bf16[768,256]{1,0:T(8,128)(2,1)}, u32[]{:S(2)}, u32[]{:S(2)}) collective-permute-start(bf16[768,256]{1,0:T(8,128)(2,1)} %get-tuple-element.28), channel_id=1, source_target_pairs={{0,6},{2,0},{4,2},{6,4},{1,7},{3,1},{5,3},{7,5},{8,14},{10,8},{12,... | collective-permute-start | bytes 1179656 | tf_op jit(solution)/shard_map/ppermute | solution.py:419
  17.7 102.4 %all-to-all-start = ((bf16[32,8,7680]{2,1,0:T(8,128)(2,1)}), bf16[32,8,7680]{2,1,0:T(8,128)(2,1)}, u32[]{:S(2)}, u32[]{:S(2)}) async-start(bf16[32,8,7680]{2,1,0:T(8,128)(2,1)} %bitcast.28), calls=%async_computation | async-start | bytes 7864320 | tf_op jit(solution)/shard_map/all_to_all | solution.py:426
  29.1 88.7 %collective-permute-start.2 = (bf16[6912,256]{1,0:T(8,128)(2,1)}, bf16[6912,256]{1,0:T(8,128)(2,1)S(1)}, u32[]{:S(2)}, u32[]{:S(2)}) collective-permute-start(bf16[6912,256]{1,0:T(8,128)(2,1)} %get-tuple-element.34), channel_id=1, source_target_pairs={{0,2},{2,4},{4,6},{6,0},{1,3},{3,5},{5,7},{7,1},{8,10},{10,12},{12... | collective-permute-start | bytes 10616840 | tf_op jit(solution)/shard_map/ppermute | solution.py:430
  30.6 87.9 %collective-permute-start.3 = (bf16[6912,256]{1,0:T(8,128)(2,1)}, bf16[6912,256]{1,0:T(8,128)(2,1)}, u32[]{:S(2)}, u32[]{:S(2)}) collective-permute-start(bf16[6912,256]{1,0:T(8,128)(2,1)} %get-tuple-element.35), channel_id=1, source_target_pairs={{0,6},{2,0},{4,2},{6,4},{1,7},{3,1},{5,3},{7,5},{8,14},{10,8},{12,... | collective-permute-start | bytes 10616840 | tf_op jit(solution)/shard_map/ppermute | solution.py:431
  31.2 84.0 %collective-permute-start.4 = (bf16[768,256]{1,0:T(8,128)(2,1)}, bf16[768,256]{1,0:T(8,128)(2,1)S(1)}, u32[]{:S(2)}, u32[]{:S(2)}) collective-permute-start(bf16[768,256]{1,0:T(8,128)(2,1)} %collective-permute-done), channel_id=1, source_target_pairs={{0,2},{2,4},{4,6},{6,0},{1,3},{3,5},{5,7},{7,1},{8,10},{10,12},{12... | collective-permute-start | bytes 1179656 | tf_op jit(solution)/shard_map/ppermute | solution.py:432
  33.9 83.9 %collective-permute-start.5 = (bf16[768,256]{1,0:T(8,128)(2,1)}, bf16[768,256]{1,0:T(8,128)(2,1)S(1)}, u32[]{:S(2)}, u32[]{:S(2)}) collective-permute-start(bf16[768,256]{1,0:T(8,128)(2,1)} %collective-permute-done.1), channel_id=1, source_target_pairs={{0,6},{2,0},{4,2},{6,4},{1,7},{3,1},{5,3},{7,5},{8,14},{10,8},{12,... | collective-permute-start | bytes 1179656 | tf_op jit(solution)/shard_map/ppermute | solution.py:433
  115.2 2.5 %copy-start.6 = (bf16[768,256]{1,0:T(8,128)(2,1)}, bf16[768,256]{1,0:T(8,128)(2,1)S(1)}, u32[]{:S(2)}) copy-start(bf16[768,256]{1,0:T(8,128)(2,1)S(1)} %collective-permute-done.4) | copy-start | bytes 1179652
  117.8 0.8 copy-start.7
  118.5 3.2 %copy-start.5 = (bf16[6912,256]{1,0:T(8,128)(2,1)}, bf16[6912,256]{1,0:T(8,128)(2,1)S(1)}, u32[]{:S(2)}) copy-start(bf16[6912,256]{1,0:T(8,128)(2,1)S(1)} %collective-permute-done.2) | copy-start | bytes 10616836
  120.0 7.1 %collective-permute-start.8 = (bf16[256,7680]{1,0:T(8,128)(2,1)}, bf16[256,7680]{1,0:T(8,128)(2,1)}, u32[]{:S(2)}, u32[]{:S(2)}) collective-permute-start(bf16[256,7680]{1,0:T(8,128)(2,1)} %bitcast.8.refs_0_), channel_id=1, source_target_pairs={{0,1},{1,0},{2,3},{3,2},{4,5},{5,4},{6,7},{7,6},{8,9},{9,8},{10,11... | collective-permute-start | bytes 11796488 | tf_op jit(solution)/shard_map/ppermute | solution.py:440
  120.1 36.9 %collective-permute-start.6 = (bf16[3072,256]{1,0:T(8,128)(2,1)S(1)}, bf16[3072,256]{1,0:T(8,128)(2,1)S(1)}, u32[]{:S(2)}, u32[]{:S(2)}) collective-permute-start(bf16[3072,256]{1,0:T(8,128)(2,1)S(1)} %slice.6), channel_id=1, source_target_pairs={{0,2},{2,4},{4,6},{6,0},{1,3},{3,5},{5,7},{7,1},{8,10},{10,12},{12... | collective-permute-start | bytes 4718600 | tf_op jit(solution)/shard_map/ppermute | solution.py:438
  123.2 38.0 %collective-permute-start.7 = (bf16[3072,256]{1,0:T(8,128)(2,1)S(1)}, bf16[3072,256]{1,0:T(8,128)(2,1)S(1)}, u32[]{:S(2)}, u32[]{:S(2)}) collective-permute-start(bf16[3072,256]{1,0:T(8,128)(2,1)S(1)} %slice.7), channel_id=1, source_target_pairs={{0,6},{2,0},{4,2},{6,4},{1,7},{3,1},{5,3},{7,5},{8,14},{10,8},{12,... | collective-permute-start | bytes 4718600 | tf_op jit(solution)/shard_map/ppermute | solution.py:439
  157.0 4.2 %copy-start.3 = (bf16[3072,256]{1,0:T(8,128)(2,1)}, bf16[3072,256]{1,0:T(8,128)(2,1)S(1)}, u32[]{:S(2)}) copy-start(bf16[3072,256]{1,0:T(8,128)(2,1)S(1)} %collective-permute-done.6) | copy-start | bytes 4718596
  161.2 1.2 copy-start.4
  175.9 4.4 %collective-permute-start.9 = (bf16[256,3968]{1,0:T(8,128)(2,1)}, bf16[256,3968]{1,0:T(8,128)(2,1)S(1)}, u32[]{:S(2)}, u32[]{:S(2)}) collective-permute-start(bf16[256,3968]{1,0:T(8,128)(2,1)} %get-tuple-element.49), channel_id=1, source_target_pairs={{0,1},{1,0},{2,3},{3,2},{4,5},{5,4},{6,7},{7,6},{8,9},{9,8},{10,11... | collective-permute-start | bytes 6094856 | tf_op jit(solution)/shard_map/ppermute | solution.py:449
  183.6 7.1 %copy-start = (bf16[128,5120]{1,0:T(8,128)(2,1)S(1)}, bf16[128,5120]{1,0:T(8,128)(2,1)}, u32[]{:S(2)}) copy-start(bf16[128,5120]{1,0:T(8,128)(2,1)} %out_grad_ref.1) | copy-start | bytes 3932164
  183.6 56.1 %copy-start.1 = (s32[128,1]{0,1:T(1,128)S(1)}, s32[128,1]{0,1:T(1,128)}, u32[]{:S(2)}) copy-start(s32[128,1]{0,1:T(1,128)} %param.10) | copy-start | bytes 1540
  183.6 56.1 %copy-start.2 = (f32[128]{0:T(128)S(1)}, f32[128]{0:T(128)}, u32[]{:S(2)}) copy-start(f32[128]{0:T(128)} %param.9) | copy-start | bytes 1540
  183.6 56.1 %all-to-all-start.1 = ((bf16[32,8,3968]{2,1,0:T(8,128)(2,1)}), bf16[32,8,3968]{2,1,0:T(8,128)(2,1)S(1)}, u32[]{:S(2)}, u32[]{:S(2)}) async-start(bf16[32,8,3968]{2,1,0:T(8,128)(2,1)} %fusion), calls=%async_computation.1 | async-start | bytes 4063232 | tf_op jit(solution)/shard_map/all_to_all | solution.py:451

commit v5 on v4

--- a/solution.py
+++ b/solution.py
@@ -14,10 +14,18 @@
 TERM_LANES = 128
 PARTS = 60
 UP_PARTS = 40
-HEAD = 6
 HALF = 30
+HEAD = 16
+ENDS = ((0, HEAD), (PARTS - HEAD, PARTS))
+RESTS = ((HEAD, PARTS), (0, PARTS - HEAD))
+WEIGHT_CHUNKS = (ENDS[0], ENDS[1], (HEAD, PARTS - HEAD))
+FAR_FLOPS = 62000000000
+FIRST_FLOPS = 1000
 VMEM_ALL = 56 * 1024 * 1024
 SMALL_VMEM = 20 * 1024 * 1024
+FIRST_VMEM = 38 * 1024 * 1024
+LAST_VMEM = 34 * 1024 * 1024
+COLUMN_PIECES = 1
 
 
 def dot(a, b):
@@ -103,46 +111,79 @@
     return copies
 
 
-def weights_kernel(read, write, core_ref, gate, up, down, *refs):
-    outs, held, sems = refs[: len(write)], refs[len(write) : -1], refs[-1]
-    hidden = held[0].shape[1] // 2
+def weights_kernel(core_ref, gate, up, down, head, up_rest, down_rest, tail, held, read_sems, write_sems):
+    hidden = held.shape[1] // 2
+    reads = []
+    for low, high in WEIGHT_CHUNKS:
+        rows = held.at[pl.ds(low * hidden, (high - low) * hidden)]
+        sems = read_sems.at[pl.ds(2 * low, 2 * (high - low))]
+        reads.append(part_copies((gate, up, down), core_ref[0], low, high, rows, sems))
+    writes = [
+        pltpu.make_async_copy(held.at[pl.ds(low * hidden, (high - low) * hidden)], out, write_sems.at[i])
+        for i, (out, (low, high)) in enumerate(
+            ((head, ENDS[0]), (tail, ENDS[1]), (up_rest, RESTS[0]), (down_rest, RESTS[1]))
+        )
+    ]
+    for copies in reads:
+        for copy in copies:
+            copy.start()
+    for copies, write in zip(reads, writes):
+        for copy in copies:
+            copy.wait()
+        write.start()
+    writes[3].start()
+    for write in writes:
+        write.wait()
+
+
+def weight_parts(core, weights):
+    width, span = weights[0].shape
+    hidden = span // 2
+    any_spec = pl.BlockSpec(memory_space=pl.ANY)
+    size = lambda parts: jax.ShapeDtypeStruct(((parts[1] - parts[0]) * hidden, span), BF)
+    return pl.pallas_call(
+        weights_kernel,
+        out_shape=[size(parts) for parts in (ENDS[0],) + RESTS + (ENDS[1],)],
+        in_specs=[pl.BlockSpec(memory_space=pltpu.SMEM)] + [any_spec] * 3,
+        out_specs=[any_spec] * 4,
+        scratch_shapes=[
+            pltpu.VMEM((PARTS * hidden, span), BF),
+            pltpu.SemaphoreType.DMA((2 * PARTS,)),
+            pltpu.SemaphoreType.DMA((4,)),
+        ],
+        compiler_params=pltpu.CompilerParams(vmem_limit_bytes=VMEM_ALL),
+        cost_estimate=pl.CostEstimate(flops=0, bytes_accessed=6 * PARTS * hidden * span, transcendentals=0),
+        name="weights",
+    )(core, *weights)
+
+
+def far_kernel(ranges, up_hbm, down_hbm, *refs):
+    sems = refs[-1]
     copies = []
-    for (low, high), buffer in zip(read, held):
-        copies += part_copies((gate, up, down), core_ref[0], low, high, buffer, sems.at[pl.ds(len(copies), PARTS)])
+    for i, (out, (side, low, high)) in enumerate(zip(refs[:-1], ranges)):
+        hidden = out.shape[0] // (high - low)
+        src = (up_hbm, down_hbm)[side].at[low * hidden : high * hidden, :]
+        copies.append(pltpu.make_async_copy(src, out, sems.at[i]))
     for copy in copies:
         copy.start()
     for copy in copies:
         copy.wait()
-    copies = []
-    for i, ((low, high), out) in enumerate(zip(write, outs)):
-        for (first, last), buffer in zip(read, held):
-            if first <= low and high <= last:
-                src = buffer.at[(low - first) * hidden : (high - first) * hidden, :]
-                copies.append(pltpu.make_async_copy(src, out, sems.at[i]))
-    for copy in copies:
-        copy.start()
-    for copy in copies:
-        copy.wait()
-
-
-def weight_parts(core, weights, read, write):
-    width, span = weights[0].shape
+
+
+def far_parts(from_up, from_down, ranges):
+    rows, span = from_up.shape
     hidden = span // 2
     any_spec = pl.BlockSpec(memory_space=pl.ANY)
-    size = lambda parts: ((parts[1] - parts[0]) * hidden, span)
-    return pl.pallas_call(
-        functools.partial(weights_kernel, read, write),
-        out_shape=[jax.ShapeDtypeStruct(size(parts), BF) for parts in write],
-        in_specs=[pl.BlockSpec(memory_space=pltpu.SMEM)] + [any_spec] * 3,
-        out_specs=[any_spec] * len(write),
-        scratch_shapes=[pltpu.VMEM(size(parts), BF) for parts in read]
-        + [pltpu.SemaphoreType.DMA((2 * PARTS,))],
+    return pl.pallas_call(
+        functools.partial(far_kernel, ranges),
+        out_shape=[jax.ShapeDtypeStruct(((high - low) * hidden, span), BF) for _, low, high in ranges],
+        in_specs=[any_spec] * 2,
+        out_specs=[any_spec] * len(ranges),
+        scratch_shapes=[pltpu.SemaphoreType.DMA((len(ranges),))],
         compiler_params=pltpu.CompilerParams(vmem_limit_bytes=VMEM_ALL),
-        cost_estimate=pl.CostEstimate(
-            flops=0, bytes_accessed=4 * span * hidden * sum(b - a for a, b in read + write), transcendentals=0
-        ),
-        name="weights",
-    )(core, *weights)
+        cost_estimate=pl.CostEstimate(flops=FAR_FLOPS, bytes_accessed=0, transcendentals=0),
+        name="far",
+    )(from_up, from_down)
 
 
 def block_copies(pieces, ranges, gu, down, place, sems):
@@ -218,127 +259,143 @@
     return dot_t(grads[...], gu[rows].reshape(parts // 4 * hidden, columns))
 
 
+def unpack_kernel(rows_ref, *outs):
+    packed = rows_ref.shape[0]
+    slots, width = outs[0].shape[0], rows_ref.shape[1] // 6 * 4
+    part = width // 4
+    per = len(outs) // 2
+    spread = slot_matrix(slots, packed, 0, None)
+    spread_tail = [slot_matrix(slots, packed, 0, j) for j in range(3)]
+    for k in range(2):
+        cols = [slice((3 * k + j) * part, (3 * k + j + 1) * part) for j in range(3)]
+        pieces = [dot(spread, rows_ref[:, cols[j]]) for j in range(3)]
+        last = dot(spread_tail[0], rows_ref[:, cols[0]])
+        last += dot(spread_tail[1], rows_ref[:, cols[1]])
+        last += dot(spread_tail[2], rows_ref[:, cols[2]])
+        wide = width // per
+        for j, piece in enumerate(pieces + [last]):
+            low = j * part % wide
+            outs[k * per + j * part // wide][:, low : low + part] = piece.astype(BF)
+
+
+def unpack(rows):
+    packed = rows.shape[0]
+    slots, width = packed // ROWS * CAP, rows.shape[1] // 6 * 4
+    return pl.pallas_call(
+        unpack_kernel,
+        out_shape=[jax.ShapeDtypeStruct((slots, width // COLUMN_PIECES), BF)] * (2 * COLUMN_PIECES),
+        compiler_params=pltpu.CompilerParams(vmem_limit_bytes=SMALL_VMEM),
+        cost_estimate=pl.CostEstimate(flops=FIRST_FLOPS, bytes_accessed=FIRST_FLOPS, transcendentals=0),
+        name="unpack",
+    )(rows)
+
+
+def row_copies(pieces, full, sems):
+    slots, wide = pieces[0].shape
+    return [
+        pltpu.make_async_copy(
+            piece,
+            full.at[pl.ds(i // COLUMN_PIECES * slots, slots), pl.ds(i % COLUMN_PIECES * wide, wide)],
+            sems.at[i],
+        )
+        for i, piece in enumerate(pieces)
+    ]
+
+
 def first_kernel(ranges, *refs):
-    own_hbm, other_hbm = refs[:2]
-    pieces, refs = refs[2 : 2 + sum(map(len, ranges))], refs[2 + sum(map(len, ranges)) :]
-    x_hbm, dy_hbm, sum_hbm, term_ref, raw, x, dy, gu, down, grads, total, sems = refs
-    packed = raw.shape[1]
-    slots, part = x.shape[0] // 2, x.shape[1] // 4
-    raw_copies = [pltpu.make_async_copy(src, raw.at[i], sems.at[i]) for i, src in enumerate((own_hbm, other_hbm))]
+    count = 2 * COLUMN_PIECES
+    x_pieces, dy_pieces, refs = refs[:count], refs[count : 2 * count], refs[2 * count :]
+    pieces, refs = refs[: sum(map(len, ranges))], refs[sum(map(len, ranges)) :]
+    sum_hbm, term_ref, x, dy, gu, down, grads, total, sems = refs
+    part = x.shape[1] // 4
+    x_copies = row_copies(x_pieces, x, sems.at[pl.ds(0, count)])
+    dy_copies = row_copies(dy_pieces, dy, sems.at[pl.ds(count, count)])
     up_copies, down_copies, used = [], [], 0
     for b, block in enumerate(ranges):
         here = pieces[used : used + len(block)]
-        ups, downs = block_copies(here, block, gu, down, b, sems.at[pl.ds(5 + 2 * used, 2 * len(block))])
+        ups, downs = block_copies(here, block, gu, down, b, sems.at[pl.ds(2 * count + 4 + 2 * used, 2 * len(block))])
         used += len(block)
         up_copies.append(ups)
         down_copies.append(downs)
-    for copies in [raw_copies] + up_copies + down_copies:
+    for copies in [x_copies] + up_copies + [dy_copies] + down_copies:
         for copy in copies:
             copy.start()
-    spread = slot_matrix(slots, packed, 0, None)
-    spread_tail = [slot_matrix(slots, packed, 0, j) for j in range(3)]
-    for i in range(2):
-        raw_copies[i].wait()
-        rows = slice(i * slots, (i + 1) * slots)
-        for k, full in enumerate((x, dy)):
-            cols = [slice((3 * k + j) * part, (3 * k + j + 1) * part) for j in range(3)]
-            for j in range(3):
-                full[rows, j * part : (j + 1) * part] = dot(spread, raw[i, :, cols[j]]).astype(BF)
-            last = dot(spread_tail[0], raw[i, :, cols[0]])
-            last += dot(spread_tail[1], raw[i, :, cols[1]])
-            last += dot(spread_tail[2], raw[i, :, cols[2]])
-            full[rows, 3 * part :] = last.astype(BF)
-    outs = [
-        pltpu.make_async_copy(src, dst, sems.at[2 + i])
-        for i, (src, dst) in enumerate(((x, x_hbm), (dy, dy_hbm), (total, sum_hbm)))
-    ]
-    outs[0].start()
-    outs[1].start()
-    term_ref[...] = hidden_grads(x, dy, gu, down, grads, up_copies, down_copies)
+    for copy in x_copies:
+        copy.wait()
+    term_ref[...] = hidden_grads(x, dy, gu, down, grads, up_copies, down_copies + [dy_copies])
+    outs = []
     for j in range(4):
-        total[:, j * part : (j + 1) * part] = row_grads(grads, gu, j).astype(BF)
-    outs[2].start()
+        cols = pl.ds(j * part, part)
+        total[:, cols] = row_grads(grads, gu, j).astype(BF)
+        outs.append(pltpu.make_async_copy(total.at[:, cols], sum_hbm.at[:, cols], sems.at[2 * count + j]))
+        outs[j].start()
     for copy in outs:
         copy.wait()
 
 
-def first_blocks(own, other, blocks, ranges, width):
-    packed = own.shape[0]
-    slots = packed // ROWS * CAP
+def first_blocks(x, dy, blocks, ranges):
+    slots, wide = x[0].shape
+    width = wide * COLUMN_PIECES
     hidden, span = blocks[0][0].shape[1:]
     count = len(blocks)
     pieces = [piece for block in blocks for piece in block]
-    full = jax.ShapeDtypeStruct((2 * slots, width), BF)
     any_spec = pl.BlockSpec(memory_space=pl.ANY)
     return pl.pallas_call(
         functools.partial(first_kernel, ranges),
-        out_shape=(full, full, full, jax.ShapeDtypeStruct((2 * slots, hidden), F32)),
-        in_specs=[any_spec] * (2 + len(pieces)),
-        out_specs=(any_spec,) * 3 + (pl.BlockSpec(memory_space=pltpu.VMEM),),
+        out_shape=(jax.ShapeDtypeStruct((2 * slots, width), BF), jax.ShapeDtypeStruct((2 * slots, hidden), F32)),
+        in_specs=[any_spec] * (len(x) + len(dy) + len(pieces)),
+        out_specs=(any_spec, pl.BlockSpec(memory_space=pltpu.VMEM)),
         scratch_shapes=[
-            pltpu.VMEM((2,) + own.shape, BF),
             pltpu.VMEM((2 * slots, width), BF),
             pltpu.VMEM((2 * slots, width), BF),
             pltpu.VMEM((UP_PARTS, hidden, count * span), BF),
             pltpu.VMEM((PARTS - UP_PARTS, count * hidden, span), BF),
             pltpu.VMEM((2 * slots, count * span), BF),
             pltpu.VMEM((2 * slots, width), BF),
-            pltpu.SemaphoreType.DMA((5 + 2 * len(pieces),)),
+            pltpu.SemaphoreType.DMA((4 * COLUMN_PIECES + 4 + 2 * len(pieces),)),
         ],
-        compiler_params=pltpu.CompilerParams(vmem_limit_bytes=VMEM_ALL),
-        cost_estimate=pl.CostEstimate(
-            flops=2 * 2 * slots * width * hidden * count * 5,
-            bytes_accessed=2 * (count * 3 * width * hidden + 2 * own.size + 6 * slots * width),
-            transcendentals=2 * slots * hidden * count,
-        ),
+        compiler_params=pltpu.CompilerParams(vmem_limit_bytes=FIRST_VMEM),
+        cost_estimate=pl.CostEstimate(flops=FIRST_FLOPS, bytes_accessed=FIRST_FLOPS, transcendentals=0),
         name="first",
-    )(own, other, *pieces)
+    )(*x, *dy, *pieces)
 
 
 def last_kernel(ranges, *refs):
+    count = 2 * COLUMN_PIECES
+    x_pieces, dy_pieces, refs = refs[:count], refs[count : 2 * count], refs[2 * count :]
     pieces, refs = refs[: len(ranges)], refs[len(ranges) :]
-    x_hbm, dy_hbm, sum_hbm, term_ref, own_ref, other_ref, x, dy, gu, down, total, grads, sems = refs
-    packed = own_ref.shape[0]
+    sum_hbm, term_ref, own_ref, other_ref, x, dy, gu, down, total, grads, sems = refs
     slots, part = x.shape[0] // 2, x.shape[1] // 4
-    x_copy = pltpu.make_async_copy(x_hbm, x, sems.at[0])
-    dy_copy = pltpu.make_async_copy(dy_hbm, dy, sems.at[1])
-    sum_copy = pltpu.make_async_copy(sum_hbm, total, sems.at[2])
-    up_copies, down_copies = block_copies(pieces, ranges, gu, down, 0, sems.at[pl.ds(3, 2 * len(ranges))])
-    for copy in [x_copy] + up_copies + [dy_copy] + down_copies + [sum_copy]:
+    x_copies = row_copies(x_pieces, x, sems.at[pl.ds(0, count)])
+    dy_copies = row_copies(dy_pieces, dy, sems.at[pl.ds(count, count)])
+    up_copies, down_copies = block_copies(pieces, ranges, gu, down, 0, sems.at[pl.ds(2 * count + 1, 2 * len(ranges))])
+    sum_copy = pltpu.make_async_copy(sum_hbm, total, sems.at[2 * count])
+    for copy in x_copies + up_copies + dy_copies + down_copies + [sum_copy]:
         copy.start()
-    gather = slot_matrix(slots, packed, 1, None)
-    gather_tail = [slot_matrix(slots, packed, 1, j) for j in range(3)]
-    x_copy.wait()
-    terms = hidden_grads(x, dy, gu, down, grads, [up_copies], [down_copies + [dy_copy]]) + term_ref[...]
+    for copy in x_copies:
+        copy.wait()
+    terms = hidden_grads(x, dy, gu, down, grads, [up_copies], [down_copies + dy_copies]) + term_ref[...]
     terms = jnp.broadcast_to(jnp.sum(terms, axis=1, keepdims=True), (2 * slots, TERM_LANES)).astype(BF)
+    own_ref[:, 4 * part :] = terms[:slots]
+    other_ref[:, 4 * part :] = terms[slots:]
     sum_copy.wait()
-
-    def backward(j):
-        return (total[:, j * part : (j + 1) * part].astype(F32) + row_grads(grads, gu, j)).astype(BF)
-
-    outs = (own_ref, other_ref)
-    spans = [slice(i * slots, (i + 1) * slots) for i in range(2)]
-    for i in range(2):
-        outs[i][:, 3 * part :] = dot(gather, terms[spans[i]]).astype(BF)
-    last = backward(3)
-    for j in range(3):
-        rows = backward(j)
-        for i in range(2):
-            outs[i][:, j * part : (j + 1) * part] = (
-                dot(gather, rows[spans[i]]) + dot(gather_tail[j], last[spans[i]])
-            ).astype(BF)
-
-
-def last_block(pieces, ranges, x, dy, total, term, packed):
-    rows, width = x.shape
+    for j in range(4):
+        cols = slice(j * part, (j + 1) * part)
+        rows = (total[:, cols].astype(F32) + row_grads(grads, gu, j)).astype(BF)
+        own_ref[:, cols] = rows[:slots]
+        other_ref[:, cols] = rows[slots:]
+
+
+def last_block(x, dy, pieces, ranges, total, term):
+    rows, width = total.shape
     hidden, span = pieces[0].shape[1:]
-    out = jax.ShapeDtypeStruct((packed, width // 4 * 3 + TERM_LANES), BF)
+    out = jax.ShapeDtypeStruct((rows // 2, width + TERM_LANES), BF)
     any_spec = pl.BlockSpec(memory_space=pl.ANY)
     vmem_spec = pl.BlockSpec(memory_space=pltpu.VMEM)
     return pl.pallas_call(
         functools.partial(last_kernel, ranges),
         out_shape=(out, out),
-        in_specs=[any_spec] * (len(pieces) + 3) + [vmem_spec],
+        in_specs=[any_spec] * (len(x) + len(dy) + len(pieces) + 1) + [vmem_spec],
         out_specs=(vmem_spec, vmem_spec),
         scratch_shapes=[
             pltpu.VMEM((rows, width), BF),
@@ -347,16 +404,48 @@
             pltpu.VMEM((PARTS - UP_PARTS, hidden, span), BF),
             pltpu.VMEM((rows, width), BF),
             pltpu.VMEM((rows, span), BF),
-            pltpu.SemaphoreType.DMA((3 + 2 * len(pieces),)),
+            pltpu.SemaphoreType.DMA((4 * COLUMN_PIECES + 1 + 2 * len(pieces),)),
         ],
-        compiler_params=pltpu.CompilerParams(vmem_limit_bytes=VMEM_ALL),
+        compiler_params=pltpu.CompilerParams(vmem_limit_bytes=LAST_VMEM),
         cost_estimate=pl.CostEstimate(
             flops=2 * rows * width * hidden * 5,
             bytes_accessed=2 * (3 * width * hidden + 5 * rows * width),
             transcendentals=rows * hidden,
         ),
         name="last",
-    )(*pieces, x, dy, total, term)
+    )(*x, *dy, *pieces, total, term)
+
+
+def add_pack_kernel(a_ref, b_ref, out_ref):
+    slots, packed = a_ref.shape[0], out_ref.shape[0]
+    part = (a_ref.shape[1] - TERM_LANES) // 4
+    gather = slot_matrix(slots, packed, 1, None)
+    gather_tail = [slot_matrix(slots, packed, 1, j) for j in range(3)]
+
+    def total(low, size):
+        cols = pl.ds(low, size)
+        return (a_ref[:, cols].astype(F32) + b_ref[:, cols].astype(F32)).astype(BF)
+
+    out_ref[:, 3 * part :] = dot(gather, total(4 * part, TERM_LANES)).astype(BF)
+    last = total(3 * part, part)
+    for j in range(3):
+        out_ref[:, j * part : (j + 1) * part] = (
+            dot(gather, total(j * part, part)) + dot(gather_tail[j], last)
+        ).astype(BF)
+
+
+def add_pack(a, b):
+    slots, columns = a.shape
+    packed, part = slots // CAP * ROWS, (columns - TERM_LANES) // 4
+    return pl.pallas_call(
+        add_pack_kernel,
+        out_shape=jax.ShapeDtypeStruct((packed, 3 * part + TERM_LANES), BF),
+        compiler_params=pltpu.CompilerParams(vmem_limit_bytes=SMALL_VMEM),
+        cost_estimate=pl.CostEstimate(
+            flops=2 * packed * slots * part * 6, bytes_accessed=6 * slots * columns, transcendentals=0
+        ),
+        name="add_pack",
+    )(a, b)
 
 
 def combine_kernel(route_ref, gate_ref, own_term_ref, out_grad_ref, ret_ref, token_grad_ref, gate_grad_ref):
@@ -412,42 +501,39 @@
 
     core = lax.axis_index("dp").reshape(1)
     weights = (gate_weight[0], up_weight[0], down_weight[0])
-    ends = ((0, HEAD), (PARTS - HEAD, PARTS))
-    rests = ((HEAD, PARTS), (0, PARTS - HEAD))
-    head, tail = weight_parts(core, weights, ends, ends)
+    head, up_rest, down_rest, tail = weight_parts(core, weights)
     up_head = lax.ppermute(head, "tensor", up)
     down_tail = lax.ppermute(tail, "tensor", down)
-    core, head, tail = lax.optimization_barrier((core, head, tail))
-    up_rest, down_rest = weight_parts(core, weights, ((0, PARTS),), rests)
-
-    route_row, up_rest, down_rest = lax.optimization_barrier((route_row, up_rest, down_rest))
-    packed = pack(route_row, tokens, out_grad, experts)
-    packed, up_head, down_tail = lax.optimization_barrier((packed, up_head, down_tail))
-    got = lax.all_to_all(
-        packed.reshape(experts, ROWS, -1), "expert", split_axis=0, concat_axis=0, tiled=True
-    ).reshape(experts * ROWS, -1)
-
     from_up = lax.ppermute(up_rest, "tensor", up)
     from_down = lax.ppermute(down_rest, "tensor", down)
     far_head = lax.ppermute(up_head, "tensor", up)
     far_tail = lax.ppermute(down_tail, "tensor", down)
-    got, from_up, from_down, far_head, far_tail = lax.optimization_barrier(
-        (got, from_up, from_down, far_head, far_tail)
-    )
+
+    route_row, head = lax.optimization_barrier((route_row, head))
+    packed = pack(route_row, tokens, out_grad, experts)
+    got = lax.all_to_all(
+        packed.reshape(experts, ROWS, -1), "expert", split_axis=0, concat_axis=0, tiled=True
+    ).reshape(experts * ROWS, -1)
+
+    from_up, from_down, far_head, far_tail = lax.optimization_barrier((from_up, from_down, far_head, far_tail))
+    far_up, far_down = far_parts(from_up, from_down, ((0, 0, HALF - HEAD), (1, HALF, PARTS - HEAD)))
+    got, far_up, far_down = lax.optimization_barrier((got, far_up, far_down))
+    far_up = lax.ppermute(far_up, "tensor", up)
+    far_down = lax.ppermute(far_down, "tensor", down)
+    rows = list(unpack(got))
+    other_rows = [lax.ppermute(piece, "dp", swap) for piece in rows]
+    x = rows[:COLUMN_PIECES] + other_rows[:COLUMN_PIECES]
+    dy = rows[COLUMN_PIECES:] + other_rows[COLUMN_PIECES:]
+
     part = width // UP_PARTS
-    far_up = lax.ppermute(from_up[: (HALF - HEAD) * part], "tensor", up)
-    far_down = lax.ppermute(from_down[HALF * part :], "tensor", down)
-    got_other = lax.ppermute(got, "dp", swap)
-
     squares = lambda piece: piece.reshape(-1, part, 2 * part)
-    blocks = ((head, up_rest), (up_head, from_up), (from_down, down_tail))
-    ranges = ((ends[0], rests[0]),) * 2 + ((rests[1], ends[1]),)
-    x, dy, total, term = first_blocks(got, got_other, [list(map(squares, b)) for b in blocks], ranges, width)
+    blocks = [list(map(squares, b)) for b in ((head, up_rest), (up_head, from_up), (from_down, down_tail))]
+    ranges = ((ENDS[0], RESTS[0]),) * 2 + ((RESTS[1], ENDS[1]),)
     far = (far_head, far_up, far_down, far_tail)
-    far_ranges = (ends[0], (HEAD, HALF), (HALF, PARTS - HEAD), ends[1])
-    own, other = last_block(list(map(squares, far)), far_ranges, x, dy, total, term, experts * ROWS)
-    from_other = lax.ppermute(other, "dp", swap)
-    back = (own.astype(F32) + from_other.astype(F32)).astype(BF).reshape(experts, ROWS, -1)
+    far_ranges = (ENDS[0], (HEAD, HALF), (HALF, PARTS - HEAD), ENDS[1])
+    total, term = first_blocks(x, dy, blocks, ranges)
+    own, other = last_block(x, dy, list(map(squares, far)), far_ranges, total, term)
+    back = add_pack(own, lax.ppermute(other, "dp", swap)).reshape(experts, ROWS, -1)
     ret = lax.all_to_all(back, "expert", split_axis=0, concat_axis=0, tiled=True)
     own_term = jnp.sum(out_grad.astype(F32) * tokens.astype(F32), axis=1)
     token_grad, gate_grad = combine(

time: 242 us -> 289 us (1.19)
  Pallas kernels: 53.9 us -> 103 us
  waiting for transfers between devices: 151 us -> 142 us
  starting transfers between devices: 27.8 us -> 33.3 us
  local copies, waits for them, and re-layouts: 3.58 us -> 8.55 us
  other arithmetic: 5.09 us -> 1.75 us
    ppermute x1, waiting for transfers between devices: 0.01 us -> 65.5 us  [per_device(): up_head = lax.ppermute(head, 'tensor', up)]
    ppermute x1, waiting for transfers between devices: 81.4 us -> 20 us  [per_device(): far_head = lax.ppermute(up_head, 'tensor', up)]
    pallas_call x3 -> x5, Pallas kernels: 32.4 us -> 86.5 us  [the longest x1 56.7 us: far_parts(): pl.pallas_call(functools.partial(far_kernel, ranges), out_shape=[jax.Shap...]
    ppermute x4 -> x5, waiting for transfers between devices: 18.1 us -> 8.16 us  [the longest x2 4.25 us: per_device(): other_rows = [lax.ppermute(piece, 'dp', swap) for piece in rows]]
    unnamed x16 -> x28, local copies, waits for them, and re-layouts: 1.96 us -> 8.55 us
    all_to_all x1, starting transfers between devices: 7.07 us -> 12.8 us  [per_device(): lax.all_to_all(back, 'expert', split_axis=0, concat_axis=0, tiled=True)]
    pallas_call x1, Pallas kernels: 13.4 us -> 8.01 us  [last_block(): pl.pallas_call(functools.partial(last_kernel, ranges), out_shape=(out, ou...]
    reshape x1 -> x0, other arithmetic: 3.35 us -> none  [per_device(): (own.astype(F32) + from_other.astype(F32)).astype(BF)]
  transfers between devices with their start and end apart: 12 -> 13, of which waited for: 8 -> 7; matrix products, arithmetic and copies ran while one was open for 1% -> 1% of each run, Pallas kernels for 15% -> 28%
where the time goes in v5:
time: 289 us
  waiting for transfers between devices  142 us (49%)
  Pallas kernels  103 us (36%)
  starting transfers between devices  33.3 us (12%)
  local copies, waits for them, and re-layouts  8.55 us (3%)
    ppermute x1, waiting for transfers between devices, per_device(): up_head = lax.ppermute(head, 'tensor', up)  65.5 us
    pallas_call x1, Pallas kernels, far_parts(): pl.pallas_call(functools.partial(far_kernel, ranges), out_shape=[jax.Shap...  56.7 us
    all_to_all x1, waiting for transfers between devices, per_device(): lax.all_to_all(back, 'expert', split_axis=0, concat_axis=0, tiled=True)  47.2 us
    ppermute x1, waiting for transfers between devices, per_device(): far_head = lax.ppermute(up_head, 'tensor', up)  20 us
    pallas_call x1, Pallas kernels, first_blocks(): pl.pallas_call(functools.partial(first_kernel, ranges), out_shape=(jax.Sh...  17.5 us
    all_to_all x1, starting transfers between devices, per_device(): lax.all_to_all(back, 'expert', split_axis=0, concat_axis=0, tiled=True)  12.8 us
    all_to_all x1, starting transfers between devices, per_device(): lax.all_to_all(packed.reshape(experts, ROWS, -1), 'expert', split_axis=0,...  10.3 us
    unnamed x28, local copies, waits for them, and re-layouts  8.55 us
  transfers between devices with their start and end apart: 13, of which 7 were waited for; matrix products, arithmetic and copies ran while one was open for 1% of the time, Pallas kernels for 28%

profile of v5, /device:TPU:24, one launch (start us, length us, event | category | flops | bytes accessed | tf_op | source)
XLA Modules:
  0.0 289.0 jit_solution(10708241552579155357)
XLA Ops:
  0.6 5.7 %weights.1 = (bf16[2048,256]{1,0:T(8,128)(2,1)}, bf16[5632,256]{1,0:T(8,128)(2,1)}, bf16[5632,256]{1,0:T(8,128)(2,1)}, bf16[2048,256]{1,0:T(8,128)(2,1)}) custom-call(s32[1]{0:T(128)} %bitcast.1.core_ref, bf16[5120,256]{1,0:T(8,128)(2,1)} %bitcast.36, bf16[5120,256]{1,0:T(8,128)(2,1)} %bitcast.37, bf16[256,5120]{1,0:T(8,128)(2,1)} %bitcast.38), custom_call_target="tpu_custom_call" | custom-call | bytes 11796480 | tf_op jit(solution)/shard_map/weights/pallas_call | solution.py:144
  6.3 2.0 collective-permute-start
  8.3 0.1 collective-permute-start.1
  8.4 3.2 %collective-permute-start.2 = (bf16[2048,256]{1,0:T(8,128)(2,1)}, bf16[2048,256]{1,0:T(8,128)(2,1)S(1)}, u32[]{:S(2)}, u32[]{:S(2)}) collective-permute-start(bf16[2048,256]{1,0:T(8,128)(2,1)} %get-tuple-element.41), channel_id=1, source_target_pairs={{0,2},{2,4},{4,6},{6,0},{1,3},{3,5},{5,7},{7,1},{8,10},{10,12},{12... | collective-permute-start | bytes 3145736 | tf_op jit(solution)/shard_map/ppermute | solution.py:505
  11.6 0.0 collective-permute-start.4
  11.6 5.9 %pack.1 = bf16[256,7680]{1,0:T(8,128)(2,1)} custom-call(s32[1,128]{1,0:T(1,128)} %bitcast.32, bf16[128,5120]{1,0:T(8,128)(2,1)} %x_ref.1, bf16[128,5120]{1,0:T(8,128)(2,1)} %out_grad_ref.1), custom_call_target="tpu_custom_call" | custom-call | flops 1006632960 | bytes 6553600 | tf_op jit(solution)/shard_map/pack/pallas_call | solution.py:83
  17.5 10.3 %all-to-all-start = ((bf16[32,8,7680]{2,1,0:T(8,128)(2,1)}), bf16[32,8,7680]{2,1,0:T(8,128)(2,1)}, u32[]{:S(2)}, u32[]{:S(2)}) async-start(bf16[32,8,7680]{2,1,0:T(8,128)(2,1)} %bitcast.35), calls=%async_computation | async-start | bytes 7864320 | tf_op jit(solution)/shard_map/all_to_all | solution.py:514
  27.8 65.5 %collective-permute-done.2 = bf16[2048,256]{1,0:T(8,128)(2,1)S(1)} collective-permute-done((bf16[2048,256]{1,0:T(8,128)(2,1)}, bf16[2048,256]{1,0:T(8,128)(2,1)S(1)}, u32[]{:S(2)}, u32[]{:S(2)}) %collective-permute-start.2) | collective-permute-done | bytes 1048608 | tf_op jit(solution)/shard_map/ppermute | solution.py:505
  93.3 1.5 collective-permute-start.3
  94.8 0.0 copy-start.4
  94.8 1.0 copy-done.4
  95.8 0.0 collective-permute-done.4
  95.8 0.5 collective-permute-start.5
  96.3 0.0 copy-start.6
  96.3 1.0 copy-done.6
  97.3 20.0 %collective-permute-done.3 = bf16[2048,256]{1,0:T(8,128)(2,1)S(1)} collective-permute-done((bf16[2048,256]{1,0:T(8,128)(2,1)S(1)}, bf16[2048,256]{1,0:T(8,128)(2,1)S(1)}, u32[]{:S(2)}, u32[]{:S(2)}) %collective-permute-start.3) | collective-permute-done | bytes 1048608 | tf_op jit(solution)/shard_map/ppermute | solution.py:509
  117.3 0.0 copy-start.8
  117.3 1.0 copy-done.8
  118.3 1.2 collective-permute-done.5
  119.5 0.0 copy-start.10
  119.5 1.0 copy-done.10
  120.5 0.0 collective-permute-done.up_hbm
  120.5 0.0 collective-permute-done.1.down_hbm
  120.5 56.7 %far.1 = (bf16[1792,256]{1,0:T(8,128)(2,1)}, bf16[1792,256]{1,0:T(8,128)(2,1)}) custom-call(bf16[5632,256]{1,0:T(8,128)(2,1)} %collective-permute-done.up_hbm, bf16[5632,256]{1,0:T(8,128)(2,1)} %collective-permute-done.1.down_hbm), custom_call_target="tpu_custom_call" | custom-call | flops 62000001024 | tf_op jit(solution)/shard_map/far/pallas_call | solution.py:177
  177.2 0.0 copy-start.2
  177.2 0.0 all-to-all-done
  177.3 0.0 copy-start.3
  177.3 4.0 %unpack.1 = (bf16[192,5120]{1,0:T(8,128)(2,1)S(1)}, bf16[192,5120]{1,0:T(8,128)(2,1)S(1)}) custom-call(bf16[256,7680]{1,0:T(8,128)(2,1)} %bitcast.8.rows_ref), custom_call_target="tpu_custom_call" | custom-call | flops 1000 | bytes 1000 | tf_op jit(solution)/shard_map/unpack/pallas_call | solution.py:284
  181.2 0.1 collective-permute-start.6
  181.3 0.5 collective-permute-start.7
  181.8 0.3 collective-permute-start.8
  182.1 1.8 collective-permute-start.9
  183.9 1.4 collective-permute-done.6.refs_1_
  185.3 2.8 collective-permute-done.7.refs_3_
  188.1 0.0 copy-done.2
  188.1 0.0 copy-done.3
  188.1 0.0 copy-start.5
  188.1 1.2 copy-done.5
  189.3 0.0 copy-start.7
  189.3 1.2 copy-done.7
  190.6 0.0 copy-start.9
  190.6 0.0 copy-start.11
  190.6 17.5 %first.1 = (bf16[384,5120]{1,0:T(8,128)(2,1)}, f32[384,128]{1,0:T(8,128)S(1)}) custom-call(bf16[192,5120]{1,0:T(8,128)(2,1)S(1)} %get-tuple-element.35.refs_0_, bf16[192,5120]{1,0:T(8,128)(2,1)S(1)} %collective-permute-done.6.refs_1_, bf16[192,5120]{1,0:T(8,128)(2,1)S(1)} %get-tuple-element.36.refs_2_, bf16[192,5120]{1,0:T(8,128)(2,1)S(1)} %collective-permute-done.7.refs_3_, ...), custom_call_target="tpu_custom_call" | custom-call | flops 1000 | bytes 1000 | tf_op jit(solution)/shard_map/first/pallas_call | solution.py:343
  208.1 0.0 collective-permute-done.8
  208.1 0.0 collective-permute-done.9
  208.1 0.0 copy-done.9
  208.1 0.0 copy-done.11
  208.2 0.0 copy-start.1
  208.2 2.1 copy-done.1
  210.3 8.0 %last.1 = (bf16[192,5248]{1,0:T(8,128)(2,1)S(1)}, bf16[192,5248]{1,0:T(8,128)(2,1)S(1)}) custom-call(bf16[192,5120]{1,0:T(8,128)(2,1)S(1)} %get-tuple-element.35.refs_0_, bf16[192,5120]{1,0:T(8,128)(2,1)S(1)} %collective-permute-done.6.refs_1_, bf16[192,5120]{1,0:T(8,128)(2,1)S(1)} %get-tuple-element.36.refs_2_, ...), custom_call_target="tpu_custom_call" | custom-call | flops 2516582400 | bytes 23592960 | tf_op jit(solution)/shard_map/last/pallas_call | solution.py:395
  218.3 0.2 collective-permute-start.10
  218.5 3.9 %collective-permute-done.10.b_ref = bf16[192,5248]{1,0:T(8,128)(2,1)S(1)} collective-permute-done((bf16[192,5248]{1,0:T(8,128)(2,1)S(1)}, bf16[192,5248]{1,0:T(8,128)(2,1)S(1)}, u32[]{:S(2)}, u32[]{:S(2)}) %collective-permute-start.10) | collective-permute-done | bytes 2015264 | tf_op jit(solution)/shard_map/ppermute | solution.py:536
  222.4 2.6 add_pack.1
  225.0 0.0 copy-start
  225.0 12.8 %all-to-all-start.1 = ((bf16[32,8,3968]{2,1,0:T(8,128)(2,1)}), bf16[32,8,3968]{2,1,0:T(8,128)(2,1)S(1)}, u32[]{:S(2)}, u32[]{:S(2)}) async-start(bf16[32,8,3968]{2,1,0:T(8,128)(2,1)} %bitcast.19), calls=%async_computation.1 | async-start | bytes 4063232 | tf_op jit(solution)/shard_map/all_to_all | solution.py:537
  237.9 0.0 copy-done
  237.9 0.0 copy-start.12
  237.9 0.0 copy-start.13
  237.9 1.8 multiply_reduce_fusion
  239.7 47.2 %all-to-all-done.1 = bf16[32,8,3968]{2,1,0:T(8,128)(2,1)S(1)} async-done(((bf16[32,8,3968]{2,1,0:T(8,128)(2,1)}), bf16[32,8,3968]{2,1,0:T(8,128)(2,1)S(1)}, u32[]{:S(2)}, u32[]{:S(2)}) %all-to-all-start.1) | async-done | bytes 2031648 | tf_op jit(solution)/shard_map/all_to_all | solution.py:537
  286.9 0.0 copy-done.12
  286.9 0.0 copy-done.13
  286.9 2.1 combine.1
Async XLA Ops:
  6.3 114.2 %collective-permute-start = (bf16[5632,256]{1,0:T(8,128)(2,1)}, bf16[5632,256]{1,0:T(8,128)(2,1)}, u32[]{:S(2)}, u32[]{:S(2)}) collective-permute-start(bf16[5632,256]{1,0:T(8,128)(2,1)} %get-tuple-element.27), channel_id=1, source_target_pairs={{0,2},{2,4},{4,6},{6,0},{1,3},{3,5},{5,7},{7,1},{8,10},{10,12},{12... | collective-permute-start | bytes 8650760 | tf_op jit(solution)/shard_map/ppermute | solution.py:507
  8.3 112.2 %collective-permute-start.1 = (bf16[5632,256]{1,0:T(8,128)(2,1)}, bf16[5632,256]{1,0:T(8,128)(2,1)}, u32[]{:S(2)}, u32[]{:S(2)}) collective-permute-start(bf16[5632,256]{1,0:T(8,128)(2,1)} %get-tuple-element.28), channel_id=1, source_target_pairs={{0,6},{2,0},{4,2},{6,4},{1,7},{3,1},{5,3},{7,5},{8,14},{10,8},{12,... | collective-permute-start | bytes 8650760 | tf_op jit(solution)/shard_map/ppermute | solution.py:508
  8.4 84.9 %collective-permute-start.2 = (bf16[2048,256]{1,0:T(8,128)(2,1)}, bf16[2048,256]{1,0:T(8,128)(2,1)S(1)}, u32[]{:S(2)}, u32[]{:S(2)}) collective-permute-start(bf16[2048,256]{1,0:T(8,128)(2,1)} %get-tuple-element.41), channel_id=1, source_target_pairs={{0,2},{2,4},{4,6},{6,0},{1,3},{3,5},{5,7},{7,1},{8,10},{10,12},{12... | collective-permute-start | bytes 3145736 | tf_op jit(solution)/shard_map/ppermute | solution.py:505
  11.6 84.2 %collective-permute-start.4 = (bf16[2048,256]{1,0:T(8,128)(2,1)}, bf16[2048,256]{1,0:T(8,128)(2,1)S(1)}, u32[]{:S(2)}, u32[]{:S(2)}) collective-permute-start(bf16[2048,256]{1,0:T(8,128)(2,1)} %get-tuple-element.29), channel_id=1, source_target_pairs={{0,6},{2,0},{4,2},{6,4},{1,7},{3,1},{5,3},{7,5},{8,14},{10,8},{12,... | collective-permute-start | bytes 3145736 | tf_op jit(solution)/shard_map/ppermute | solution.py:506
  17.5 159.8 %all-to-all-start = ((bf16[32,8,7680]{2,1,0:T(8,128)(2,1)}), bf16[32,8,7680]{2,1,0:T(8,128)(2,1)}, u32[]{:S(2)}, u32[]{:S(2)}) async-start(bf16[32,8,7680]{2,1,0:T(8,128)(2,1)} %bitcast.35), calls=%async_computation | async-start | bytes 7864320 | tf_op jit(solution)/shard_map/all_to_all | solution.py:514
  93.3 24.0 %collective-permute-start.3 = (bf16[2048,256]{1,0:T(8,128)(2,1)S(1)}, bf16[2048,256]{1,0:T(8,128)(2,1)S(1)}, u32[]{:S(2)}, u32[]{:S(2)}) collective-permute-start(bf16[2048,256]{1,0:T(8,128)(2,1)S(1)} %collective-permute-done.2), channel_id=1, source_target_pairs={{0,2},{2,4},{4,6},{6,0},{1,3},{3,5},{5,7},{7,1},{8,10},{10,12},{12... | collective-permute-start | bytes 3145736 | tf_op jit(solution)/shard_map/ppermute | solution.py:509
  94.8 1.0 copy-start.4
  95.8 23.7 %collective-permute-start.5 = (bf16[2048,256]{1,0:T(8,128)(2,1)S(1)}, bf16[2048,256]{1,0:T(8,128)(2,1)S(1)}, u32[]{:S(2)}, u32[]{:S(2)}) collective-permute-start(bf16[2048,256]{1,0:T(8,128)(2,1)S(1)} %collective-permute-done.4), channel_id=1, source_target_pairs={{0,6},{2,0},{4,2},{6,4},{1,7},{3,1},{5,3},{7,5},{8,14},{10,8},{12,... | collective-permute-start | bytes 3145736 | tf_op jit(solution)/shard_map/ppermute | solution.py:510
  96.3 1.0 copy-start.6
  117.3 1.0 copy-start.8
  119.5 1.0 copy-start.10
  177.2 10.9 %copy-start.2 = (bf16[5632,256]{1,0:T(8,128)(2,1)S(1)}, bf16[5632,256]{1,0:T(8,128)(2,1)}, u32[]{:S(2)}) copy-start(bf16[5632,256]{1,0:T(8,128)(2,1)} %get-tuple-element.27) | copy-start | bytes 8650756
  177.3 10.9 %copy-start.3 = (bf16[2048,256]{1,0:T(8,128)(2,1)S(1)}, bf16[2048,256]{1,0:T(8,128)(2,1)}, u32[]{:S(2)}) copy-start(bf16[2048,256]{1,0:T(8,128)(2,1)} %get-tuple-element.41) | copy-start | bytes 3145732
  181.2 4.1 %collective-permute-start.6 = (bf16[192,5120]{1,0:T(8,128)(2,1)S(1)}, bf16[192,5120]{1,0:T(8,128)(2,1)S(1)}, u32[]{:S(2)}, u32[]{:S(2)}) collective-permute-start(bf16[192,5120]{1,0:T(8,128)(2,1)S(1)} %get-tuple-element.35.refs_0_), channel_id=1, source_target_pairs={{0,1},{1,0},{2,3},{3,2},{4,5},{5,4},{6,7},{7,6},{8,9},{9,8},{10,11... | collective-permute-start | bytes 5898248 | tf_op jit(solution)/shard_map/ppermute | solution.py:524
  181.3 6.8 %collective-permute-start.7 = (bf16[192,5120]{1,0:T(8,128)(2,1)S(1)}, bf16[192,5120]{1,0:T(8,128)(2,1)S(1)}, u32[]{:S(2)}, u32[]{:S(2)}) collective-permute-start(bf16[192,5120]{1,0:T(8,128)(2,1)S(1)} %get-tuple-element.36.refs_2_), channel_id=1, source_target_pairs={{0,1},{1,0},{2,3},{3,2},{4,5},{5,4},{6,7},{7,6},{8,9},{9,8},{10,11... | collective-permute-start | bytes 5898248 | tf_op jit(solution)/shard_map/ppermute | solution.py:524
  181.8 26.3 %collective-permute-start.8 = (bf16[1792,256]{1,0:T(8,128)(2,1)}, bf16[1792,256]{1,0:T(8,128)(2,1)S(1)}, u32[]{:S(2)}, u32[]{:S(2)}) collective-permute-start(bf16[1792,256]{1,0:T(8,128)(2,1)} %get-tuple-element.38), channel_id=1, source_target_pairs={{0,2},{2,4},{4,6},{6,0},{1,3},{3,5},{5,7},{7,1},{8,10},{10,12},{12... | collective-permute-start | bytes 2752520 | tf_op jit(solution)/shard_map/ppermute | solution.py:521
  182.1 26.0 %collective-permute-start.9 = (bf16[1792,256]{1,0:T(8,128)(2,1)}, bf16[1792,256]{1,0:T(8,128)(2,1)S(1)}, u32[]{:S(2)}, u32[]{:S(2)}) collective-permute-start(bf16[1792,256]{1,0:T(8,128)(2,1)} %get-tuple-element.39), channel_id=1, source_target_pairs={{0,6},{2,0},{4,2},{6,4},{1,7},{3,1},{5,3},{7,5},{8,14},{10,8},{12,... | collective-permute-start | bytes 2752520 | tf_op jit(solution)/shard_map/ppermute | solution.py:522
  188.1 1.2 copy-start.5
  189.3 1.2 copy-start.7
  190.6 17.6 %copy-start.9 = (bf16[2048,256]{1,0:T(8,128)(2,1)S(1)}, bf16[2048,256]{1,0:T(8,128)(2,1)}, u32[]{:S(2)}) copy-start(bf16[2048,256]{1,0:T(8,128)(2,1)} %copy-done.8) | copy-start | bytes 3145732
  190.6 17.6 %copy-start.11 = (bf16[2048,256]{1,0:T(8,128)(2,1)S(1)}, bf16[2048,256]{1,0:T(8,128)(2,1)}, u32[]{:S(2)}) copy-start(bf16[2048,256]{1,0:T(8,128)(2,1)} %copy-done.10) | copy-start | bytes 3145732
  208.2 2.1 copy-start.1
  218.3 4.1 %collective-permute-start.10 = (bf16[192,5248]{1,0:T(8,128)(2,1)S(1)}, bf16[192,5248]{1,0:T(8,128)(2,1)S(1)}, u32[]{:S(2)}, u32[]{:S(2)}) collective-permute-start(bf16[192,5248]{1,0:T(8,128)(2,1)S(1)} %get-tuple-element.45), channel_id=1, source_target_pairs={{0,1},{1,0},{2,3},{3,2},{4,5},{5,4},{6,7},{7,6},{8,9},{9,8},{10,11... | collective-permute-start | bytes 6045704 | tf_op jit(solution)/shard_map/ppermute | solution.py:536
  225.0 12.9 %copy-start = (bf16[128,5120]{1,0:T(8,128)(2,1)S(1)}, bf16[128,5120]{1,0:T(8,128)(2,1)}, u32[]{:S(2)}) copy-start(bf16[128,5120]{1,0:T(8,128)(2,1)} %out_grad_ref.1) | copy-start | bytes 3932164
  225.0 61.8 %all-to-all-start.1 = ((bf16[32,8,3968]{2,1,0:T(8,128)(2,1)}), bf16[32,8,3968]{2,1,0:T(8,128)(2,1)S(1)}, u32[]{:S(2)}, u32[]{:S(2)}) async-start(bf16[32,8,3968]{2,1,0:T(8,128)(2,1)} %bitcast.19), calls=%async_computation.1 | async-start | bytes 4063232 | tf_op jit(solution)/shard_map/all_to_all | solution.py:537
  237.9 49.0 %copy-start.12 = (s32[128,1]{0,1:T(1,128)S(1)}, s32[128,1]{0,1:T(1,128)}, u32[]{:S(2)}) copy-start(s32[128,1]{0,1:T(1,128)} %param.10) | copy-start | bytes 1540
  237.9 49.0 %copy-start.13 = (f32[128]{0:T(128)S(1)}, f32[128]{0:T(128)}, u32[]{:S(2)}) copy-start(f32[128]{0:T(128)} %param.9) | copy-start | bytes 1540

commit v6 on v5

--- a/solution.py
+++ b/solution.py
@@ -15,7 +15,7 @@
 PARTS = 60
 UP_PARTS = 40
 HALF = 30
-HEAD = 16
+HEAD = 15
 ENDS = ((0, HEAD), (PARTS - HEAD, PARTS))
 RESTS = ((HEAD, PARTS), (0, PARTS - HEAD))
 WEIGHT_CHUNKS = (ENDS[0], ENDS[1], (HEAD, PARTS - HEAD))
@@ -23,8 +23,8 @@
 FIRST_FLOPS = 1000
 VMEM_ALL = 56 * 1024 * 1024
 SMALL_VMEM = 20 * 1024 * 1024
-FIRST_VMEM = 38 * 1024 * 1024
-LAST_VMEM = 34 * 1024 * 1024
+FIRST_VMEM = 46 * 1024 * 1024
+LAST_VMEM = 46 * 1024 * 1024
 COLUMN_PIECES = 1
 
 
@@ -158,16 +158,21 @@
 
 
 def far_kernel(ranges, up_hbm, down_hbm, *refs):
-    sems = refs[-1]
-    copies = []
-    for i, (out, (side, low, high)) in enumerate(zip(refs[:-1], ranges)):
-        hidden = out.shape[0] // (high - low)
+    count = len(ranges)
+    outs, held, sems = refs[:count], refs[count : 2 * count], refs[-1]
+    reads, writes = [], []
+    for i, (side, low, high) in enumerate(ranges):
+        hidden = outs[i].shape[0] // (high - low)
         src = (up_hbm, down_hbm)[side].at[low * hidden : high * hidden, :]
-        copies.append(pltpu.make_async_copy(src, out, sems.at[i]))
-    for copy in copies:
-        copy.start()
-    for copy in copies:
-        copy.wait()
+        reads.append(pltpu.make_async_copy(src, held[i], sems.at[i]))
+        writes.append(pltpu.make_async_copy(held[i], outs[i], sems.at[count + i]))
+    for read in reads:
+        read.start()
+    for read, write in zip(reads, writes):
+        read.wait()
+        write.start()
+    for write in writes:
+        write.wait()
 
 
 def far_parts(from_up, from_down, ranges):
@@ -179,7 +184,8 @@
         out_shape=[jax.ShapeDtypeStruct(((high - low) * hidden, span), BF) for _, low, high in ranges],
         in_specs=[any_spec] * 2,
         out_specs=[any_spec] * len(ranges),
-        scratch_shapes=[pltpu.SemaphoreType.DMA((len(ranges),))],
+        scratch_shapes=[pltpu.VMEM(((high - low) * hidden, span), BF) for _, low, high in ranges]
+        + [pltpu.SemaphoreType.DMA((2 * len(ranges),))],
         compiler_params=pltpu.CompilerParams(vmem_limit_bytes=VMEM_ALL),
         cost_estimate=pl.CostEstimate(flops=FAR_FLOPS, bytes_accessed=0, transcendentals=0),
         name="far",
@@ -515,9 +521,10 @@
         packed.reshape(experts, ROWS, -1), "expert", split_axis=0, concat_axis=0, tiled=True
     ).reshape(experts * ROWS, -1)
 
-    from_up, from_down, far_head, far_tail = lax.optimization_barrier((from_up, from_down, far_head, far_tail))
     far_up, far_down = far_parts(from_up, from_down, ((0, 0, HALF - HEAD), (1, HALF, PARTS - HEAD)))
-    got, far_up, far_down = lax.optimization_barrier((got, far_up, far_down))
+    got, far_up, far_down, far_head, far_tail = lax.optimization_barrier(
+        (got, far_up, far_down, far_head, far_tail)
+    )
     far_up = lax.ppermute(far_up, "tensor", up)
     far_down = lax.ppermute(far_down, "tensor", down)
     rows = list(unpack(got))

time: 289 us -> 231 us (0.80)
  Pallas kernels: 103 us -> 50.3 us
  local copies, waits for them, and re-layouts: 8.55 us -> 4.77 us
    pallas_call x1, Pallas kernels: 56.7 us -> 2.52 us  [far_parts(): pl.pallas_call(functools.partial(far_kernel, ranges), out_shape=[jax.Shap...]
    unnamed x28 -> x26, local copies, waits for them, and re-layouts: 8.55 us -> 4.77 us
  transfers between devices with their start and end apart: 13 -> 13, of which waited for: 7 -> 8; matrix products, arithmetic and copies ran while one was open for 1% -> 1% of each run, Pallas kernels for 28% -> 11%
where the time goes in v6:
time: 231 us
  waiting for transfers between devices  140 us (61%)
  Pallas kernels  50.3 us (22%)
  starting transfers between devices  33.5 us (15%)
  local copies, waits for them, and re-layouts  4.77 us (2%)
    ppermute x1, waiting for transfers between devices, per_device(): up_head = lax.ppermute(head, 'tensor', up)  65.3 us
    all_to_all x1, waiting for transfers between devices, per_device(): lax.all_to_all(back, 'expert', split_axis=0, concat_axis=0, tiled=True)  47.2 us
    ppermute x1, waiting for transfers between devices, per_device(): far_head = lax.ppermute(up_head, 'tensor', up)  18.2 us
    pallas_call x1, Pallas kernels, first_blocks(): pl.pallas_call(functools.partial(first_kernel, ranges), out_shape=(jax.Sh...  18 us
    all_to_all x1, starting transfers between devices, per_device(): lax.all_to_all(back, 'expert', split_axis=0, concat_axis=0, tiled=True)  12.7 us
    all_to_all x1, starting transfers between devices, per_device(): lax.all_to_all(packed.reshape(experts, ROWS, -1), 'expert', split_axis=0,...  11.6 us
    pallas_call x1, Pallas kernels, last_block(): pl.pallas_call(functools.partial(last_kernel, ranges), out_shape=(out, ou...  9.46 us
    pallas_call x1, Pallas kernels, pack(): pl.pallas_call(pack_kernel, out_shape=jax.ShapeDtypeStruct((experts * ROW...  5.92 us
  transfers between devices with their start and end apart: 13, of which 8 were waited for; matrix products, arithmetic and copies ran while one was open for 1% of the time, Pallas kernels for 11%

profile of v6, /device:TPU:24, one launch (start us, length us, event | category | flops | bytes accessed | tf_op | source)
XLA Modules:
  0.0 230.8 jit_solution(16111945403896142670)
XLA Ops:
  0.6 5.7 %weights.1 = (bf16[1920,256]{1,0:T(8,128)(2,1)}, bf16[5760,256]{1,0:T(8,128)(2,1)}, bf16[5760,256]{1,0:T(8,128)(2,1)}, bf16[1920,256]{1,0:T(8,128)(2,1)}) custom-call(s32[1]{0:T(128)} %bitcast.1.core_ref, bf16[5120,256]{1,0:T(8,128)(2,1)} %bitcast.36, bf16[5120,256]{1,0:T(8,128)(2,1)} %bitcast.37, bf16[256,5120]{1,0:T(8,128)(2,1)} %bitcast.38), custom_call_target="tpu_custom_call" | custom-call | bytes 11796480 | tf_op jit(solution)/shard_map/weights/pallas_call | solution.py:144
  6.3 2.0 collective-permute-start
  8.4 0.1 collective-permute-start.1
  8.4 5.9 %pack.1 = bf16[256,7680]{1,0:T(8,128)(2,1)} custom-call(s32[1,128]{1,0:T(1,128)} %bitcast.31, bf16[128,5120]{1,0:T(8,128)(2,1)} %x_ref.1, bf16[128,5120]{1,0:T(8,128)(2,1)} %out_grad_ref.1), custom_call_target="tpu_custom_call" | custom-call | flops 1006632960 | bytes 6553600 | tf_op jit(solution)/shard_map/pack/pallas_call | solution.py:83
  14.4 0.0 copy-start.3
  14.4 11.6 %all-to-all-start = ((bf16[32,8,7680]{2,1,0:T(8,128)(2,1)}), bf16[32,8,7680]{2,1,0:T(8,128)(2,1)}, u32[]{:S(2)}, u32[]{:S(2)}) async-start(bf16[32,8,7680]{2,1,0:T(8,128)(2,1)} %bitcast.34), calls=%async_computation | async-start | bytes 7864320 | tf_op jit(solution)/shard_map/all_to_all | solution.py:520
  25.9 0.0 copy-done.3
  25.9 1.5 collective-permute-start.2
  27.5 0.6 collective-permute-start.4
  28.0 65.3 %collective-permute-done.2 = bf16[1920,256]{1,0:T(8,128)(2,1)S(1)} collective-permute-done((bf16[1920,256]{1,0:T(8,128)(2,1)S(1)}, bf16[1920,256]{1,0:T(8,128)(2,1)S(1)}, u32[]{:S(2)}, u32[]{:S(2)}) %collective-permute-start.2) | collective-permute-done | bytes 983072 | tf_op jit(solution)/shard_map/ppermute | solution.py:511
  93.3 1.5 collective-permute-start.3
  94.8 0.0 collective-permute-done.4
  94.8 0.5 collective-permute-start.5
  95.4 0.0 collective-permute-done.up_hbm
  95.4 0.0 collective-permute-done.1.down_hbm
  95.4 2.5 %far.1 = (bf16[1920,256]{1,0:T(8,128)(2,1)}, bf16[1920,256]{1,0:T(8,128)(2,1)}) custom-call(bf16[5760,256]{1,0:T(8,128)(2,1)} %collective-permute-done.up_hbm, bf16[5760,256]{1,0:T(8,128)(2,1)} %collective-permute-done.1.down_hbm), custom_call_target="tpu_custom_call" | custom-call | flops 62000001024 | tf_op jit(solution)/shard_map/far/pallas_call | solution.py:182
  97.9 18.2 %collective-permute-done.3 = bf16[1920,256]{1,0:T(8,128)(2,1)S(1)} collective-permute-done((bf16[1920,256]{1,0:T(8,128)(2,1)S(1)}, bf16[1920,256]{1,0:T(8,128)(2,1)S(1)}, u32[]{:S(2)}, u32[]{:S(2)}) %collective-permute-start.3) | collective-permute-done | bytes 983072 | tf_op jit(solution)/shard_map/ppermute | solution.py:515
  116.1 0.0 copy-start.4
  116.1 0.9 copy-done.4
  117.0 0.3 collective-permute-done.5
  117.3 0.0 copy-start.6
  117.3 0.9 copy-done.6
  118.2 0.0 all-to-all-done
  118.2 0.0 copy-start.12
  118.2 0.0 copy-start.11
  118.2 4.0 %unpack.1 = (bf16[192,5120]{1,0:T(8,128)(2,1)S(1)}, bf16[192,5120]{1,0:T(8,128)(2,1)S(1)}) custom-call(bf16[256,7680]{1,0:T(8,128)(2,1)} %bitcast.8.rows_ref), custom_call_target="tpu_custom_call" | custom-call | flops 1000 | bytes 1000 | tf_op jit(solution)/shard_map/unpack/pallas_call | solution.py:290
  122.2 0.0 copy-start.1
  122.2 0.1 collective-permute-start.6
  122.3 0.5 collective-permute-start.7
  122.8 0.0 copy-done.12
  122.8 1.2 collective-permute-start.8
  124.0 0.0 copy-done.11
  124.0 0.8 collective-permute-start.9
  124.8 1.4 collective-permute-done.6.refs_1_
  126.3 2.8 %collective-permute-done.7.refs_3_ = bf16[192,5120]{1,0:T(8,128)(2,1)S(1)} collective-permute-done((bf16[192,5120]{1,0:T(8,128)(2,1)S(1)}, bf16[192,5120]{1,0:T(8,128)(2,1)S(1)}, u32[]{:S(2)}, u32[]{:S(2)}) %collective-permute-start.7) | collective-permute-done | bytes 1966112 | tf_op jit(solution)/shard_map/ppermute | solution.py:531
  129.1 0.0 copy-start.10
  129.1 0.0 copy-done.1
  129.1 1.3 copy-done.10
  130.4 0.0 copy-start.5
  130.4 0.0 copy-start.7
  130.4 18.0 %first.1 = (bf16[384,5120]{1,0:T(8,128)(2,1)}, f32[384,128]{1,0:T(8,128)S(1)}) custom-call(bf16[192,5120]{1,0:T(8,128)(2,1)S(1)} %get-tuple-element.31.refs_0_, bf16[192,5120]{1,0:T(8,128)(2,1)S(1)} %collective-permute-done.6.refs_1_, bf16[192,5120]{1,0:T(8,128)(2,1)} %copy-done.1, bf16[192,5120]{1,0:T(8,128)(2,1)} %copy-done.10, ...), custom_call_target="tpu_custom_call" | custom-call | flops 1000 | bytes 1000 | tf_op jit(solution)/shard_map/first/pallas_call | solution.py:349
  148.4 0.0 collective-permute-done.8
  148.4 0.3 collective-permute-done.9
  148.7 0.0 copy-done.5
  148.7 0.0 copy-done.7
  148.7 9.5 %last.1 = (bf16[192,5248]{1,0:T(8,128)(2,1)}, bf16[192,5248]{1,0:T(8,128)(2,1)}) custom-call(bf16[192,5120]{1,0:T(8,128)(2,1)S(1)} %get-tuple-element.31.refs_0_, bf16[192,5120]{1,0:T(8,128)(2,1)S(1)} %collective-permute-done.6.refs_1_, bf16[192,5120]{1,0:T(8,128)(2,1)} %copy-done.1, bf16[192,5120]{1,0:T(8,128)(2,1)} %copy-done.10, ...), custom_call_target="tpu_custom_call" | custom-call | flops 2516582400 | bytes 23592960 | tf_op jit(solution)/shard_map/last/pallas_call | solution.py:401
  158.2 0.3 collective-permute-start.10
  158.5 4.2 %collective-permute-done.10.b_ref = bf16[192,5248]{1,0:T(8,128)(2,1)S(1)} collective-permute-done((bf16[192,5248]{1,0:T(8,128)(2,1)}, bf16[192,5248]{1,0:T(8,128)(2,1)S(1)}, u32[]{:S(2)}, u32[]{:S(2)}) %collective-permute-start.10) | collective-permute-done | bytes 2015264 | tf_op jit(solution)/shard_map/ppermute | solution.py:543
  162.8 0.0 copy-start.2
  162.8 1.6 copy-done.2
  164.3 2.6 %add_pack.1 = bf16[256,3968]{1,0:T(8,128)(2,1)} custom-call(bf16[192,5248]{1,0:T(8,128)(2,1)S(1)} %copy-done.2, bf16[192,5248]{1,0:T(8,128)(2,1)S(1)} %collective-permute-done.10.b_ref), custom_call_target="tpu_custom_call" | custom-call | flops 754974720 | bytes 6045696 | tf_op jit(solution)/shard_map/add_pack/pallas_call | solution.py:446
  166.9 0.0 copy-start
  166.9 12.7 %all-to-all-start.1 = ((bf16[32,8,3968]{2,1,0:T(8,128)(2,1)}), bf16[32,8,3968]{2,1,0:T(8,128)(2,1)S(1)}, u32[]{:S(2)}, u32[]{:S(2)}) async-start(bf16[32,8,3968]{2,1,0:T(8,128)(2,1)} %bitcast.19), calls=%async_computation.1 | async-start | bytes 4063232 | tf_op jit(solution)/shard_map/all_to_all | solution.py:544
  179.7 0.0 copy-done
  179.7 0.0 copy-start.8
  179.7 0.0 copy-start.9
  179.7 1.8 multiply_reduce_fusion
  181.5 47.2 %all-to-all-done.1 = bf16[32,8,3968]{2,1,0:T(8,128)(2,1)S(1)} async-done(((bf16[32,8,3968]{2,1,0:T(8,128)(2,1)}), bf16[32,8,3968]{2,1,0:T(8,128)(2,1)S(1)}, u32[]{:S(2)}, u32[]{:S(2)}) %all-to-all-start.1) | async-done | bytes 2031648 | tf_op jit(solution)/shard_map/all_to_all | solution.py:544
  228.7 0.0 copy-done.8
  228.7 0.0 copy-done.9
  228.7 2.1 combine.1
Async XLA Ops:
  6.3 89.0 %collective-permute-start = (bf16[5760,256]{1,0:T(8,128)(2,1)}, bf16[5760,256]{1,0:T(8,128)(2,1)}, u32[]{:S(2)}, u32[]{:S(2)}) collective-permute-start(bf16[5760,256]{1,0:T(8,128)(2,1)} %get-tuple-element.25), channel_id=1, source_target_pairs={{0,2},{2,4},{4,6},{6,0},{1,3},{3,5},{5,7},{7,1},{8,10},{10,12},{12... | collective-permute-start | bytes 8847368 | tf_op jit(solution)/shard_map/ppermute | solution.py:513
  8.4 87.0 %collective-permute-start.1 = (bf16[5760,256]{1,0:T(8,128)(2,1)}, bf16[5760,256]{1,0:T(8,128)(2,1)}, u32[]{:S(2)}, u32[]{:S(2)}) collective-permute-start(bf16[5760,256]{1,0:T(8,128)(2,1)} %get-tuple-element.26), channel_id=1, source_target_pairs={{0,6},{2,0},{4,2},{6,4},{1,7},{3,1},{5,3},{7,5},{8,14},{10,8},{12,... | collective-permute-start | bytes 8847368 | tf_op jit(solution)/shard_map/ppermute | solution.py:514
  14.4 11.6 %copy-start.3 = (bf16[1920,256]{1,0:T(8,128)(2,1)S(1)}, bf16[1920,256]{1,0:T(8,128)(2,1)}, u32[]{:S(2)}) copy-start(bf16[1920,256]{1,0:T(8,128)(2,1)} %get-tuple-element.37) | copy-start | bytes 2949124
  14.4 103.9 %all-to-all-start = ((bf16[32,8,7680]{2,1,0:T(8,128)(2,1)}), bf16[32,8,7680]{2,1,0:T(8,128)(2,1)}, u32[]{:S(2)}, u32[]{:S(2)}) async-start(bf16[32,8,7680]{2,1,0:T(8,128)(2,1)} %bitcast.34), calls=%async_computation | async-start | bytes 7864320 | tf_op jit(solution)/shard_map/all_to_all | solution.py:520
  25.9 67.4 %collective-permute-start.2 = (bf16[1920,256]{1,0:T(8,128)(2,1)S(1)}, bf16[1920,256]{1,0:T(8,128)(2,1)S(1)}, u32[]{:S(2)}, u32[]{:S(2)}) collective-permute-start(bf16[1920,256]{1,0:T(8,128)(2,1)S(1)} %copy-done.3), channel_id=1, source_target_pairs={{0,2},{2,4},{4,6},{6,0},{1,3},{3,5},{5,7},{7,1},{8,10},{10,12},{12... | collective-permute-start | bytes 2949128 | tf_op jit(solution)/shard_map/ppermute | solution.py:511
  27.5 67.4 %collective-permute-start.4 = (bf16[1920,256]{1,0:T(8,128)(2,1)}, bf16[1920,256]{1,0:T(8,128)(2,1)S(1)}, u32[]{:S(2)}, u32[]{:S(2)}) collective-permute-start(bf16[1920,256]{1,0:T(8,128)(2,1)} %get-tuple-element.29), channel_id=1, source_target_pairs={{0,6},{2,0},{4,2},{6,4},{1,7},{3,1},{5,3},{7,5},{8,14},{10,8},{12,... | collective-permute-start | bytes 2949128 | tf_op jit(solution)/shard_map/ppermute | solution.py:512
  93.3 22.7 %collective-permute-start.3 = (bf16[1920,256]{1,0:T(8,128)(2,1)S(1)}, bf16[1920,256]{1,0:T(8,128)(2,1)S(1)}, u32[]{:S(2)}, u32[]{:S(2)}) collective-permute-start(bf16[1920,256]{1,0:T(8,128)(2,1)S(1)} %collective-permute-done.2), channel_id=1, source_target_pairs={{0,2},{2,4},{4,6},{6,0},{1,3},{3,5},{5,7},{7,1},{8,10},{10,12},{12... | collective-permute-start | bytes 2949128 | tf_op jit(solution)/shard_map/ppermute | solution.py:515
  94.8 22.4 %collective-permute-start.5 = (bf16[1920,256]{1,0:T(8,128)(2,1)S(1)}, bf16[1920,256]{1,0:T(8,128)(2,1)S(1)}, u32[]{:S(2)}, u32[]{:S(2)}) collective-permute-start(bf16[1920,256]{1,0:T(8,128)(2,1)S(1)} %collective-permute-done.4), channel_id=1, source_target_pairs={{0,6},{2,0},{4,2},{6,4},{1,7},{3,1},{5,3},{7,5},{8,14},{10,8},{12,... | collective-permute-start | bytes 2949128 | tf_op jit(solution)/shard_map/ppermute | solution.py:516
  116.1 0.9 copy-start.4
  117.3 0.9 copy-start.6
  118.2 4.6 %copy-start.12 = (bf16[1920,256]{1,0:T(8,128)(2,1)S(1)}, bf16[1920,256]{1,0:T(8,128)(2,1)}, u32[]{:S(2)}) copy-start(bf16[1920,256]{1,0:T(8,128)(2,1)} %get-tuple-element.34) | copy-start | bytes 2949124
  118.2 5.8 %copy-start.11 = (bf16[1920,256]{1,0:T(8,128)(2,1)S(1)}, bf16[1920,256]{1,0:T(8,128)(2,1)}, u32[]{:S(2)}) copy-start(bf16[1920,256]{1,0:T(8,128)(2,1)} %get-tuple-element.35) | copy-start | bytes 2949124
  122.2 6.9 %copy-start.1 = (bf16[192,5120]{1,0:T(8,128)(2,1)}, bf16[192,5120]{1,0:T(8,128)(2,1)S(1)}, u32[]{:S(2)}) copy-start(bf16[192,5120]{1,0:T(8,128)(2,1)S(1)} %get-tuple-element.32.refs_2_) | copy-start | bytes 5898244
  122.2 4.1 %collective-permute-start.6 = (bf16[192,5120]{1,0:T(8,128)(2,1)S(1)}, bf16[192,5120]{1,0:T(8,128)(2,1)S(1)}, u32[]{:S(2)}, u32[]{:S(2)}) collective-permute-start(bf16[192,5120]{1,0:T(8,128)(2,1)S(1)} %get-tuple-element.31.refs_0_), channel_id=1, source_target_pairs={{0,1},{1,0},{2,3},{3,2},{4,5},{5,4},{6,7},{7,6},{8,9},{9,8},{10,11... | collective-permute-start | bytes 5898248 | tf_op jit(solution)/shard_map/ppermute | solution.py:531
  122.3 6.8 %collective-permute-start.7 = (bf16[192,5120]{1,0:T(8,128)(2,1)S(1)}, bf16[192,5120]{1,0:T(8,128)(2,1)S(1)}, u32[]{:S(2)}, u32[]{:S(2)}) collective-permute-start(bf16[192,5120]{1,0:T(8,128)(2,1)S(1)} %get-tuple-element.32.refs_2_), channel_id=1, source_target_pairs={{0,1},{1,0},{2,3},{3,2},{4,5},{5,4},{6,7},{7,6},{8,9},{9,8},{10,11... | collective-permute-start | bytes 5898248 | tf_op jit(solution)/shard_map/ppermute | solution.py:531
  122.8 25.6 %collective-permute-start.8 = (bf16[1920,256]{1,0:T(8,128)(2,1)S(1)}, bf16[1920,256]{1,0:T(8,128)(2,1)S(1)}, u32[]{:S(2)}, u32[]{:S(2)}) collective-permute-start(bf16[1920,256]{1,0:T(8,128)(2,1)S(1)} %copy-done.12), channel_id=1, source_target_pairs={{0,2},{2,4},{4,6},{6,0},{1,3},{3,5},{5,7},{7,1},{8,10},{10,12},{12... | collective-permute-start | bytes 2949128 | tf_op jit(solution)/shard_map/ppermute | solution.py:528
  124.0 24.7 %collective-permute-start.9 = (bf16[1920,256]{1,0:T(8,128)(2,1)S(1)}, bf16[1920,256]{1,0:T(8,128)(2,1)S(1)}, u32[]{:S(2)}, u32[]{:S(2)}) collective-permute-start(bf16[1920,256]{1,0:T(8,128)(2,1)S(1)} %copy-done.11), channel_id=1, source_target_pairs={{0,6},{2,0},{4,2},{6,4},{1,7},{3,1},{5,3},{7,5},{8,14},{10,8},{12,... | collective-permute-start | bytes 2949128 | tf_op jit(solution)/shard_map/ppermute | solution.py:529
  129.1 1.3 copy-start.10
  130.4 18.4 %copy-start.5 = (bf16[1920,256]{1,0:T(8,128)(2,1)S(1)}, bf16[1920,256]{1,0:T(8,128)(2,1)}, u32[]{:S(2)}) copy-start(bf16[1920,256]{1,0:T(8,128)(2,1)} %copy-done.4) | copy-start | bytes 2949124
  130.4 18.4 %copy-start.7 = (bf16[1920,256]{1,0:T(8,128)(2,1)S(1)}, bf16[1920,256]{1,0:T(8,128)(2,1)}, u32[]{:S(2)}) copy-start(bf16[1920,256]{1,0:T(8,128)(2,1)} %copy-done.6) | copy-start | bytes 2949124
  158.2 4.6 %collective-permute-start.10 = (bf16[192,5248]{1,0:T(8,128)(2,1)}, bf16[192,5248]{1,0:T(8,128)(2,1)S(1)}, u32[]{:S(2)}, u32[]{:S(2)}) collective-permute-start(bf16[192,5248]{1,0:T(8,128)(2,1)} %get-tuple-element.41), channel_id=1, source_target_pairs={{0,1},{1,0},{2,3},{3,2},{4,5},{5,4},{6,7},{7,6},{8,9},{9,8},{10,11... | collective-permute-start | bytes 6045704 | tf_op jit(solution)/shard_map/ppermute | solution.py:543
  162.8 1.6 copy-start.2
  166.9 12.8 %copy-start = (bf16[128,5120]{1,0:T(8,128)(2,1)S(1)}, bf16[128,5120]{1,0:T(8,128)(2,1)}, u32[]{:S(2)}) copy-start(bf16[128,5120]{1,0:T(8,128)(2,1)} %out_grad_ref.1) | copy-start | bytes 3932164
  166.9 61.8 %all-to-all-start.1 = ((bf16[32,8,3968]{2,1,0:T(8,128)(2,1)}), bf16[32,8,3968]{2,1,0:T(8,128)(2,1)S(1)}, u32[]{:S(2)}, u32[]{:S(2)}) async-start(bf16[32,8,3968]{2,1,0:T(8,128)(2,1)} %bitcast.19), calls=%async_computation.1 | async-start | bytes 4063232 | tf_op jit(solution)/shard_map/all_to_all | solution.py:544
  179.7 49.0 %copy-start.8 = (s32[128,1]{0,1:T(1,128)S(1)}, s32[128,1]{0,1:T(1,128)}, u32[]{:S(2)}) copy-start(s32[128,1]{0,1:T(1,128)} %param.10) | copy-start | bytes 1540
  179.7 49.0 %copy-start.9 = (f32[128]{0:T(128)S(1)}, f32[128]{0:T(128)}, u32[]{:S(2)}) copy-start(f32[128]{0:T(128)} %param.9) | copy-start | bytes 1540

commit v7 on v6

--- a/solution.py
+++ b/solution.py
@@ -18,13 +18,15 @@
 HEAD = 15
 ENDS = ((0, HEAD), (PARTS - HEAD, PARTS))
 RESTS = ((HEAD, PARTS), (0, PARTS - HEAD))
-WEIGHT_CHUNKS = (ENDS[0], ENDS[1], (HEAD, PARTS - HEAD))
+MIDDLE = (PARTS - 2 * HEAD) // 3
+WEIGHT_CUTS = (0, HEAD, HEAD + MIDDLE, HEAD + 2 * MIDDLE, PARTS - HEAD, PARTS)
 FAR_FLOPS = 62000000000
 FIRST_FLOPS = 1000
+LAST_FLOPS = 1000
 VMEM_ALL = 56 * 1024 * 1024
 SMALL_VMEM = 20 * 1024 * 1024
-FIRST_VMEM = 46 * 1024 * 1024
-LAST_VMEM = 46 * 1024 * 1024
+FIRST_VMEM = 28 * 1024 * 1024
+LAST_VMEM = 20 * 1024 * 1024
 COLUMN_PIECES = 1
 
 
@@ -61,28 +63,51 @@
     return base + slot, base + CAP + second, slot - 3 * second
 
 
-def pack_kernel(route_ref, x_ref, dy_ref, out_ref):
-    n, width = x_ref.shape
-    total = out_ref.shape[0]
+def pack_kernel(route_ref, x_hbm, dy_hbm, out_hbm, x, dy, out, in_sems, out_sems):
+    n, width = x.shape
+    total = out.shape[0]
     part = width // 4
+    columns = [pl.ds(j * part, part) for j in range(4)]
+    reads = [
+        [pltpu.make_async_copy(src.at[:, columns[j]], dst.at[:, columns[j]], in_sems.at[4 * i + j]) for j in range(4)]
+        for i, (src, dst) in enumerate(((x_hbm, x), (dy_hbm, dy)))
+    ]
+    for copies in reads:
+        for j in (3, 0, 1, 2):
+            copies[j].start()
     main, tail, block = places(route_ref[...])
     row = lax.broadcasted_iota(jnp.int32, (total, n), 0)
     select = jnp.where(row == main, 1.0, 0.0).astype(BF)
-    for j in range(3):
-        tail_select = jnp.where((row == tail) & (block == j), 1.0, 0.0).astype(BF)
-        cols = pl.ds(j * part, part)
-        for i, rows_ref in enumerate((x_ref, dy_ref)):
-            last = rows_ref[:, 3 * part :]
-            out_ref[:, pl.ds((3 * i + j) * part, part)] = (
-                dot(select, rows_ref[:, cols]) + dot(tail_select, last)
-            ).astype(BF)
+    tail_select = [jnp.where((row == tail) & (block == j), 1.0, 0.0).astype(BF) for j in range(3)]
+    writes = []
+    for i, rows in enumerate((x, dy)):
+        reads[i][3].wait()
+        for j in range(3):
+            reads[i][j].wait()
+            cols = pl.ds((3 * i + j) * part, part)
+            out[:, cols] = (dot(select, rows[:, columns[j]]) + dot(tail_select[j], rows[:, columns[3]])).astype(BF)
+            writes.append(pltpu.make_async_copy(out.at[:, cols], out_hbm.at[:, cols], out_sems.at[3 * i + j]))
+            writes[-1].start()
+    for write in writes:
+        write.wait()
 
 
 def pack(route_row, x, dy, experts):
     n, width = x.shape
+    shape = (experts * ROWS, width // 4 * 6)
+    any_spec = pl.BlockSpec(memory_space=pl.ANY)
     return pl.pallas_call(
         pack_kernel,
-        out_shape=jax.ShapeDtypeStruct((experts * ROWS, width // 4 * 6), BF),
+        out_shape=jax.ShapeDtypeStruct(shape, BF),
+        in_specs=[pl.BlockSpec(memory_space=pltpu.VMEM), any_spec, any_spec],
+        out_specs=any_spec,
+        scratch_shapes=[
+            pltpu.VMEM((n, width), BF),
+            pltpu.VMEM((n, width), BF),
+            pltpu.VMEM(shape, BF),
+            pltpu.SemaphoreType.DMA((8,)),
+            pltpu.SemaphoreType.DMA((6,)),
+        ],
         compiler_params=pltpu.CompilerParams(vmem_limit_bytes=VMEM_ALL),
         cost_estimate=pl.CostEstimate(
             flops=2 * experts * ROWS * n * width * 3,
@@ -113,27 +138,28 @@
 
 def weights_kernel(core_ref, gate, up, down, head, up_rest, down_rest, tail, held, read_sems, write_sems):
     hidden = held.shape[1] // 2
-    reads = []
-    for low, high in WEIGHT_CHUNKS:
+    reads, writes = [], []
+    outs = ((head, ENDS[0]), (tail, ENDS[1]), (up_rest, RESTS[0]), (down_rest, RESTS[1]))
+    for low, high in zip(WEIGHT_CUTS, WEIGHT_CUTS[1:]):
         rows = held.at[pl.ds(low * hidden, (high - low) * hidden)]
         sems = read_sems.at[pl.ds(2 * low, 2 * (high - low))]
         reads.append(part_copies((gate, up, down), core_ref[0], low, high, rows, sems))
-    writes = [
-        pltpu.make_async_copy(held.at[pl.ds(low * hidden, (high - low) * hidden)], out, write_sems.at[i])
-        for i, (out, (low, high)) in enumerate(
-            ((head, ENDS[0]), (tail, ENDS[1]), (up_rest, RESTS[0]), (down_rest, RESTS[1]))
-        )
-    ]
+        writes.append([])
+        for i, (out, (first, last)) in enumerate(outs):
+            if first <= low and high <= last:
+                dst = out.at[pl.ds((low - first) * hidden, (high - low) * hidden)]
+                writes[-1].append(pltpu.make_async_copy(rows, dst, write_sems.at[4 * len(writes) + i - 4]))
     for copies in reads:
         for copy in copies:
             copy.start()
-    for copies, write in zip(reads, writes):
+    for copies, ready in zip(reads, writes):
         for copy in copies:
             copy.wait()
-        write.start()
-    writes[3].start()
-    for write in writes:
-        write.wait()
+        for copy in ready:
+            copy.start()
+    for copies in writes:
+        for copy in copies:
+            copy.wait()
 
 
 def weight_parts(core, weights):
@@ -149,7 +175,7 @@
         scratch_shapes=[
             pltpu.VMEM((PARTS * hidden, span), BF),
             pltpu.SemaphoreType.DMA((2 * PARTS,)),
-            pltpu.SemaphoreType.DMA((4,)),
+            pltpu.SemaphoreType.DMA((4 * len(WEIGHT_CUTS),)),
         ],
         compiler_params=pltpu.CompilerParams(vmem_limit_bytes=VMEM_ALL),
         cost_estimate=pl.CostEstimate(flops=0, bytes_accessed=6 * PARTS * hidden * span, transcendentals=0),
@@ -265,21 +291,29 @@
     return dot_t(grads[...], gu[rows].reshape(parts // 4 * hidden, columns))
 
 
-def unpack_kernel(rows_ref, *outs):
-    packed = rows_ref.shape[0]
-    slots, width = outs[0].shape[0], rows_ref.shape[1] // 6 * 4
+def unpack_kernel(rows_hbm, *refs):
+    outs, rows, sems = refs[:-2], refs[-2], refs[-1]
+    packed = rows.shape[0]
+    slots, width = outs[0].shape[0], rows.shape[1] // 6 * 4
     part = width // 4
     per = len(outs) // 2
+    cols = [slice(j * part, (j + 1) * part) for j in range(6)]
+    copies = [pltpu.make_async_copy(rows_hbm.at[:, c], rows.at[:, c], sems.at[j]) for j, c in enumerate(cols)]
+    for copy in copies:
+        copy.start()
     spread = slot_matrix(slots, packed, 0, None)
     spread_tail = [slot_matrix(slots, packed, 0, j) for j in range(3)]
+    wide = width // per
     for k in range(2):
-        cols = [slice((3 * k + j) * part, (3 * k + j + 1) * part) for j in range(3)]
-        pieces = [dot(spread, rows_ref[:, cols[j]]) for j in range(3)]
-        last = dot(spread_tail[0], rows_ref[:, cols[0]])
-        last += dot(spread_tail[1], rows_ref[:, cols[1]])
-        last += dot(spread_tail[2], rows_ref[:, cols[2]])
-        wide = width // per
-        for j, piece in enumerate(pieces + [last]):
+        last = None
+        for j in range(4):
+            if j < 3:
+                copies[3 * k + j].wait()
+                piece = dot(spread, rows[:, cols[3 * k + j]])
+                more = dot(spread_tail[j], rows[:, cols[3 * k + j]])
+                last = more if last is None else last + more
+            else:
+                piece = last
             low = j * part % wide
             outs[k * per + j * part // wide][:, low : low + part] = piece.astype(BF)
 
@@ -290,6 +324,8 @@
     return pl.pallas_call(
         unpack_kernel,
         out_shape=[jax.ShapeDtypeStruct((slots, width // COLUMN_PIECES), BF)] * (2 * COLUMN_PIECES),
+        in_specs=[pl.BlockSpec(memory_space=pl.ANY)],
+        scratch_shapes=[pltpu.VMEM(rows.shape, BF), pltpu.SemaphoreType.DMA((6,))],
         compiler_params=pltpu.CompilerParams(vmem_limit_bytes=SMALL_VMEM),
         cost_estimate=pl.CostEstimate(flops=FIRST_FLOPS, bytes_accessed=FIRST_FLOPS, transcendentals=0),
         name="unpack",
@@ -297,19 +333,14 @@
 
 
 def row_copies(pieces, full, sems):
-    slots, wide = pieces[0].shape
+    wide = pieces[0].shape[1]
     return [
-        pltpu.make_async_copy(
-            piece,
-            full.at[pl.ds(i // COLUMN_PIECES * slots, slots), pl.ds(i % COLUMN_PIECES * wide, wide)],
-            sems.at[i],
-        )
-        for i, piece in enumerate(pieces)
+        pltpu.make_async_copy(piece, full.at[:, pl.ds(i * wide, wide)], sems.at[i]) for i, piece in enumerate(pieces)
     ]
 
 
 def first_kernel(ranges, *refs):
-    count = 2 * COLUMN_PIECES
+    count = COLUMN_PIECES
     x_pieces, dy_pieces, refs = refs[:count], refs[count : 2 * count], refs[2 * count :]
     pieces, refs = refs[: sum(map(len, ranges))], refs[sum(map(len, ranges)) :]
     sum_hbm, term_ref, x, dy, gu, down, grads, total, sems = refs
@@ -348,17 +379,17 @@
     any_spec = pl.BlockSpec(memory_space=pl.ANY)
     return pl.pallas_call(
         functools.partial(first_kernel, ranges),
-        out_shape=(jax.ShapeDtypeStruct((2 * slots, width), BF), jax.ShapeDtypeStruct((2 * slots, hidden), F32)),
+        out_shape=(jax.ShapeDtypeStruct((slots, width), BF), jax.ShapeDtypeStruct((slots, hidden), F32)),
         in_specs=[any_spec] * (len(x) + len(dy) + len(pieces)),
         out_specs=(any_spec, pl.BlockSpec(memory_space=pltpu.VMEM)),
         scratch_shapes=[
-            pltpu.VMEM((2 * slots, width), BF),
-            pltpu.VMEM((2 * slots, width), BF),
+            pltpu.VMEM((slots, width), BF),
+            pltpu.VMEM((slots, width), BF),
             pltpu.VMEM((UP_PARTS, hidden, count * span), BF),
             pltpu.VMEM((PARTS - UP_PARTS, count * hidden, span), BF),
-            pltpu.VMEM((2 * slots, count * span), BF),
-            pltpu.VMEM((2 * slots, width), BF),
-            pltpu.SemaphoreType.DMA((4 * COLUMN_PIECES + 4 + 2 * len(pieces),)),
+            pltpu.VMEM((slots, count * span), BF),
+            pltpu.VMEM((slots, width), BF),
+            pltpu.SemaphoreType.DMA((2 * COLUMN_PIECES + 4 + 2 * len(pieces),)),
         ],
         compiler_params=pltpu.CompilerParams(vmem_limit_bytes=FIRST_VMEM),
         cost_estimate=pl.CostEstimate(flops=FIRST_FLOPS, bytes_accessed=FIRST_FLOPS, transcendentals=0),
@@ -367,11 +398,11 @@
 
 
 def last_kernel(ranges, *refs):
-    count = 2 * COLUMN_PIECES
+    count = COLUMN_PIECES
     x_pieces, dy_pieces, refs = refs[:count], refs[count : 2 * count], refs[2 * count :]
     pieces, refs = refs[: len(ranges)], refs[len(ranges) :]
-    sum_hbm, term_ref, own_ref, other_ref, x, dy, gu, down, total, grads, sems = refs
-    slots, part = x.shape[0] // 2, x.shape[1] // 4
+    sum_hbm, term_ref, out_ref, x, dy, gu, down, total, grads, sems = refs
+    slots, part = x.shape[0], x.shape[1] // 4
     x_copies = row_copies(x_pieces, x, sems.at[pl.ds(0, count)])
     dy_copies = row_copies(dy_pieces, dy, sems.at[pl.ds(count, count)])
     up_copies, down_copies = block_copies(pieces, ranges, gu, down, 0, sems.at[pl.ds(2 * count + 1, 2 * len(ranges))])
@@ -381,28 +412,24 @@
     for copy in x_copies:
         copy.wait()
     terms = hidden_grads(x, dy, gu, down, grads, [up_copies], [down_copies + dy_copies]) + term_ref[...]
-    terms = jnp.broadcast_to(jnp.sum(terms, axis=1, keepdims=True), (2 * slots, TERM_LANES)).astype(BF)
-    own_ref[:, 4 * part :] = terms[:slots]
-    other_ref[:, 4 * part :] = terms[slots:]
+    terms = jnp.broadcast_to(jnp.sum(terms, axis=1, keepdims=True), (slots, TERM_LANES))
+    out_ref[:, 4 * part :] = terms.astype(BF)
     sum_copy.wait()
     for j in range(4):
         cols = slice(j * part, (j + 1) * part)
-        rows = (total[:, cols].astype(F32) + row_grads(grads, gu, j)).astype(BF)
-        own_ref[:, cols] = rows[:slots]
-        other_ref[:, cols] = rows[slots:]
+        out_ref[:, cols] = (total[:, cols].astype(F32) + row_grads(grads, gu, j)).astype(BF)
 
 
 def last_block(x, dy, pieces, ranges, total, term):
     rows, width = total.shape
     hidden, span = pieces[0].shape[1:]
-    out = jax.ShapeDtypeStruct((rows // 2, width + TERM_LANES), BF)
     any_spec = pl.BlockSpec(memory_space=pl.ANY)
     vmem_spec = pl.BlockSpec(memory_space=pltpu.VMEM)
     return pl.pallas_call(
         functools.partial(last_kernel, ranges),
-        out_shape=(out, out),
+        out_shape=jax.ShapeDtypeStruct((rows, width + TERM_LANES), BF),
         in_specs=[any_spec] * (len(x) + len(dy) + len(pieces) + 1) + [vmem_spec],
-        out_specs=(vmem_spec, vmem_spec),
+        out_specs=vmem_spec,
         scratch_shapes=[
             pltpu.VMEM((rows, width), BF),
             pltpu.VMEM((rows, width), BF),
@@ -410,14 +437,10 @@
             pltpu.VMEM((PARTS - UP_PARTS, hidden, span), BF),
             pltpu.VMEM((rows, width), BF),
             pltpu.VMEM((rows, span), BF),
-            pltpu.SemaphoreType.DMA((4 * COLUMN_PIECES + 1 + 2 * len(pieces),)),
+            pltpu.SemaphoreType.DMA((2 * COLUMN_PIECES + 1 + 2 * len(pieces),)),
         ],
         compiler_params=pltpu.CompilerParams(vmem_limit_bytes=LAST_VMEM),
-        cost_estimate=pl.CostEstimate(
-            flops=2 * rows * width * hidden * 5,
-            bytes_accessed=2 * (3 * width * hidden + 5 * rows * width),
-            transcendentals=rows * hidden,
-        ),
+        cost_estimate=pl.CostEstimate(flops=LAST_FLOPS, bytes_accessed=LAST_FLOPS, transcendentals=0),
         name="last",
     )(*x, *dy, *pieces, total, term)
 
@@ -529,18 +552,20 @@
     far_down = lax.ppermute(far_down, "tensor", down)
     rows = list(unpack(got))
     other_rows = [lax.ppermute(piece, "dp", swap) for piece in rows]
-    x = rows[:COLUMN_PIECES] + other_rows[:COLUMN_PIECES]
-    dy = rows[COLUMN_PIECES:] + other_rows[COLUMN_PIECES:]
-
     part = width // UP_PARTS
     squares = lambda piece: piece.reshape(-1, part, 2 * part)
     blocks = [list(map(squares, b)) for b in ((head, up_rest), (up_head, from_up), (from_down, down_tail))]
     ranges = ((ENDS[0], RESTS[0]),) * 2 + ((RESTS[1], ENDS[1]),)
     far = (far_head, far_up, far_down, far_tail)
     far_ranges = (ENDS[0], (HEAD, HALF), (HALF, PARTS - HEAD), ENDS[1])
-    total, term = first_blocks(x, dy, blocks, ranges)
-    own, other = last_block(x, dy, list(map(squares, far)), far_ranges, total, term)
-    back = add_pack(own, lax.ppermute(other, "dp", swap)).reshape(experts, ROWS, -1)
+    cut = lambda r: (r[:COLUMN_PIECES], r[COLUMN_PIECES:])
+    own_total, own_gate_term = first_blocks(*cut(rows), blocks, ranges)
+    own_total, *other_rows = lax.optimization_barrier((own_total, *other_rows))
+    total, term = first_blocks(*cut(other_rows), blocks, ranges)
+    far = list(map(squares, far))
+    other_sums = lax.ppermute(last_block(*cut(other_rows), far, far_ranges, total, term), "dp", swap)
+    own_sums = last_block(*cut(rows), far, far_ranges, own_total, own_gate_term)
+    back = add_pack(own_sums, other_sums).reshape(experts, ROWS, -1)
     ret = lax.all_to_all(back, "expert", split_axis=0, concat_axis=0, tiled=True)
     own_term = jnp.sum(out_grad.astype(F32) * tokens.astype(F32), axis=1)
     token_grad, gate_grad = combine(

time: 231 us -> 232 us (level)
  waiting for transfers between devices: 140 us -> 129 us
  Pallas kernels: 50.3 us -> 56.4 us
  local copies, waits for them, and re-layouts: 4.77 us -> 9.73 us
    unnamed x26 -> x34, local copies, waits for them, and re-layouts: 4.77 us -> 9.73 us
    pallas_call x1 -> x2, Pallas kernels: 18 us -> 22.3 us  [first_blocks(): pl.pallas_call(functools.partial(first_kernel, ranges), out_shape=(jax.Sh...]
    ppermute x1, waiting for transfers between devices: 4.24 us -> 0.01 us  [per_device(): lax.ppermute(last_block(*cut(other_rows), far, far_ranges, total, term),...]
    ppermute x2, waiting for transfers between devices: 4.24 us -> 0.01 us  [per_device(): other_rows = [lax.ppermute(piece, 'dp', swap) for piece in rows]]
    ppermute x1, waiting for transfers between devices: 18.2 us -> 14.7 us  [per_device(): far_head = lax.ppermute(up_head, 'tensor', up)]
    pallas_call x2 -> x3, Pallas kernels: 15.4 us -> 17.6 us  [the longest x2 11.5 us: last_block(): pl.pallas_call(functools.partial(last_kernel, ranges), out_shape=jax.Shap...]
  transfers between devices with their start and end apart: 13 -> 13, of which waited for: 8 -> 4; matrix products, arithmetic and copies ran while one was open for 1% -> 1% of each run, Pallas kernels for 11% -> 16%
where the time goes in v7:
time: 232 us; the launch traced here: 230 us
  waiting for transfers between devices  129 us (56%)
  Pallas kernels  56.4 us (24%)
  starting transfers between devices  33.1 us (14%)
  local copies, waits for them, and re-layouts  9.73 us (4%)
    ppermute x1, waiting for transfers between devices, per_device(): up_head = lax.ppermute(head, 'tensor', up)  65.2 us
    all_to_all x1, waiting for transfers between devices, per_device(): lax.all_to_all(back, 'expert', split_axis=0, concat_axis=0, tiled=True)  47.5 us
    pallas_call x2, Pallas kernels, first_blocks(): pl.pallas_call(functools.partial(first_kernel, ranges), out_shape=(jax.Sh...  22.3 us
    ppermute x1, waiting for transfers between devices, per_device(): far_head = lax.ppermute(up_head, 'tensor', up)  14.7 us
    all_to_all x1, starting transfers between devices, per_device(): lax.all_to_all(back, 'expert', split_axis=0, concat_axis=0, tiled=True)  12.7 us
    pallas_call x2, Pallas kernels, last_block(): pl.pallas_call(functools.partial(last_kernel, ranges), out_shape=jax.Shap...  11.5 us
    all_to_all x1, starting transfers between devices, per_device(): lax.all_to_all(packed.reshape(experts, ROWS, -1), 'expert', split_axis=0,...  11.4 us
    unnamed x34, local copies, waits for them, and re-layouts  9.73 us
  transfers between devices with their start and end apart: 13, of which 4 were waited for; matrix products, arithmetic and copies ran while one was open for 1% of the time, Pallas kernels for 16%

profile of v7, /device:TPU:24, one launch (start us, length us, event | category | flops | bytes accessed | tf_op | source)
XLA Modules:
  0.0 230.4 jit_solution(10181638265664253755)
XLA Ops:
  0.6 5.6 %weights.1 = (bf16[1920,256]{1,0:T(8,128)(2,1)}, bf16[5760,256]{1,0:T(8,128)(2,1)}, bf16[5760,256]{1,0:T(8,128)(2,1)}, bf16[1920,256]{1,0:T(8,128)(2,1)}) custom-call(s32[1]{0:T(128)} %bitcast.1.core_ref, bf16[5120,256]{1,0:T(8,128)(2,1)} %bitcast.46, bf16[5120,256]{1,0:T(8,128)(2,1)} %bitcast.47, bf16[256,5120]{1,0:T(8,128)(2,1)} %bitcast.48), custom_call_target="tpu_custom_call" | custom-call | bytes 11796480 | tf_op jit(solution)/shard_map/weights/pallas_call | solution.py:170
  6.3 2.0 collective-permute-start
  8.3 0.1 collective-permute-start.1
  8.4 6.1 %pack.1 = bf16[256,7680]{1,0:T(8,128)(2,1)} custom-call(s32[1,128]{1,0:T(1,128)} %bitcast.42, bf16[128,5120]{1,0:T(8,128)(2,1)} %x_hbm.1, bf16[128,5120]{1,0:T(8,128)(2,1)} %out_grad_ref.1), custom_call_target="tpu_custom_call" | custom-call | flops 1006632960 | bytes 6553600 | tf_op jit(solution)/shard_map/pack/pallas_call | solution.py:99
  14.5 11.4 %all-to-all-start = ((bf16[32,8,7680]{2,1,0:T(8,128)(2,1)}), bf16[32,8,7680]{2,1,0:T(8,128)(2,1)}, u32[]{:S(2)}, u32[]{:S(2)}) async-start(bf16[32,8,7680]{2,1,0:T(8,128)(2,1)} %bitcast.45), calls=%async_computation | async-start | bytes 7864320 | tf_op jit(solution)/shard_map/all_to_all | solution.py:543
  25.9 1.5 collective-permute-start.2
  27.4 0.6 collective-permute-start.4
  28.0 65.2 %collective-permute-done.2 = bf16[1920,256]{1,0:T(8,128)(2,1)S(1)} collective-permute-done((bf16[1920,256]{1,0:T(8,128)(2,1)}, bf16[1920,256]{1,0:T(8,128)(2,1)S(1)}, u32[]{:S(2)}, u32[]{:S(2)}) %collective-permute-start.2) | collective-permute-done | bytes 983072 | tf_op jit(solution)/shard_map/ppermute | solution.py:534
  93.2 1.5 collective-permute-start.3
  94.7 0.0 copy-start.10
  94.7 1.0 copy-done.10
  95.7 0.0 collective-permute-done.4
  95.7 0.5 collective-permute-start.5
  96.2 0.0 copy-start.13
  96.2 1.0 copy-done.13
  97.2 0.0 collective-permute-done.up_hbm
  97.2 0.0 copy-start.2
  97.2 0.0 collective-permute-done.1.down_hbm
  97.2 1.6 copy-done.2
  98.8 2.5 %far.1 = (bf16[1920,256]{1,0:T(8,128)(2,1)}, bf16[1920,256]{1,0:T(8,128)(2,1)}) custom-call(bf16[5760,256]{1,0:T(8,128)(2,1)} %copy-done.2, bf16[5760,256]{1,0:T(8,128)(2,1)} %collective-permute-done.1.down_hbm), custom_call_target="tpu_custom_call" | custom-call | flops 62000001024 | tf_op jit(solution)/shard_map/far/pallas_call | solution.py:208
  101.3 0.0 copy-start.1
  101.3 14.7 %collective-permute-done.3 = bf16[1920,256]{1,0:T(8,128)(2,1)S(1)} collective-permute-done((bf16[1920,256]{1,0:T(8,128)(2,1)S(1)}, bf16[1920,256]{1,0:T(8,128)(2,1)S(1)}, u32[]{:S(2)}, u32[]{:S(2)}) %collective-permute-start.3) | collective-permute-done | bytes 983072 | tf_op jit(solution)/shard_map/ppermute | solution.py:538
  116.0 0.0 copy-start.5
  116.0 1.0 copy-done.5
  116.9 1.2 collective-permute-done.5
  118.2 0.0 copy-start.7
  118.2 1.0 copy-done.7
  119.1 0.0 all-to-all-done
  119.1 3.7 %unpack.1 = (bf16[192,5120]{1,0:T(8,128)(2,1)S(1)}, bf16[192,5120]{1,0:T(8,128)(2,1)S(1)}) custom-call(bf16[256,7680]{1,0:T(8,128)(2,1)} %bitcast.8.rows_hbm), custom_call_target="tpu_custom_call" | custom-call | flops 1000 | bytes 1000 | tf_op jit(solution)/shard_map/unpack/pallas_call | solution.py:324
  122.8 0.1 collective-permute-start.8
  122.9 0.5 collective-permute-start.9
  123.4 0.3 collective-permute-start.6
  123.7 1.8 collective-permute-start.7
  125.4 0.0 copy-done.1
  125.4 0.0 copy-done.9
  125.4 1.8 copy-done.3
  127.3 1.2 copy-done.11
  128.5 1.2 copy-done.14
  129.7 11.2 %first.2 = (bf16[192,5120]{1,0:T(8,128)(2,1)S(1)}, f32[192,128]{1,0:T(8,128)S(1)}) custom-call(bf16[192,5120]{1,0:T(8,128)(2,1)S(1)} %get-tuple-element.34.refs_0_, bf16[192,5120]{1,0:T(8,128)(2,1)S(1)} %get-tuple-element.35.refs_1_, bf16[15,128,256]{2,1,0:T(8,128)(2,1)S(1)} %bitcast.35, bf16[45,128,256]{2,1,0:T(8,128)(2,1)S(1)} %bitcast.22, ...), custom_call_target="tpu_custom_call" | custom-call | flops 1000 | bytes 1000 | tf_op jit(solution)/shard_map/first/pallas_call | solution.py:380
  140.8 0.0 collective-permute-done.8.refs_0_
  140.8 0.0 collective-permute-done.9.refs_1_
  140.8 0.0 copy-done.4
  140.9 0.0 copy-done.12
  140.9 0.0 copy-start.6
  140.9 0.0 copy-start.8
  140.9 11.2 %first.3 = (bf16[192,5120]{1,0:T(8,128)(2,1)S(1)}, f32[192,128]{1,0:T(8,128)S(1)}) custom-call(bf16[192,5120]{1,0:T(8,128)(2,1)S(1)} %collective-permute-done.8.refs_0_, bf16[192,5120]{1,0:T(8,128)(2,1)S(1)} %collective-permute-done.9.refs_1_, bf16[15,128,256]{2,1,0:T(8,128)(2,1)S(1)} %bitcast.36, bf16[45,128,256]{2,1,0:T(8,128)(2,1)S(1)} %bitcast.23, ...), custom_call_target="tpu_custom_call" | custom-call | flops 1000 | bytes 1000 | tf_op jit(solution)/shard_map/first/pallas_call | solution.py:380
  152.1 0.0 collective-permute-done.6
  152.1 0.0 collective-permute-done.7
  152.1 0.0 copy-done.6
  152.1 0.0 copy-done.8
  152.1 5.9 %last.3 = bf16[192,5248]{1,0:T(8,128)(2,1)S(1)} custom-call(bf16[192,5120]{1,0:T(8,128)(2,1)S(1)} %collective-permute-done.8.refs_0_, bf16[192,5120]{1,0:T(8,128)(2,1)S(1)} %collective-permute-done.9.refs_1_, bf16[15,128,256]{2,1,0:T(8,128)(2,1)S(1)} %bitcast.27, bf16[15,128,256]{2,1,0:T(8,128)(2,1)S(1)} %bitcast.31, bf16[15,128,256]{2,1,0:T(8,128)(2,1)S(1)} %bitcast.33, ...), custom_call_target="tpu_custom_call" | custom-call | flops 1000 | bytes 1000 | tf_op jit(solution)/shard_map/last/pallas_call | solution.py:428
  158.0 0.1 collective-permute-start.10
  158.1 5.6 %last.2.a_ref = bf16[192,5248]{1,0:T(8,128)(2,1)S(1)} custom-call(bf16[192,5120]{1,0:T(8,128)(2,1)S(1)} %get-tuple-element.34.refs_0_, bf16[192,5120]{1,0:T(8,128)(2,1)S(1)} %get-tuple-element.35.refs_1_, bf16[15,128,256]{2,1,0:T(8,128)(2,1)S(1)} %bitcast.28, bf16[15,128,256]{2,1,0:T(8,128)(2,1)S(1)} %bitcast.32, bf16[15,128,256]{2,1,0:T(8,128)(2,1)S(1)} %bitcast.34, ...), custom_call_target="tpu_custom_call" | custom-call | flops 1000 | bytes 1000 | tf_op jit(solution)/shard_map/last/pallas_call | solution.py:428
  163.7 0.0 collective-permute-done.10.b_ref
  163.7 2.6 %add_pack.1 = bf16[256,3968]{1,0:T(8,128)(2,1)} custom-call(bf16[192,5248]{1,0:T(8,128)(2,1)S(1)} %last.2.a_ref, bf16[192,5248]{1,0:T(8,128)(2,1)S(1)} %collective-permute-done.10.b_ref), custom_call_target="tpu_custom_call" | custom-call | flops 754974720 | bytes 6045696 | tf_op jit(solution)/shard_map/add_pack/pallas_call | solution.py:469
  166.3 12.7 %all-to-all-start.1 = ((bf16[32,8,3968]{2,1,0:T(8,128)(2,1)}), bf16[32,8,3968]{2,1,0:T(8,128)(2,1)S(1)}, u32[]{:S(2)}, u32[]{:S(2)}) async-start(bf16[32,8,3968]{2,1,0:T(8,128)(2,1)} %bitcast.19), calls=%async_computation.1 | async-start | bytes 4063232 | tf_op jit(solution)/shard_map/all_to_all | solution.py:569
  179.1 0.0 copy-done
  179.1 0.0 copy-start.15
  179.1 0.0 copy-start.16
  179.1 1.8 multiply_reduce_fusion
  180.9 47.5 %all-to-all-done.1 = bf16[32,8,3968]{2,1,0:T(8,128)(2,1)S(1)} async-done(((bf16[32,8,3968]{2,1,0:T(8,128)(2,1)}), bf16[32,8,3968]{2,1,0:T(8,128)(2,1)S(1)}, u32[]{:S(2)}, u32[]{:S(2)}) %all-to-all-start.1) | async-done | bytes 2031648 | tf_op jit(solution)/shard_map/all_to_all | solution.py:569
  228.3 0.0 copy-done.15
  228.3 0.0 copy-done.16
  228.3 2.1 combine.1
  (7 shorter events, 0.0 us)
Async XLA Ops:
  6.3 91.0 %collective-permute-start = (bf16[5760,256]{1,0:T(8,128)(2,1)}, bf16[5760,256]{1,0:T(8,128)(2,1)S(1)}, u32[]{:S(2)}, u32[]{:S(2)}) collective-permute-start(bf16[5760,256]{1,0:T(8,128)(2,1)} %get-tuple-element.28), channel_id=1, source_target_pairs={{0,2},{2,4},{4,6},{6,0},{1,3},{3,5},{5,7},{7,1},{8,10},{10,12},{12... | collective-permute-start | bytes 8847368 | tf_op jit(solution)/shard_map/ppermute | solution.py:536
  8.3 88.9 %collective-permute-start.1 = (bf16[5760,256]{1,0:T(8,128)(2,1)}, bf16[5760,256]{1,0:T(8,128)(2,1)}, u32[]{:S(2)}, u32[]{:S(2)}) collective-permute-start(bf16[5760,256]{1,0:T(8,128)(2,1)} %get-tuple-element.29), channel_id=1, source_target_pairs={{0,6},{2,0},{4,2},{6,4},{1,7},{3,1},{5,3},{7,5},{8,14},{10,8},{12,... | collective-permute-start | bytes 8847368 | tf_op jit(solution)/shard_map/ppermute | solution.py:537
  14.5 104.6 %all-to-all-start = ((bf16[32,8,7680]{2,1,0:T(8,128)(2,1)}), bf16[32,8,7680]{2,1,0:T(8,128)(2,1)}, u32[]{:S(2)}, u32[]{:S(2)}) async-start(bf16[32,8,7680]{2,1,0:T(8,128)(2,1)} %bitcast.45), calls=%async_computation | async-start | bytes 7864320 | tf_op jit(solution)/shard_map/all_to_all | solution.py:543
  25.9 67.3 %collective-permute-start.2 = (bf16[1920,256]{1,0:T(8,128)(2,1)}, bf16[1920,256]{1,0:T(8,128)(2,1)S(1)}, u32[]{:S(2)}, u32[]{:S(2)}) collective-permute-start(bf16[1920,256]{1,0:T(8,128)(2,1)} %get-tuple-element.40), channel_id=1, source_target_pairs={{0,2},{2,4},{4,6},{6,0},{1,3},{3,5},{5,7},{7,1},{8,10},{10,12},{12... | collective-permute-start | bytes 2949128 | tf_op jit(solution)/shard_map/ppermute | solution.py:534
  27.4 68.3 %collective-permute-start.4 = (bf16[1920,256]{1,0:T(8,128)(2,1)}, bf16[1920,256]{1,0:T(8,128)(2,1)S(1)}, u32[]{:S(2)}, u32[]{:S(2)}) collective-permute-start(bf16[1920,256]{1,0:T(8,128)(2,1)} %get-tuple-element.32), channel_id=1, source_target_pairs={{0,6},{2,0},{4,2},{6,4},{1,7},{3,1},{5,3},{7,5},{8,14},{10,8},{12,... | collective-permute-start | bytes 2949128 | tf_op jit(solution)/shard_map/ppermute | solution.py:535
  93.2 22.7 %collective-permute-start.3 = (bf16[1920,256]{1,0:T(8,128)(2,1)S(1)}, bf16[1920,256]{1,0:T(8,128)(2,1)S(1)}, u32[]{:S(2)}, u32[]{:S(2)}) collective-permute-start(bf16[1920,256]{1,0:T(8,128)(2,1)S(1)} %collective-permute-done.2), channel_id=1, source_target_pairs={{0,2},{2,4},{4,6},{6,0},{1,3},{3,5},{5,7},{7,1},{8,10},{10,12},{12... | collective-permute-start | bytes 2949128 | tf_op jit(solution)/shard_map/ppermute | solution.py:538
  94.7 1.0 copy-start.10
  95.7 22.4 %collective-permute-start.5 = (bf16[1920,256]{1,0:T(8,128)(2,1)S(1)}, bf16[1920,256]{1,0:T(8,128)(2,1)S(1)}, u32[]{:S(2)}, u32[]{:S(2)}) collective-permute-start(bf16[1920,256]{1,0:T(8,128)(2,1)S(1)} %collective-permute-done.4), channel_id=1, source_target_pairs={{0,6},{2,0},{4,2},{6,4},{1,7},{3,1},{5,3},{7,5},{8,14},{10,8},{12,... | collective-permute-start | bytes 2949128 | tf_op jit(solution)/shard_map/ppermute | solution.py:539
  96.2 1.0 copy-start.13
  97.2 1.6 copy-start.2
  101.3 24.1 %copy-start.1 = (bf16[5760,256]{1,0:T(8,128)(2,1)S(1)}, bf16[5760,256]{1,0:T(8,128)(2,1)}, u32[]{:S(2)}) copy-start(bf16[5760,256]{1,0:T(8,128)(2,1)} %get-tuple-element.28) | copy-start | bytes 8847364
  116.0 1.0 copy-start.5
  118.2 1.0 copy-start.7
  119.1 6.3 %copy-start.9 = (bf16[1920,256]{1,0:T(8,128)(2,1)S(1)}, bf16[1920,256]{1,0:T(8,128)(2,1)}, u32[]{:S(2)}) copy-start(bf16[1920,256]{1,0:T(8,128)(2,1)} %get-tuple-element.40) | copy-start | bytes 2949124
  122.8 18.0 %collective-permute-start.8 = (bf16[192,5120]{1,0:T(8,128)(2,1)S(1)}, bf16[192,5120]{1,0:T(8,128)(2,1)S(1)}, u32[]{:S(2)}, u32[]{:S(2)}) collective-permute-start(bf16[192,5120]{1,0:T(8,128)(2,1)S(1)} %get-tuple-element.34.refs_0_), channel_id=1, source_target_pairs={{0,1},{1,0},{2,3},{3,2},{4,5},{5,4},{6,7},{7,6},{8,9},{9,8},{10,11... | collective-permute-start | bytes 5898248 | tf_op jit(solution)/shard_map/ppermute | solution.py:554
  122.9 17.9 %collective-permute-start.9 = (bf16[192,5120]{1,0:T(8,128)(2,1)S(1)}, bf16[192,5120]{1,0:T(8,128)(2,1)S(1)}, u32[]{:S(2)}, u32[]{:S(2)}) collective-permute-start(bf16[192,5120]{1,0:T(8,128)(2,1)S(1)} %get-tuple-element.35.refs_1_), channel_id=1, source_target_pairs={{0,1},{1,0},{2,3},{3,2},{4,5},{5,4},{6,7},{7,6},{8,9},{9,8},{10,11... | collective-permute-start | bytes 5898248 | tf_op jit(solution)/shard_map/ppermute | solution.py:554
  123.4 28.7 %collective-permute-start.6 = (bf16[1920,256]{1,0:T(8,128)(2,1)}, bf16[1920,256]{1,0:T(8,128)(2,1)S(1)}, u32[]{:S(2)}, u32[]{:S(2)}) collective-permute-start(bf16[1920,256]{1,0:T(8,128)(2,1)} %get-tuple-element.37), channel_id=1, source_target_pairs={{0,2},{2,4},{4,6},{6,0},{1,3},{3,5},{5,7},{7,1},{8,10},{10,12},{12... | collective-permute-start | bytes 2949128 | tf_op jit(solution)/shard_map/ppermute | solution.py:551
  123.7 28.4 %collective-permute-start.7 = (bf16[1920,256]{1,0:T(8,128)(2,1)}, bf16[1920,256]{1,0:T(8,128)(2,1)S(1)}, u32[]{:S(2)}, u32[]{:S(2)}) collective-permute-start(bf16[1920,256]{1,0:T(8,128)(2,1)} %get-tuple-element.38), channel_id=1, source_target_pairs={{0,6},{2,0},{4,2},{6,4},{1,7},{3,1},{5,3},{7,5},{8,14},{10,8},{12,... | collective-permute-start | bytes 2949128 | tf_op jit(solution)/shard_map/ppermute | solution.py:552
  125.4 1.8 copy-start.3
  127.3 1.2 copy-start.11
  128.5 1.2 copy-start.14
  129.7 11.2 %copy-start.4 = (bf16[5760,256]{1,0:T(8,128)(2,1)S(1)}, bf16[5760,256]{1,0:T(8,128)(2,1)}, u32[]{:S(2)}) copy-start(bf16[5760,256]{1,0:T(8,128)(2,1)} %copy-done.2) | copy-start | bytes 8847364
  129.7 11.2 %copy-start.12 = (bf16[1920,256]{1,0:T(8,128)(2,1)S(1)}, bf16[1920,256]{1,0:T(8,128)(2,1)}, u32[]{:S(2)}) copy-start(bf16[1920,256]{1,0:T(8,128)(2,1)} %copy-done.10) | copy-start | bytes 2949124
  140.9 11.2 %copy-start.6 = (bf16[1920,256]{1,0:T(8,128)(2,1)S(1)}, bf16[1920,256]{1,0:T(8,128)(2,1)}, u32[]{:S(2)}) copy-start(bf16[1920,256]{1,0:T(8,128)(2,1)} %copy-done.5) | copy-start | bytes 2949124
  140.9 11.2 %copy-start.8 = (bf16[1920,256]{1,0:T(8,128)(2,1)S(1)}, bf16[1920,256]{1,0:T(8,128)(2,1)}, u32[]{:S(2)}) copy-start(bf16[1920,256]{1,0:T(8,128)(2,1)} %copy-done.7) | copy-start | bytes 2949124
  158.0 5.7 %collective-permute-start.10 = (bf16[192,5248]{1,0:T(8,128)(2,1)S(1)}, bf16[192,5248]{1,0:T(8,128)(2,1)S(1)}, u32[]{:S(2)}, u32[]{:S(2)}) collective-permute-start(bf16[192,5248]{1,0:T(8,128)(2,1)S(1)} %last.3), channel_id=1, source_target_pairs={{0,1},{1,0},{2,3},{3,2},{4,5},{5,4},{6,7},{7,6},{8,9},{9,8},{10,11... | collective-permute-start | bytes 6045704 | tf_op jit(solution)/shard_map/ppermute | solution.py:566
  166.3 12.7 %copy-start = (bf16[128,5120]{1,0:T(8,128)(2,1)S(1)}, bf16[128,5120]{1,0:T(8,128)(2,1)}, u32[]{:S(2)}) copy-start(bf16[128,5120]{1,0:T(8,128)(2,1)} %out_grad_ref.1) | copy-start | bytes 3932164
  166.3 62.0 %all-to-all-start.1 = ((bf16[32,8,3968]{2,1,0:T(8,128)(2,1)}), bf16[32,8,3968]{2,1,0:T(8,128)(2,1)S(1)}, u32[]{:S(2)}, u32[]{:S(2)}) async-start(bf16[32,8,3968]{2,1,0:T(8,128)(2,1)} %bitcast.19), calls=%async_computation.1 | async-start | bytes 4063232 | tf_op jit(solution)/shard_map/all_to_all | solution.py:569
  179.1 49.2 %copy-start.15 = (s32[128,1]{0,1:T(1,128)S(1)}, s32[128,1]{0,1:T(1,128)}, u32[]{:S(2)}) copy-start(s32[128,1]{0,1:T(1,128)} %param.10) | copy-start | bytes 1540
  179.1 49.2 %copy-start.16 = (f32[128]{0:T(128)S(1)}, f32[128]{0:T(128)}, u32[]{:S(2)}) copy-start(f32[128]{0:T(128)} %param.9) | copy-start | bytes 1540

commit v8 on v7

--- a/solution.py
+++ b/solution.py
@@ -15,7 +15,7 @@
 PARTS = 60
 UP_PARTS = 40
 HALF = 30
-HEAD = 15
+HEAD = 16
 ENDS = ((0, HEAD), (PARTS - HEAD, PARTS))
 RESTS = ((HEAD, PARTS), (0, PARTS - HEAD))
 MIDDLE = (PARTS - 2 * HEAD) // 3
@@ -25,9 +25,8 @@
 LAST_FLOPS = 1000
 VMEM_ALL = 56 * 1024 * 1024
 SMALL_VMEM = 20 * 1024 * 1024
-FIRST_VMEM = 28 * 1024 * 1024
-LAST_VMEM = 20 * 1024 * 1024
-COLUMN_PIECES = 1
+FIRST_VMEM = 38 * 1024 * 1024
+LAST_VMEM = 24 * 1024 * 1024
 
 
 def dot(a, b):
@@ -63,31 +62,38 @@
     return base + slot, base + CAP + second, slot - 3 * second
 
 
-def pack_kernel(route_ref, x_hbm, dy_hbm, out_hbm, x, dy, out, in_sems, out_sems):
-    n, width = x.shape
-    total = out.shape[0]
-    part = width // 4
-    columns = [pl.ds(j * part, part) for j in range(4)]
-    reads = [
-        [pltpu.make_async_copy(src.at[:, columns[j]], dst.at[:, columns[j]], in_sems.at[4 * i + j]) for j in range(4)]
-        for i, (src, dst) in enumerate(((x_hbm, x), (dy_hbm, dy)))
-    ]
-    for copies in reads:
-        for j in (3, 0, 1, 2):
-            copies[j].start()
+def pack_kernel(route_ref, x_hbm, dy_hbm, out_hbm, rows, out, in_sems, out_sems):
+    n, total = route_ref.shape[1], out.shape[0]
+    part = rows.shape[2]
+    reads = []
+    for i, src in enumerate((x_hbm, dy_hbm)):
+        for j in range(3):
+            k = 3 * i + j
+            reads.append(
+                [
+                    pltpu.make_async_copy(
+                        src.at[:, pl.ds(quarter * part, part)], rows.at[k, pl.ds(low, n)], in_sems.at[2 * k + low // n]
+                    )
+                    for quarter, low in ((j, 0), (3, n))
+                ]
+            )
+            for copy in reads[-1]:
+                copy.start()
     main, tail, block = places(route_ref[...])
     row = lax.broadcasted_iota(jnp.int32, (total, n), 0)
     select = jnp.where(row == main, 1.0, 0.0).astype(BF)
-    tail_select = [jnp.where((row == tail) & (block == j), 1.0, 0.0).astype(BF) for j in range(3)]
+    selects = [
+        jnp.concatenate([select, jnp.where((row == tail) & (block == j), 1.0, 0.0).astype(BF)], axis=1)
+        for j in range(3)
+    ]
     writes = []
-    for i, rows in enumerate((x, dy)):
-        reads[i][3].wait()
-        for j in range(3):
-            reads[i][j].wait()
-            cols = pl.ds((3 * i + j) * part, part)
-            out[:, cols] = (dot(select, rows[:, columns[j]]) + dot(tail_select[j], rows[:, columns[3]])).astype(BF)
-            writes.append(pltpu.make_async_copy(out.at[:, cols], out_hbm.at[:, cols], out_sems.at[3 * i + j]))
-            writes[-1].start()
+    for k in range(6):
+        for copy in reads[k]:
+            copy.wait()
+        cols = pl.ds(k * part, part)
+        out[:, cols] = dot(selects[k % 3], rows[k]).astype(BF)
+        writes.append(pltpu.make_async_copy(out.at[:, cols], out_hbm.at[:, cols], out_sems.at[k]))
+        writes[-1].start()
     for write in writes:
         write.wait()
 
@@ -102,10 +108,9 @@
         in_specs=[pl.BlockSpec(memory_space=pltpu.VMEM), any_spec, any_spec],
         out_specs=any_spec,
         scratch_shapes=[
-            pltpu.VMEM((n, width), BF),
-            pltpu.VMEM((n, width), BF),
+            pltpu.VMEM((6, 2 * n, width // 4), BF),
             pltpu.VMEM(shape, BF),
-            pltpu.SemaphoreType.DMA((8,)),
+            pltpu.SemaphoreType.DMA((12,)),
             pltpu.SemaphoreType.DMA((6,)),
         ],
         compiler_params=pltpu.CompilerParams(vmem_limit_bytes=VMEM_ALL),
@@ -291,31 +296,24 @@
     return dot_t(grads[...], gu[rows].reshape(parts // 4 * hidden, columns))
 
 
-def unpack_kernel(rows_hbm, *refs):
-    outs, rows, sems = refs[:-2], refs[-2], refs[-1]
+def unpack_kernel(rows_hbm, x_ref, dy_ref, rows, sems):
     packed = rows.shape[0]
-    slots, width = outs[0].shape[0], rows.shape[1] // 6 * 4
+    slots, width = x_ref.shape
     part = width // 4
-    per = len(outs) // 2
     cols = [slice(j * part, (j + 1) * part) for j in range(6)]
     copies = [pltpu.make_async_copy(rows_hbm.at[:, c], rows.at[:, c], sems.at[j]) for j, c in enumerate(cols)]
     for copy in copies:
         copy.start()
     spread = slot_matrix(slots, packed, 0, None)
-    spread_tail = [slot_matrix(slots, packed, 0, j) for j in range(3)]
-    wide = width // per
-    for k in range(2):
+    both = [jnp.concatenate([spread, slot_matrix(slots, packed, 0, j)], axis=0) for j in range(3)]
+    for k, out_ref in enumerate((x_ref, dy_ref)):
         last = None
-        for j in range(4):
-            if j < 3:
-                copies[3 * k + j].wait()
-                piece = dot(spread, rows[:, cols[3 * k + j]])
-                more = dot(spread_tail[j], rows[:, cols[3 * k + j]])
-                last = more if last is None else last + more
-            else:
-                piece = last
-            low = j * part % wide
-            outs[k * per + j * part // wide][:, low : low + part] = piece.astype(BF)
+        for j in range(3):
+            copies[3 * k + j].wait()
+            pieces = dot(both[j], rows[:, cols[3 * k + j]])
+            out_ref[:, cols[j]] = pieces[:slots].astype(BF)
+            last = pieces[slots:] if last is None else last + pieces[slots:]
+        out_ref[:, cols[3]] = last.astype(BF)
 
 
 def unpack(rows):
@@ -323,7 +321,7 @@
     slots, width = packed // ROWS * CAP, rows.shape[1] // 6 * 4
     return pl.pallas_call(
         unpack_kernel,
-        out_shape=[jax.ShapeDtypeStruct((slots, width // COLUMN_PIECES), BF)] * (2 * COLUMN_PIECES),
+        out_shape=[jax.ShapeDtypeStruct((slots, width), BF)] * 2,
         in_specs=[pl.BlockSpec(memory_space=pl.ANY)],
         scratch_shapes=[pltpu.VMEM(rows.shape, BF), pltpu.SemaphoreType.DMA((6,))],
         compiler_params=pltpu.CompilerParams(vmem_limit_bytes=SMALL_VMEM),
@@ -332,86 +330,83 @@
     )(rows)
 
 
-def row_copies(pieces, full, sems):
-    wide = pieces[0].shape[1]
-    return [
-        pltpu.make_async_copy(piece, full.at[:, pl.ds(i * wide, wide)], sems.at[i]) for i, piece in enumerate(pieces)
+def first_kernel(ranges, *refs):
+    row_refs, refs = refs[:4], refs[4:]
+    pieces, refs = refs[: sum(map(len, ranges))], refs[sum(map(len, ranges)) :]
+    own_hbm, other_hbm, own_term, other_term, x, dy, gu, down, grads, total, sems = refs
+    slots, part = x.shape[0] // 2, x.shape[1] // 4
+    row_copies = [
+        pltpu.make_async_copy(src, full.at[pl.ds(i * slots, slots)], sems.at[2 * k + i])
+        for k, full in enumerate((x, dy))
+        for i, src in enumerate(row_refs[2 * k : 2 * k + 2])
     ]
-
-
-def first_kernel(ranges, *refs):
-    count = COLUMN_PIECES
-    x_pieces, dy_pieces, refs = refs[:count], refs[count : 2 * count], refs[2 * count :]
-    pieces, refs = refs[: sum(map(len, ranges))], refs[sum(map(len, ranges)) :]
-    sum_hbm, term_ref, x, dy, gu, down, grads, total, sems = refs
-    part = x.shape[1] // 4
-    x_copies = row_copies(x_pieces, x, sems.at[pl.ds(0, count)])
-    dy_copies = row_copies(dy_pieces, dy, sems.at[pl.ds(count, count)])
     up_copies, down_copies, used = [], [], 0
     for b, block in enumerate(ranges):
         here = pieces[used : used + len(block)]
-        ups, downs = block_copies(here, block, gu, down, b, sems.at[pl.ds(2 * count + 4 + 2 * used, 2 * len(block))])
+        ups, downs = block_copies(here, block, gu, down, b, sems.at[pl.ds(12 + 2 * used, 2 * len(block))])
         used += len(block)
         up_copies.append(ups)
         down_copies.append(downs)
-    for copies in [x_copies] + up_copies + [dy_copies] + down_copies:
+    for copies in [row_copies[:2]] + up_copies + [row_copies[2:]] + down_copies:
         for copy in copies:
             copy.start()
-    for copy in x_copies:
+    for copy in row_copies[:2]:
         copy.wait()
-    term_ref[...] = hidden_grads(x, dy, gu, down, grads, up_copies, down_copies + [dy_copies])
+    terms = hidden_grads(x, dy, gu, down, grads, up_copies, down_copies + [row_copies[2:]])
+    own_term[...] = terms[:slots]
+    other_term[...] = terms[slots:]
     outs = []
     for j in range(4):
         cols = pl.ds(j * part, part)
         total[:, cols] = row_grads(grads, gu, j).astype(BF)
-        outs.append(pltpu.make_async_copy(total.at[:, cols], sum_hbm.at[:, cols], sems.at[2 * count + j]))
-        outs[j].start()
+        for i, out in enumerate((own_hbm, other_hbm)):
+            src = total.at[pl.ds(i * slots, slots), cols]
+            outs.append(pltpu.make_async_copy(src, out.at[:, cols], sems.at[4 + 2 * j + i]))
+            outs[-1].start()
     for copy in outs:
         copy.wait()
 
 
-def first_blocks(x, dy, blocks, ranges):
-    slots, wide = x[0].shape
-    width = wide * COLUMN_PIECES
+def first_blocks(rows, blocks, ranges):
+    slots, width = rows[0].shape
     hidden, span = blocks[0][0].shape[1:]
     count = len(blocks)
     pieces = [piece for block in blocks for piece in block]
     any_spec = pl.BlockSpec(memory_space=pl.ANY)
+    vmem_spec = pl.BlockSpec(memory_space=pltpu.VMEM)
     return pl.pallas_call(
         functools.partial(first_kernel, ranges),
-        out_shape=(jax.ShapeDtypeStruct((slots, width), BF), jax.ShapeDtypeStruct((slots, hidden), F32)),
-        in_specs=[any_spec] * (len(x) + len(dy) + len(pieces)),
-        out_specs=(any_spec, pl.BlockSpec(memory_space=pltpu.VMEM)),
+        out_shape=[jax.ShapeDtypeStruct((slots, width), BF)] * 2 + [jax.ShapeDtypeStruct((slots, hidden), F32)] * 2,
+        in_specs=[any_spec] * (4 + len(pieces)),
+        out_specs=[any_spec] * 2 + [vmem_spec] * 2,
         scratch_shapes=[
-            pltpu.VMEM((slots, width), BF),
-            pltpu.VMEM((slots, width), BF),
+            pltpu.VMEM((2 * slots, width), BF),
+            pltpu.VMEM((2 * slots, width), BF),
             pltpu.VMEM((UP_PARTS, hidden, count * span), BF),
             pltpu.VMEM((PARTS - UP_PARTS, count * hidden, span), BF),
-            pltpu.VMEM((slots, count * span), BF),
-            pltpu.VMEM((slots, width), BF),
-            pltpu.SemaphoreType.DMA((2 * COLUMN_PIECES + 4 + 2 * len(pieces),)),
+            pltpu.VMEM((2 * slots, count * span), BF),
+            pltpu.VMEM((2 * slots, width), BF),
+            pltpu.SemaphoreType.DMA((12 + 2 * len(pieces),)),
         ],
         compiler_params=pltpu.CompilerParams(vmem_limit_bytes=FIRST_VMEM),
         cost_estimate=pl.CostEstimate(flops=FIRST_FLOPS, bytes_accessed=FIRST_FLOPS, transcendentals=0),
         name="first",
-    )(*x, *dy, *pieces)
+    )(*rows, *pieces)
 
 
 def last_kernel(ranges, *refs):
-    count = COLUMN_PIECES
-    x_pieces, dy_pieces, refs = refs[:count], refs[count : 2 * count], refs[2 * count :]
+    x_hbm, dy_hbm, refs = refs[0], refs[1], refs[2:]
     pieces, refs = refs[: len(ranges)], refs[len(ranges) :]
     sum_hbm, term_ref, out_ref, x, dy, gu, down, total, grads, sems = refs
     slots, part = x.shape[0], x.shape[1] // 4
-    x_copies = row_copies(x_pieces, x, sems.at[pl.ds(0, count)])
-    dy_copies = row_copies(dy_pieces, dy, sems.at[pl.ds(count, count)])
-    up_copies, down_copies = block_copies(pieces, ranges, gu, down, 0, sems.at[pl.ds(2 * count + 1, 2 * len(ranges))])
-    sum_copy = pltpu.make_async_copy(sum_hbm, total, sems.at[2 * count])
-    for copy in x_copies + up_copies + dy_copies + down_copies + [sum_copy]:
+    x_copy = pltpu.make_async_copy(x_hbm, x, sems.at[0])
+    dy_copy = pltpu.make_async_copy(dy_hbm, dy, sems.at[1])
+    sum_copy = pltpu.make_async_copy(sum_hbm, total, sems.at[2])
+    up_copies, down_copies = block_copies(pieces, ranges, gu, down, 0, sems.at[pl.ds(3, 2 * len(ranges))])
+    for copy in [x_copy] + up_copies + [dy_copy] + down_copies + [sum_copy]:
         copy.start()
-    for copy in x_copies:
-        copy.wait()
-    terms = hidden_grads(x, dy, gu, down, grads, [up_copies], [down_copies + dy_copies]) + term_ref[...]
+    x_copy.wait()
+    terms = hidden_grads(x, dy, gu, down, grads, [up_copies], [down_copies + [dy_copy]]) + term_ref[...]
     terms = jnp.broadcast_to(jnp.sum(terms, axis=1, keepdims=True), (slots, TERM_LANES))
     out_ref[:, 4 * part :] = terms.astype(BF)
     sum_copy.wait()
@@ -428,7 +423,7 @@
     return pl.pallas_call(
         functools.partial(last_kernel, ranges),
         out_shape=jax.ShapeDtypeStruct((rows, width + TERM_LANES), BF),
-        in_specs=[any_spec] * (len(x) + len(dy) + len(pieces) + 1) + [vmem_spec],
+        in_specs=[any_spec] * (len(pieces) + 3) + [vmem_spec],
         out_specs=vmem_spec,
         scratch_shapes=[
             pltpu.VMEM((rows, width), BF),
@@ -437,12 +432,12 @@
             pltpu.VMEM((PARTS - UP_PARTS, hidden, span), BF),
             pltpu.VMEM((rows, width), BF),
             pltpu.VMEM((rows, span), BF),
-            pltpu.SemaphoreType.DMA((2 * COLUMN_PIECES + 1 + 2 * len(pieces),)),
+            pltpu.SemaphoreType.DMA((3 + 2 * len(pieces),)),
         ],
         compiler_params=pltpu.CompilerParams(vmem_limit_bytes=LAST_VMEM),
         cost_estimate=pl.CostEstimate(flops=LAST_FLOPS, bytes_accessed=LAST_FLOPS, transcendentals=0),
         name="last",
-    )(*x, *dy, *pieces, total, term)
+    )(x, dy, *pieces, total, term)
 
 
 def add_pack_kernel(a_ref, b_ref, out_ref):
@@ -545,26 +540,23 @@
     ).reshape(experts * ROWS, -1)
 
     far_up, far_down = far_parts(from_up, from_down, ((0, 0, HALF - HEAD), (1, HALF, PARTS - HEAD)))
-    got, far_up, far_down, far_head, far_tail = lax.optimization_barrier(
-        (got, far_up, far_down, far_head, far_tail)
-    )
+    got, far_up, far_down = lax.optimization_barrier((got, far_up, far_down))
     far_up = lax.ppermute(far_up, "tensor", up)
     far_down = lax.ppermute(far_down, "tensor", down)
-    rows = list(unpack(got))
-    other_rows = [lax.ppermute(piece, "dp", swap) for piece in rows]
+    x, dy, far_head, far_tail = lax.optimization_barrier((*unpack(got), far_head, far_tail))
+    x_other, dy_other = (lax.ppermute(rows, "dp", swap) for rows in (x, dy))
+
     part = width // UP_PARTS
     squares = lambda piece: piece.reshape(-1, part, 2 * part)
     blocks = [list(map(squares, b)) for b in ((head, up_rest), (up_head, from_up), (from_down, down_tail))]
     ranges = ((ENDS[0], RESTS[0]),) * 2 + ((RESTS[1], ENDS[1]),)
     far = (far_head, far_up, far_down, far_tail)
     far_ranges = (ENDS[0], (HEAD, HALF), (HALF, PARTS - HEAD), ENDS[1])
-    cut = lambda r: (r[:COLUMN_PIECES], r[COLUMN_PIECES:])
-    own_total, own_gate_term = first_blocks(*cut(rows), blocks, ranges)
-    own_total, *other_rows = lax.optimization_barrier((own_total, *other_rows))
-    total, term = first_blocks(*cut(other_rows), blocks, ranges)
+    own_sums, other_sums, own_terms, other_terms = first_blocks((x, x_other, dy, dy_other), blocks, ranges)
     far = list(map(squares, far))
-    other_sums = lax.ppermute(last_block(*cut(other_rows), far, far_ranges, total, term), "dp", swap)
-    own_sums = last_block(*cut(rows), far, far_ranges, own_total, own_gate_term)
+    other_sums = last_block(x_other, dy_other, far, far_ranges, other_sums, other_terms)
+    other_sums = lax.ppermute(other_sums, "dp", swap)
+    own_sums = last_block(x, dy, far, far_ranges, own_sums, own_terms)
     back = add_pack(own_sums, other_sums).reshape(experts, ROWS, -1)
     ret = lax.all_to_all(back, "expert", split_axis=0, concat_axis=0, tiled=True)
     own_term = jnp.sum(out_grad.astype(F32) * tokens.astype(F32), axis=1)

time: 232 us -> 221 us (0.953)
  local copies, waits for them, and re-layouts: 9.73 us -> 0.03 us
  waiting for transfers between devices: 129 us -> 136 us
  Pallas kernels: 56.4 us -> 50.4 us
    all_to_all x1, waiting for transfers between devices: 0.01 us -> 18 us  [per_device(): lax.all_to_all(packed.reshape(experts, ROWS, -1), 'expert', split_axis=0,...]
    ppermute x1, waiting for transfers between devices: 14.7 us -> 0.01 us  [per_device(): far_head = lax.ppermute(up_head, 'tensor', up)]
    unnamed x34 -> x14, local copies, waits for them, and re-layouts: 9.73 us -> 0.03 us
    ppermute x3, waiting for transfers between devices: 0.01 us -> 4.24 us  [the longest x2 4.24 us: per_device(): x_other, dy_other = (lax.ppermute(rows, 'dp', swap) for rows in (x, dy))]
    pallas_call x2 -> x1, Pallas kernels: 22.3 us -> 18.2 us  [first_blocks(): pl.pallas_call(functools.partial(first_kernel, ranges), out_shape=[jax.Sh...]
  transfers between devices with their start and end apart: 13 -> 13, of which waited for: 4 -> 6; matrix products, arithmetic and copies ran while one was open for 1% -> 1% of each run, Pallas kernels for 16% -> 16%
where the time goes in v8:
time: 221 us
  waiting for transfers between devices  136 us (62%)
  Pallas kernels  50.4 us (23%)
  starting transfers between devices  31.6 us (14%)
    ppermute x1, waiting for transfers between devices, per_device(): up_head = lax.ppermute(head, 'tensor', up)  66.3 us
    all_to_all x1, waiting for transfers between devices, per_device(): lax.all_to_all(back, 'expert', split_axis=0, concat_axis=0, tiled=True)  47.3 us
    pallas_call x1, Pallas kernels, first_blocks(): pl.pallas_call(functools.partial(first_kernel, ranges), out_shape=[jax.Sh...  18.2 us
    all_to_all x1, waiting for transfers between devices, per_device(): lax.all_to_all(packed.reshape(experts, ROWS, -1), 'expert', split_axis=0,...  18 us
    all_to_all x1, starting transfers between devices, per_device(): lax.all_to_all(packed.reshape(experts, ROWS, -1), 'expert', split_axis=0,...  11.6 us
    all_to_all x1, starting transfers between devices, per_device(): lax.all_to_all(back, 'expert', split_axis=0, concat_axis=0, tiled=True)  10.9 us
    pallas_call x2, Pallas kernels, last_block(): pl.pallas_call(functools.partial(last_kernel, ranges), out_shape=jax.Shap...  9.98 us
    pallas_call x1, Pallas kernels, weight_parts(): pl.pallas_call(weights_kernel, out_shape=[size(parts) for parts in (ENDS[...  5.65 us
  transfers between devices with their start and end apart: 13, of which 6 were waited for; matrix products, arithmetic and copies ran while one was open for 1% of the time, Pallas kernels for 16%

profile of v8, /device:TPU:24, one launch (start us, length us, event | category | flops | bytes accessed | tf_op | source)
XLA Modules:
  0.0 220.9 jit_solution(8723776922866447659)
XLA Ops:
  0.6 5.7 %weights.1 = (bf16[2048,256]{1,0:T(8,128)(2,1)}, bf16[5632,256]{1,0:T(8,128)(2,1)}, bf16[5632,256]{1,0:T(8,128)(2,1)}, bf16[2048,256]{1,0:T(8,128)(2,1)}) custom-call(s32[1]{0:T(128)} %bitcast.1.core_ref, bf16[5120,256]{1,0:T(8,128)(2,1)} %bitcast.38, bf16[5120,256]{1,0:T(8,128)(2,1)} %bitcast.39, bf16[256,5120]{1,0:T(8,128)(2,1)} %bitcast.40), custom_call_target="tpu_custom_call" | custom-call | bytes 11796480 | tf_op jit(solution)/shard_map/weights/pallas_call | solution.py:175
  6.3 2.0 collective-permute-start
  8.3 0.1 collective-permute-start.1
  8.4 5.0 %pack.1 = bf16[256,7680]{1,0:T(8,128)(2,1)} custom-call(s32[1,128]{1,0:T(1,128)} %bitcast.33, bf16[128,5120]{1,0:T(8,128)(2,1)} %x_hbm.1, bf16[128,5120]{1,0:T(8,128)(2,1)} %out_grad_ref.1), custom_call_target="tpu_custom_call" | custom-call | flops 1006632960 | bytes 6553600 | tf_op jit(solution)/shard_map/pack/pallas_call | solution.py:105
  13.4 0.0 copy-start.1
  13.4 0.0 copy-start.4
  13.4 11.6 %all-to-all-start = ((bf16[32,8,7680]{2,1,0:T(8,128)(2,1)}), bf16[32,8,7680]{2,1,0:T(8,128)(2,1)}, u32[]{:S(2)}, u32[]{:S(2)}) async-start(bf16[32,8,7680]{2,1,0:T(8,128)(2,1)} %bitcast.36), calls=%async_computation | async-start | bytes 7864320 | tf_op jit(solution)/shard_map/all_to_all | solution.py:538
  25.0 0.0 copy-done.1
  25.0 1.5 collective-permute-start.2
  26.5 0.0 copy-done.4
  26.5 0.6 collective-permute-start.4
  27.1 66.3 %collective-permute-done.2 = bf16[2048,256]{1,0:T(8,128)(2,1)} collective-permute-done((bf16[2048,256]{1,0:T(8,128)(2,1)S(1)}, bf16[2048,256]{1,0:T(8,128)(2,1)}, u32[]{:S(2)}, u32[]{:S(2)}) %collective-permute-start.2) | collective-permute-done | bytes 1048608 | tf_op jit(solution)/shard_map/ppermute | solution.py:529
  93.4 1.5 collective-permute-start.3
  94.9 0.0 collective-permute-done.4
  94.9 0.5 collective-permute-start.5
  95.4 0.0 collective-permute-done.up_hbm
  95.4 0.0 collective-permute-done.1.down_hbm
  95.4 2.5 %far.1 = (bf16[1792,256]{1,0:T(8,128)(2,1)}, bf16[1792,256]{1,0:T(8,128)(2,1)}) custom-call(bf16[5632,256]{1,0:T(8,128)(2,1)} %collective-permute-done.up_hbm, bf16[5632,256]{1,0:T(8,128)(2,1)} %collective-permute-done.1.down_hbm), custom_call_target="tpu_custom_call" | custom-call | flops 62000001024 | tf_op jit(solution)/shard_map/far/pallas_call | solution.py:213
  97.9 18.0 %all-to-all-done = bf16[32,8,7680]{2,1,0:T(8,128)(2,1)} async-done(((bf16[32,8,7680]{2,1,0:T(8,128)(2,1)}), bf16[32,8,7680]{2,1,0:T(8,128)(2,1)}, u32[]{:S(2)}, u32[]{:S(2)}) %all-to-all-start) | async-done | bytes 3932192 | tf_op jit(solution)/shard_map/all_to_all | solution.py:538
  115.9 0.0 copy-start.6
  115.9 0.0 copy-start.5
  115.9 4.4 %unpack.1 = (bf16[192,5120]{1,0:T(8,128)(2,1)S(1)}, bf16[192,5120]{1,0:T(8,128)(2,1)S(1)}) custom-call(bf16[256,7680]{1,0:T(8,128)(2,1)} %bitcast.8.rows_hbm), custom_call_target="tpu_custom_call" | custom-call | flops 1000 | bytes 1000 | tf_op jit(solution)/shard_map/unpack/pallas_call | solution.py:322
  120.3 0.0 collective-permute-done.3
  120.4 0.0 collective-permute-done.5
  120.4 0.1 collective-permute-start.8
  120.5 0.5 collective-permute-start.9
  121.0 0.0 copy-done.6
  121.0 1.5 collective-permute-start.6
  122.5 0.0 copy-done.5
  122.5 0.5 collective-permute-start.7
  123.0 1.4 collective-permute-done.8.refs_1_.refs_0_
  124.4 2.8 %collective-permute-done.9.refs_3_.refs_1_ = bf16[192,5120]{1,0:T(8,128)(2,1)S(1)} collective-permute-done((bf16[192,5120]{1,0:T(8,128)(2,1)S(1)}, bf16[192,5120]{1,0:T(8,128)(2,1)S(1)}, u32[]{:S(2)}, u32[]{:S(2)}) %collective-permute-start.9) | collective-permute-done | bytes 1966112 | tf_op jit(solution)/shard_map/ppermute | solution.py:547
  127.2 18.2 %first.1 = (bf16[192,5120]{1,0:T(8,128)(2,1)S(1)}, bf16[192,5120]{1,0:T(8,128)(2,1)S(1)}, f32[192,128]{1,0:T(8,128)S(1)}, f32[192,128]{1,0:T(8,128)S(1)}) custom-call(bf16[192,5120]{1,0:T(8,128)(2,1)S(1)} %get-tuple-element.35.refs_0_, bf16[192,5120]{1,0:T(8,128)(2,1)S(1)} %collective-permute-done.8.refs_1_.refs_0_, ...), custom_call_target="tpu_custom_call" | custom-call | flops 1000 | bytes 1000 | tf_op jit(solution)/shard_map/first/pallas_call | solution.py:377
  145.4 0.0 collective-permute-done.6
  145.4 0.3 collective-permute-done.7
  145.8 5.0 %last.3 = bf16[192,5248]{1,0:T(8,128)(2,1)S(1)} custom-call(bf16[192,5120]{1,0:T(8,128)(2,1)S(1)} %collective-permute-done.8.refs_1_.refs_0_, bf16[192,5120]{1,0:T(8,128)(2,1)S(1)} %collective-permute-done.9.refs_3_.refs_1_, bf16[16,128,256]{2,1,0:T(8,128)(2,1)S(1)} %bitcast.23, bf16[14,128,256]{2,1,0:T(8,128)(2,1)S(1)} %bitcast.27, ...), custom_call_target="tpu_custom_call" | custom-call | flops 1000 | bytes 1000 | tf_op jit(solution)/shard_map/last/pallas_call | solution.py:423
  150.8 0.3 collective-permute-start.10
  151.1 5.0 %last.2.a_ref = bf16[192,5248]{1,0:T(8,128)(2,1)S(1)} custom-call(bf16[192,5120]{1,0:T(8,128)(2,1)S(1)} %get-tuple-element.35.refs_0_, bf16[192,5120]{1,0:T(8,128)(2,1)S(1)} %get-tuple-element.36.refs_2_.refs_1_, bf16[16,128,256]{2,1,0:T(8,128)(2,1)S(1)} %bitcast.24, bf16[14,128,256]{2,1,0:T(8,128)(2,1)S(1)} %bitcast.28, bf16[14,128,256]{2,1,0:T(8,128)(2,1)S(1)} %bitcast.30, ...), custom_call_target="tpu_custom_call" | custom-call | flops 1000 | bytes 1000 | tf_op jit(solution)/shard_map/last/pallas_call | solution.py:423
  156.1 0.0 collective-permute-done.10.b_ref
  156.1 2.6 %add_pack.1 = bf16[256,3968]{1,0:T(8,128)(2,1)} custom-call(bf16[192,5248]{1,0:T(8,128)(2,1)S(1)} %last.2.a_ref, bf16[192,5248]{1,0:T(8,128)(2,1)S(1)} %collective-permute-done.10.b_ref), custom_call_target="tpu_custom_call" | custom-call | flops 754974720 | bytes 6045696 | tf_op jit(solution)/shard_map/add_pack/pallas_call | solution.py:464
  158.7 0.0 copy-start
  158.7 10.9 %all-to-all-start.1 = ((bf16[32,8,3968]{2,1,0:T(8,128)(2,1)}), bf16[32,8,3968]{2,1,0:T(8,128)(2,1)S(1)}, u32[]{:S(2)}, u32[]{:S(2)}) async-start(bf16[32,8,3968]{2,1,0:T(8,128)(2,1)} %bitcast.19), calls=%async_computation.1 | async-start | bytes 4063232 | tf_op jit(solution)/shard_map/all_to_all | solution.py:561
  169.6 0.0 copy-done
  169.7 0.0 copy-start.2
  169.7 0.0 copy-start.3
  169.7 1.8 multiply_reduce_fusion
  171.4 47.3 %all-to-all-done.1 = bf16[32,8,3968]{2,1,0:T(8,128)(2,1)S(1)} async-done(((bf16[32,8,3968]{2,1,0:T(8,128)(2,1)}), bf16[32,8,3968]{2,1,0:T(8,128)(2,1)S(1)}, u32[]{:S(2)}, u32[]{:S(2)}) %all-to-all-start.1) | async-done | bytes 2031648 | tf_op jit(solution)/shard_map/all_to_all | solution.py:561
  218.8 0.0 copy-done.2
  218.8 0.0 copy-done.3
  218.8 2.1 combine.1
Async XLA Ops:
  6.3 89.1 %collective-permute-start = (bf16[5632,256]{1,0:T(8,128)(2,1)}, bf16[5632,256]{1,0:T(8,128)(2,1)}, u32[]{:S(2)}, u32[]{:S(2)}) collective-permute-start(bf16[5632,256]{1,0:T(8,128)(2,1)} %get-tuple-element.27), channel_id=1, source_target_pairs={{0,2},{2,4},{4,6},{6,0},{1,3},{3,5},{5,7},{7,1},{8,10},{10,12},{12... | collective-permute-start | bytes 8650760 | tf_op jit(solution)/shard_map/ppermute | solution.py:531
  8.3 87.1 %collective-permute-start.1 = (bf16[5632,256]{1,0:T(8,128)(2,1)}, bf16[5632,256]{1,0:T(8,128)(2,1)}, u32[]{:S(2)}, u32[]{:S(2)}) collective-permute-start(bf16[5632,256]{1,0:T(8,128)(2,1)} %get-tuple-element.28), channel_id=1, source_target_pairs={{0,6},{2,0},{4,2},{6,4},{1,7},{3,1},{5,3},{7,5},{8,14},{10,8},{12,... | collective-permute-start | bytes 8650760 | tf_op jit(solution)/shard_map/ppermute | solution.py:532
  13.4 11.6 %copy-start.1 = (bf16[2048,256]{1,0:T(8,128)(2,1)S(1)}, bf16[2048,256]{1,0:T(8,128)(2,1)}, u32[]{:S(2)}) copy-start(bf16[2048,256]{1,0:T(8,128)(2,1)} %get-tuple-element.41) | copy-start | bytes 3145732
  13.4 13.1 %copy-start.4 = (bf16[2048,256]{1,0:T(8,128)(2,1)S(1)}, bf16[2048,256]{1,0:T(8,128)(2,1)}, u32[]{:S(2)}) copy-start(bf16[2048,256]{1,0:T(8,128)(2,1)} %get-tuple-element.34) | copy-start | bytes 3145732
  13.4 102.5 %all-to-all-start = ((bf16[32,8,7680]{2,1,0:T(8,128)(2,1)}), bf16[32,8,7680]{2,1,0:T(8,128)(2,1)}, u32[]{:S(2)}, u32[]{:S(2)}) async-start(bf16[32,8,7680]{2,1,0:T(8,128)(2,1)} %bitcast.36), calls=%async_computation | async-start | bytes 7864320 | tf_op jit(solution)/shard_map/all_to_all | solution.py:538
  25.0 68.4 %collective-permute-start.2 = (bf16[2048,256]{1,0:T(8,128)(2,1)S(1)}, bf16[2048,256]{1,0:T(8,128)(2,1)}, u32[]{:S(2)}, u32[]{:S(2)}) collective-permute-start(bf16[2048,256]{1,0:T(8,128)(2,1)S(1)} %copy-done.1), channel_id=1, source_target_pairs={{0,2},{2,4},{4,6},{6,0},{1,3},{3,5},{5,7},{7,1},{8,10},{10,12},{12... | collective-permute-start | bytes 3145736 | tf_op jit(solution)/shard_map/ppermute | solution.py:529
  26.5 68.4 %collective-permute-start.4 = (bf16[2048,256]{1,0:T(8,128)(2,1)S(1)}, bf16[2048,256]{1,0:T(8,128)(2,1)}, u32[]{:S(2)}, u32[]{:S(2)}) collective-permute-start(bf16[2048,256]{1,0:T(8,128)(2,1)S(1)} %copy-done.4), channel_id=1, source_target_pairs={{0,6},{2,0},{4,2},{6,4},{1,7},{3,1},{5,3},{7,5},{8,14},{10,8},{12,... | collective-permute-start | bytes 3145736 | tf_op jit(solution)/shard_map/ppermute | solution.py:530
  93.4 27.0 %collective-permute-start.3 = (bf16[2048,256]{1,0:T(8,128)(2,1)}, bf16[2048,256]{1,0:T(8,128)(2,1)S(1)}, u32[]{:S(2)}, u32[]{:S(2)}) collective-permute-start(bf16[2048,256]{1,0:T(8,128)(2,1)} %collective-permute-done.2), channel_id=1, source_target_pairs={{0,2},{2,4},{4,6},{6,0},{1,3},{3,5},{5,7},{7,1},{8,10},{10,12},{12... | collective-permute-start | bytes 3145736 | tf_op jit(solution)/shard_map/ppermute | solution.py:533
  94.9 25.5 %collective-permute-start.5 = (bf16[2048,256]{1,0:T(8,128)(2,1)}, bf16[2048,256]{1,0:T(8,128)(2,1)S(1)}, u32[]{:S(2)}, u32[]{:S(2)}) collective-permute-start(bf16[2048,256]{1,0:T(8,128)(2,1)} %collective-permute-done.4), channel_id=1, source_target_pairs={{0,6},{2,0},{4,2},{6,4},{1,7},{3,1},{5,3},{7,5},{8,14},{10,8},{12,... | collective-permute-start | bytes 3145736 | tf_op jit(solution)/shard_map/ppermute | solution.py:534
  115.9 5.1 %copy-start.6 = (bf16[1792,256]{1,0:T(8,128)(2,1)S(1)}, bf16[1792,256]{1,0:T(8,128)(2,1)}, u32[]{:S(2)}) copy-start(bf16[1792,256]{1,0:T(8,128)(2,1)} %get-tuple-element.38) | copy-start | bytes 2752516
  115.9 6.6 %copy-start.5 = (bf16[1792,256]{1,0:T(8,128)(2,1)S(1)}, bf16[1792,256]{1,0:T(8,128)(2,1)}, u32[]{:S(2)}) copy-start(bf16[1792,256]{1,0:T(8,128)(2,1)} %get-tuple-element.39) | copy-start | bytes 2752516
  120.4 4.1 %collective-permute-start.8 = (bf16[192,5120]{1,0:T(8,128)(2,1)S(1)}, bf16[192,5120]{1,0:T(8,128)(2,1)S(1)}, u32[]{:S(2)}, u32[]{:S(2)}) collective-permute-start(bf16[192,5120]{1,0:T(8,128)(2,1)S(1)} %get-tuple-element.35.refs_0_), channel_id=1, source_target_pairs={{0,1},{1,0},{2,3},{3,2},{4,5},{5,4},{6,7},{7,6},{8,9},{9,8},{10,11... | collective-permute-start | bytes 5898248 | tf_op jit(solution)/shard_map/ppermute | solution.py:547
  120.5 6.8 %collective-permute-start.9 = (bf16[192,5120]{1,0:T(8,128)(2,1)S(1)}, bf16[192,5120]{1,0:T(8,128)(2,1)S(1)}, u32[]{:S(2)}, u32[]{:S(2)}) collective-permute-start(bf16[192,5120]{1,0:T(8,128)(2,1)S(1)} %get-tuple-element.36.refs_2_.refs_1_), channel_id=1, source_target_pairs={{0,1},{1,0},{2,3},{3,2},{4,5},{5,4},{6,7},{7,6},{8,9},{9,8},{10,11... | collective-permute-start | bytes 5898248 | tf_op jit(solution)/shard_map/ppermute | solution.py:547
  121.0 24.5 %collective-permute-start.6 = (bf16[1792,256]{1,0:T(8,128)(2,1)S(1)}, bf16[1792,256]{1,0:T(8,128)(2,1)S(1)}, u32[]{:S(2)}, u32[]{:S(2)}) collective-permute-start(bf16[1792,256]{1,0:T(8,128)(2,1)S(1)} %copy-done.6), channel_id=1, source_target_pairs={{0,2},{2,4},{4,6},{6,0},{1,3},{3,5},{5,7},{7,1},{8,10},{10,12},{12... | collective-permute-start | bytes 2752520 | tf_op jit(solution)/shard_map/ppermute | solution.py:544
  122.5 23.3 %collective-permute-start.7 = (bf16[1792,256]{1,0:T(8,128)(2,1)S(1)}, bf16[1792,256]{1,0:T(8,128)(2,1)S(1)}, u32[]{:S(2)}, u32[]{:S(2)}) collective-permute-start(bf16[1792,256]{1,0:T(8,128)(2,1)S(1)} %copy-done.5), channel_id=1, source_target_pairs={{0,6},{2,0},{4,2},{6,4},{1,7},{3,1},{5,3},{7,5},{8,14},{10,8},{12,... | collective-permute-start | bytes 2752520 | tf_op jit(solution)/shard_map/ppermute | solution.py:545
  150.8 5.3 %collective-permute-start.10 = (bf16[192,5248]{1,0:T(8,128)(2,1)S(1)}, bf16[192,5248]{1,0:T(8,128)(2,1)S(1)}, u32[]{:S(2)}, u32[]{:S(2)}) collective-permute-start(bf16[192,5248]{1,0:T(8,128)(2,1)S(1)} %last.3), channel_id=1, source_target_pairs={{0,1},{1,0},{2,3},{3,2},{4,5},{5,4},{6,7},{7,6},{8,9},{9,8},{10,11... | collective-permute-start | bytes 6045704 | tf_op jit(solution)/shard_map/ppermute | solution.py:558
  158.7 10.9 %copy-start = (bf16[128,5120]{1,0:T(8,128)(2,1)S(1)}, bf16[128,5120]{1,0:T(8,128)(2,1)}, u32[]{:S(2)}) copy-start(bf16[128,5120]{1,0:T(8,128)(2,1)} %out_grad_ref.1) | copy-start | bytes 3932164
  158.7 60.0 %all-to-all-start.1 = ((bf16[32,8,3968]{2,1,0:T(8,128)(2,1)}), bf16[32,8,3968]{2,1,0:T(8,128)(2,1)S(1)}, u32[]{:S(2)}, u32[]{:S(2)}) async-start(bf16[32,8,3968]{2,1,0:T(8,128)(2,1)} %bitcast.19), calls=%async_computation.1 | async-start | bytes 4063232 | tf_op jit(solution)/shard_map/all_to_all | solution.py:561
  169.7 49.1 %copy-start.2 = (s32[128,1]{0,1:T(1,128)S(1)}, s32[128,1]{0,1:T(1,128)}, u32[]{:S(2)}) copy-start(s32[128,1]{0,1:T(1,128)} %param.10) | copy-start | bytes 1540
  169.7 49.1 %copy-start.3 = (f32[128]{0:T(128)S(1)}, f32[128]{0:T(128)}, u32[]{:S(2)}) copy-start(f32[128]{0:T(128)} %param.9) | copy-start | bytes 1540

commit v9 on v8

--- a/solution.py
+++ b/solution.py
@@ -15,7 +15,7 @@
 PARTS = 60
 UP_PARTS = 40
 HALF = 30
-HEAD = 16
+HEAD = 18
 ENDS = ((0, HEAD), (PARTS - HEAD, PARTS))
 RESTS = ((HEAD, PARTS), (0, PARTS - HEAD))
 MIDDLE = (PARTS - 2 * HEAD) // 3
@@ -35,6 +35,15 @@
 
 def dot_t(a, b):
     return lax.dot_general(a, b, (((1,), (1,)), ((), ())), preferred_element_type=F32)
+
+
+def in_turn(steps):
+    def body(i, carry):
+        for k, step in enumerate(steps):
+            pl.when(i == k)(step)
+        return carry
+
+    lax.fori_loop(0, len(steps), body, 0)
 
 
 def eye(n):
@@ -123,7 +132,7 @@
     )(route_row, x, dy)
 
 
-def part_copies(weights, core, low, high, out, sems):
+def part_copies(weights, core, low, high, out, sem):
     gate, up, down = weights
     hidden, span = out.shape[0] // (high - low), out.shape[1]
     columns = pl.ds(pl.multiple_of(core * hidden, hidden), hidden)
@@ -133,35 +142,38 @@
         rows = slice(low * hidden, last_up * hidden)
         for i, ref in enumerate((gate, up)):
             dst = out.at[0 : (last_up - low) * hidden, i * hidden : (i + 1) * hidden]
-            copies.append(pltpu.make_async_copy(ref.at[rows, columns], dst, sems.at[len(copies)]))
+            copies.append(pltpu.make_async_copy(ref.at[rows, columns], dst, sem))
     for k in range(max(low, UP_PARTS), high):
         src = down.at[columns, (k - UP_PARTS) * span : (k - UP_PARTS + 1) * span]
         dst = out.at[(k - low) * hidden : (k - low + 1) * hidden, :]
-        copies.append(pltpu.make_async_copy(src, dst, sems.at[len(copies)]))
+        copies.append(pltpu.make_async_copy(src, dst, sem))
     return copies
 
 
 def weights_kernel(core_ref, gate, up, down, head, up_rest, down_rest, tail, held, read_sems, write_sems):
     hidden = held.shape[1] // 2
-    reads, writes = [], []
+    reads, waits, writes = [], [], []
     outs = ((head, ENDS[0]), (tail, ENDS[1]), (up_rest, RESTS[0]), (down_rest, RESTS[1]))
-    for low, high in zip(WEIGHT_CUTS, WEIGHT_CUTS[1:]):
+    count = 0
+    for i, (low, high) in enumerate(zip(WEIGHT_CUTS, WEIGHT_CUTS[1:])):
         rows = held.at[pl.ds(low * hidden, (high - low) * hidden)]
-        sems = read_sems.at[pl.ds(2 * low, 2 * (high - low))]
-        reads.append(part_copies((gate, up, down), core_ref[0], low, high, rows, sems))
+        reads += part_copies((gate, up, down), core_ref[0], low, high, rows, read_sems.at[i])
+        waits.append(pltpu.make_async_copy(rows, rows, read_sems.at[i]))
         writes.append([])
-        for i, (out, (first, last)) in enumerate(outs):
+        for out, (first, last) in outs:
             if first <= low and high <= last:
                 dst = out.at[pl.ds((low - first) * hidden, (high - low) * hidden)]
-                writes[-1].append(pltpu.make_async_copy(rows, dst, write_sems.at[4 * len(writes) + i - 4]))
-    for copies in reads:
-        for copy in copies:
+                writes[-1].append(pltpu.make_async_copy(rows, dst, write_sems.at[count]))
+                count += 1
+    for copy in reads:
+        copy.start()
+
+    def step(i):
+        waits[i].wait()
+        for copy in writes[i]:
             copy.start()
-    for copies, ready in zip(reads, writes):
-        for copy in copies:
-            copy.wait()
-        for copy in ready:
-            copy.start()
+
+    in_turn([functools.partial(step, i) for i in range(len(waits))])
     for copies in writes:
         for copy in copies:
             copy.wait()
@@ -179,8 +191,8 @@
         out_specs=[any_spec] * 4,
         scratch_shapes=[
             pltpu.VMEM((PARTS * hidden, span), BF),
-            pltpu.SemaphoreType.DMA((2 * PARTS,)),
-            pltpu.SemaphoreType.DMA((4 * len(WEIGHT_CUTS),)),
+            pltpu.SemaphoreType.DMA((len(WEIGHT_CUTS) - 1,)),
+            pltpu.SemaphoreType.DMA((2 * len(WEIGHT_CUTS),)),
         ],
         compiler_params=pltpu.CompilerParams(vmem_limit_bytes=VMEM_ALL),
         cost_estimate=pl.CostEstimate(flops=0, bytes_accessed=6 * PARTS * hidden * span, transcendentals=0),
@@ -259,35 +271,49 @@
     return jnp.where(hit, 1.0, 0.0).astype(BF)
 
 
-def hidden_grads(x, dy, gu, down, grads, up_copies, down_copies):
+def hidden_grads(x, dy, gu, down, pre, grads, x_copies, up_copies, dy_copies, down_copies):
     spans, total, span = down.shape
     blocks = len(up_copies)
     hidden = total // blocks
     width = x.shape[1]
-    pres = []
-    for b in range(blocks):
-        for copy in up_copies[b]:
+    stages = [x_copies + up_copies[0]] + up_copies[1:] + [dy_copies + [c for copies in down_copies for c in copies]]
+
+    def start(i):
+        for copy in stages[i] if i < len(stages) else []:
+            copy.start()
+
+    def wait(i):
+        for copy in stages[i]:
             copy.wait()
-        pres.append(dot(x[...], gu[:, :, b * span : (b + 1) * span].reshape(width, span)))
-    for copies in down_copies:
-        for copy in copies:
-            copy.wait()
-    back = dot_t(dy[:, :span], down[0])
-    for k in range(1, spans):
-        back += dot_t(dy[:, k * span : (k + 1) * span], down[k])
-    terms = None
-    for b in range(blocks):
-        pre_gate, pre_up = pres[b][:, :hidden], pres[b][:, hidden:]
-        here = back[:, b * hidden : (b + 1) * hidden]
-        s = jax.nn.sigmoid(pre_gate)
-        activated = pre_gate * s
-        slope = s * (1.0 + pre_gate * (1.0 - s))
-        low = b * span
-        grads[:, low : low + hidden] = (here * pre_up * slope).astype(BF)
-        grads[:, low + hidden : low + span] = (here * activated).astype(BF)
-        term = activated * pre_up * here
-        terms = term if terms is None else terms + term
-    return terms
+
+    def forward(b):
+        wait(b)
+        start(b + 2)
+        cols = slice(b * span, (b + 1) * span)
+        pre[:, cols] = dot(x[...], gu[:, :, cols].reshape(width, span))
+
+    def finish():
+        wait(blocks)
+        back = dot_t(dy[:, :span], down[0])
+        for k in range(1, spans):
+            back += dot_t(dy[:, k * span : (k + 1) * span], down[k])
+        terms = None
+        for b in range(blocks):
+            low = b * span
+            pre_gate, pre_up = pre[:, low : low + hidden], pre[:, low + hidden : low + span]
+            here = back[:, b * hidden : (b + 1) * hidden]
+            s = jax.nn.sigmoid(pre_gate)
+            activated = pre_gate * s
+            slope = s * (1.0 + pre_gate * (1.0 - s))
+            grads[:, low : low + hidden] = (here * pre_up * slope).astype(BF)
+            grads[:, low + hidden : low + span] = (here * activated).astype(BF)
+            term = activated * pre_up * here
+            terms = term if terms is None else terms + term
+        pre[:, :hidden] = terms
+
+    start(0)
+    start(1)
+    return [functools.partial(forward, b) for b in range(blocks)] + [finish]
 
 
 def row_grads(grads, gu, j):
@@ -305,14 +331,15 @@
     for copy in copies:
         copy.start()
     spread = slot_matrix(slots, packed, 0, None)
-    both = [jnp.concatenate([spread, slot_matrix(slots, packed, 0, j)], axis=0) for j in range(3)]
+    spread_tail = [slot_matrix(slots, packed, 0, j) for j in range(3)]
     for k, out_ref in enumerate((x_ref, dy_ref)):
         last = None
         for j in range(3):
             copies[3 * k + j].wait()
-            pieces = dot(both[j], rows[:, cols[3 * k + j]])
-            out_ref[:, cols[j]] = pieces[:slots].astype(BF)
-            last = pieces[slots:] if last is None else last + pieces[slots:]
+            piece = rows[:, cols[3 * k + j]]
+            out_ref[:, cols[j]] = dot(spread, piece).astype(BF)
+            more = dot(spread_tail[j], piece)
+            last = more if last is None else last + more
         out_ref[:, cols[3]] = last.astype(BF)
 
 
@@ -333,7 +360,7 @@
 def first_kernel(ranges, *refs):
     row_refs, refs = refs[:4], refs[4:]
     pieces, refs = refs[: sum(map(len, ranges))], refs[sum(map(len, ranges)) :]
-    own_hbm, other_hbm, own_term, other_term, x, dy, gu, down, grads, total, sems = refs
+    own_hbm, other_hbm, own_term, other_term, x, dy, gu, down, pre, grads, total, sems = refs
     slots, part = x.shape[0] // 2, x.shape[1] // 4
     row_copies = [
         pltpu.make_async_copy(src, full.at[pl.ds(i * slots, slots)], sems.at[2 * k + i])
@@ -347,24 +374,28 @@
         used += len(block)
         up_copies.append(ups)
         down_copies.append(downs)
-    for copies in [row_copies[:2]] + up_copies + [row_copies[2:]] + down_copies:
+    steps = hidden_grads(x, dy, gu, down, pre, grads, row_copies[:2], up_copies, row_copies[2:], down_copies)
+    columns = [pl.ds(j * part, part) for j in range(4)]
+    outs = [
+        [
+            pltpu.make_async_copy(total.at[pl.ds(i * slots, slots), cols], out.at[:, cols], sems.at[4 + 2 * j + i])
+            for i, out in enumerate((own_hbm, other_hbm))
+        ]
+        for j, cols in enumerate(columns)
+    ]
+
+    def backward(j):
+        total[:, columns[j]] = row_grads(grads, gu, j).astype(BF)
+        for copy in outs[j]:
+            copy.start()
+
+    in_turn(steps + [functools.partial(backward, j) for j in range(4)])
+    hidden = own_term.shape[1]
+    own_term[...] = pre[:slots, :hidden]
+    other_term[...] = pre[slots:, :hidden]
+    for copies in outs:
         for copy in copies:
-            copy.start()
-    for copy in row_copies[:2]:
-        copy.wait()
-    terms = hidden_grads(x, dy, gu, down, grads, up_copies, down_copies + [row_copies[2:]])
-    own_term[...] = terms[:slots]
-    other_term[...] = terms[slots:]
-    outs = []
-    for j in range(4):
-        cols = pl.ds(j * part, part)
-        total[:, cols] = row_grads(grads, gu, j).astype(BF)
-        for i, out in enumerate((own_hbm, other_hbm)):
-            src = total.at[pl.ds(i * slots, slots), cols]
-            outs.append(pltpu.make_async_copy(src, out.at[:, cols], sems.at[4 + 2 * j + i]))
-            outs[-1].start()
-    for copy in outs:
-        copy.wait()
+            copy.wait()
 
 
 def first_blocks(rows, blocks, ranges):
@@ -384,6 +415,7 @@
             pltpu.VMEM((2 * slots, width), BF),
             pltpu.VMEM((UP_PARTS, hidden, count * span), BF),
             pltpu.VMEM((PARTS - UP_PARTS, count * hidden, span), BF),
+            pltpu.VMEM((2 * slots, count * span), F32),
             pltpu.VMEM((2 * slots, count * span), BF),
             pltpu.VMEM((2 * slots, width), BF),
             pltpu.SemaphoreType.DMA((12 + 2 * len(pieces),)),
@@ -397,22 +429,24 @@
 def last_kernel(ranges, *refs):
     x_hbm, dy_hbm, refs = refs[0], refs[1], refs[2:]
     pieces, refs = refs[: len(ranges)], refs[len(ranges) :]
-    sum_hbm, term_ref, out_ref, x, dy, gu, down, total, grads, sems = refs
+    sum_hbm, term_ref, out_ref, x, dy, gu, down, total, pre, grads, sems = refs
     slots, part = x.shape[0], x.shape[1] // 4
     x_copy = pltpu.make_async_copy(x_hbm, x, sems.at[0])
     dy_copy = pltpu.make_async_copy(dy_hbm, dy, sems.at[1])
     sum_copy = pltpu.make_async_copy(sum_hbm, total, sems.at[2])
     up_copies, down_copies = block_copies(pieces, ranges, gu, down, 0, sems.at[pl.ds(3, 2 * len(ranges))])
-    for copy in [x_copy] + up_copies + [dy_copy] + down_copies + [sum_copy]:
-        copy.start()
-    x_copy.wait()
-    terms = hidden_grads(x, dy, gu, down, grads, [up_copies], [down_copies + [dy_copy]]) + term_ref[...]
-    terms = jnp.broadcast_to(jnp.sum(terms, axis=1, keepdims=True), (slots, TERM_LANES))
-    out_ref[:, 4 * part :] = terms.astype(BF)
-    sum_copy.wait()
-    for j in range(4):
-        cols = slice(j * part, (j + 1) * part)
-        out_ref[:, cols] = (total[:, cols].astype(F32) + row_grads(grads, gu, j)).astype(BF)
+    steps = hidden_grads(
+        x, dy, gu, down, pre, grads, [x_copy], [up_copies], [dy_copy], [down_copies + [sum_copy]]
+    )
+
+    def backward():
+        for j in range(4):
+            cols = slice(j * part, (j + 1) * part)
+            out_ref[:, cols] = (total[:, cols].astype(F32) + row_grads(grads, gu, j)).astype(BF)
+        terms = jnp.sum(pre[:, : term_ref.shape[1]] + term_ref[...], axis=1, keepdims=True)
+        out_ref[:, 4 * part :] = jnp.broadcast_to(terms, (slots, TERM_LANES)).astype(BF)
+
+    in_turn(steps + [backward])
 
 
 def last_block(x, dy, pieces, ranges, total, term):
@@ -431,6 +465,7 @@
             pltpu.VMEM((UP_PARTS, hidden, span), BF),
             pltpu.VMEM((PARTS - UP_PARTS, hidden, span), BF),
             pltpu.VMEM((rows, width), BF),
+            pltpu.VMEM((rows, span), F32),
             pltpu.VMEM((rows, span), BF),
             pltpu.SemaphoreType.DMA((3 + 2 * len(pieces),)),
         ],

time: 221 us -> 218 us (0.986)
  Pallas kernels: 50.4 us -> 42.2 us
  waiting for transfers between devices: 136 us -> 140 us
    pallas_call x1, Pallas kernels: 18.2 us -> 13.3 us  [first_blocks(): pl.pallas_call(functools.partial(first_kernel, ranges), out_shape=[jax.Sh...]
  transfers between devices with their start and end apart: 13 -> 13, of which waited for: 6 -> 8; matrix products, arithmetic and copies ran while one was open for 1% -> 1% of each run, Pallas kernels for 16% -> 13%
where the time goes in v9:
time: 218 us
  waiting for transfers between devices  140 us (64%)
  Pallas kernels  42.2 us (19%)
  starting transfers between devices  33.4 us (15%)
    ppermute x1, waiting for transfers between devices, per_device(): up_head = lax.ppermute(head, 'tensor', up)  66.3 us
    all_to_all x1, waiting for transfers between devices, per_device(): lax.all_to_all(back, 'expert', split_axis=0, concat_axis=0, tiled=True)  47.4 us
    all_to_all x1, waiting for transfers between devices, per_device(): lax.all_to_all(packed.reshape(experts, ROWS, -1), 'expert', split_axis=0,...  18.2 us
    pallas_call x1, Pallas kernels, first_blocks(): pl.pallas_call(functools.partial(first_kernel, ranges), out_shape=[jax.Sh...  13.3 us
    all_to_all x1, starting transfers between devices, per_device(): lax.all_to_all(back, 'expert', split_axis=0, concat_axis=0, tiled=True)  12.7 us
    all_to_all x1, starting transfers between devices, per_device(): lax.all_to_all(packed.reshape(experts, ROWS, -1), 'expert', split_axis=0,...  11.6 us
    pallas_call x2, Pallas kernels, last_block(): pl.pallas_call(functools.partial(last_kernel, ranges), out_shape=jax.Shap...  8.6 us
    pallas_call x1, Pallas kernels, pack(): pl.pallas_call(pack_kernel, out_shape=jax.ShapeDtypeStruct(shape, BF), in...  5 us
  transfers between devices with their start and end apart: 13, of which 8 were waited for; matrix products, arithmetic and copies ran while one was open for 1% of the time, Pallas kernels for 13%

profile of v9, /device:TPU:24, one launch (start us, length us, event | category | flops | bytes accessed | tf_op | source)
XLA Modules:
  0.0 217.7 jit_solution(9207088661306508308)
XLA Ops:
  0.6 4.6 %weights.1 = (bf16[2304,256]{1,0:T(8,128)(2,1)}, bf16[5376,256]{1,0:T(8,128)(2,1)}, bf16[5376,256]{1,0:T(8,128)(2,1)}, bf16[2304,256]{1,0:T(8,128)(2,1)}) custom-call(s32[1]{0:T(128)} %bitcast.1.core_ref, bf16[5120,256]{1,0:T(8,128)(2,1)} %bitcast.38, bf16[5120,256]{1,0:T(8,128)(2,1)} %bitcast.39, bf16[256,5120]{1,0:T(8,128)(2,1)} %bitcast.40), custom_call_target="tpu_custom_call" | custom-call | bytes 11796480 | tf_op jit(solution)/shard_map/weights/pallas_call | solution.py:187
  5.2 2.0 collective-permute-start
  7.3 0.1 collective-permute-start.1
  7.3 5.0 %pack.1 = bf16[256,7680]{1,0:T(8,128)(2,1)} custom-call(s32[1,128]{1,0:T(1,128)} %bitcast.33, bf16[128,5120]{1,0:T(8,128)(2,1)} %x_hbm.1, bf16[128,5120]{1,0:T(8,128)(2,1)} %out_grad_ref.1), custom_call_target="tpu_custom_call" | custom-call | flops 1006632960 | bytes 6553600 | tf_op jit(solution)/shard_map/pack/pallas_call | solution.py:114
  12.3 0.0 copy-start.1
  12.3 0.0 copy-start.4
  12.4 11.6 %all-to-all-start = ((bf16[32,8,7680]{2,1,0:T(8,128)(2,1)}), bf16[32,8,7680]{2,1,0:T(8,128)(2,1)}, u32[]{:S(2)}, u32[]{:S(2)}) async-start(bf16[32,8,7680]{2,1,0:T(8,128)(2,1)} %bitcast.36), calls=%async_computation | async-start | bytes 7864320 | tf_op jit(solution)/shard_map/all_to_all | solution.py:573
  23.9 0.0 copy-done.1
  23.9 1.5 collective-permute-start.2
  25.5 0.0 copy-done.4
  25.5 0.6 collective-permute-start.4
  26.0 66.3 %collective-permute-done.2 = bf16[2304,256]{1,0:T(8,128)(2,1)} collective-permute-done((bf16[2304,256]{1,0:T(8,128)(2,1)S(1)}, bf16[2304,256]{1,0:T(8,128)(2,1)}, u32[]{:S(2)}, u32[]{:S(2)}) %collective-permute-start.2) | collective-permute-done | bytes 1179680 | tf_op jit(solution)/shard_map/ppermute | solution.py:564
  92.3 1.5 collective-permute-start.3
  93.8 0.0 collective-permute-done.4
  93.8 0.5 collective-permute-start.5
  94.3 0.0 collective-permute-done.up_hbm
  94.3 0.0 collective-permute-done.1.down_hbm
  94.3 2.3 %far.1 = (bf16[1536,256]{1,0:T(8,128)(2,1)}, bf16[1536,256]{1,0:T(8,128)(2,1)}) custom-call(bf16[5376,256]{1,0:T(8,128)(2,1)} %collective-permute-done.up_hbm, bf16[5376,256]{1,0:T(8,128)(2,1)} %collective-permute-done.1.down_hbm), custom_call_target="tpu_custom_call" | custom-call | flops 62000001024 | tf_op jit(solution)/shard_map/far/pallas_call | solution.py:225
  96.7 18.2 %all-to-all-done = bf16[32,8,7680]{2,1,0:T(8,128)(2,1)} async-done(((bf16[32,8,7680]{2,1,0:T(8,128)(2,1)}), bf16[32,8,7680]{2,1,0:T(8,128)(2,1)}, u32[]{:S(2)}, u32[]{:S(2)}) %all-to-all-start) | async-done | bytes 3932192 | tf_op jit(solution)/shard_map/all_to_all | solution.py:573
  114.8 0.0 copy-start.6
  114.8 0.0 copy-start.5
  114.9 3.7 %unpack.1 = (bf16[192,5120]{1,0:T(8,128)(2,1)S(1)}, bf16[192,5120]{1,0:T(8,128)(2,1)S(1)}) custom-call(bf16[256,7680]{1,0:T(8,128)(2,1)} %bitcast.8.rows_hbm), custom_call_target="tpu_custom_call" | custom-call | flops 1000 | bytes 1000 | tf_op jit(solution)/shard_map/unpack/pallas_call | solution.py:349
  118.5 0.8 collective-permute-done.3
  119.4 1.2 collective-permute-done.5
  120.6 0.0 collective-permute-start.8
  120.6 0.5 collective-permute-start.9
  121.1 0.0 copy-done.6
  121.1 0.3 collective-permute-start.6
  121.4 0.0 copy-done.5
  121.4 1.7 collective-permute-start.7
  123.1 1.4 collective-permute-done.8.refs_1_.refs_0_
  124.5 2.8 %collective-permute-done.9.refs_3_.refs_1_ = bf16[192,5120]{1,0:T(8,128)(2,1)S(1)} collective-permute-done((bf16[192,5120]{1,0:T(8,128)(2,1)S(1)}, bf16[192,5120]{1,0:T(8,128)(2,1)S(1)}, u32[]{:S(2)}, u32[]{:S(2)}) %collective-permute-start.9) | collective-permute-done | bytes 1966112 | tf_op jit(solution)/shard_map/ppermute | solution.py:582
  127.4 13.3 %first.1 = (bf16[192,5120]{1,0:T(8,128)(2,1)S(1)}, bf16[192,5120]{1,0:T(8,128)(2,1)S(1)}, f32[192,128]{1,0:T(8,128)S(1)}, f32[192,128]{1,0:T(8,128)S(1)}) custom-call(bf16[192,5120]{1,0:T(8,128)(2,1)S(1)} %get-tuple-element.35.refs_0_, bf16[192,5120]{1,0:T(8,128)(2,1)S(1)} %collective-permute-done.8.refs_1_.refs_0_, ...), custom_call_target="tpu_custom_call" | custom-call | flops 1000 | bytes 1000 | tf_op jit(solution)/shard_map/first/pallas_call | solution.py:408
  140.6 0.0 collective-permute-done.6
  140.7 1.4 collective-permute-done.7
  142.0 4.3 %last.3 = bf16[192,5248]{1,0:T(8,128)(2,1)S(1)} custom-call(bf16[192,5120]{1,0:T(8,128)(2,1)S(1)} %collective-permute-done.8.refs_1_.refs_0_, bf16[192,5120]{1,0:T(8,128)(2,1)S(1)} %collective-permute-done.9.refs_3_.refs_1_, bf16[18,128,256]{2,1,0:T(8,128)(2,1)S(1)} %bitcast.23, bf16[12,128,256]{2,1,0:T(8,128)(2,1)S(1)} %bitcast.27, ...), custom_call_target="tpu_custom_call" | custom-call | flops 1000 | bytes 1000 | tf_op jit(solution)/shard_map/last/pallas_call | solution.py:457
  146.3 0.3 collective-permute-start.10
  146.6 4.3 %last.2.a_ref = bf16[192,5248]{1,0:T(8,128)(2,1)S(1)} custom-call(bf16[192,5120]{1,0:T(8,128)(2,1)S(1)} %get-tuple-element.35.refs_0_, bf16[192,5120]{1,0:T(8,128)(2,1)S(1)} %get-tuple-element.36.refs_2_.refs_1_, bf16[18,128,256]{2,1,0:T(8,128)(2,1)S(1)} %bitcast.24, bf16[12,128,256]{2,1,0:T(8,128)(2,1)S(1)} %bitcast.28, bf16[12,128,256]{2,1,0:T(8,128)(2,1)S(1)} %bitcast.30, ...), custom_call_target="tpu_custom_call" | custom-call | flops 1000 | bytes 1000 | tf_op jit(solution)/shard_map/last/pallas_call | solution.py:457
  151.0 0.0 collective-permute-done.10.b_ref
  151.0 2.6 %add_pack.1 = bf16[256,3968]{1,0:T(8,128)(2,1)} custom-call(bf16[192,5248]{1,0:T(8,128)(2,1)S(1)} %last.2.a_ref, bf16[192,5248]{1,0:T(8,128)(2,1)S(1)} %collective-permute-done.10.b_ref), custom_call_target="tpu_custom_call" | custom-call | flops 754974720 | bytes 6045696 | tf_op jit(solution)/shard_map/add_pack/pallas_call | solution.py:499
  153.6 0.0 copy-start
  153.6 12.7 %all-to-all-start.1 = ((bf16[32,8,3968]{2,1,0:T(8,128)(2,1)}), bf16[32,8,3968]{2,1,0:T(8,128)(2,1)S(1)}, u32[]{:S(2)}, u32[]{:S(2)}) async-start(bf16[32,8,3968]{2,1,0:T(8,128)(2,1)} %bitcast.19), calls=%async_computation.1 | async-start | bytes 4063232 | tf_op jit(solution)/shard_map/all_to_all | solution.py:596
  166.3 0.0 copy-done
  166.3 0.0 copy-start.2
  166.4 0.0 copy-start.3
  166.4 1.8 multiply_reduce_fusion
  168.1 47.4 %all-to-all-done.1 = bf16[32,8,3968]{2,1,0:T(8,128)(2,1)S(1)} async-done(((bf16[32,8,3968]{2,1,0:T(8,128)(2,1)}), bf16[32,8,3968]{2,1,0:T(8,128)(2,1)S(1)}, u32[]{:S(2)}, u32[]{:S(2)}) %all-to-all-start.1) | async-done | bytes 2031648 | tf_op jit(solution)/shard_map/all_to_all | solution.py:596
  215.6 0.0 copy-done.2
  215.6 0.0 copy-done.3
  215.6 2.1 combine.1
Async XLA Ops:
  5.2 89.1 %collective-permute-start = (bf16[5376,256]{1,0:T(8,128)(2,1)}, bf16[5376,256]{1,0:T(8,128)(2,1)}, u32[]{:S(2)}, u32[]{:S(2)}) collective-permute-start(bf16[5376,256]{1,0:T(8,128)(2,1)} %get-tuple-element.27), channel_id=1, source_target_pairs={{0,2},{2,4},{4,6},{6,0},{1,3},{3,5},{5,7},{7,1},{8,10},{10,12},{12... | collective-permute-start | bytes 8257544 | tf_op jit(solution)/shard_map/ppermute | solution.py:566
  7.3 87.1 %collective-permute-start.1 = (bf16[5376,256]{1,0:T(8,128)(2,1)}, bf16[5376,256]{1,0:T(8,128)(2,1)}, u32[]{:S(2)}, u32[]{:S(2)}) collective-permute-start(bf16[5376,256]{1,0:T(8,128)(2,1)} %get-tuple-element.28), channel_id=1, source_target_pairs={{0,6},{2,0},{4,2},{6,4},{1,7},{3,1},{5,3},{7,5},{8,14},{10,8},{12,... | collective-permute-start | bytes 8257544 | tf_op jit(solution)/shard_map/ppermute | solution.py:567
  12.3 11.6 %copy-start.1 = (bf16[2304,256]{1,0:T(8,128)(2,1)S(1)}, bf16[2304,256]{1,0:T(8,128)(2,1)}, u32[]{:S(2)}) copy-start(bf16[2304,256]{1,0:T(8,128)(2,1)} %get-tuple-element.41) | copy-start | bytes 3538948
  12.3 13.1 %copy-start.4 = (bf16[2304,256]{1,0:T(8,128)(2,1)S(1)}, bf16[2304,256]{1,0:T(8,128)(2,1)}, u32[]{:S(2)}) copy-start(bf16[2304,256]{1,0:T(8,128)(2,1)} %get-tuple-element.34) | copy-start | bytes 3538948
  12.4 102.5 %all-to-all-start = ((bf16[32,8,7680]{2,1,0:T(8,128)(2,1)}), bf16[32,8,7680]{2,1,0:T(8,128)(2,1)}, u32[]{:S(2)}, u32[]{:S(2)}) async-start(bf16[32,8,7680]{2,1,0:T(8,128)(2,1)} %bitcast.36), calls=%async_computation | async-start | bytes 7864320 | tf_op jit(solution)/shard_map/all_to_all | solution.py:573
  23.9 68.4 %collective-permute-start.2 = (bf16[2304,256]{1,0:T(8,128)(2,1)S(1)}, bf16[2304,256]{1,0:T(8,128)(2,1)}, u32[]{:S(2)}, u32[]{:S(2)}) collective-permute-start(bf16[2304,256]{1,0:T(8,128)(2,1)S(1)} %copy-done.1), channel_id=1, source_target_pairs={{0,2},{2,4},{4,6},{6,0},{1,3},{3,5},{5,7},{7,1},{8,10},{10,12},{12... | collective-permute-start | bytes 3538952 | tf_op jit(solution)/shard_map/ppermute | solution.py:564
  25.5 68.4 %collective-permute-start.4 = (bf16[2304,256]{1,0:T(8,128)(2,1)S(1)}, bf16[2304,256]{1,0:T(8,128)(2,1)}, u32[]{:S(2)}, u32[]{:S(2)}) collective-permute-start(bf16[2304,256]{1,0:T(8,128)(2,1)S(1)} %copy-done.4), channel_id=1, source_target_pairs={{0,6},{2,0},{4,2},{6,4},{1,7},{3,1},{5,3},{7,5},{8,14},{10,8},{12,... | collective-permute-start | bytes 3538952 | tf_op jit(solution)/shard_map/ppermute | solution.py:565
  92.3 27.0 %collective-permute-start.3 = (bf16[2304,256]{1,0:T(8,128)(2,1)}, bf16[2304,256]{1,0:T(8,128)(2,1)S(1)}, u32[]{:S(2)}, u32[]{:S(2)}) collective-permute-start(bf16[2304,256]{1,0:T(8,128)(2,1)} %collective-permute-done.2), channel_id=1, source_target_pairs={{0,2},{2,4},{4,6},{6,0},{1,3},{3,5},{5,7},{7,1},{8,10},{10,12},{12... | collective-permute-start | bytes 3538952 | tf_op jit(solution)/shard_map/ppermute | solution.py:568
  93.8 26.8 %collective-permute-start.5 = (bf16[2304,256]{1,0:T(8,128)(2,1)}, bf16[2304,256]{1,0:T(8,128)(2,1)S(1)}, u32[]{:S(2)}, u32[]{:S(2)}) collective-permute-start(bf16[2304,256]{1,0:T(8,128)(2,1)} %collective-permute-done.4), channel_id=1, source_target_pairs={{0,6},{2,0},{4,2},{6,4},{1,7},{3,1},{5,3},{7,5},{8,14},{10,8},{12,... | collective-permute-start | bytes 3538952 | tf_op jit(solution)/shard_map/ppermute | solution.py:569
  114.8 6.2 %copy-start.6 = (bf16[1536,256]{1,0:T(8,128)(2,1)S(1)}, bf16[1536,256]{1,0:T(8,128)(2,1)}, u32[]{:S(2)}) copy-start(bf16[1536,256]{1,0:T(8,128)(2,1)} %get-tuple-element.38) | copy-start | bytes 2359300
  114.8 6.5 %copy-start.5 = (bf16[1536,256]{1,0:T(8,128)(2,1)S(1)}, bf16[1536,256]{1,0:T(8,128)(2,1)}, u32[]{:S(2)}) copy-start(bf16[1536,256]{1,0:T(8,128)(2,1)} %get-tuple-element.39) | copy-start | bytes 2359300
  120.6 4.0 %collective-permute-start.8 = (bf16[192,5120]{1,0:T(8,128)(2,1)S(1)}, bf16[192,5120]{1,0:T(8,128)(2,1)S(1)}, u32[]{:S(2)}, u32[]{:S(2)}) collective-permute-start(bf16[192,5120]{1,0:T(8,128)(2,1)S(1)} %get-tuple-element.35.refs_0_), channel_id=1, source_target_pairs={{0,1},{1,0},{2,3},{3,2},{4,5},{5,4},{6,7},{7,6},{8,9},{9,8},{10,11... | collective-permute-start | bytes 5898248 | tf_op jit(solution)/shard_map/ppermute | solution.py:582
  120.6 6.8 %collective-permute-start.9 = (bf16[192,5120]{1,0:T(8,128)(2,1)S(1)}, bf16[192,5120]{1,0:T(8,128)(2,1)S(1)}, u32[]{:S(2)}, u32[]{:S(2)}) collective-permute-start(bf16[192,5120]{1,0:T(8,128)(2,1)S(1)} %get-tuple-element.36.refs_2_.refs_1_), channel_id=1, source_target_pairs={{0,1},{1,0},{2,3},{3,2},{4,5},{5,4},{6,7},{7,6},{8,9},{9,8},{10,11... | collective-permute-start | bytes 5898248 | tf_op jit(solution)/shard_map/ppermute | solution.py:582
  121.1 19.6 %collective-permute-start.6 = (bf16[1536,256]{1,0:T(8,128)(2,1)S(1)}, bf16[1536,256]{1,0:T(8,128)(2,1)S(1)}, u32[]{:S(2)}, u32[]{:S(2)}) collective-permute-start(bf16[1536,256]{1,0:T(8,128)(2,1)S(1)} %copy-done.6), channel_id=1, source_target_pairs={{0,2},{2,4},{4,6},{6,0},{1,3},{3,5},{5,7},{7,1},{8,10},{10,12},{12... | collective-permute-start | bytes 2359304 | tf_op jit(solution)/shard_map/ppermute | solution.py:579
  121.4 20.7 %collective-permute-start.7 = (bf16[1536,256]{1,0:T(8,128)(2,1)S(1)}, bf16[1536,256]{1,0:T(8,128)(2,1)S(1)}, u32[]{:S(2)}, u32[]{:S(2)}) collective-permute-start(bf16[1536,256]{1,0:T(8,128)(2,1)S(1)} %copy-done.5), channel_id=1, source_target_pairs={{0,6},{2,0},{4,2},{6,4},{1,7},{3,1},{5,3},{7,5},{8,14},{10,8},{12,... | collective-permute-start | bytes 2359304 | tf_op jit(solution)/shard_map/ppermute | solution.py:580
  146.3 4.6 %collective-permute-start.10 = (bf16[192,5248]{1,0:T(8,128)(2,1)S(1)}, bf16[192,5248]{1,0:T(8,128)(2,1)S(1)}, u32[]{:S(2)}, u32[]{:S(2)}) collective-permute-start(bf16[192,5248]{1,0:T(8,128)(2,1)S(1)} %last.3), channel_id=1, source_target_pairs={{0,1},{1,0},{2,3},{3,2},{4,5},{5,4},{6,7},{7,6},{8,9},{9,8},{10,11... | collective-permute-start | bytes 6045704 | tf_op jit(solution)/shard_map/ppermute | solution.py:593
  153.6 12.7 %copy-start = (bf16[128,5120]{1,0:T(8,128)(2,1)S(1)}, bf16[128,5120]{1,0:T(8,128)(2,1)}, u32[]{:S(2)}) copy-start(bf16[128,5120]{1,0:T(8,128)(2,1)} %out_grad_ref.1) | copy-start | bytes 3932164
  153.6 62.0 %all-to-all-start.1 = ((bf16[32,8,3968]{2,1,0:T(8,128)(2,1)}), bf16[32,8,3968]{2,1,0:T(8,128)(2,1)S(1)}, u32[]{:S(2)}, u32[]{:S(2)}) async-start(bf16[32,8,3968]{2,1,0:T(8,128)(2,1)} %bitcast.19), calls=%async_computation.1 | async-start | bytes 4063232 | tf_op jit(solution)/shard_map/all_to_all | solution.py:596
  166.3 49.2 %copy-start.2 = (s32[128,1]{0,1:T(1,128)S(1)}, s32[128,1]{0,1:T(1,128)}, u32[]{:S(2)}) copy-start(s32[128,1]{0,1:T(1,128)} %param.10) | copy-start | bytes 1540
  166.4 49.2 %copy-start.3 = (f32[128]{0:T(128)S(1)}, f32[128]{0:T(128)}, u32[]{:S(2)}) copy-start(f32[128]{0:T(128)} %param.9) | copy-start | bytes 1540

commit v10 on v9

--- a/solution.py
+++ b/solution.py
@@ -15,12 +15,10 @@
 PARTS = 60
 UP_PARTS = 40
 HALF = 30
-HEAD = 18
-ENDS = ((0, HEAD), (PARTS - HEAD, PARTS))
-RESTS = ((HEAD, PARTS), (0, PARTS - HEAD))
-MIDDLE = (PARTS - 2 * HEAD) // 3
-WEIGHT_CUTS = (0, HEAD, HEAD + MIDDLE, HEAD + 2 * MIDDLE, PARTS - HEAD, PARTS)
-FAR_FLOPS = 62000000000
+FAR = 17
+HALVES = ((0, HALF), (HALF, PARTS))
+WEIGHT_CUTS = (0, 15, 30, 45, 60)
+FAR_FLOPS = (50000000000, 75000000000)
 FIRST_FLOPS = 1000
 LAST_FLOPS = 1000
 VMEM_ALL = 56 * 1024 * 1024
@@ -150,10 +148,10 @@
     return copies
 
 
-def weights_kernel(core_ref, gate, up, down, head, up_rest, down_rest, tail, held, read_sems, write_sems):
+def weights_kernel(core_ref, gate, up, down, low_half, high_half, held, read_sems, write_sems):
     hidden = held.shape[1] // 2
     reads, waits, writes = [], [], []
-    outs = ((head, ENDS[0]), (tail, ENDS[1]), (up_rest, RESTS[0]), (down_rest, RESTS[1]))
+    outs = tuple(zip((low_half, high_half), HALVES))
     count = 0
     for i, (low, high) in enumerate(zip(WEIGHT_CUTS, WEIGHT_CUTS[1:])):
         rows = held.at[pl.ds(low * hidden, (high - low) * hidden)]
@@ -186,9 +184,9 @@
     size = lambda parts: jax.ShapeDtypeStruct(((parts[1] - parts[0]) * hidden, span), BF)
     return pl.pallas_call(
         weights_kernel,
-        out_shape=[size(parts) for parts in (ENDS[0],) + RESTS + (ENDS[1],)],
+        out_shape=[size(parts) for parts in HALVES],
         in_specs=[pl.BlockSpec(memory_space=pltpu.SMEM)] + [any_spec] * 3,
-        out_specs=[any_spec] * 4,
+        out_specs=[any_spec] * 2,
         scratch_shapes=[
             pltpu.VMEM((PARTS * hidden, span), BF),
             pltpu.SemaphoreType.DMA((len(WEIGHT_CUTS) - 1,)),
@@ -218,7 +216,7 @@
         write.wait()
 
 
-def far_parts(from_up, from_down, ranges):
+def far_parts(from_up, from_down, ranges, flops):
     rows, span = from_up.shape
     hidden = span // 2
     any_spec = pl.BlockSpec(memory_space=pl.ANY)
@@ -230,7 +228,7 @@
         scratch_shapes=[pltpu.VMEM(((high - low) * hidden, span), BF) for _, low, high in ranges]
         + [pltpu.SemaphoreType.DMA((2 * len(ranges),))],
         compiler_params=pltpu.CompilerParams(vmem_limit_bytes=VMEM_ALL),
-        cost_estimate=pl.CostEstimate(flops=FAR_FLOPS, bytes_accessed=0, transcendentals=0),
+        cost_estimate=pl.CostEstimate(flops=flops, bytes_accessed=0, transcendentals=0),
         name="far",
     )(from_up, from_down)
 
@@ -560,21 +558,23 @@
 
     core = lax.axis_index("dp").reshape(1)
     weights = (gate_weight[0], up_weight[0], down_weight[0])
-    head, up_rest, down_rest, tail = weight_parts(core, weights)
-    up_head = lax.ppermute(head, "tensor", up)
-    down_tail = lax.ppermute(tail, "tensor", down)
-    from_up = lax.ppermute(up_rest, "tensor", up)
-    from_down = lax.ppermute(down_rest, "tensor", down)
-    far_head = lax.ppermute(up_head, "tensor", up)
-    far_tail = lax.ppermute(down_tail, "tensor", down)
-
-    route_row, head = lax.optimization_barrier((route_row, head))
+    low_half, high_half = weight_parts(core, weights)
+    up_low = lax.ppermute(low_half, "tensor", up)
+    down_high = lax.ppermute(high_half, "tensor", down)
+    up_high = lax.ppermute(high_half, "tensor", up)
+    down_low = lax.ppermute(low_half, "tensor", down)
+
+    route_row, low_half = lax.optimization_barrier((route_row, low_half))
     packed = pack(route_row, tokens, out_grad, experts)
     got = lax.all_to_all(
         packed.reshape(experts, ROWS, -1), "expert", split_axis=0, concat_axis=0, tiled=True
     ).reshape(experts * ROWS, -1)
 
-    far_up, far_down = far_parts(from_up, from_down, ((0, 0, HALF - HEAD), (1, HALF, PARTS - HEAD)))
+    far_head, far_tail = far_parts(up_low, down_high, ((0, 0, FAR), (1, HALF - FAR, HALF)), FAR_FLOPS[0])
+    far_head = lax.ppermute(far_head, "tensor", up)
+    far_tail = lax.ppermute(far_tail, "tensor", down)
+    up_low, down_high, up_high, down_low = lax.optimization_barrier((up_low, down_high, up_high, down_low))
+    far_up, far_down = far_parts(up_low, down_high, ((0, FAR, HALF), (1, 0, HALF - FAR)), FAR_FLOPS[1])
     got, far_up, far_down = lax.optimization_barrier((got, far_up, far_down))
     far_up = lax.ppermute(far_up, "tensor", up)
     far_down = lax.ppermute(far_down, "tensor", down)
@@ -583,10 +583,10 @@
 
     part = width // UP_PARTS
     squares = lambda piece: piece.reshape(-1, part, 2 * part)
-    blocks = [list(map(squares, b)) for b in ((head, up_rest), (up_head, from_up), (from_down, down_tail))]
-    ranges = ((ENDS[0], RESTS[0]),) * 2 + ((RESTS[1], ENDS[1]),)
+    blocks = [list(map(squares, b)) for b in ((low_half, high_half), (up_low, up_high), (down_low, down_high))]
+    ranges = (HALVES,) * 3
     far = (far_head, far_up, far_down, far_tail)
-    far_ranges = (ENDS[0], (HEAD, HALF), (HALF, PARTS - HEAD), ENDS[1])
+    far_ranges = ((0, FAR), (FAR, HALF), (HALF, PARTS - FAR), (PARTS - FAR, PARTS))
     own_sums, other_sums, own_terms, other_terms = first_blocks((x, x_other, dy, dy_other), blocks, ranges)
     far = list(map(squares, far))
     other_sums = last_block(x_other, dy_other, far, far_ranges, other_sums, other_terms)

time: 218 us -> 217 us (level)
  starting transfers between devices: 33.4 us -> 30.6 us
    all_to_all x1, starting transfers between devices: 12.7 us -> 9.22 us  [per_device(): lax.all_to_all(back, 'expert', split_axis=0, concat_axis=0, tiled=True)]
    ppermute x6, waiting for transfers between devices: 68.3 us -> 65.2 us  [the longest x1 35.1 us: per_device(): up_high = lax.ppermute(high_half, 'tensor', up)]
    ppermute x1, waiting for transfers between devices: 0.01 us -> 2.79 us  [per_device(): far_up = lax.ppermute(far_up, 'tensor', up)]
    pallas_call x1 -> x2, Pallas kernels: 2.33 us -> 5.09 us  [far_parts(): pl.pallas_call(functools.partial(far_kernel, ranges), out_shape=[jax.Shap...]
    ppermute x1, starting transfers between devices: 0.28 us -> 2.83 us  [per_device(): far_up = lax.ppermute(far_up, 'tensor', up)]
  transfers between devices with their start and end apart: 13 -> 13, of which waited for: 8 -> 10; matrix products, arithmetic and copies ran while one was open for 1% -> 1% of each run, Pallas kernels for 13% -> 14%
where the time goes in v10:
time: 217 us; the launch traced here: 216 us
  waiting for transfers between devices  140 us (65%)
  Pallas kernels  42.9 us (20%)
  starting transfers between devices  30.6 us (14%)
    all_to_all x1, waiting for transfers between devices, per_device(): lax.all_to_all(back, 'expert', split_axis=0, concat_axis=0, tiled=True)  47.5 us
    ppermute x1, waiting for transfers between devices, per_device(): up_high = lax.ppermute(high_half, 'tensor', up)  35.1 us
    ppermute x1, waiting for transfers between devices, per_device(): up_low = lax.ppermute(low_half, 'tensor', up)  25.4 us
    all_to_all x1, waiting for transfers between devices, per_device(): lax.all_to_all(packed.reshape(experts, ROWS, -1), 'expert', split_axis=0,...  18.1 us
    pallas_call x1, Pallas kernels, first_blocks(): pl.pallas_call(functools.partial(first_kernel, ranges), out_shape=[jax.Sh...  12.5 us
    all_to_all x1, starting transfers between devices, per_device(): lax.all_to_all(packed.reshape(experts, ROWS, -1), 'expert', split_axis=0,...  10.3 us
    all_to_all x1, starting transfers between devices, per_device(): lax.all_to_all(back, 'expert', split_axis=0, concat_axis=0, tiled=True)  9.22 us
    pallas_call x2, Pallas kernels, last_block(): pl.pallas_call(functools.partial(last_kernel, ranges), out_shape=jax.Shap...  8.6 us
  transfers between devices with their start and end apart: 13, of which 10 were waited for; matrix products, arithmetic and copies ran while one was open for 1% of the time, Pallas kernels for 14%

profile of v10, /device:TPU:24, one launch (start us, length us, event | category | flops | bytes accessed | tf_op | source)
XLA Modules:
  0.0 216.3 jit_solution(2236184573471754211)
XLA Ops:
  0.6 3.2 %weights.1 = (bf16[3840,256]{1,0:T(8,128)(2,1)}, bf16[3840,256]{1,0:T(8,128)(2,1)}) custom-call(s32[1]{0:T(128)} %bitcast.1.core_ref, bf16[5120,256]{1,0:T(8,128)(2,1)} %bitcast.38, bf16[5120,256]{1,0:T(8,128)(2,1)} %bitcast.39, bf16[256,5120]{1,0:T(8,128)(2,1)} %bitcast.40), custom_call_target="tpu_custom_call" | custom-call | bytes 11796480 | tf_op jit(solution)/shard_map/weights/pallas_call | solution.py:185
  3.9 2.0 collective-permute-start
  5.9 0.1 collective-permute-start.1
  6.0 3.2 %collective-permute-start.2 = (bf16[3840,256]{1,0:T(8,128)(2,1)}, bf16[3840,256]{1,0:T(8,128)(2,1)}, u32[]{:S(2)}, u32[]{:S(2)}) collective-permute-start(bf16[3840,256]{1,0:T(8,128)(2,1)} %get-tuple-element.31), channel_id=1, source_target_pairs={{0,2},{2,4},{4,6},{6,0},{1,3},{3,5},{5,7},{7,1},{8,10},{10,12},{12... | collective-permute-start | bytes 5898248 | tf_op jit(solution)/shard_map/ppermute | solution.py:564
  9.2 0.0 collective-permute-start.3
  9.2 5.0 %pack.1 = bf16[256,7680]{1,0:T(8,128)(2,1)} custom-call(s32[1,128]{1,0:T(1,128)} %bitcast.34, bf16[128,5120]{1,0:T(8,128)(2,1)} %x_hbm.1, bf16[128,5120]{1,0:T(8,128)(2,1)} %out_grad_ref.1), custom_call_target="tpu_custom_call" | custom-call | flops 1006632960 | bytes 6553600 | tf_op jit(solution)/shard_map/pack/pallas_call | solution.py:112
  14.1 10.3 %all-to-all-start = ((bf16[32,8,7680]{2,1,0:T(8,128)(2,1)}), bf16[32,8,7680]{2,1,0:T(8,128)(2,1)}, u32[]{:S(2)}, u32[]{:S(2)}) async-start(bf16[32,8,7680]{2,1,0:T(8,128)(2,1)} %bitcast.37), calls=%async_computation | async-start | bytes 7864320 | tf_op jit(solution)/shard_map/all_to_all | solution.py:569
  24.4 25.4 %collective-permute-done.up_hbm = bf16[3840,256]{1,0:T(8,128)(2,1)S(1)} collective-permute-done((bf16[3840,256]{1,0:T(8,128)(2,1)}, bf16[3840,256]{1,0:T(8,128)(2,1)S(1)}, u32[]{:S(2)}, u32[]{:S(2)}) %collective-permute-start) | collective-permute-done | bytes 1966112 | tf_op jit(solution)/shard_map/ppermute | solution.py:562
  49.9 0.0 copy-start.5
  49.9 3.3 %collective-permute-done.1.down_hbm = bf16[3840,256]{1,0:T(8,128)(2,1)} collective-permute-done((bf16[3840,256]{1,0:T(8,128)(2,1)}, bf16[3840,256]{1,0:T(8,128)(2,1)}, u32[]{:S(2)}, u32[]{:S(2)}) %collective-permute-start.1) | collective-permute-done | bytes 1966112 | tf_op jit(solution)/shard_map/ppermute | solution.py:563
  53.2 0.0 copy-done.5
  53.2 2.7 %far.3 = (bf16[2176,256]{1,0:T(8,128)(2,1)}, bf16[2176,256]{1,0:T(8,128)(2,1)}) custom-call(bf16[3840,256]{1,0:T(8,128)(2,1)} %copy-done.5, bf16[3840,256]{1,0:T(8,128)(2,1)} %collective-permute-done.1.down_hbm), custom_call_target="tpu_custom_call" | custom-call | flops 49999998976 | tf_op jit(solution)/shard_map/far/pallas_call | solution.py:223
  55.9 35.1 %collective-permute-done.2 = bf16[3840,256]{1,0:T(8,128)(2,1)} collective-permute-done((bf16[3840,256]{1,0:T(8,128)(2,1)}, bf16[3840,256]{1,0:T(8,128)(2,1)}, u32[]{:S(2)}, u32[]{:S(2)}) %collective-permute-start.2) | collective-permute-done | bytes 1966112 | tf_op jit(solution)/shard_map/ppermute | solution.py:564
  91.0 1.3 collective-permute-done.3
  92.3 0.2 collective-permute-start.4
  92.5 1.8 collective-permute-start.5
  94.3 2.4 %far.2 = (bf16[1664,256]{1,0:T(8,128)(2,1)}, bf16[1664,256]{1,0:T(8,128)(2,1)}) custom-call(bf16[3840,256]{1,0:T(8,128)(2,1)} %copy-done.5, bf16[3840,256]{1,0:T(8,128)(2,1)} %collective-permute-done.1.down_hbm), custom_call_target="tpu_custom_call" | custom-call | flops 74999996416 | tf_op jit(solution)/shard_map/far/pallas_call | solution.py:223
  96.7 18.1 %all-to-all-done = bf16[32,8,7680]{2,1,0:T(8,128)(2,1)} async-done(((bf16[32,8,7680]{2,1,0:T(8,128)(2,1)}), bf16[32,8,7680]{2,1,0:T(8,128)(2,1)}, u32[]{:S(2)}, u32[]{:S(2)}) %all-to-all-start) | async-done | bytes 3932192 | tf_op jit(solution)/shard_map/all_to_all | solution.py:569
  114.8 0.0 copy-start.1
  114.9 0.0 copy-start.2
  114.9 3.7 %unpack.1 = (bf16[192,5120]{1,0:T(8,128)(2,1)S(1)}, bf16[192,5120]{1,0:T(8,128)(2,1)S(1)}) custom-call(bf16[256,7680]{1,0:T(8,128)(2,1)} %bitcast.8.rows_hbm), custom_call_target="tpu_custom_call" | custom-call | flops 1000 | bytes 1000 | tf_op jit(solution)/shard_map/unpack/pallas_call | solution.py:347
  118.6 0.0 collective-permute-done.4
  118.6 0.0 collective-permute-done.5
  118.6 0.1 collective-permute-start.8
  118.7 0.5 collective-permute-start.9
  119.2 2.8 %collective-permute-start.6 = (bf16[1664,256]{1,0:T(8,128)(2,1)}, bf16[1664,256]{1,0:T(8,128)(2,1)S(1)}, u32[]{:S(2)}, u32[]{:S(2)}) collective-permute-start(bf16[1664,256]{1,0:T(8,128)(2,1)} %get-tuple-element.44), channel_id=1, source_target_pairs={{0,2},{2,4},{4,6},{6,0},{1,3},{3,5},{5,7},{7,1},{8,10},{10,12},{12... | collective-permute-start | bytes 2555912 | tf_op jit(solution)/shard_map/ppermute | solution.py:579
  122.0 0.0 collective-permute-start.7
  122.0 0.6 collective-permute-done.8.refs_1_.refs_0_
  122.7 2.8 %collective-permute-done.9.refs_3_.refs_1_ = bf16[192,5120]{1,0:T(8,128)(2,1)S(1)} collective-permute-done((bf16[192,5120]{1,0:T(8,128)(2,1)S(1)}, bf16[192,5120]{1,0:T(8,128)(2,1)S(1)}, u32[]{:S(2)}, u32[]{:S(2)}) %collective-permute-start.9) | collective-permute-done | bytes 1966112 | tf_op jit(solution)/shard_map/ppermute | solution.py:582
  125.5 0.0 copy-done.1
  125.5 0.0 copy-done.2
  125.5 12.5 %first.1 = (bf16[192,5120]{1,0:T(8,128)(2,1)S(1)}, bf16[192,5120]{1,0:T(8,128)(2,1)S(1)}, f32[192,128]{1,0:T(8,128)S(1)}, f32[192,128]{1,0:T(8,128)S(1)}) custom-call(bf16[192,5120]{1,0:T(8,128)(2,1)S(1)} %get-tuple-element.41.refs_0_, bf16[192,5120]{1,0:T(8,128)(2,1)S(1)} %collective-permute-done.8.refs_1_.refs_0_, ...), custom_call_target="tpu_custom_call" | custom-call | flops 1000 | bytes 1000 | tf_op jit(solution)/shard_map/first/pallas_call | solution.py:406
  138.0 2.8 %collective-permute-done.6 = bf16[1664,256]{1,0:T(8,128)(2,1)S(1)} collective-permute-done((bf16[1664,256]{1,0:T(8,128)(2,1)}, bf16[1664,256]{1,0:T(8,128)(2,1)S(1)}, u32[]{:S(2)}, u32[]{:S(2)}) %collective-permute-start.6) | collective-permute-done | bytes 852000 | tf_op jit(solution)/shard_map/ppermute | solution.py:579
  140.8 3.3 %collective-permute-done.7 = bf16[1664,256]{1,0:T(8,128)(2,1)S(1)} collective-permute-done((bf16[1664,256]{1,0:T(8,128)(2,1)}, bf16[1664,256]{1,0:T(8,128)(2,1)S(1)}, u32[]{:S(2)}, u32[]{:S(2)}) %collective-permute-start.7) | collective-permute-done | bytes 852000 | tf_op jit(solution)/shard_map/ppermute | solution.py:580
  144.1 4.3 %last.3 = bf16[192,5248]{1,0:T(8,128)(2,1)S(1)} custom-call(bf16[192,5120]{1,0:T(8,128)(2,1)S(1)} %collective-permute-done.8.refs_1_.refs_0_, bf16[192,5120]{1,0:T(8,128)(2,1)S(1)} %collective-permute-done.9.refs_3_.refs_1_, bf16[17,128,256]{2,1,0:T(8,128)(2,1)S(1)} %bitcast.23, bf16[13,128,256]{2,1,0:T(8,128)(2,1)S(1)} %bitcast.27, ...), custom_call_target="tpu_custom_call" | custom-call | flops 1000 | bytes 1000 | tf_op jit(solution)/shard_map/last/pallas_call | solution.py:455
  148.4 0.3 collective-permute-start.10
  148.8 4.3 %last.2.a_ref = bf16[192,5248]{1,0:T(8,128)(2,1)S(1)} custom-call(bf16[192,5120]{1,0:T(8,128)(2,1)S(1)} %get-tuple-element.41.refs_0_, bf16[192,5120]{1,0:T(8,128)(2,1)S(1)} %get-tuple-element.42.refs_2_.refs_1_, bf16[17,128,256]{2,1,0:T(8,128)(2,1)S(1)} %bitcast.24, bf16[13,128,256]{2,1,0:T(8,128)(2,1)S(1)} %bitcast.28, bf16[13,128,256]{2,1,0:T(8,128)(2,1)S(1)} %bitcast.30, ...), custom_call_target="tpu_custom_call" | custom-call | flops 1000 | bytes 1000 | tf_op jit(solution)/shard_map/last/pallas_call | solution.py:455
  153.1 0.0 collective-permute-done.10.b_ref
  153.1 2.6 %add_pack.1 = bf16[256,3968]{1,0:T(8,128)(2,1)} custom-call(bf16[192,5248]{1,0:T(8,128)(2,1)S(1)} %last.2.a_ref, bf16[192,5248]{1,0:T(8,128)(2,1)S(1)} %collective-permute-done.10.b_ref), custom_call_target="tpu_custom_call" | custom-call | flops 754974720 | bytes 6045696 | tf_op jit(solution)/shard_map/add_pack/pallas_call | solution.py:497
  155.7 0.0 copy-start
  155.7 9.2 %all-to-all-start.1 = ((bf16[32,8,3968]{2,1,0:T(8,128)(2,1)}), bf16[32,8,3968]{2,1,0:T(8,128)(2,1)S(1)}, u32[]{:S(2)}, u32[]{:S(2)}) async-start(bf16[32,8,3968]{2,1,0:T(8,128)(2,1)} %bitcast.19), calls=%async_computation.1 | async-start | bytes 4063232 | tf_op jit(solution)/shard_map/all_to_all | solution.py:596
  164.9 0.0 copy-done
  164.9 0.0 copy-start.3
  164.9 0.0 copy-start.4
  165.0 1.8 multiply_reduce_fusion
  166.7 47.5 %all-to-all-done.1 = bf16[32,8,3968]{2,1,0:T(8,128)(2,1)S(1)} async-done(((bf16[32,8,3968]{2,1,0:T(8,128)(2,1)}), bf16[32,8,3968]{2,1,0:T(8,128)(2,1)S(1)}, u32[]{:S(2)}, u32[]{:S(2)}) %all-to-all-start.1) | async-done | bytes 2031648 | tf_op jit(solution)/shard_map/all_to_all | solution.py:596
  214.2 0.0 copy-done.3
  214.2 0.0 copy-done.4
  214.2 2.1 combine.1
Async XLA Ops:
  3.9 46.0 %collective-permute-start = (bf16[3840,256]{1,0:T(8,128)(2,1)}, bf16[3840,256]{1,0:T(8,128)(2,1)S(1)}, u32[]{:S(2)}, u32[]{:S(2)}) collective-permute-start(bf16[3840,256]{1,0:T(8,128)(2,1)} %get-tuple-element.47), channel_id=1, source_target_pairs={{0,2},{2,4},{4,6},{6,0},{1,3},{3,5},{5,7},{7,1},{8,10},{10,12},{12... | collective-permute-start | bytes 5898248 | tf_op jit(solution)/shard_map/ppermute | solution.py:562
  5.9 47.3 %collective-permute-start.1 = (bf16[3840,256]{1,0:T(8,128)(2,1)}, bf16[3840,256]{1,0:T(8,128)(2,1)}, u32[]{:S(2)}, u32[]{:S(2)}) collective-permute-start(bf16[3840,256]{1,0:T(8,128)(2,1)} %get-tuple-element.31), channel_id=1, source_target_pairs={{0,6},{2,0},{4,2},{6,4},{1,7},{3,1},{5,3},{7,5},{8,14},{10,8},{12,... | collective-permute-start | bytes 5898248 | tf_op jit(solution)/shard_map/ppermute | solution.py:563
  6.0 85.0 %collective-permute-start.2 = (bf16[3840,256]{1,0:T(8,128)(2,1)}, bf16[3840,256]{1,0:T(8,128)(2,1)}, u32[]{:S(2)}, u32[]{:S(2)}) collective-permute-start(bf16[3840,256]{1,0:T(8,128)(2,1)} %get-tuple-element.31), channel_id=1, source_target_pairs={{0,2},{2,4},{4,6},{6,0},{1,3},{3,5},{5,7},{7,1},{8,10},{10,12},{12... | collective-permute-start | bytes 5898248 | tf_op jit(solution)/shard_map/ppermute | solution.py:564
  9.2 83.1 %collective-permute-start.3 = (bf16[3840,256]{1,0:T(8,128)(2,1)}, bf16[3840,256]{1,0:T(8,128)(2,1)}, u32[]{:S(2)}, u32[]{:S(2)}) collective-permute-start(bf16[3840,256]{1,0:T(8,128)(2,1)} %get-tuple-element.47), channel_id=1, source_target_pairs={{0,6},{2,0},{4,2},{6,4},{1,7},{3,1},{5,3},{7,5},{8,14},{10,8},{12,... | collective-permute-start | bytes 5898248 | tf_op jit(solution)/shard_map/ppermute | solution.py:565
  14.1 100.7 %all-to-all-start = ((bf16[32,8,7680]{2,1,0:T(8,128)(2,1)}), bf16[32,8,7680]{2,1,0:T(8,128)(2,1)}, u32[]{:S(2)}, u32[]{:S(2)}) async-start(bf16[32,8,7680]{2,1,0:T(8,128)(2,1)} %bitcast.37), calls=%async_computation | async-start | bytes 7864320 | tf_op jit(solution)/shard_map/all_to_all | solution.py:569
  49.9 3.3 %copy-start.5 = (bf16[3840,256]{1,0:T(8,128)(2,1)}, bf16[3840,256]{1,0:T(8,128)(2,1)S(1)}, u32[]{:S(2)}) copy-start(bf16[3840,256]{1,0:T(8,128)(2,1)S(1)} %collective-permute-done.up_hbm) | copy-start | bytes 5898244
  92.3 26.3 %collective-permute-start.4 = (bf16[2176,256]{1,0:T(8,128)(2,1)}, bf16[2176,256]{1,0:T(8,128)(2,1)S(1)}, u32[]{:S(2)}, u32[]{:S(2)}) collective-permute-start(bf16[2176,256]{1,0:T(8,128)(2,1)} %get-tuple-element.39), channel_id=1, source_target_pairs={{0,2},{2,4},{4,6},{6,0},{1,3},{3,5},{5,7},{7,1},{8,10},{10,12},{12... | collective-permute-start | bytes 3342344 | tf_op jit(solution)/shard_map/ppermute | solution.py:574
  92.5 26.1 %collective-permute-start.5 = (bf16[2176,256]{1,0:T(8,128)(2,1)}, bf16[2176,256]{1,0:T(8,128)(2,1)S(1)}, u32[]{:S(2)}, u32[]{:S(2)}) collective-permute-start(bf16[2176,256]{1,0:T(8,128)(2,1)} %get-tuple-element.40), channel_id=1, source_target_pairs={{0,6},{2,0},{4,2},{6,4},{1,7},{3,1},{5,3},{7,5},{8,14},{10,8},{12,... | collective-permute-start | bytes 3342344 | tf_op jit(solution)/shard_map/ppermute | solution.py:575
  114.8 10.6 %copy-start.1 = (bf16[3840,256]{1,0:T(8,128)(2,1)S(1)}, bf16[3840,256]{1,0:T(8,128)(2,1)}, u32[]{:S(2)}) copy-start(bf16[3840,256]{1,0:T(8,128)(2,1)} %get-tuple-element.47) | copy-start | bytes 5898244
  114.9 10.6 %copy-start.2 = (bf16[3840,256]{1,0:T(8,128)(2,1)S(1)}, bf16[3840,256]{1,0:T(8,128)(2,1)}, u32[]{:S(2)}) copy-start(bf16[3840,256]{1,0:T(8,128)(2,1)} %get-tuple-element.31) | copy-start | bytes 5898244
  118.6 4.1 %collective-permute-start.8 = (bf16[192,5120]{1,0:T(8,128)(2,1)S(1)}, bf16[192,5120]{1,0:T(8,128)(2,1)S(1)}, u32[]{:S(2)}, u32[]{:S(2)}) collective-permute-start(bf16[192,5120]{1,0:T(8,128)(2,1)S(1)} %get-tuple-element.41.refs_0_), channel_id=1, source_target_pairs={{0,1},{1,0},{2,3},{3,2},{4,5},{5,4},{6,7},{7,6},{8,9},{9,8},{10,11... | collective-permute-start | bytes 5898248 | tf_op jit(solution)/shard_map/ppermute | solution.py:582
  118.7 6.8 %collective-permute-start.9 = (bf16[192,5120]{1,0:T(8,128)(2,1)S(1)}, bf16[192,5120]{1,0:T(8,128)(2,1)S(1)}, u32[]{:S(2)}, u32[]{:S(2)}) collective-permute-start(bf16[192,5120]{1,0:T(8,128)(2,1)S(1)} %get-tuple-element.42.refs_2_.refs_1_), channel_id=1, source_target_pairs={{0,1},{1,0},{2,3},{3,2},{4,5},{5,4},{6,7},{7,6},{8,9},{9,8},{10,11... | collective-permute-start | bytes 5898248 | tf_op jit(solution)/shard_map/ppermute | solution.py:582
  119.2 21.6 %collective-permute-start.6 = (bf16[1664,256]{1,0:T(8,128)(2,1)}, bf16[1664,256]{1,0:T(8,128)(2,1)S(1)}, u32[]{:S(2)}, u32[]{:S(2)}) collective-permute-start(bf16[1664,256]{1,0:T(8,128)(2,1)} %get-tuple-element.44), channel_id=1, source_target_pairs={{0,2},{2,4},{4,6},{6,0},{1,3},{3,5},{5,7},{7,1},{8,10},{10,12},{12... | collective-permute-start | bytes 2555912 | tf_op jit(solution)/shard_map/ppermute | solution.py:579
  122.0 22.1 %collective-permute-start.7 = (bf16[1664,256]{1,0:T(8,128)(2,1)}, bf16[1664,256]{1,0:T(8,128)(2,1)S(1)}, u32[]{:S(2)}, u32[]{:S(2)}) collective-permute-start(bf16[1664,256]{1,0:T(8,128)(2,1)} %get-tuple-element.45), channel_id=1, source_target_pairs={{0,6},{2,0},{4,2},{6,4},{1,7},{3,1},{5,3},{7,5},{8,14},{10,8},{12,... | collective-permute-start | bytes 2555912 | tf_op jit(solution)/shard_map/ppermute | solution.py:580
  148.4 4.6 %collective-permute-start.10 = (bf16[192,5248]{1,0:T(8,128)(2,1)S(1)}, bf16[192,5248]{1,0:T(8,128)(2,1)S(1)}, u32[]{:S(2)}, u32[]{:S(2)}) collective-permute-start(bf16[192,5248]{1,0:T(8,128)(2,1)S(1)} %last.3), channel_id=1, source_target_pairs={{0,1},{1,0},{2,3},{3,2},{4,5},{5,4},{6,7},{7,6},{8,9},{9,8},{10,11... | collective-permute-start | bytes 6045704 | tf_op jit(solution)/shard_map/ppermute | solution.py:593
  155.7 9.2 %copy-start = (bf16[128,5120]{1,0:T(8,128)(2,1)S(1)}, bf16[128,5120]{1,0:T(8,128)(2,1)}, u32[]{:S(2)}) copy-start(bf16[128,5120]{1,0:T(8,128)(2,1)} %out_grad_ref.1) | copy-start | bytes 3932164
  155.7 58.5 %all-to-all-start.1 = ((bf16[32,8,3968]{2,1,0:T(8,128)(2,1)}), bf16[32,8,3968]{2,1,0:T(8,128)(2,1)S(1)}, u32[]{:S(2)}, u32[]{:S(2)}) async-start(bf16[32,8,3968]{2,1,0:T(8,128)(2,1)} %bitcast.19), calls=%async_computation.1 | async-start | bytes 4063232 | tf_op jit(solution)/shard_map/all_to_all | solution.py:596
  164.9 49.2 %copy-start.3 = (s32[128,1]{0,1:T(1,128)S(1)}, s32[128,1]{0,1:T(1,128)}, u32[]{:S(2)}) copy-start(s32[128,1]{0,1:T(1,128)} %param.10) | copy-start | bytes 1540
  164.9 49.2 %copy-start.4 = (f32[128]{0:T(128)S(1)}, f32[128]{0:T(128)}, u32[]{:S(2)}) copy-start(f32[128]{0:T(128)} %param.9) | copy-start | bytes 1540

commit v11 on v10

--- a/solution.py
+++ b/solution.py
@@ -15,10 +15,10 @@
 PARTS = 60
 UP_PARTS = 40
 HALF = 30
-FAR = 17
+FAR = 18
 HALVES = ((0, HALF), (HALF, PARTS))
 WEIGHT_CUTS = (0, 15, 30, 45, 60)
-FAR_FLOPS = (50000000000, 75000000000)
+FAR_FLOPS = (62000000000, 1000)
 FIRST_FLOPS = 1000
 LAST_FLOPS = 1000
 VMEM_ALL = 56 * 1024 * 1024

time: 217 us -> 214 us (0.986)
  waiting for transfers between devices: 140 us -> 136 us
    ppermute x1, waiting for transfers between devices: 2.79 us -> 0.01 us  [per_device(): far_up = lax.ppermute(far_up, 'tensor', up)]
    all_to_all x1, waiting for transfers between devices: 18.1 us -> 15.6 us  [per_device(): lax.all_to_all(packed.reshape(experts, ROWS, -1), 'expert', split_axis=0,...]
  transfers between devices with their start and end apart: 13 -> 13, of which waited for: 10 -> 10; matrix products, arithmetic and copies ran while one was open for 1% -> 1% of each run, Pallas kernels for 14% -> 15%
where the time goes in v11:
time: 214 us; the launch traced here: 213 us
  waiting for transfers between devices  136 us (64%)
  Pallas kernels  43.8 us (20%)
  starting transfers between devices  31.3 us (15%)
    all_to_all x1, waiting for transfers between devices, per_device(): lax.all_to_all(back, 'expert', split_axis=0, concat_axis=0, tiled=True)  47.4 us
    ppermute x1, waiting for transfers between devices, per_device(): up_high = lax.ppermute(high_half, 'tensor', up)  34 us
    ppermute x1, waiting for transfers between devices, per_device(): up_low = lax.ppermute(low_half, 'tensor', up)  25.4 us
    all_to_all x1, waiting for transfers between devices, per_device(): lax.all_to_all(packed.reshape(experts, ROWS, -1), 'expert', split_axis=0,...  15.6 us
    pallas_call x1, Pallas kernels, first_blocks(): pl.pallas_call(functools.partial(first_kernel, ranges), out_shape=[jax.Sh...  13.5 us
    all_to_all x1, starting transfers between devices, per_device(): lax.all_to_all(packed.reshape(experts, ROWS, -1), 'expert', split_axis=0,...  11.4 us
    all_to_all x1, starting transfers between devices, per_device(): lax.all_to_all(back, 'expert', split_axis=0, concat_axis=0, tiled=True)  10.7 us
    pallas_call x2, Pallas kernels, last_block(): pl.pallas_call(functools.partial(last_kernel, ranges), out_shape=jax.Shap...  8.6 us
  transfers between devices with their start and end apart: 13, of which 10 were waited for; matrix products, arithmetic and copies ran while one was open for 1% of the time, Pallas kernels for 15%

profile of v11, /device:TPU:24, one launch (start us, length us, event | category | flops | bytes accessed | tf_op | source)
XLA Modules:
  0.0 213.3 jit_solution(2863128760668169581)
XLA Ops:
  0.6 3.2 %weights.1 = (bf16[3840,256]{1,0:T(8,128)(2,1)}, bf16[3840,256]{1,0:T(8,128)(2,1)}) custom-call(s32[1]{0:T(128)} %bitcast.1.core_ref, bf16[5120,256]{1,0:T(8,128)(2,1)} %bitcast.37, bf16[5120,256]{1,0:T(8,128)(2,1)} %bitcast.38, bf16[256,5120]{1,0:T(8,128)(2,1)} %bitcast.39), custom_call_target="tpu_custom_call" | custom-call | bytes 11796480 | tf_op jit(solution)/shard_map/weights/pallas_call | solution.py:185
  3.9 2.0 collective-permute-start
  5.9 0.1 collective-permute-start.1
  6.0 5.0 %pack.1 = bf16[256,7680]{1,0:T(8,128)(2,1)} custom-call(s32[1,128]{1,0:T(1,128)} %bitcast.32, bf16[128,5120]{1,0:T(8,128)(2,1)} %x_hbm.1, bf16[128,5120]{1,0:T(8,128)(2,1)} %out_grad_ref.1), custom_call_target="tpu_custom_call" | custom-call | flops 1006632960 | bytes 6553600 | tf_op jit(solution)/shard_map/pack/pallas_call | solution.py:112
  11.0 11.4 %all-to-all-start = ((bf16[32,8,7680]{2,1,0:T(8,128)(2,1)}), bf16[32,8,7680]{2,1,0:T(8,128)(2,1)}, u32[]{:S(2)}, u32[]{:S(2)}) async-start(bf16[32,8,7680]{2,1,0:T(8,128)(2,1)} %bitcast.35), calls=%async_computation | async-start | bytes 7864320 | tf_op jit(solution)/shard_map/all_to_all | solution.py:569
  22.4 1.5 collective-permute-start.2
  23.9 0.6 collective-permute-start.3
  24.5 25.4 %collective-permute-done.up_hbm = bf16[3840,256]{1,0:T(8,128)(2,1)S(1)} collective-permute-done((bf16[3840,256]{1,0:T(8,128)(2,1)}, bf16[3840,256]{1,0:T(8,128)(2,1)S(1)}, u32[]{:S(2)}, u32[]{:S(2)}) %collective-permute-start) | collective-permute-done | bytes 1966112 | tf_op jit(solution)/shard_map/ppermute | solution.py:562
  49.9 0.0 copy-start.3
  49.9 3.3 %collective-permute-done.1.down_hbm = bf16[3840,256]{1,0:T(8,128)(2,1)} collective-permute-done((bf16[3840,256]{1,0:T(8,128)(2,1)}, bf16[3840,256]{1,0:T(8,128)(2,1)}, u32[]{:S(2)}, u32[]{:S(2)}) %collective-permute-start.1) | collective-permute-done | bytes 1966112 | tf_op jit(solution)/shard_map/ppermute | solution.py:563
  53.2 0.0 copy-done.3
  53.2 2.7 %far.3 = (bf16[2304,256]{1,0:T(8,128)(2,1)}, bf16[2304,256]{1,0:T(8,128)(2,1)}) custom-call(bf16[3840,256]{1,0:T(8,128)(2,1)} %copy-done.3, bf16[3840,256]{1,0:T(8,128)(2,1)} %collective-permute-done.1.down_hbm), custom_call_target="tpu_custom_call" | custom-call | flops 62000001024 | tf_op jit(solution)/shard_map/far/pallas_call | solution.py:223
  56.0 1.2 collective-permute-start.4
  57.2 0.9 collective-permute-start.5
  58.1 34.0 %collective-permute-done.2 = bf16[3840,256]{1,0:T(8,128)(2,1)} collective-permute-done((bf16[3840,256]{1,0:T(8,128)(2,1)}, bf16[3840,256]{1,0:T(8,128)(2,1)}, u32[]{:S(2)}, u32[]{:S(2)}) %collective-permute-start.2) | collective-permute-done | bytes 1966112 | tf_op jit(solution)/shard_map/ppermute | solution.py:564
  92.1 3.2 %collective-permute-done.3 = bf16[3840,256]{1,0:T(8,128)(2,1)} collective-permute-done((bf16[3840,256]{1,0:T(8,128)(2,1)}, bf16[3840,256]{1,0:T(8,128)(2,1)}, u32[]{:S(2)}, u32[]{:S(2)}) %collective-permute-start.3) | collective-permute-done | bytes 1966112 | tf_op jit(solution)/shard_map/ppermute | solution.py:565
  95.3 2.4 %far.2 = (bf16[1536,256]{1,0:T(8,128)(2,1)}, bf16[1536,256]{1,0:T(8,128)(2,1)}) custom-call(bf16[3840,256]{1,0:T(8,128)(2,1)} %copy-done.3, bf16[3840,256]{1,0:T(8,128)(2,1)} %collective-permute-done.1.down_hbm), custom_call_target="tpu_custom_call" | custom-call | flops 1000 | tf_op jit(solution)/shard_map/far/pallas_call | solution.py:223
  97.7 15.6 %all-to-all-done = bf16[32,8,7680]{2,1,0:T(8,128)(2,1)} async-done(((bf16[32,8,7680]{2,1,0:T(8,128)(2,1)}), bf16[32,8,7680]{2,1,0:T(8,128)(2,1)}, u32[]{:S(2)}, u32[]{:S(2)}) %all-to-all-start) | async-done | bytes 3932192 | tf_op jit(solution)/shard_map/all_to_all | solution.py:569
  113.3 0.0 copy-start.5
  113.3 0.0 copy-start.4
  113.3 3.7 %unpack.1 = (bf16[192,5120]{1,0:T(8,128)(2,1)S(1)}, bf16[192,5120]{1,0:T(8,128)(2,1)S(1)}) custom-call(bf16[256,7680]{1,0:T(8,128)(2,1)} %bitcast.8.rows_hbm), custom_call_target="tpu_custom_call" | custom-call | flops 1000 | bytes 1000 | tf_op jit(solution)/shard_map/unpack/pallas_call | solution.py:347
  117.0 0.0 collective-permute-done.4
  117.0 0.4 collective-permute-done.5
  117.4 0.0 collective-permute-start.8
  117.4 0.5 collective-permute-start.9
  118.0 0.0 copy-done.5
  118.0 1.2 collective-permute-start.6
  119.2 0.0 copy-done.4
  119.2 0.8 collective-permute-start.7
  120.0 1.4 collective-permute-done.8.refs_1_.refs_0_
  121.4 2.8 %collective-permute-done.9.refs_3_.refs_1_ = bf16[192,5120]{1,0:T(8,128)(2,1)S(1)} collective-permute-done((bf16[192,5120]{1,0:T(8,128)(2,1)S(1)}, bf16[192,5120]{1,0:T(8,128)(2,1)S(1)}, u32[]{:S(2)}, u32[]{:S(2)}) %collective-permute-start.9) | collective-permute-done | bytes 1966112 | tf_op jit(solution)/shard_map/ppermute | solution.py:582
  124.2 13.5 %first.1 = (bf16[192,5120]{1,0:T(8,128)(2,1)S(1)}, bf16[192,5120]{1,0:T(8,128)(2,1)S(1)}, f32[192,128]{1,0:T(8,128)S(1)}, f32[192,128]{1,0:T(8,128)S(1)}) custom-call(bf16[192,5120]{1,0:T(8,128)(2,1)S(1)} %get-tuple-element.41.refs_0_, bf16[192,5120]{1,0:T(8,128)(2,1)S(1)} %collective-permute-done.8.refs_1_.refs_0_, ...), custom_call_target="tpu_custom_call" | custom-call | flops 1000 | bytes 1000 | tf_op jit(solution)/shard_map/first/pallas_call | solution.py:406
  137.8 0.0 collective-permute-done.6
  137.8 1.9 collective-permute-done.7
  139.6 4.3 %last.3 = bf16[192,5248]{1,0:T(8,128)(2,1)S(1)} custom-call(bf16[192,5120]{1,0:T(8,128)(2,1)S(1)} %collective-permute-done.8.refs_1_.refs_0_, bf16[192,5120]{1,0:T(8,128)(2,1)S(1)} %collective-permute-done.9.refs_3_.refs_1_, bf16[18,128,256]{2,1,0:T(8,128)(2,1)S(1)} %bitcast.23, bf16[12,128,256]{2,1,0:T(8,128)(2,1)S(1)} %bitcast.27, ...), custom_call_target="tpu_custom_call" | custom-call | flops 1000 | bytes 1000 | tf_op jit(solution)/shard_map/last/pallas_call | solution.py:455
  143.9 0.3 collective-permute-start.10
  144.3 4.3 %last.2.a_ref = bf16[192,5248]{1,0:T(8,128)(2,1)S(1)} custom-call(bf16[192,5120]{1,0:T(8,128)(2,1)S(1)} %get-tuple-element.41.refs_0_, bf16[192,5120]{1,0:T(8,128)(2,1)S(1)} %get-tuple-element.42.refs_2_.refs_1_, bf16[18,128,256]{2,1,0:T(8,128)(2,1)S(1)} %bitcast.24, bf16[12,128,256]{2,1,0:T(8,128)(2,1)S(1)} %bitcast.28, bf16[12,128,256]{2,1,0:T(8,128)(2,1)S(1)} %bitcast.30, ...), custom_call_target="tpu_custom_call" | custom-call | flops 1000 | bytes 1000 | tf_op jit(solution)/shard_map/last/pallas_call | solution.py:455
  148.6 0.0 collective-permute-done.10.b_ref
  148.6 2.6 %add_pack.1 = bf16[256,3968]{1,0:T(8,128)(2,1)} custom-call(bf16[192,5248]{1,0:T(8,128)(2,1)S(1)} %last.2.a_ref, bf16[192,5248]{1,0:T(8,128)(2,1)S(1)} %collective-permute-done.10.b_ref), custom_call_target="tpu_custom_call" | custom-call | flops 754974720 | bytes 6045696 | tf_op jit(solution)/shard_map/add_pack/pallas_call | solution.py:497
  151.2 0.0 copy-start
  151.2 10.7 %all-to-all-start.1 = ((bf16[32,8,3968]{2,1,0:T(8,128)(2,1)}), bf16[32,8,3968]{2,1,0:T(8,128)(2,1)S(1)}, u32[]{:S(2)}, u32[]{:S(2)}) async-start(bf16[32,8,3968]{2,1,0:T(8,128)(2,1)} %bitcast.19), calls=%async_computation.1 | async-start | bytes 4063232 | tf_op jit(solution)/shard_map/all_to_all | solution.py:596
  161.9 0.0 copy-done
  161.9 0.0 copy-start.1
  161.9 0.0 copy-start.2
  162.0 1.8 multiply_reduce_fusion
  163.7 47.4 %all-to-all-done.1 = bf16[32,8,3968]{2,1,0:T(8,128)(2,1)S(1)} async-done(((bf16[32,8,3968]{2,1,0:T(8,128)(2,1)}), bf16[32,8,3968]{2,1,0:T(8,128)(2,1)S(1)}, u32[]{:S(2)}, u32[]{:S(2)}) %all-to-all-start.1) | async-done | bytes 2031648 | tf_op jit(solution)/shard_map/all_to_all | solution.py:596
  211.2 0.0 copy-done.1
  211.2 0.0 copy-done.2
  211.2 2.1 combine.1
Async XLA Ops:
  3.9 46.0 %collective-permute-start = (bf16[3840,256]{1,0:T(8,128)(2,1)}, bf16[3840,256]{1,0:T(8,128)(2,1)S(1)}, u32[]{:S(2)}, u32[]{:S(2)}) collective-permute-start(bf16[3840,256]{1,0:T(8,128)(2,1)} %get-tuple-element.47), channel_id=1, source_target_pairs={{0,2},{2,4},{4,6},{6,0},{1,3},{3,5},{5,7},{7,1},{8,10},{10,12},{12... | collective-permute-start | bytes 5898248 | tf_op jit(solution)/shard_map/ppermute | solution.py:562
  5.9 47.3 %collective-permute-start.1 = (bf16[3840,256]{1,0:T(8,128)(2,1)}, bf16[3840,256]{1,0:T(8,128)(2,1)}, u32[]{:S(2)}, u32[]{:S(2)}) collective-permute-start(bf16[3840,256]{1,0:T(8,128)(2,1)} %get-tuple-element.31), channel_id=1, source_target_pairs={{0,6},{2,0},{4,2},{6,4},{1,7},{3,1},{5,3},{7,5},{8,14},{10,8},{12,... | collective-permute-start | bytes 5898248 | tf_op jit(solution)/shard_map/ppermute | solution.py:563
  11.0 102.4 %all-to-all-start = ((bf16[32,8,7680]{2,1,0:T(8,128)(2,1)}), bf16[32,8,7680]{2,1,0:T(8,128)(2,1)}, u32[]{:S(2)}, u32[]{:S(2)}) async-start(bf16[32,8,7680]{2,1,0:T(8,128)(2,1)} %bitcast.35), calls=%async_computation | async-start | bytes 7864320 | tf_op jit(solution)/shard_map/all_to_all | solution.py:569
  22.4 69.7 %collective-permute-start.2 = (bf16[3840,256]{1,0:T(8,128)(2,1)}, bf16[3840,256]{1,0:T(8,128)(2,1)}, u32[]{:S(2)}, u32[]{:S(2)}) collective-permute-start(bf16[3840,256]{1,0:T(8,128)(2,1)} %get-tuple-element.31), channel_id=1, source_target_pairs={{0,2},{2,4},{4,6},{6,0},{1,3},{3,5},{5,7},{7,1},{8,10},{10,12},{12... | collective-permute-start | bytes 5898248 | tf_op jit(solution)/shard_map/ppermute | solution.py:564
  23.9 71.4 %collective-permute-start.3 = (bf16[3840,256]{1,0:T(8,128)(2,1)}, bf16[3840,256]{1,0:T(8,128)(2,1)}, u32[]{:S(2)}, u32[]{:S(2)}) collective-permute-start(bf16[3840,256]{1,0:T(8,128)(2,1)} %get-tuple-element.47), channel_id=1, source_target_pairs={{0,6},{2,0},{4,2},{6,4},{1,7},{3,1},{5,3},{7,5},{8,14},{10,8},{12,... | collective-permute-start | bytes 5898248 | tf_op jit(solution)/shard_map/ppermute | solution.py:565
  49.9 3.3 %copy-start.3 = (bf16[3840,256]{1,0:T(8,128)(2,1)}, bf16[3840,256]{1,0:T(8,128)(2,1)S(1)}, u32[]{:S(2)}) copy-start(bf16[3840,256]{1,0:T(8,128)(2,1)S(1)} %collective-permute-done.up_hbm) | copy-start | bytes 5898244
  56.0 61.1 %collective-permute-start.4 = (bf16[2304,256]{1,0:T(8,128)(2,1)}, bf16[2304,256]{1,0:T(8,128)(2,1)S(1)}, u32[]{:S(2)}, u32[]{:S(2)}) collective-permute-start(bf16[2304,256]{1,0:T(8,128)(2,1)} %get-tuple-element.39), channel_id=1, source_target_pairs={{0,2},{2,4},{4,6},{6,0},{1,3},{3,5},{5,7},{7,1},{8,10},{10,12},{12... | collective-permute-start | bytes 3538952 | tf_op jit(solution)/shard_map/ppermute | solution.py:574
  57.2 60.2 %collective-permute-start.5 = (bf16[2304,256]{1,0:T(8,128)(2,1)}, bf16[2304,256]{1,0:T(8,128)(2,1)S(1)}, u32[]{:S(2)}, u32[]{:S(2)}) collective-permute-start(bf16[2304,256]{1,0:T(8,128)(2,1)} %get-tuple-element.40), channel_id=1, source_target_pairs={{0,6},{2,0},{4,2},{6,4},{1,7},{3,1},{5,3},{7,5},{8,14},{10,8},{12,... | collective-permute-start | bytes 3538952 | tf_op jit(solution)/shard_map/ppermute | solution.py:575
  113.3 4.6 %copy-start.5 = (bf16[1536,256]{1,0:T(8,128)(2,1)S(1)}, bf16[1536,256]{1,0:T(8,128)(2,1)}, u32[]{:S(2)}) copy-start(bf16[1536,256]{1,0:T(8,128)(2,1)} %get-tuple-element.44) | copy-start | bytes 2359300
  113.3 5.8 %copy-start.4 = (bf16[1536,256]{1,0:T(8,128)(2,1)S(1)}, bf16[1536,256]{1,0:T(8,128)(2,1)}, u32[]{:S(2)}) copy-start(bf16[1536,256]{1,0:T(8,128)(2,1)} %get-tuple-element.45) | copy-start | bytes 2359300
  117.4 4.0 %collective-permute-start.8 = (bf16[192,5120]{1,0:T(8,128)(2,1)S(1)}, bf16[192,5120]{1,0:T(8,128)(2,1)S(1)}, u32[]{:S(2)}, u32[]{:S(2)}) collective-permute-start(bf16[192,5120]{1,0:T(8,128)(2,1)S(1)} %get-tuple-element.41.refs_0_), channel_id=1, source_target_pairs={{0,1},{1,0},{2,3},{3,2},{4,5},{5,4},{6,7},{7,6},{8,9},{9,8},{10,11... | collective-permute-start | bytes 5898248 | tf_op jit(solution)/shard_map/ppermute | solution.py:582
  117.4 6.8 %collective-permute-start.9 = (bf16[192,5120]{1,0:T(8,128)(2,1)S(1)}, bf16[192,5120]{1,0:T(8,128)(2,1)S(1)}, u32[]{:S(2)}, u32[]{:S(2)}) collective-permute-start(bf16[192,5120]{1,0:T(8,128)(2,1)S(1)} %get-tuple-element.42.refs_2_.refs_1_), channel_id=1, source_target_pairs={{0,1},{1,0},{2,3},{3,2},{4,5},{5,4},{6,7},{7,6},{8,9},{9,8},{10,11... | collective-permute-start | bytes 5898248 | tf_op jit(solution)/shard_map/ppermute | solution.py:582
  118.0 19.8 %collective-permute-start.6 = (bf16[1536,256]{1,0:T(8,128)(2,1)S(1)}, bf16[1536,256]{1,0:T(8,128)(2,1)S(1)}, u32[]{:S(2)}, u32[]{:S(2)}) collective-permute-start(bf16[1536,256]{1,0:T(8,128)(2,1)S(1)} %copy-done.5), channel_id=1, source_target_pairs={{0,2},{2,4},{4,6},{6,0},{1,3},{3,5},{5,7},{7,1},{8,10},{10,12},{12... | collective-permute-start | bytes 2359304 | tf_op jit(solution)/shard_map/ppermute | solution.py:579
  119.2 20.5 %collective-permute-start.7 = (bf16[1536,256]{1,0:T(8,128)(2,1)S(1)}, bf16[1536,256]{1,0:T(8,128)(2,1)S(1)}, u32[]{:S(2)}, u32[]{:S(2)}) collective-permute-start(bf16[1536,256]{1,0:T(8,128)(2,1)S(1)} %copy-done.4), channel_id=1, source_target_pairs={{0,6},{2,0},{4,2},{6,4},{1,7},{3,1},{5,3},{7,5},{8,14},{10,8},{12,... | collective-permute-start | bytes 2359304 | tf_op jit(solution)/shard_map/ppermute | solution.py:580
  143.9 4.6 %collective-permute-start.10 = (bf16[192,5248]{1,0:T(8,128)(2,1)S(1)}, bf16[192,5248]{1,0:T(8,128)(2,1)S(1)}, u32[]{:S(2)}, u32[]{:S(2)}) collective-permute-start(bf16[192,5248]{1,0:T(8,128)(2,1)S(1)} %last.3), channel_id=1, source_target_pairs={{0,1},{1,0},{2,3},{3,2},{4,5},{5,4},{6,7},{7,6},{8,9},{9,8},{10,11... | collective-permute-start | bytes 6045704 | tf_op jit(solution)/shard_map/ppermute | solution.py:593
  151.2 10.7 %copy-start = (bf16[128,5120]{1,0:T(8,128)(2,1)S(1)}, bf16[128,5120]{1,0:T(8,128)(2,1)}, u32[]{:S(2)}) copy-start(bf16[128,5120]{1,0:T(8,128)(2,1)} %out_grad_ref.1) | copy-start | bytes 3932164
  151.2 59.9 %all-to-all-start.1 = ((bf16[32,8,3968]{2,1,0:T(8,128)(2,1)}), bf16[32,8,3968]{2,1,0:T(8,128)(2,1)S(1)}, u32[]{:S(2)}, u32[]{:S(2)}) async-start(bf16[32,8,3968]{2,1,0:T(8,128)(2,1)} %bitcast.19), calls=%async_computation.1 | async-start | bytes 4063232 | tf_op jit(solution)/shard_map/all_to_all | solution.py:596
  161.9 49.2 %copy-start.1 = (s32[128,1]{0,1:T(1,128)S(1)}, s32[128,1]{0,1:T(1,128)}, u32[]{:S(2)}) copy-start(s32[128,1]{0,1:T(1,128)} %param.10) | copy-start | bytes 1540
  161.9 49.2 %copy-start.2 = (f32[128]{0:T(128)S(1)}, f32[128]{0:T(128)}, u32[]{:S(2)}) copy-start(f32[128]{0:T(128)} %param.9) | copy-start | bytes 1540
